TPU v7x, 128 devices: a whole 4x4x4 slice. The times are simulated.
128 devices in a mesh: lang: 8 (over y, core), pair: 16 (over x, z).
Axes of the slice: x: 4, y: 4, z: 4, core: 2. Of those that a mesh axis runs over, the one named last changes fastest.
Arguments:
- sentences: bfloat16 [512, 128, 1024], P(('lang', 'pair')), may hold values from -16 to 16
- cotangent: bfloat16 [512, 128, 1024], P(('lang', 'pair')), may hold values from -6 to 6
- w_query: bfloat16 [1024, 1024], replicated, may hold values from -0.1875 to 0.1875
- w_key: bfloat16 [1024, 1024], replicated, may hold values from -0.1875 to 0.1875
- w_value: bfloat16 [1024, 1024], replicated, may hold values from -0.1875 to 0.1875
- send_rows: int32 [128, 8, 1], P(('lang', 'pair')), may hold values from 0 to 3
- pair_src: int32 [128, 16], P(('lang', 'pair')), may hold values from 0 to 3
- pair_slot: int32 [128, 16], P(('lang', 'pair')), may hold values from 0 to 7
- pair_valid: int32 [128, 16], P(('lang', 'pair')), may hold values 0 or 1
Outputs:
- attended: bfloat16 [512, 128, 1024], P(('lang', 'pair'))
- grad_sentences: bfloat16 [512, 128, 1024], P(('lang', 'pair'))
- grad_wq: bfloat16 [1024, 1024], replicated
- grad_wk: bfloat16 [1024, 1024], replicated
- grad_wv: bfloat16 [1024, 1024], replicated
All inputs are finite; a program needn't handle non-finite values. No bound on the sum of `pair_valid` on one device may be relied on, other than what follows from the above.
Results may differ from a plain program's by a relative error of at most 0.015.
The roundings to bfloat16 on the way count: a program that leaves them out, or rounds other values in their place, can miss the bound.
Values may be sent and summed in bfloat16 or wider, within the bound.
No kernel may reach another device: no remote copies, remote signals or barrier semaphores. Data moves between devices by JAX's collectives and lax.ppermute only.
A program may use at most 128 MiB of HBM per device.

v0:
```python
import jax
import jax.numpy as jnp
from jax import lax
from jax.sharding import PartitionSpec as P

HEADS = 16


def attend_block(q_rows, k_rows, v_rows, g_rows, valid, heads):
    count, length, width = q_rows.shape
    size = width // heads
    scale = size ** (-0.5)
    qh = q_rows.reshape(count, length, heads, size)
    kh = k_rows.reshape(count, length, heads, size)
    vh = v_rows.reshape(count, length, heads, size)
    mult = valid.astype(jnp.float32)[:, None, None, None]
    gh = (
        g_rows.reshape(count, length, heads, size) * valid.astype(jnp.bfloat16)[:, None, None, None]
    )
    scores = jnp.einsum("bqhd,bkhd->bhqk", qh, kh, preferred_element_type=jnp.float32) * scale
    scores = scores - jnp.max(scores, axis=-1, keepdims=True)
    prob = jnp.exp(scores)
    prob = prob / jnp.sum(prob, axis=-1, keepdims=True)
    prob_b = prob.astype(jnp.bfloat16)
    outp = jnp.einsum("bhqk,bkhd->bqhd", prob_b, vh, preferred_element_type=jnp.float32) * mult
    dvalue = jnp.einsum("bhqk,bqhd->bkhd", prob_b, gh, preferred_element_type=jnp.float32)
    dprob = jnp.einsum("bqhd,bkhd->bhqk", gh, vh, preferred_element_type=jnp.float32)
    dscore = prob * (dprob - jnp.sum(prob * dprob, axis=-1, keepdims=True)) * scale
    dscore = dscore.astype(jnp.bfloat16)
    dquery = jnp.einsum("bhqk,bkhd->bqhd", dscore, kh, preferred_element_type=jnp.float32)
    dkey = jnp.einsum("bhqk,bqhd->bkhd", dscore, qh, preferred_element_type=jnp.float32)
    shape = (count, length, width)
    return (outp.reshape(shape), dquery.reshape(shape), dkey.reshape(shape), dvalue.reshape(shape))


def project(rows, weight):
    return (
        jnp.dot(rows.reshape(-1, rows.shape[-1]), weight, preferred_element_type=jnp.float32)
        .astype(jnp.bfloat16)
        .reshape(rows.shape)
    )


def body(sentences, cotangent, w_query, w_key, w_value, send_rows, pair_src, pair_slot, pair_valid):
    sent_dev, length, width = sentences.shape
    n_lang = lax.axis_size("lang")
    n_pair = lax.axis_size("pair")
    cap = send_rows.shape[2]
    slots = n_lang * cap
    listed = send_rows[0].reshape(-1)
    outgoing = jnp.take(sentences, listed, axis=0).reshape(n_lang, cap, length, width)
    received = lax.all_to_all(outgoing, "lang", split_axis=0, concat_axis=0, tiled=True).reshape(
        slots, length, width
    )
    queries = project(sentences, w_query)
    keys = project(received, w_key)
    values = project(received, w_value)
    local_src = pair_src[0]
    pslot = pair_slot[0]
    valid = pair_valid[0]
    block = 4
    zeros_s = jnp.zeros((sent_dev, length, width), jnp.float32)
    zeros_t = jnp.zeros((slots, length, width), jnp.float32)

    def step(i, acc):
        out_acc, dq_acc, dk_acc, dv_acc = acc
        lo = i * block
        locs = lax.dynamic_slice_in_dim(local_src, lo, block)
        chosen = lax.dynamic_slice_in_dim(pslot, lo, block)
        flags = lax.dynamic_slice_in_dim(valid, lo, block)
        outp, dquery, dkey, dvalue = attend_block(
            queries[locs], keys[chosen], values[chosen], cotangent[locs], flags, HEADS
        )
        return (
            out_acc.at[locs].add(outp),
            dq_acc.at[locs].add(dquery),
            dk_acc.at[chosen].add(dkey),
            dv_acc.at[chosen].add(dvalue),
        )

    out_acc, dq_acc, dk_acc, dv_acc = lax.fori_loop(
        0, pair_src.shape[1] // block, step, (zeros_s, zeros_s, zeros_t, zeros_t)
    )
    dq_b = dq_acc.astype(jnp.bfloat16).reshape(-1, width)
    dk_b = dk_acc.astype(jnp.bfloat16).reshape(-1, width)
    dv_b = dv_acc.astype(jnp.bfloat16).reshape(-1, width)
    grad_src = jnp.dot(dq_b, w_query.T, preferred_element_type=jnp.float32).reshape(
        sent_dev, length, width
    )
    dxt = jnp.dot(dk_b, w_key.T, preferred_element_type=jnp.float32) + jnp.dot(
        dv_b, w_value.T, preferred_element_type=jnp.float32
    )
    returned = lax.all_to_all(
        dxt.reshape(n_lang, cap, length, width), "lang", split_axis=0, concat_axis=0, tiled=True
    )
    grad_total = grad_src.at[listed].add(returned.reshape(slots, length, width))
    contract = (((0,), (0,)), ((), ()))
    gwq = lax.dot_general(
        sentences.reshape(-1, width), dq_b, contract, preferred_element_type=jnp.float32
    )
    recv_flat = received.reshape(-1, width)
    gwk = lax.dot_general(recv_flat, dk_b, contract, preferred_element_type=jnp.float32)
    gwv = lax.dot_general(recv_flat, dv_b, contract, preferred_element_type=jnp.float32)
    factor = 1.0 / (sent_dev * n_lang * n_pair * length) ** 0.5
    total_q, total_k, total_v = lax.psum((gwq, gwk, gwv), ("lang", "pair"))
    grad_wq = (total_q * factor).astype(jnp.bfloat16)
    grad_wk = (total_k * factor).astype(jnp.bfloat16)
    grad_wv = (total_v * factor).astype(jnp.bfloat16)
    return (
        out_acc.astype(jnp.bfloat16),
        grad_total.astype(jnp.bfloat16),
        grad_wq,
        grad_wk,
        grad_wv,
    )


def solution(mesh):
    in_specs = (
        P(("lang", "pair"), None, None),
        P(("lang", "pair"), None, None),
        P(),
        P(),
        P(),
        P(("lang", "pair"), None, None),
        P(("lang", "pair"), None),
        P(("lang", "pair"), None),
        P(("lang", "pair"), None),
    )
    out_specs = (P(("lang", "pair"), None, None), P(("lang", "pair"), None, None), P(), P(), P())
    return jax.shard_map(body, mesh=mesh, in_specs=in_specs, out_specs=out_specs, check_vma=False)
```

profile of v0, /device:TPU:1, one launch (start us, length us, event | category | flops | bytes accessed | tf_op | source)
XLA Modules:
  0.0 674.8 jit_solution(6130148172438716841)
XLA Ops:
  15.1 6.1 all-to-all-start
  25.0 22.6 %all-to-all-done = bf16[8,1,128,1024]{3,2,1,0:T(8,128)(2,1)} async-done(((bf16[8,1,128,1024]{3,2,1,0:T(8,128)(2,1)}), bf16[8,1,128,1024]{3,2,1,0:T(8,128)(2,1)}, u32[]{:S(2)}, u32[]{:S(2)}) %all-to-all-start) | async-done | bytes 2097184 | tf_op jit(solution)/shard_map/all_to_all | solution.py:52
  47.6 5.9 convolution_convert_fusion.1
  53.5 5.3 convolution_convert_fusion
  66.9 347.6 %while.19 = (s32[]{:T(128)}, f32[4,128,1024]{2,1,0:T(8,128)}, f32[4,128,1024]{2,1,0:T(8,128)}, f32[8,128,1024]{2,1,0:T(8,128)}, f32[8,128,1024]{2,1,0:T(8,128)},...) while((s32[]{:T(128)}, f32[4,128,1024]{2,1,0:T(8,128)}, ...), condition=%wide.region_8.9_spmd, body=%wide.region_0.8_spmd.sunk | while | flops 831015296 | bytes 117613112 | solution.py:81
  82.5 5.1 fusion.93
  87.7 4.2 convolution_multiply_fusion.2
  94.7 4.6 scatter_fusion
  108.5 8.8 %fusion.95 = f32[4,16,64,128]{3,2,1,0:T(8,128)} fusion(bf16[4,128,16,64]{1,3,2,0:T(8,128)(2,1)} %bitcast.108, f32[4,16,128,128]{2,3,1,0:T(8,128)} %fusion.94, f32[4,16,128,128]{2,3,1,0:T(8,128)} %get-tuple-element.348, f32[4,16,128]{2,1,0:T(8,128)S(1)} %get-tuple-element.349), kind=kOutput, calls=%fused_computation.19.clone.1 | convolution fusion | flops 141566080 | bytes 11567104 | tf_op jit(solution)/shard_map/while/body/eval_jaxpr/bhqk,bkhd->bqhd/dot_general | solution.py:30
  120.2 4.6 scatter_fusion.1
  124.8 8.5 %fusion.96 = f32[4,16,64,128]{3,2,1,0:T(8,128)} fusion(bf16[4,128,16,64]{1,3,2,0:T(8,128)(2,1)S(1)} %bitcast.106, f32[4,16,128,128]{2,3,1,0:T(8,128)} %fusion.94, f32[4,16,128,128]{2,3,1,0:T(8,128)} %get-tuple-element.348, f32[4,16,128]{2,1,0:T(8,128)S(1)} %get-tuple-element.349), kind=kOutput, calls=%fused_computation.18.clone.1 | convolution fusion | flops 141566080 | bytes 11567104 | tf_op jit(solution)/shard_map/while/body/eval_jaxpr/bhqk,bqhd->bkhd/dot_general | solution.py:31
  136.2 4.8 scatter_fusion.2
  141.0 5.1 fusion.97
  149.0 4.9 scatter_fusion.3
  169.3 5.1 fusion.93
  174.4 4.2 convolution_multiply_fusion.2
  181.5 4.6 scatter_fusion
  195.3 8.8 %fusion.95 = f32[4,16,64,128]{3,2,1,0:T(8,128)} fusion(bf16[4,128,16,64]{1,3,2,0:T(8,128)(2,1)} %bitcast.108, f32[4,16,128,128]{2,3,1,0:T(8,128)} %fusion.94, f32[4,16,128,128]{2,3,1,0:T(8,128)} %get-tuple-element.348, f32[4,16,128]{2,1,0:T(8,128)S(1)} %get-tuple-element.349), kind=kOutput, calls=%fused_computation.19.clone.1 | convolution fusion | flops 141566080 | bytes 11567104 | tf_op jit(solution)/shard_map/while/body/eval_jaxpr/bhqk,bkhd->bqhd/dot_general | solution.py:30
  206.9 4.6 scatter_fusion.1
  211.6 8.5 %fusion.96 = f32[4,16,64,128]{3,2,1,0:T(8,128)} fusion(bf16[4,128,16,64]{1,3,2,0:T(8,128)(2,1)S(1)} %bitcast.106, f32[4,16,128,128]{2,3,1,0:T(8,128)} %fusion.94, f32[4,16,128,128]{2,3,1,0:T(8,128)} %get-tuple-element.348, f32[4,16,128]{2,1,0:T(8,128)S(1)} %get-tuple-element.349), kind=kOutput, calls=%fused_computation.18.clone.1 | convolution fusion | flops 141566080 | bytes 11567104 | tf_op jit(solution)/shard_map/while/body/eval_jaxpr/bhqk,bqhd->bkhd/dot_general | solution.py:31
  222.9 4.8 scatter_fusion.2
  227.8 5.1 fusion.97
  235.8 4.8 scatter_fusion.3
  256.0 5.1 fusion.93
  268.3 4.7 scatter_fusion
  282.1 8.8 %fusion.95 = f32[4,16,64,128]{3,2,1,0:T(8,128)} fusion(bf16[4,128,16,64]{1,3,2,0:T(8,128)(2,1)} %bitcast.108, f32[4,16,128,128]{2,3,1,0:T(8,128)} %fusion.94, f32[4,16,128,128]{2,3,1,0:T(8,128)} %get-tuple-element.348, f32[4,16,128]{2,1,0:T(8,128)S(1)} %get-tuple-element.349), kind=kOutput, calls=%fused_computation.19.clone.1 | convolution fusion | flops 141566080 | bytes 11567104 | tf_op jit(solution)/shard_map/while/body/eval_jaxpr/bhqk,bkhd->bqhd/dot_general | solution.py:30
  293.8 4.6 scatter_fusion.1
  298.4 8.5 %fusion.96 = f32[4,16,64,128]{3,2,1,0:T(8,128)} fusion(bf16[4,128,16,64]{1,3,2,0:T(8,128)(2,1)S(1)} %bitcast.106, f32[4,16,128,128]{2,3,1,0:T(8,128)} %fusion.94, f32[4,16,128,128]{2,3,1,0:T(8,128)} %get-tuple-element.348, f32[4,16,128]{2,1,0:T(8,128)S(1)} %get-tuple-element.349), kind=kOutput, calls=%fused_computation.18.clone.1 | convolution fusion | flops 141566080 | bytes 11567104 | tf_op jit(solution)/shard_map/while/body/eval_jaxpr/bhqk,bqhd->bkhd/dot_general | solution.py:31
  309.8 4.8 scatter_fusion.2
  314.6 5.1 fusion.97
  322.6 4.8 scatter_fusion.3
  342.8 5.1 fusion.93
  355.1 4.6 scatter_fusion
  368.8 8.8 %fusion.95 = f32[4,16,64,128]{3,2,1,0:T(8,128)} fusion(bf16[4,128,16,64]{1,3,2,0:T(8,128)(2,1)} %bitcast.108, f32[4,16,128,128]{2,3,1,0:T(8,128)} %fusion.94, f32[4,16,128,128]{2,3,1,0:T(8,128)} %get-tuple-element.348, f32[4,16,128]{2,1,0:T(8,128)S(1)} %get-tuple-element.349), kind=kOutput, calls=%fused_computation.19.clone.1 | convolution fusion | flops 141566080 | bytes 11567104 | tf_op jit(solution)/shard_map/while/body/eval_jaxpr/bhqk,bkhd->bqhd/dot_general | solution.py:30
  380.5 4.6 scatter_fusion.1
  385.1 8.5 %fusion.96 = f32[4,16,64,128]{3,2,1,0:T(8,128)} fusion(bf16[4,128,16,64]{1,3,2,0:T(8,128)(2,1)S(1)} %bitcast.106, f32[4,16,128,128]{2,3,1,0:T(8,128)} %fusion.94, f32[4,16,128,128]{2,3,1,0:T(8,128)} %get-tuple-element.348, f32[4,16,128]{2,1,0:T(8,128)S(1)} %get-tuple-element.349), kind=kOutput, calls=%fused_computation.18.clone.1 | convolution fusion | flops 141566080 | bytes 11567104 | tf_op jit(solution)/shard_map/while/body/eval_jaxpr/bhqk,bqhd->bkhd/dot_general | solution.py:31
  396.5 5.0 scatter_fusion.2
  401.4 5.1 fusion.97
  409.4 5.0 scatter_fusion.3
  423.7 5.9 fusion.39
  429.7 5.9 fusion.40
  439.7 4.3 convolution_add_fusion
  444.1 6.5 all-to-all-start.1
  453.6 4.2 fusion.32
  457.8 58.1 %all-to-all-done.1 = f32[8,1,128,1024]{3,2,1,0:T(8,128)} async-done(((f32[8,1,128,1024]{3,2,1,0:T(8,128)}), f32[8,1,128,1024]{3,2,1,0:T(8,128)}, u32[]{:S(2)}, u32[]{:S(2)}) %all-to-all-start.1) | async-done | bytes 4194336 | tf_op jit(solution)/shard_map/all_to_all | solution.py:93
  515.9 9.0 %scatter_fusion.4 = f32[4,128,1024]{2,1,0:T(8,128)} fusion(f32[4,128,1024]{2,1,0:T(8,128)} %fusion.32, s32[8]{0:T(128)S(1)} %copy-done.15, f32[8,128,1024]{2,1,0:T(8,128)} %bitcast.29), kind=kCustom, calls=%fused_computation.9 | custom fusion | flops 1048576 | bytes 12582944 | tf_op jit(solution)/shard_map/scatter-add | solution.py:96
  527.7 117.6 %all-reduce.3.cloned.1.call-done = (f32[1024,1024]{0,1:T(8,128)}, f32[1024,1024]{0,1:T(8,128)}, f32[1024,1024]{0,1:T(8,128)}) async-done(((f32[1024,1024]{0,1:T(8,128)}, f32[1024,1024]{0,1:T(8,128)}, f32[1024,1024]{0,1:T(8,128)}), (f32[1024,1024]{0,1:T(8,128)}, f32[1024,1024]{0,1:T(8,128)}, f32[1024,1024]{0,1:T(8,128)})) %all-reduce.3.cloned.1.call-update) | async-done | bytes 12582928 | tf_op jit(solution)/shard_map/psum | solution.py:105
  653.3 6.8 %multiply_convert_fusion.1 = (bf16[1024,1024]{0,1:T(8,128)(2,1)}, bf16[1024,1024]{0,1:T(8,128)(2,1)}) fusion(f32[1024,1024]{0,1:T(8,128)} %get-tuple-element.257, f32[1024,1024]{0,1:T(8,128)} %get-tuple-element.256), kind=kLoop, calls=%fused_computation.45 | loop fusion | flops 4194304 | bytes 12582912 | tf_op jit(solution)/shard_map/convert_element_type | solution.py:108
  (138 shorter events, 207.9 us)
Async XLA Ops:
  7.2 46.3 %copy-start = (bf16[1024,1024]{1,0:T(8,128)(2,1)S(1)}, bf16[1024,1024]{1,0:T(8,128)(2,1)}, u32[]{:S(2)}) copy-start(bf16[1024,1024]{1,0:T(8,128)(2,1)} %param.14) | copy-start | bytes 6291460
  8.0 0.7 copy-start.14
  15.1 6.1 copy-start.6
  15.1 32.5 %all-to-all-start = ((bf16[8,1,128,1024]{3,2,1,0:T(8,128)(2,1)}), bf16[8,1,128,1024]{3,2,1,0:T(8,128)(2,1)}, u32[]{:S(2)}, u32[]{:S(2)}) async-start(bf16[8,1,128,1024]{3,2,1,0:T(8,128)(2,1)} %bitcast_select_fusion), calls=%async_computation | async-start | bytes 4194304 | tf_op jit(solution)/shard_map/all_to_all | solution.py:52
  21.2 624.1 %all-reduce.3.cloned.1.call-start = ((), (), s32[]{:S(2)}) async-start(), calls=%async_computation.2 | async-start | bytes 25165824 | tf_op jit(solution)/shard_map/psum | solution.py:105
  64.4 2.5 copy-start.11
  64.4 2.5 copy-start.12
  64.4 2.5 copy-start.13
  120.2 4.6 copy-start.5
  136.2 4.8 copy-start.1
  206.9 4.6 copy-start.5
  222.9 4.8 copy-start.1
  293.8 4.6 copy-start.5
  309.8 4.8 copy-start.1
  380.5 4.6 copy-start.5
  396.5 5.0 copy-start.1
  414.4 3.4 copy-start.2
  417.1 6.6 copy-start.8
  417.9 2.3 copy-start.3
  417.9 2.6 copy-start.7
  418.2 11.5 %copy-start.9 = (bf16[8,128,1024]{2,1,0:T(8,128)(2,1)}, bf16[8,128,1024]{2,1,0:T(8,128)(2,1)S(1)}, u32[]{:S(2)}) copy-start(bf16[8,128,1024]{2,1,0:T(8,128)(2,1)S(1)} %convert_element_type.67) | copy-start | bytes 6291460
  435.6 4.1 copy-start.10
  435.6 4.1 copy-start.16
  444.1 71.8 %all-to-all-start.1 = ((f32[8,1,128,1024]{3,2,1,0:T(8,128)}), f32[8,1,128,1024]{3,2,1,0:T(8,128)}, u32[]{:S(2)}, u32[]{:S(2)}) async-start(f32[8,1,128,1024]{3,2,1,0:T(8,128)} %bitcast.111), calls=%async_computation.1 | async-start | bytes 8388608 | tf_op jit(solution)/shard_map/all_to_all | solution.py:93
  450.5 3.0 copy-start.4
  453.6 62.3 %copy-start.15 = (s32[8]{0:T(128)S(1)}, s32[8]{0:T(128)}, u32[]{:S(2)}) copy-start(s32[8]{0:T(128)} %copy-done.14) | copy-start | bytes 100
Sparse Core Ops, SparseCore 0:
  435.7 209.5 all-reduce.2
where the time goes:
time: 678 us; the launch traced here: 675 us
  waiting for transfers between devices  198 us (29%)
  matrix products  185 us (27%)
  local copies, waits for them, and re-layouts  154 us (23%)
  other arithmetic  110 us (16%)
  between operations  14.1 us (2%)
  starting transfers between devices  12.6 us (2%)
    psum x1, waiting for transfers between devices, body(): total_q, total_k, total_v = lax.psum((gwq, gwk, gwv), ('lang', 'pair'))  118 us
    all_to_all x1, waiting for transfers between devices, body(): lax.all_to_all(dxt.reshape(n_lang, cap, length, width), 'lang', split_axi...  58.1 us
    dot_general x4, matrix products, attend_block(): jnp.einsum('bhqk,bkhd->bqhd', dscore, kh, preferred_element_type=jnp.floa...  35.1 us
    dot_general x4, matrix products, attend_block(): jnp.einsum('bhqk,bqhd->bkhd', dscore, qh, preferred_element_type=jnp.floa...  34 us
    all_to_all x1, waiting for transfers between devices, body(): lax.all_to_all(outgoing, 'lang', split_axis=0, concat_axis=0, tiled=True)  22.6 us
    gather x8, local copies, waits for them, and re-layouts, step(): keys[chosen]  21.8 us
    gather x8, local copies, waits for them, and re-layouts, step(): cotangent[locs]  20.5 us
    sub x4, matrix products, attend_block(): scores = scores - jnp.max(scores, axis=-1, keepdims=True)  20.5 us
  transfers between devices with their start and end apart: 3, of which 3 were waited for; matrix products, arithmetic and copies ran while one was open for 5% of the time, Pallas kernels for 0%

commit v1 on v0

v1 whole, which is shorter than its diff:
```python
import functools
import jax
import jax.numpy as jnp
from jax import lax
from jax.experimental import pallas as pl
from jax.experimental.pallas import tpu as pltpu
from jax.sharding import PartitionSpec as P

SIZE = 64
BF, F32 = jnp.bfloat16, jnp.float32
NT = (((1,), (1,)), ((), ()))


def mm(a, b):
    return jnp.dot(a, b, preferred_element_type=F32)


def mm_nt(a, b):
    return lax.dot_general(a, b, NT, preferred_element_type=F32)


def attend_kernel(src_ref, slot_ref, valid_ref, x_ref, r_ref, c_ref, wq_ref, wk_ref, wv_ref,
                  att_ref, dq_ref, dk_ref, dv_ref,
                  mult, q2, g2, k_s, v_s, kt, vt, ot, dqt, dk_acc, dv_acc, *, n_src, n_slot, length, width, unroll):
    heads = width // 128
    n_pairs = src_ref.shape[-1]
    for i in range(n_src * n_slot):
        mult[i] = 0
    for j in range(n_pairs):
        at = slot_ref[0, j] * n_src + src_ref[0, j]
        mult[at] = mult[at] + valid_ref[0, j]
    low = lax.broadcasted_iota(jnp.int32, (length, 128), 1) < SIZE
    zero = jnp.zeros((length, 128), BF)

    for s in range(n_src):
        rows = pl.ds(s * length, length)
        q = (mm(x_ref[rows, :], wq_ref[...]).astype(BF) * BF(0.125)).astype(BF)
        for h in range(heads):
            cols = slice(h * 128, (h + 1) * 128)
            qh = q[:, cols]
            gh = c_ref[rows, cols]
            q2[s, h, :length, :] = jnp.where(low, qh, zero)
            q2[s, h, length:, :] = jnp.where(low, zero, qh)
            g2[s, h, :length, :] = jnp.where(low, gh, zero)
            g2[s, h, length:, :] = jnp.where(low, zero, gh)

    def project(t, _):
        rows = pl.ds(pl.multiple_of(t * length, length), length)
        k = mm(r_ref[rows, :], wk_ref[...]).astype(BF)
        v = mm(r_ref[rows, :], wv_ref[...]).astype(BF)
        k_s[t] = k
        v_s[t] = v
        kt[t] = k.T
        vt[t] = v.T
        return 0

    lax.fori_loop(0, n_slot, project, 0)
    ot[...] = jnp.zeros_like(ot)
    dqt[...] = jnp.zeros_like(dqt)
    dk_acc[...] = jnp.zeros_like(dk_acc)
    dv_acc[...] = jnp.zeros_like(dv_acc)

    def combo(i, _):
        count = mult[i]

        @pl.when(count > 0)
        def _():
            t = i // n_src
            s = i % n_src
            m = count.astype(F32)

            def one(h):
                off = h * 128 if isinstance(h, int) else pl.multiple_of(h * 128, 128)
                cols = pl.ds(off, 128)
                kh = k_s[t, :, cols]
                vh = v_s[t, :, cols]
                qd = q2[s, h]
                gd = g2[s, h]
                st = mm_nt(kh, qd)
                dp = mm_nt(vh, gd)
                e = jnp.exp(st - jnp.max(st, axis=0, keepdims=True))
                inv = 1.0 / jnp.sum(e, axis=0, keepdims=True)
                delta = jnp.sum(e * dp, axis=0, keepdims=True) * inv
                p = e * (inv * m)
                pb = p.astype(BF)
                ds = (p * (dp - delta)).astype(BF)
                dv_acc[t, :, cols] += mm(pb, gd)
                dk_acc[t, :, cols] += mm(ds, qd)
                for half in range(2):
                    rows = pl.ds(off + half * SIZE, SIZE)
                    part = slice(half * length, (half + 1) * length)
                    ot[s, rows, :] += mm(vt[t, rows, :], pb[:, part])
                    dqt[s, rows, :] += mm(kt[t, rows, :], ds[:, part])

            if unroll >= heads:
                for h in range(heads):
                    one(h)
            else:
                def group(b, _):
                    for u in range(unroll):
                        one(b * unroll + u)
                    return 0
                lax.fori_loop(0, heads // unroll, group, 0)
        return 0

    lax.fori_loop(0, n_src * n_slot, combo, 0)
    for s in range(n_src):
        rows = slice(s * length, (s + 1) * length)
        att_ref[rows, :] = ot[s].T.astype(BF)
        dq_ref[rows, :] = (dqt[s].T * 0.125).astype(BF)
    for t in range(n_slot):
        rows = slice(t * length, (t + 1) * length)
        dk_ref[rows, :] = dk_acc[t].astype(BF)
        dv_ref[rows, :] = dv_acc[t].astype(BF)


def attend(src, slot, valid, x, r, c, wq, wk, wv, *, width, at=0, length=128, unroll=4):
    n_src, n_slot = x.shape[0] // length, r.shape[0] // length
    heads = width // 128
    smem = pl.BlockSpec(memory_space=pltpu.SMEM)
    whole = lambda a: pl.BlockSpec(a.shape, lambda i: (0, 0))
    cols = lambda a: pl.BlockSpec((a.shape[0], width), lambda i: (0, at))
    out = lambda n: jax.ShapeDtypeStruct((n * length, width), BF)
    outb = lambda n: pl.BlockSpec((n * length, width), lambda i: (0, 0))
    d = x.shape[1]
    macs = (n_src + 2 * n_slot) * length * d * width + 12 * 6 * length * length * width
    return pl.pallas_call(
        functools.partial(attend_kernel, n_src=n_src, n_slot=n_slot, length=length, width=width, unroll=unroll),
        grid=(1,),
        in_specs=[smem, smem, smem, whole(x), whole(r), cols(c), cols(wq), cols(wk), cols(wv)],
        out_specs=[outb(n_src), outb(n_src), outb(n_slot), outb(n_slot)],
        out_shape=[out(n_src), out(n_src), out(n_slot), out(n_slot)],
        scratch_shapes=[
            pltpu.SMEM((n_src * n_slot,), jnp.int32),
            pltpu.VMEM((n_src, heads, 2 * length, 128), BF),
            pltpu.VMEM((n_src, heads, 2 * length, 128), BF),
            pltpu.VMEM((n_slot, length, width), BF),
            pltpu.VMEM((n_slot, length, width), BF),
            pltpu.VMEM((n_slot, width, length), BF),
            pltpu.VMEM((n_slot, width, length), BF),
            pltpu.VMEM((n_src, width, length), F32),
            pltpu.VMEM((n_src, width, length), F32),
            pltpu.VMEM((n_slot, length, width), F32),
            pltpu.VMEM((n_slot, length, width), F32),
        ],
        compiler_params=pltpu.CompilerParams(vmem_limit_bytes=56 * 2**20),
        cost_estimate=pl.CostEstimate(flops=2 * macs * 4, bytes_accessed=8 * 2**20, transcendentals=0),
        name="attend",
    )(src, slot, valid, x, r, c, wq, wk, wv)


def body(sentences, cotangent, w_query, w_key, w_value, send_rows, pair_src, pair_slot, pair_valid):
    sent_dev, length, width = sentences.shape
    n_lang = lax.axis_size("lang")
    n_pair = lax.axis_size("pair")
    slots = n_lang * send_rows.shape[2]
    listed = send_rows[0].reshape(-1)
    outgoing = jnp.take(sentences, listed, axis=0)
    received = lax.all_to_all(outgoing, "lang", split_axis=0, concat_axis=0, tiled=True)
    x = sentences.reshape(-1, width)
    r = received.reshape(-1, width)
    c = cotangent.reshape(-1, width)
    attended, dq_b, dk_b, dv_b = attend(
        pair_src, pair_slot, pair_valid, x, r, c, w_query, w_key, w_value, width=width, length=length
    )
    grad_src = jnp.dot(dq_b, w_query.T, preferred_element_type=F32).reshape(sent_dev, length, width)
    dxt = jnp.dot(dk_b, w_key.T, preferred_element_type=F32) + jnp.dot(dv_b, w_value.T, preferred_element_type=F32)
    returned = lax.all_to_all(
        dxt.astype(BF).reshape(slots, length, width), "lang", split_axis=0, concat_axis=0, tiled=True
    )
    grad_total = grad_src.at[listed].add(returned.astype(F32))
    contract = (((0,), (0,)), ((), ()))
    gwq = lax.dot_general(x, dq_b, contract, preferred_element_type=F32)
    gwk = lax.dot_general(r, dk_b, contract, preferred_element_type=F32)
    gwv = lax.dot_general(r, dv_b, contract, preferred_element_type=F32)
    factor = 1.0 / (sent_dev * n_lang * n_pair * length) ** 0.5
    grads = lax.psum((gwq, gwk, gwv), ("lang", "pair"))
    grads = tuple((g * factor).astype(BF) for g in grads)
    return (attended.reshape(sentences.shape), grad_total.astype(BF)) + grads


def solution(mesh):
    split3, split2 = P(("lang", "pair"), None, None), P(("lang", "pair"), None)
    in_specs = (split3, split3, P(), P(), P(), split3, split2, split2, split2)
    out_specs = (split3, split3, P(), P(), P())
    return jax.shard_map(body, mesh=mesh, in_specs=in_specs, out_specs=out_specs, check_vma=False)
```

time: 678 us -> 322 us (0.47)
  matrix products: 185 us -> 24.2 us
  local copies, waits for them, and re-layouts: 154 us -> 12.5 us
  other arithmetic: 110 us -> 21.6 us
  Pallas kernels: 0 us -> 44.9 us
  waiting for transfers between devices: 198 us -> 160 us
  blocking collectives: 0 us -> 32.4 us
    dot_general x29 -> x6, matrix products: 165 us -> 24.2 us  [the longest x1 4.65 us: body(): gwq = lax.dot_general(x, dq_b, contract, preferred_element_type=F32)]
    gather x33 -> x1, local copies, waits for them, and re-layouts: 84.8 us -> 1.91 us  [body(): outgoing = jnp.take(sentences, listed, axis=0)]
    scatter-add x17 -> x1, other arithmetic: 85 us -> 5.91 us  [body(): grad_total = grad_src.at[listed].add(returned.astype(F32))]
    reshape x16 -> x0, local copies, waits for them, and re-layouts: 46.4 us -> none  [the longest x4 11.7 us: attend_block(): outp.reshape(shape)]
    all_to_all x2 -> x1, waiting for transfers between devices: 80.7 us -> 34.8 us  [body(): lax.all_to_all(dxt.astype(BF).reshape(slots, length, width), 'lang', spli...]
    pallas_call x0 -> x1, Pallas kernels: none -> 44.9 us  [attend(): pl.pallas_call(functools.partial(attend_kernel, n_src=n_src, n_slot=n_slo...]
    all_to_all x0 -> x1, blocking collectives: none -> 32.4 us  [body(): lax.all_to_all(outgoing, 'lang', split_axis=0, concat_axis=0, tiled=True)]
    sub x4 -> x0, matrix products: 20.5 us -> none  [attend_block(): scores = scores - jnp.max(scores, axis=-1, keepdims=True)]
  transfers between devices with their start and end apart: 3 -> 2, of which waited for: 3 -> 2; matrix products, arithmetic and copies ran while one was open for 5% -> 7% of each run, Pallas kernels for 0% -> 0%
where the time goes in v1:
time: 322 us; the launch traced here: 321 us
  waiting for transfers between devices  160 us (50%)
  Pallas kernels  44.9 us (14%)
  blocking collectives  32.4 us (10%)
  matrix products  24.2 us (8%)
  other arithmetic  21.6 us (7%)
  between operations  14.1 us (4%)
  local copies, waits for them, and re-layouts  12.5 us (4%)
  starting transfers between devices  11 us (3%)
    psum x1, waiting for transfers between devices, body(): grads = lax.psum((gwq, gwk, gwv), ('lang', 'pair'))  125 us
    pallas_call x1, Pallas kernels, attend(): pl.pallas_call(functools.partial(attend_kernel, n_src=n_src, n_slot=n_slo...  44.9 us
    all_to_all x1, waiting for transfers between devices, body(): lax.all_to_all(dxt.astype(BF).reshape(slots, length, width), 'lang', spli...  34.8 us
    all_to_all x1, blocking collectives, body(): lax.all_to_all(outgoing, 'lang', split_axis=0, concat_axis=0, tiled=True)  32.4 us
    all_to_all x1, starting transfers between devices, body(): lax.all_to_all(dxt.astype(BF).reshape(slots, length, width), 'lang', spli...  11 us
    unnamed x19, local copies, waits for them, and re-layouts  10.6 us
    convert_element_type x2, other arithmetic, body(): grads = tuple(((g * factor).astype(BF) for g in grads))  8.81 us
  transfers between devices with their start and end apart: 2, of which 2 were waited for; matrix products, arithmetic and copies ran while one was open for 7% of the time, Pallas kernels for 0%

profile of v1, /device:TPU:1, one launch (start us, length us, event | category | flops | bytes accessed | tf_op | source)
XLA Modules:
  0.0 321.0 jit_solution(10270633187574628826)
XLA Ops:
  7.2 0.0 all-reduce.3.cloned.1.call-start
  7.2 0.7 fusion
  7.9 0.7 compare_and_fusion
  8.5 1.9 gather_fusion
  10.5 0.3 broadcast_select_fusion
  10.7 32.4 %all_to_all.10 = bf16[8,128,1024]{2,1,0:T(8,128)(2,1)} all-to-all(bf16[8,128,1024]{2,1,0:T(8,128)(2,1)S(1)} %broadcast_select_fusion), channel_id=1, replica_groups=mesh['lang'=8,'pair'=16] {'lang'}, dimensions={0} | all-to-all | bytes 4194304 | tf_op jit(solution)/shard_map/all_to_all | solution.py:159
  43.1 0.0 copy-start
  43.1 44.9 %attend.1 = (bf16[512,1024]{1,0:T(8,128)(2,1)}, bf16[512,1024]{1,0:T(8,128)(2,1)}, bf16[1024,1024]{1,0:T(8,128)(2,1)}, bf16[1024,1024]{1,0:T(8,128)(2,1)}) custom-call(s32[1,16]{1,0:T(1,128)} %src_ref.1, s32[1,16]{1,0:T(1,128)} %slot_ref.1, s32[1,16]{1,0:T(1,128)} %valid_ref.1, bf16[512,1024]{1,0:T(8,128)(2,1)} %bitcast.27, bf16[1024,1024]{1,0:T(8,128)(2,1)} %bitcast.29, ...), custom_call_target="tpu_custom_call" | custom-call | flops 31138512896 | bytes 8388608 | tf_op jit(solution)/shard_map/attend/pallas_call | solution.py:127
  88.0 0.0 copy-done
  88.0 0.0 copy-start.1
  88.0 0.0 copy-start.5
  88.0 4.7 %convolution_bitcast_fusion = f32[1024,1024]{0,1:T(8,128)} fusion(bf16[512,1024]{1,0:T(8,128)(2,1)} %get-tuple-element.10, bf16[512,1024]{1,0:T(8,128)(2,1)S(1)} %bitcast.28), kind=kOutput, calls=%fused_computation.6 | convolution fusion | flops 1073741824 | bytes 6291456 | tf_op jit(solution)/shard_map/dot_general | solution.py:173
  92.7 0.0 copy-done.1
  92.7 0.0 copy-done.5
  92.7 0.0 copy-start.6
  92.7 4.4 %fusion.3 = f32[1024,1024]{0,1:T(8,128)} fusion(bf16[1024,1024]{1,0:T(8,128)(2,1)S(1)} %bitcast.30, bf16[1024,1024]{1,0:T(8,128)(2,1)S(1)} %copy-done.5), kind=kOutput, calls=%fused_computation.15 | convolution fusion | flops 2147483648 | bytes 8388608 | tf_op jit(solution)/shard_map/dot_general | solution.py:174
  97.1 0.0 copy-done.6
  97.1 4.4 %fusion.4 = f32[1024,1024]{0,1:T(8,128)} fusion(bf16[1024,1024]{1,0:T(8,128)(2,1)S(1)} %bitcast.31, bf16[1024,1024]{1,0:T(8,128)(2,1)S(1)} %copy-done.6), kind=kOutput, calls=%fused_computation.16 | convolution fusion | flops 2147483648 | bytes 8388608 | tf_op jit(solution)/shard_map/dot_general | solution.py:175
  101.5 0.0 copy-start.3
  101.5 0.0 all-reduce.3.cloned.1.call-update
  101.5 1.6 copy-done.3
  103.1 0.0 copy-start.4
  103.1 0.0 copy-start.7
  103.1 4.1 %fusion.2 = f32[1024,1024]{1,0:T(8,128)S(1)} fusion(bf16[1024,1024]{1,0:T(8,128)(2,1)} %get-tuple-element.11, bf16[1024,1024]{1,0:T(8,128)(2,1)S(1)} %copy-done.3), kind=kOutput, calls=%fused_computation.14 | convolution fusion | flops 2147483648 | bytes 8388608 | tf_op jit(solution)/shard_map/dot_general | solution.py:167
  107.2 0.0 copy-done.4
  107.2 0.0 copy-done.7
  107.2 3.7 %add_convert_fusion = bf16[1024,1024]{1,0:T(8,128)(2,1)} fusion(f32[1024,1024]{1,0:T(8,128)S(1)} %fusion.2, bf16[1024,1024]{1,0:T(8,128)(2,1)S(1)} %copy-done.7, bf16[1024,1024]{1,0:T(8,128)(2,1)S(1)} %copy-done.4), kind=kOutput, calls=%fused_computation.5 | convolution fusion | flops 2149580800 | bytes 10485760 | tf_op jit(solution)/shard_map/dot_general | solution.py:167
  110.9 0.0 copy-start.2
  110.9 11.0 %all-to-all-start.1 = ((bf16[8,128,1024]{2,1,0:T(8,128)(2,1)}), bf16[8,128,1024]{2,1,0:T(8,128)(2,1)}, u32[]{:S(2)}, u32[]{:S(2)}) async-start(bf16[8,128,1024]{2,1,0:T(8,128)(2,1)} %bitcast.8), calls=%async_computation.1 | async-start | bytes 4194304 | tf_op jit(solution)/shard_map/all_to_all | solution.py:168
  121.9 0.0 copy-done.2
  121.9 2.9 fusion.1
  124.9 34.8 %all-to-all-done.1 = bf16[8,128,1024]{2,1,0:T(8,128)(2,1)} async-done(((bf16[8,128,1024]{2,1,0:T(8,128)(2,1)}), bf16[8,128,1024]{2,1,0:T(8,128)(2,1)}, u32[]{:S(2)}, u32[]{:S(2)}) %all-to-all-start.1) | async-done | bytes 2097184 | tf_op jit(solution)/shard_map/all_to_all | solution.py:168
  159.7 4.1 %convert_element_type.19 = f32[8,128,1024]{2,1,0:T(8,128)} convert(bf16[8,128,1024]{2,1,0:T(8,128)(2,1)} %all-to-all-done.1) | non-fusion elementwise | flops 1048576 | bytes 6291456 | tf_op jit(solution)/shard_map/convert_element_type | solution.py:171
  163.8 5.9 %scatter_fusion = f32[4,128,1024]{2,1,0:T(8,128)S(1)} fusion(f32[4,128,1024]{2,1,0:T(8,128)S(1)} %bitcast.26, s32[8]{0:T(128)S(1)} %fusion, f32[8,128,1024]{2,1,0:T(8,128)} %convert_element_type.19), kind=kCustom, calls=%fused_computation.1 | custom fusion | flops 1048576 | bytes 12582944 | tf_op jit(solution)/shard_map/scatter-add | solution.py:171
  169.8 1.1 convert_element_type.20
  170.9 125.4 %all-reduce.3.cloned.1.call-done = (f32[1024,1024]{0,1:T(8,128)}, f32[1024,1024]{0,1:T(8,128)}, f32[1024,1024]{0,1:T(8,128)}) async-done(((f32[1024,1024]{0,1:T(8,128)}, f32[1024,1024]{0,1:T(8,128)}, f32[1024,1024]{0,1:T(8,128)}), (f32[1024,1024]{0,1:T(8,128)}, f32[1024,1024]{0,1:T(8,128)}, f32[1024,1024]{0,1:T(8,128)})) %all-reduce.3.cloned.1.call-update) | async-done | bytes 12582928 | tf_op jit(solution)/shard_map/psum | solution.py:177
  296.3 2.8 multiply_convert_fusion.2
  299.1 2.6 copy.21
  301.6 6.0 %multiply_convert_fusion = (bf16[1024,1024]{0,1:T(8,128)(2,1)S(1)}, bf16[1024,1024]{0,1:T(8,128)(2,1)}) fusion(f32[1024,1024]{0,1:T(8,128)} %get-tuple-element.25, f32[1024,1024]{0,1:T(8,128)} %get-tuple-element.24), kind=kLoop, calls=%fused_computation.2 | loop fusion | flops 4194304 | bytes 12582912 | tf_op jit(solution)/shard_map/convert_element_type | solution.py:178
  307.7 3.9 %copy.22 = bf16[1024,1024]{1,0:T(8,128)(2,1)} copy(bf16[1024,1024]{0,1:T(8,128)(2,1)} %get-tuple-element.27) | data formatting | bytes 4194304
  311.6 2.5 copy.23
  (1 shorter events, 0.0 us)
Async XLA Ops:
  7.2 289.1 %all-reduce.3.cloned.1.call-start = ((), (), s32[]{:S(2)}) async-start(), calls=%async_computation.2 | async-start | bytes 25165824 | tf_op jit(solution)/shard_map/psum | solution.py:177
  43.1 45.0 %copy-start = (bf16[4,128,1024]{2,1,0:T(8,128)(2,1)S(1)}, bf16[4,128,1024]{2,1,0:T(8,128)(2,1)}, u32[]{:S(2)}) copy-start(bf16[4,128,1024]{2,1,0:T(8,128)(2,1)} %param.9) | copy-start | bytes 3145732
  88.0 4.7 %copy-start.1 = (bf16[8,128,1024]{2,1,0:T(8,128)(2,1)S(1)}, bf16[8,128,1024]{2,1,0:T(8,128)(2,1)}, u32[]{:S(2)}) copy-start(bf16[8,128,1024]{2,1,0:T(8,128)(2,1)} %all_to_all.10) | copy-start | bytes 6291460
  88.0 4.7 %copy-start.5 = (bf16[1024,1024]{1,0:T(8,128)(2,1)S(1)}, bf16[1024,1024]{1,0:T(8,128)(2,1)}, u32[]{:S(2)}) copy-start(bf16[1024,1024]{1,0:T(8,128)(2,1)} %get-tuple-element.11) | copy-start | bytes 6291460
  92.7 4.4 %copy-start.6 = (bf16[1024,1024]{1,0:T(8,128)(2,1)S(1)}, bf16[1024,1024]{1,0:T(8,128)(2,1)}, u32[]{:S(2)}) copy-start(bf16[1024,1024]{1,0:T(8,128)(2,1)} %get-tuple-element.12) | copy-start | bytes 6291460
  101.5 1.6 copy-start.3
  103.1 4.1 %copy-start.4 = (bf16[1024,1024]{1,0:T(8,128)(2,1)S(1)}, bf16[1024,1024]{1,0:T(8,128)(2,1)}, u32[]{:S(2)}) copy-start(bf16[1024,1024]{1,0:T(8,128)(2,1)} %wv_ref.1) | copy-start | bytes 6291460
  103.1 4.1 %copy-start.7 = (bf16[1024,1024]{1,0:T(8,128)(2,1)S(1)}, bf16[1024,1024]{1,0:T(8,128)(2,1)}, u32[]{:S(2)}) copy-start(bf16[1024,1024]{1,0:T(8,128)(2,1)} %get-tuple-element.12) | copy-start | bytes 6291460
  110.9 11.0 %copy-start.2 = (bf16[512,1024]{1,0:T(8,128)(2,1)S(1)}, bf16[512,1024]{1,0:T(8,128)(2,1)}, u32[]{:S(2)}) copy-start(bf16[512,1024]{1,0:T(8,128)(2,1)} %get-tuple-element.10) | copy-start | bytes 3145732
  110.9 48.7 %all-to-all-start.1 = ((bf16[8,128,1024]{2,1,0:T(8,128)(2,1)}), bf16[8,128,1024]{2,1,0:T(8,128)(2,1)}, u32[]{:S(2)}, u32[]{:S(2)}) async-start(bf16[8,128,1024]{2,1,0:T(8,128)(2,1)} %bitcast.8), calls=%async_computation.1 | async-start | bytes 4194304 | tf_op jit(solution)/shard_map/all_to_all | solution.py:168
Sparse Core Ops, SparseCore 0:
  101.7 194.5 all-reduce.2

commit v2 on v1

v2 whole, which is shorter than its diff:
```python
import functools
import jax
import jax.numpy as jnp
from jax import lax
from jax.experimental import pallas as pl
from jax.experimental.pallas import tpu as pltpu
from jax.sharding import PartitionSpec as P

SIZE = 64
BF, F32 = jnp.bfloat16, jnp.float32
NT = (((1,), (1,)), ((), ()))


def mm(a, b):
    return jnp.dot(a, b, preferred_element_type=F32)


def mm_nt(a, b):
    return lax.dot_general(a, b, NT, preferred_element_type=F32)


def attend_kernel(src_ref, slot_ref, valid_ref, x_ref, r_ref, c_ref, wq_ref, wk_ref, wv_ref,
                  att_ref, dq_ref, dk_ref, dv_ref, gw_ref,
                  mult, xt, rt, q2, g2, k_s, v_s, kt, vt, ot, dqt, dk_acc, dv_acc,
                  *, n_src, n_slot, length, width):
    heads = width // 128
    n_pairs = src_ref.shape[-1]
    first = pl.program_id(0) == 0

    @pl.when(first)
    def _():
        for i in range(n_src * n_slot):
            mult[i] = 0
        for j in range(n_pairs):
            at = slot_ref[0, j] * n_src + src_ref[0, j]
            mult[at] = mult[at] + valid_ref[0, j]
        for s in range(n_src):
            xt[:, s * length:(s + 1) * length] = x_ref[s * length:(s + 1) * length, :].T
        for t in range(n_slot):
            rt[:, t * length:(t + 1) * length] = r_ref[t * length:(t + 1) * length, :].T

    low = lax.broadcasted_iota(jnp.int32, (n_src * length, 128), 1) < SIZE
    zero = jnp.zeros((n_src * length, 128), BF)
    block = min(256, width)

    for n in range(0, width, block):
        q = mm(x_ref[...], wq_ref[:, n:n + block]).astype(BF) * BF(0.125)
        for h in range(n // 128, (n + block) // 128):
            qh = q[:, h * 128 - n:(h + 1) * 128 - n]
            gh = c_ref[:, h * 128:(h + 1) * 128]
            for ref, rows in ((q2, qh), (g2, gh)):
                top = jnp.where(low, rows, zero)
                bot = jnp.where(low, zero, rows)
                for s in range(n_src):
                    ref[s, h, :length, :] = top[s * length:(s + 1) * length]
                    ref[s, h, length:, :] = bot[s * length:(s + 1) * length]

    half = n_slot // 2
    for n in range(0, width, block):
        cols = slice(n, n + block)
        for w_ref, nat, tra in ((wk_ref, k_s, kt), (wv_ref, v_s, vt)):
            for lo in range(0, n_slot, half):
                k = mm(r_ref[lo * length:(lo + half) * length, :], w_ref[:, cols]).astype(BF)
                for t in range(half):
                    rows = k[t * length:(t + 1) * length]
                    nat[lo + t, :, cols] = rows
                    tra[lo + t, cols, :] = rows.T
    ot[...] = jnp.zeros_like(ot)
    dqt[...] = jnp.zeros_like(dqt)
    dk_acc[...] = jnp.zeros_like(dk_acc)
    dv_acc[...] = jnp.zeros_like(dv_acc)

    def combo(i, _):
        count = mult[i]

        @pl.when(count > 0)
        def _():
            t = i // n_src
            s = i % n_src
            m = count.astype(F32)

            def scores(h):
                cols = slice(h * 128, (h + 1) * 128)
                return mm_nt(k_s[t, :, cols], q2[s, h]), mm_nt(v_s[t, :, cols], g2[s, h])

            def soft(st, dp):
                e = jnp.exp(st - jnp.max(st, axis=0, keepdims=True))
                inv = 1.0 / jnp.sum(e, axis=0, keepdims=True)
                delta = jnp.sum(e * dp, axis=0, keepdims=True) * inv
                p = e * (inv * m)
                return p.astype(BF), (p * (dp - delta)).astype(BF)

            def grads(h, pb, ds):
                cols = slice(h * 128, (h + 1) * 128)
                dv = mm(pb, g2[s, h])
                dk = mm(ds, q2[s, h])
                o = mm(vt[t, cols, :], pb)
                dq = mm(kt[t, cols, :], ds)
                dv_acc[t, :, cols] += dv
                dk_acc[t, :, cols] += dk
                for half in range(2):
                    rows = slice(h * 128 + half * SIZE, h * 128 + (half + 1) * SIZE)
                    own = slice(half * SIZE, (half + 1) * SIZE)
                    part = slice(half * length, (half + 1) * length)
                    ot[s, rows, :] += o[own, part]
                    dqt[s, rows, :] += dq[own, part]

            ready = [scores(h) for h in range(min(2, heads))]
            waiting = []
            for h in range(heads):
                if h + 2 < heads:
                    ready.append(scores(h + 2))
                waiting.append((h,) + soft(*ready.pop(0)))
                if h > 0:
                    grads(*waiting.pop(0))
            grads(*waiting.pop(0))
        return 0

    lax.fori_loop(0, n_src * n_slot, combo, 0)
    for s in range(n_src):
        rows = slice(s * length, (s + 1) * length)
        att_ref[rows, :] = ot[s].T.astype(BF)
        dq_ref[rows, :] = (dqt[s].T * 0.125).astype(BF)
    for t in range(n_slot):
        rows = slice(t * length, (t + 1) * length)
        dk_ref[rows, :] = dk_acc[t].astype(BF)
        dv_ref[rows, :] = dv_acc[t].astype(BF)
    groups, _, each, _ = gw_ref.shape
    for n in range(0, width, block):
        cols = slice(n, n + block)
        for i, (lhs, rhs) in enumerate(((xt, dq_ref), (rt, dk_ref), (rt, dv_ref))):
            for lo in range(0, groups, groups // 2):
                g = mm(lhs[lo * each:(lo + groups // 2) * each, :], rhs[:, cols]).astype(BF)
                gw_ref[lo:lo + groups // 2, i, :, cols] = g.reshape(groups // 2, each, block)


def attend(src, slot, valid, x, r, c, wq, wk, wv, *, groups, width, at=0, steps=1, length=128):
    n_src, n_slot = x.shape[0] // length, r.shape[0] // length
    heads = width // 128
    smem = pl.BlockSpec(memory_space=pltpu.SMEM)
    whole = lambda a: pl.BlockSpec(a.shape, lambda i: (0, 0))
    cols = lambda a: pl.BlockSpec((a.shape[0], width), lambda i: (0, at + i))
    out = lambda n: jax.ShapeDtypeStruct((n * length, width * steps), BF)
    outb = lambda n: pl.BlockSpec((n * length, width), lambda i: (0, i))
    d = x.shape[1]
    each = d // groups
    macs = steps * (2 * (n_src + 2 * n_slot) * length * d * width + 12 * 6 * length * length * width)
    return pl.pallas_call(
        functools.partial(attend_kernel, n_src=n_src, n_slot=n_slot, length=length, width=width),
        grid=(steps,),
        in_specs=[smem, smem, smem, whole(x), whole(r), cols(c), cols(wq), cols(wk), cols(wv)],
        out_specs=[outb(n_src), outb(n_src), outb(n_slot), outb(n_slot),
                   pl.BlockSpec((groups, 3, each, width), lambda i: (0, 0, 0, i))],
        out_shape=[out(n_src), out(n_src), out(n_slot), out(n_slot),
                   jax.ShapeDtypeStruct((groups, 3, each, width * steps), BF)],
        scratch_shapes=[
            pltpu.SMEM((n_src * n_slot,), jnp.int32),
            pltpu.VMEM((d, n_src * length), BF),
            pltpu.VMEM((d, n_slot * length), BF),
            pltpu.VMEM((n_src, heads, 2 * length, 128), BF),
            pltpu.VMEM((n_src, heads, 2 * length, 128), BF),
            pltpu.VMEM((n_slot, length, width), BF),
            pltpu.VMEM((n_slot, length, width), BF),
            pltpu.VMEM((n_slot, width, length), BF),
            pltpu.VMEM((n_slot, width, length), BF),
            pltpu.VMEM((n_src, width, length), F32),
            pltpu.VMEM((n_src, width, length), F32),
            pltpu.VMEM((n_slot, length, width), F32),
            pltpu.VMEM((n_slot, length, width), F32),
        ],
        compiler_params=pltpu.CompilerParams(vmem_limit_bytes=56 * 2**20),
        cost_estimate=pl.CostEstimate(flops=2 * macs * 4, bytes_accessed=8 * 2**20, transcendentals=0),
        name="attend",
    )(src, slot, valid, x, r, c, wq, wk, wv)


def body(sentences, cotangent, w_query, w_key, w_value, send_rows, pair_src, pair_slot, pair_valid):
    sent_dev, length, width = sentences.shape
    n_lang = lax.axis_size("lang")
    n_pair = lax.axis_size("pair")
    slots = n_lang * send_rows.shape[2]
    listed = send_rows[0].reshape(-1)
    outgoing = jnp.take(sentences, listed, axis=0, mode="clip")
    received = lax.all_to_all(outgoing, "lang", split_axis=0, concat_axis=0, tiled=True)
    x = sentences.reshape(-1, width)
    r = received.reshape(-1, width)
    c = cotangent.reshape(-1, width)
    attended, dq_b, dk_b, dv_b, grads = attend(
        pair_src, pair_slot, pair_valid, x, r, c, w_query, w_key, w_value,
        groups=n_lang, width=width, length=length,
    )
    part = lax.psum_scatter(grads.reshape(-1, width), "lang", scatter_dimension=0, tiled=True)
    grad_src = jnp.dot(dq_b, w_query.T, preferred_element_type=F32).reshape(sent_dev, length, width)
    dxt = jnp.dot(dk_b, w_key.T, preferred_element_type=F32) + jnp.dot(dv_b, w_value.T, preferred_element_type=F32)
    returned = lax.all_to_all(
        dxt.astype(BF).reshape(slots, length, width), "lang", split_axis=0, concat_axis=0, tiled=True
    )
    part, returned = lax.optimization_barrier((part, returned))
    grad_total = grad_src.at[listed].add(returned.astype(F32))
    factor = 1.0 / (sent_dev * n_lang * n_pair * length) ** 0.5
    rows = width // n_lang // n_pair
    pieces = part.reshape(3, n_pair, rows, width).transpose(1, 0, 2, 3)
    pieces = lax.all_to_all(pieces, "pair", split_axis=0, concat_axis=0, tiled=True)
    mine = (jnp.sum(pieces.astype(F32), axis=0) * factor).astype(BF)
    copies = jnp.broadcast_to(mine[None], (n_pair, 3, rows, width))
    group = lax.all_to_all(copies, "pair", split_axis=0, concat_axis=0, tiled=True)
    group = group.transpose(1, 0, 2, 3).reshape(3 * n_pair * rows, width)
    grads = lax.all_gather(group, "lang", axis=0, tiled=True).reshape(n_lang, 3, n_pair * rows, width)
    grads = tuple(grads[:, i].reshape(width, width) for i in range(3))
    return (attended.reshape(sentences.shape), grad_total.astype(BF)) + grads


def solution(mesh):
    split3, split2 = P(("lang", "pair"), None, None), P(("lang", "pair"), None)
    in_specs = (split3, split3, P(), P(), P(), split3, split2, split2, split2)
    out_specs = (split3, split3, P(), P(), P())
    return jax.shard_map(body, mesh=mesh, in_specs=in_specs, out_specs=out_specs, check_vma=False)
```

time: 322 us -> 237 us (0.74)
  waiting for transfers between devices: 160 us -> 49.6 us
  blocking collectives: 32.4 us -> 109 us
  matrix products: 24.2 us -> 9.51 us
  Pallas kernels: 44.9 us -> 32.5 us
  other arithmetic: 21.6 us -> 10.1 us
  starting transfers between devices: 11 us -> 0.08 us
    psum x1 -> x0, waiting for transfers between devices: 125 us -> none  [body(): grads = lax.psum((gwq, gwk, gwv), ('lang', 'pair'))]
    all_to_all x0 -> x3, blocking collectives: none -> 76.5 us  [the longest x1 43.2 us: body(): lax.all_to_all(dxt.astype(BF).reshape(slots, length, width), 'lang', spli...]
    all_to_all x1 -> x0, waiting for transfers between devices: 34.8 us -> none  [body(): lax.all_to_all(dxt.astype(BF).reshape(slots, length, width), 'lang', spli...]
    all_gather x0 -> x1, waiting for transfers between devices: none -> 31.6 us  [body(): lax.all_gather(group, 'lang', axis=0, tiled=True)]
    reduce_scatter x0 -> x1, waiting for transfers between devices: none -> 18 us  [body(): lax.psum_scatter(grads.reshape(-1, width), 'lang', scatter_dimension=0, t...]
    dot_general x3 -> x0, matrix products: 13.5 us -> none  [the longest x1 4.65 us: body(): gwq = lax.dot_general(x, dq_b, contract, preferred_element_type=F32)]
    pallas_call x1, Pallas kernels: 44.9 us -> 32.5 us  [attend(): pl.pallas_call(functools.partial(attend_kernel, n_src=n_src, n_slot=n_slo...]
    all_to_all x1 -> x0, starting transfers between devices: 11 us -> none  [body(): lax.all_to_all(dxt.astype(BF).reshape(slots, length, width), 'lang', spli...]
  transfers between devices with their start and end apart: 2 -> 2, of which waited for: 2 -> 2; matrix products, arithmetic and copies ran while one was open for 7% -> 8% of each run, Pallas kernels for 0% -> 0%
where the time goes in v2:
time: 237 us; the launch traced here: 236 us
  blocking collectives  109 us (46%)
  waiting for transfers between devices  49.6 us (21%)
  Pallas kernels  32.5 us (14%)
  between operations  14.2 us (6%)
  local copies, waits for them, and re-layouts  11.4 us (5%)
  other arithmetic  10.1 us (4%)
  matrix products  9.51 us (4%)
    all_to_all x1, blocking collectives, body(): lax.all_to_all(dxt.astype(BF).reshape(slots, length, width), 'lang', spli...  43.2 us
    pallas_call x1, Pallas kernels, attend(): pl.pallas_call(functools.partial(attend_kernel, n_src=n_src, n_slot=n_slo...  32.5 us
    all_to_all x1, blocking collectives, body(): lax.all_to_all(outgoing, 'lang', split_axis=0, concat_axis=0, tiled=True)  32.4 us
    all_gather x1, waiting for transfers between devices, body(): lax.all_gather(group, 'lang', axis=0, tiled=True)  31.6 us
    all_to_all x1, blocking collectives, body(): lax.all_to_all(pieces, 'pair', split_axis=0, concat_axis=0, tiled=True)  18.6 us
    reduce_scatter x1, waiting for transfers between devices, body(): lax.psum_scatter(grads.reshape(-1, width), 'lang', scatter_dimension=0, t...  18 us
    all_to_all x1, blocking collectives, body(): lax.all_to_all(copies, 'pair', split_axis=0, concat_axis=0, tiled=True)  14.7 us
    slice x1, local copies, waits for them, and re-layouts, body(): grads = tuple((grads[:, i].reshape(width, width) for i in range(3)))  5.74 us
  transfers between devices with their start and end apart: 2, of which 2 were waited for; matrix products, arithmetic and copies ran while one was open for 8% of the time, Pallas kernels for 0%

profile of v2, /device:TPU:1, one launch (start us, length us, event | category | flops | bytes accessed | tf_op | source)
XLA Modules:
  0.0 236.2 jit_solution(13176012276393953200)
XLA Ops:
  7.2 0.0 reduce-scatter.2.cloned.1.call-start
  7.2 0.7 pad_clamp_fusion
  7.9 1.9 gather_fusion
  9.8 32.4 %all_to_all.20 = bf16[8,128,1024]{2,1,0:T(8,128)(2,1)} all-to-all(bf16[8,128,1024]{2,1,0:T(8,128)(2,1)S(1)} %gather_fusion), channel_id=1, replica_groups=mesh['lang'=8,'pair'=16] {'lang'}, dimensions={0} | all-to-all | bytes 4194304 | tf_op jit(solution)/shard_map/all_to_all | solution.py:184
  42.1 32.5 %attend.1 = (bf16[512,1024]{1,0:T(8,128)(2,1)}, bf16[512,1024]{1,0:T(8,128)(2,1)}, bf16[1024,1024]{1,0:T(8,128)(2,1)}, bf16[1024,1024]{1,0:T(8,128)(2,1)}, bf16[8,3,128,1024]{3,2,1,0:T(8,128)(2,1)}) custom-call(s32[1,16]{1,0:T(1,128)} %src_ref.1, s32[1,16]{1,0:T(1,128)} %slot_ref.1, s32[1,16]{1,0:T(1,128)} %valid_ref.1, bf16[512,1024]{1,0:T(8,128)(2,1)} %bitcast.31, ...), custom_call_target="tpu_custom_call" | custom-call | flops 52613349376 | bytes 8388608 | tf_op jit(solution)/shard_map/attend/pallas_call | solution.py:148
  74.6 0.0 copy-start.2
  74.6 0.0 reduce-scatter.2.cloned.1.call-update
  74.7 0.0 all-gather.2.cloned.1.call-start
  74.7 1.5 copy-done.2
  76.2 0.0 copy-start.3
  76.2 0.0 copy-start.5
  76.2 4.1 %fusion.3 = f32[1024,1024]{1,0:T(8,128)S(1)} fusion(bf16[1024,1024]{1,0:T(8,128)(2,1)} %get-tuple-element.15, bf16[1024,1024]{1,0:T(8,128)(2,1)S(1)} %copy-done.2), kind=kOutput, calls=%fused_computation.10 | convolution fusion | flops 2147483648 | bytes 8388608 | tf_op jit(solution)/shard_map/dot_general | solution.py:194
  80.3 0.0 copy-done.3
  80.4 0.0 copy-done.5
  80.4 2.4 %add_convert_fusion = bf16[1024,1024]{1,0:T(8,128)(2,1)S(1)} fusion(f32[1024,1024]{1,0:T(8,128)S(1)} %fusion.3, bf16[1024,1024]{1,0:T(8,128)(2,1)S(1)} %copy-done.5, bf16[1024,1024]{1,0:T(8,128)(2,1)S(1)} %copy-done.3), kind=kOutput, calls=%fused_computation.2 | convolution fusion | flops 2149580800 | bytes 10485760 | tf_op jit(solution)/shard_map/dot_general | solution.py:194
  82.7 43.2 %all_to_all.21 = bf16[8,128,1024]{2,1,0:T(8,128)(2,1)} all-to-all(bf16[8,128,1024]{2,1,0:T(8,128)(2,1)S(1)} %bitcast.34), channel_id=1, replica_groups=mesh['lang'=8,'pair'=16] {'lang'}, dimensions={0} | all-to-all | bytes 4194304 | tf_op jit(solution)/shard_map/all_to_all | solution.py:195
  125.9 18.0 %reduce-scatter.2.cloned.1.call-done = bf16[384,1024]{1,0:T(8,128)(2,1)} async-done(((bf16[3072,1024]{1,0:T(8,128)(2,1)}), bf16[384,1024]{1,0:T(8,128)(2,1)}) %reduce-scatter.2.cloned.1.call-update) | async-done | bytes 786448 | tf_op jit(solution)/shard_map/reduce_scatter | solution.py:192
  143.9 1.2 copy.15
  145.1 18.6 %all_to_all.22 = bf16[16,3,8,1024]{3,2,1,0:T(8,128)(2,1)S(1)} all-to-all(bf16[16,3,8,1024]{3,2,1,0:T(8,128)(2,1)S(1)} %copy.15), channel_id=1, replica_groups=mesh['lang'=8,'pair'=16] {'pair'}, dimensions={0} | all-to-all | bytes 1572864 | tf_op jit(solution)/shard_map/all_to_all | solution.py:203
  163.7 0.1 convert_reduce_fusion
  163.8 0.1 broadcast_in_dim.12
  163.9 0.0 copy-start.1
  163.9 0.0 copy-start.4
  163.9 14.7 %all_to_all.23 = bf16[16,3,8,1024]{3,2,1,0:T(8,128)(2,1)S(1)} all-to-all(bf16[16,3,8,1024]{3,2,1,0:T(8,128)(2,1)S(1)} %broadcast_in_dim.12), channel_id=1, replica_groups=mesh['lang'=8,'pair'=16] {'pair'}, dimensions={0} | all-to-all | bytes 1572864 | tf_op jit(solution)/shard_map/all_to_all | solution.py:206
  178.6 0.9 copy.16
  179.6 0.0 all-gather.2.cloned.1.call-update
  179.6 0.0 copy-done.1
  179.6 0.0 copy-done.4
  179.6 0.0 copy-start
  179.7 3.0 %fusion.2 = f32[512,1024]{1,0:T(8,128)S(1)} fusion(bf16[512,1024]{1,0:T(8,128)(2,1)S(1)} %copy-done.4, bf16[1024,1024]{1,0:T(8,128)(2,1)} %wq_ref.1), kind=kOutput, calls=%fused_computation.9 | convolution fusion | flops 1073741824 | bytes 5242880 | tf_op jit(solution)/shard_map/dot_general | solution.py:193
  182.7 0.0 copy-done
  182.7 2.5 %convert_element_type.20 = f32[8,128,1024]{2,1,0:T(8,128)} convert(bf16[8,128,1024]{2,1,0:T(8,128)(2,1)S(1)} %copy-done) | non-fusion elementwise | flops 1048576 | bytes 6291456 | tf_op jit(solution)/shard_map/convert_element_type | solution.py:199
  185.2 5.7 %scatter_fusion = f32[4,128,1024]{2,1,0:T(8,128)S(1)} fusion(f32[4,128,1024]{2,1,0:T(8,128)S(1)} %bitcast.28, s32[8]{0:T(128)S(1)} %fusion, f32[8,128,1024]{2,1,0:T(8,128)} %convert_element_type.20), kind=kCustom, calls=%fused_computation.1 | custom fusion | flops 1048576 | bytes 12582944 | tf_op jit(solution)/shard_map/scatter-add | solution.py:199
  190.9 1.1 convert_element_type.21
  192.0 31.6 %all-gather.2.cloned.1.call-done = bf16[3072,1024]{1,0:T(8,128)(2,1)} async-done(((bf16[384,1024]{1,0:T(8,128)(2,1)}), bf16[3072,1024]{1,0:T(8,128)(2,1)}) %all-gather.2.cloned.1.call-update) | async-done | bytes 6291472 | tf_op jit(solution)/shard_map/all_gather | solution.py:208
  223.7 5.7 %fusion.1 = (bf16[8,1,128,1024]{3,2,1,0:T(8,128)(2,1)}, bf16[8,1,128,1024]{3,2,1,0:T(8,128)(2,1)}, bf16[8,1,128,1024]{3,2,1,0:T(8,128)(2,1)}) fusion(bf16[8,3,128,1024]{3,2,1,0:T(8,128)(2,1)} %bitcast.29), kind=kLoop, calls=%fused_computation.8 | loop fusion | bytes 12582912 | tf_op jit(solution)/shard_map/slice | solution.py:209
  (2 shorter events, 0.0 us)
Async XLA Ops:
  7.2 136.7 %reduce-scatter.2.cloned.1.call-start = ((), (), s32[]{:S(2)}) async-start(), calls=%async_computation.5 | async-start | bytes 7077888 | tf_op jit(solution)/shard_map/reduce_scatter | solution.py:192
  74.6 1.6 copy-start.2
  74.7 149.0 %all-gather.2.cloned.1.call-start = ((), (), s32[]{:S(2)}) async-start(), calls=%async_computation.6 | async-start | bytes 7077888 | tf_op jit(solution)/shard_map/all_gather | solution.py:208
  76.2 4.1 %copy-start.3 = (bf16[1024,1024]{1,0:T(8,128)(2,1)S(1)}, bf16[1024,1024]{1,0:T(8,128)(2,1)}, u32[]{:S(2)}) copy-start(bf16[1024,1024]{1,0:T(8,128)(2,1)} %wv_ref.1) | copy-start | bytes 6291460
  76.2 4.1 %copy-start.5 = (bf16[1024,1024]{1,0:T(8,128)(2,1)S(1)}, bf16[1024,1024]{1,0:T(8,128)(2,1)}, u32[]{:S(2)}) copy-start(bf16[1024,1024]{1,0:T(8,128)(2,1)} %get-tuple-element.16) | copy-start | bytes 6291460
  163.9 15.7 %copy-start.1 = (s32[1,8,1]{1,2,0:T(1,128)S(1)}, s32[1,8,1]{1,2,0:T(1,128)}, u32[]{:S(2)}) copy-start(s32[1,8,1]{1,2,0:T(1,128)} %param.14) | copy-start | bytes 100
  163.9 15.7 %copy-start.4 = (bf16[512,1024]{1,0:T(8,128)(2,1)S(1)}, bf16[512,1024]{1,0:T(8,128)(2,1)}, u32[]{:S(2)}) copy-start(bf16[512,1024]{1,0:T(8,128)(2,1)} %get-tuple-element.13) | copy-start | bytes 3145732
  179.6 3.0 %copy-start = (bf16[8,128,1024]{2,1,0:T(8,128)(2,1)S(1)}, bf16[8,128,1024]{2,1,0:T(8,128)(2,1)}, u32[]{:S(2)}) copy-start(bf16[8,128,1024]{2,1,0:T(8,128)(2,1)} %all_to_all.21) | copy-start | bytes 6291460
Sparse Core Ops, SparseCore 0:
  74.8 69.0 reduce-scatter.1
  179.7 43.8 all-gather.1

commit v3 on v2

v3 whole, which is shorter than its diff:
```python
import functools

import jax
import jax.numpy as jnp
from jax import lax
from jax.experimental import pallas as pl
from jax.experimental.pallas import tpu as pltpu
from jax.sharding import PartitionSpec as P

SIZE = 64
LANES = 128
BF, F32 = jnp.bfloat16, jnp.float32
NT = (((1,), (1,)), ((), ()))


def mm(a, b):
    return jnp.dot(a, b, preferred_element_type=F32)


def mm_nt(a, b):
    return lax.dot_general(a, b, NT, preferred_element_type=F32)


def attend_kernel(me_ref, src_ref, slot_ref, valid_ref, x_hbm, r_hbm, c_hbm, wq_hbm, wk_hbm, wv_hbm,
                  *rest, n_src, n_slot, length):
    outs, scratch = rest[:4 + n_slot], rest[4 + n_slot:]
    att_hbm, dq_hbm, keep_hbm, send_hbm = outs[:4]
    dx_hbm = outs[4:]
    (mult, x_ref, r_ref, c_ref, wq_ref, wk_ref, wv_ref, att_v, dq_v, gw_v, dx_v,
     xt, rt, q2, g2, k_s, v_s, kt, vt, ot, dqt, dk_acc, dv_acc, sem_in, sem_r, sem_out) = scratch
    width = x_ref.shape[1]
    heads = width // LANES
    n_pairs = src_ref.shape[-1]
    me = me_ref[0]
    block = 256

    copies = [pltpu.make_async_copy(a, b, sem_in.at[i]) for i, (a, b) in enumerate(
        ((x_hbm, x_ref), (wq_hbm, wq_ref), (c_hbm, c_ref), (wk_hbm, wk_ref), (wv_hbm, wv_ref)))]
    slots = [pltpu.make_async_copy(r_hbm.at[lax.rem(me + p, n_slot)], r_ref.at[pl.ds(p * length, length), :],
                                   sem_r.at[p]) for p in range(n_slot)]
    for c in copies[:4] + slots + copies[4:]:
        c.start()

    for i in range(n_src * n_slot):
        mult[i] = 0
    for j in range(n_pairs):
        at = lax.rem(slot_ref[0, j] + n_slot - me, n_slot) * n_src + src_ref[0, j]
        mult[at] = mult[at] + valid_ref[0, j]
    ot[...] = jnp.zeros_like(ot)
    dqt[...] = jnp.zeros_like(dqt)
    dk_acc[...] = jnp.zeros_like(dk_acc)
    dv_acc[...] = jnp.zeros_like(dv_acc)

    for c in copies[:3]:
        c.wait()
    low = lax.broadcasted_iota(jnp.int32, (n_src * length, LANES), 1) < SIZE
    zero = jnp.zeros((n_src * length, LANES), BF)
    for n in range(0, width, block):
        q = mm(x_ref[...], wq_ref[:, n:n + block]).astype(BF) * BF(0.125)
        for h in range(n // LANES, (n + block) // LANES):
            qh = q[:, h * LANES - n:(h + 1) * LANES - n]
            gh = c_ref[:, h * LANES:(h + 1) * LANES]
            for ref, rows in ((q2, qh), (g2, gh)):
                top = jnp.where(low, rows, zero)
                bot = jnp.where(low, zero, rows)
                for s in range(n_src):
                    ref[s, h, :length, :] = top[s * length:(s + 1) * length]
                    ref[s, h, length:, :] = bot[s * length:(s + 1) * length]
    for s in range(n_src):
        xt[:, s * length:(s + 1) * length] = x_ref[s * length:(s + 1) * length, :].T

    copies[3].wait()
    for c in slots:
        c.wait()
    half = n_slot // 2
    for w_ref, nat, tra in ((wk_ref, k_s, kt), (wv_ref, v_s, vt)):
        if w_ref is wv_ref:
            copies[4].wait()
        for n in range(0, width, block):
            cols = slice(n, n + block)
            for lo in range(0, n_slot, half):
                k = mm(r_ref[lo * length:(lo + half) * length, :], w_ref[:, cols]).astype(BF)
                for t in range(half):
                    rows = k[t * length:(t + 1) * length]
                    nat[lo + t, :, cols] = rows
                    tra[lo + t, cols, :] = rows.T
    for t in range(n_slot):
        rt[:, t * length:(t + 1) * length] = r_ref[t * length:(t + 1) * length, :].T

    def combo(i, _):
        count = mult[i]

        @pl.when(count > 0)
        def _():
            t = i // n_src
            s = i % n_src
            m = count.astype(F32)

            def scores(h):
                cols = slice(h * LANES, (h + 1) * LANES)
                return mm_nt(k_s[t, :, cols], q2[s, h]), mm_nt(v_s[t, :, cols], g2[s, h])

            def soft(st, dp):
                e = jnp.exp(st - jnp.max(st, axis=0, keepdims=True))
                inv = 1.0 / jnp.sum(e, axis=0, keepdims=True)
                delta = jnp.sum(e * dp, axis=0, keepdims=True) * inv
                p = e * (inv * m)
                return p.astype(BF), (p * (dp - delta)).astype(BF)

            def grads(h, pb, ds):
                cols = slice(h * LANES, (h + 1) * LANES)
                dv = mm(pb, g2[s, h])
                dk = mm(ds, q2[s, h])
                o = mm(vt[t, cols, :], pb)
                dq = mm(kt[t, cols, :], ds)
                dv_acc[t, :, cols] += dv
                dk_acc[t, :, cols] += dk
                for part in range(2):
                    rows = slice(h * LANES + part * SIZE, h * LANES + (part + 1) * SIZE)
                    own = slice(part * SIZE, (part + 1) * SIZE)
                    keys = slice(part * length, (part + 1) * length)
                    ot[s, rows, :] += o[own, keys]
                    dqt[s, rows, :] += dq[own, keys]

            ready = [scores(h) for h in range(min(2, heads))]
            waiting = []
            for h in range(heads):
                if h + 2 < heads:
                    ready.append(scores(h + 2))
                waiting.append((h,) + soft(*ready.pop(0)))
                if h > 0:
                    grads(*waiting.pop(0))
            grads(*waiting.pop(0))
        return 0

    lax.fori_loop(0, n_src * n_slot, combo, 0)

    for t in range(n_slot):
        k_s[t] = dk_acc[t].astype(BF)
        v_s[t] = dv_acc[t].astype(BF)
    for s in range(n_src):
        dq_v[s * length:(s + 1) * length, :] = (dqt[s].T * 0.125).astype(BF)
    dk = k_s[...].reshape(n_slot * length, width)
    dv = v_s[...].reshape(n_slot * length, width)

    done = []

    def out(src, dst):
        c = pltpu.make_async_copy(src, dst, sem_out.at[len(done)])
        c.start()
        done.append(c)

    _, pieces, _, each, _ = gw_v.shape
    core = lax.rem(me, 2)
    for k, dst in enumerate((send_hbm, keep_hbm)):
        base = pl.multiple_of((core if k else 1 - core) * (pieces * each), LANES)
        rows = pl.ds(base, pieces * each)
        for n in range(0, width, block):
            cols = slice(n, n + block)
            for i, (lhs, rhs) in enumerate(((xt, dq_v[:, cols]), (rt, dk[:, cols]), (rt, dv[:, cols]))):
                gw_v[k, :, i, :, cols] = mm(lhs[rows, :], rhs).astype(BF).reshape(pieces, each, block)
        out(gw_v.at[k], dst)
        if k == 0:
            out(dq_v, dq_hbm)
    for s in range(n_src):
        att_v[s * length:(s + 1) * length, :] = ot[s].T.astype(BF)
    out(att_v, att_hbm)
    for lo in range(0, n_slot, half):
        rows = slice(lo * length, (lo + half) * length)
        for n in range(0, width, block):
            cols = slice(n, n + block)
            dx_v[rows, cols] = (mm_nt(dk[rows], wk_ref[cols, :]) + mm_nt(dv[rows], wv_ref[cols, :])).astype(BF)
        for t in range(lo, lo + half):
            out(dx_v.at[pl.ds(t * length, length), :], dx_hbm[t])
    for c in done:
        c.wait()


def attend(me, src, slot, valid, x, r, c, wq, wk, wv, *, pieces):
    n_slot, length, width = r.shape
    rows = x.shape[0]
    n_src = rows // length
    each = width // 2 // pieces
    heads = width // LANES
    smem = pl.BlockSpec(memory_space=pltpu.SMEM)
    hbm = pl.BlockSpec(memory_space=pl.ANY)
    shape = jax.ShapeDtypeStruct
    vm = pltpu.VMEM
    macs = 2 * (n_src + 3 * n_slot) * length * width * width + 12 * 6 * length * length * width
    return pl.pallas_call(
        functools.partial(attend_kernel, n_src=n_src, n_slot=n_slot, length=length),
        in_specs=[smem] * 4 + [hbm] * 6,
        out_specs=[hbm] * (4 + n_slot),
        out_shape=[shape((rows, width), BF), shape((rows, width), BF),
                   shape((pieces, 3, each, width), BF), shape((pieces, 3, each, width), BF)]
        + [shape((length, width), BF)] * n_slot,
        scratch_shapes=[
            pltpu.SMEM((n_src * n_slot,), jnp.int32),
            vm((rows, width), BF), vm((n_slot * length, width), BF), vm((rows, width), BF),
            vm((width, width), BF), vm((width, width), BF), vm((width, width), BF),
            vm((rows, width), BF), vm((rows, width), BF),
            vm((2, pieces, 3, each, width), BF), vm((n_slot * length, width), BF),
            vm((width, rows), BF), vm((width, n_slot * length), BF),
            vm((n_src, heads, 2 * length, LANES), BF), vm((n_src, heads, 2 * length, LANES), BF),
            vm((n_slot, length, width), BF), vm((n_slot, length, width), BF),
            vm((n_slot, width, length), BF), vm((n_slot, width, length), BF),
            vm((n_src, width, length), F32), vm((n_src, width, length), F32),
            vm((n_slot, length, width), F32), vm((n_slot, length, width), F32),
            pltpu.SemaphoreType.DMA((5,)), pltpu.SemaphoreType.DMA((n_slot,)),
            pltpu.SemaphoreType.DMA((4 + n_slot,)),
        ],
        compiler_params=pltpu.CompilerParams(vmem_limit_bytes=60 * 2**20),
        cost_estimate=pl.CostEstimate(flops=4 * macs, bytes_accessed=20 * 2**20, transcendentals=0),
        name="attend",
    )(me, src, slot, valid, x, r, c, wq, wk, wv)


def combine_kernel(me_ref, listed_ref, dq_ref, wq_ref, *rest):
    parts, (out_ref, acc) = rest[:-2], rest[-2:]
    n_slot = len(parts)
    length = parts[0].shape[0]
    me = me_ref[0]
    block = 256
    for n in range(0, acc.shape[2], block):
        cols = slice(n, n + block)
        acc[:, :, cols] = mm_nt(dq_ref[...], wq_ref[cols, :]).reshape(acc.shape[0], length, block)
    for s, part in enumerate(parts):
        at = listed_ref[lax.rem(me + n_slot - s, n_slot)]
        acc[at] += part[...].astype(F32)
    out_ref[...] = acc[...].astype(BF)


def combine(me, listed, dq, wq, parts):
    length, width = parts[0].shape
    n_src = dq.shape[0] // length
    smem = pl.BlockSpec(memory_space=pltpu.SMEM)
    vmem = pl.BlockSpec(memory_space=pltpu.VMEM)
    return pl.pallas_call(
        combine_kernel,
        in_specs=[smem, smem] + [vmem] * (2 + len(parts)),
        out_specs=vmem,
        out_shape=jax.ShapeDtypeStruct((n_src, length, width), BF),
        scratch_shapes=[pltpu.VMEM((n_src, length, width), F32)],
        compiler_params=pltpu.CompilerParams(vmem_limit_bytes=24 * 2**20),
        cost_estimate=pl.CostEstimate(flops=2 * dq.size * width, bytes_accessed=6 * 2**20, transcendentals=0),
        name="combine",
    )(me, listed, dq, wq, *parts)


def spread_kernel(parts_ref, out_ref, *, factor):
    total = jnp.sum(parts_ref[...].astype(F32), axis=0)
    out_ref[...] = jnp.broadcast_to((total * factor).astype(BF)[None], out_ref.shape)


def spread(parts, copies, factor):
    shape = parts.shape[1:]
    grid = shape[0]
    return pl.pallas_call(
        functools.partial(spread_kernel, factor=factor),
        grid=(grid,),
        in_specs=[pl.BlockSpec((parts.shape[0], 1) + shape[1:], lambda i: (0, i, 0, 0))],
        out_specs=pl.BlockSpec((copies, 1) + shape[1:], lambda i: (0, i, 0, 0)),
        out_shape=jax.ShapeDtypeStruct((copies,) + shape, BF),
        compiler_params=pltpu.CompilerParams(vmem_limit_bytes=16 * 2**20),
        cost_estimate=pl.CostEstimate(flops=parts.size, bytes_accessed=4 * parts.size, transcendentals=0),
        name="spread",
    )(parts)


def place_kernel(half_ref, rows_hbm, *rest):
    sem = rest[-1]
    outs = rest[-4:-1]
    copies = [pltpu.make_async_copy(rows_hbm.at[:, i], out.at[half_ref[0]], sem.at[i]) for i, out in enumerate(outs)]
    for c in copies:
        c.start()
    for c in copies:
        c.wait()


def place(half, rows, into=()):
    pieces, n, each, width = rows.shape
    hbm = pl.BlockSpec(memory_space=pl.ANY)
    return pl.pallas_call(
        place_kernel,
        in_specs=[pl.BlockSpec(memory_space=pltpu.SMEM), hbm] + [hbm] * len(into),
        out_specs=[hbm] * n,
        out_shape=[jax.ShapeDtypeStruct((2, pieces, each, width), BF)] * n,
        input_output_aliases={2 + i: i for i in range(len(into))},
        scratch_shapes=[pltpu.SemaphoreType.DMA((n,))],
        cost_estimate=pl.CostEstimate(flops=0, bytes_accessed=4 * rows.size, transcendentals=0),
        name="place",
    )(half, rows, *into)


def body(sentences, cotangent, w_query, w_key, w_value, send_rows, pair_src, pair_slot, pair_valid):
    sent_dev, length, width = sentences.shape
    n_lang = lax.axis_size("lang")
    n_pair = lax.axis_size("pair")
    me = lax.axis_index("lang")
    listed = send_rows[0].reshape(-1)
    outgoing = jnp.take(sentences, listed, axis=0, mode="clip")
    received = lax.all_to_all(outgoing, "lang", split_axis=0, concat_axis=0, tiled=True)
    x = sentences.reshape(-1, width)
    c = cotangent.reshape(-1, width)
    where = me.reshape(1).astype(jnp.int32)
    attended, dq, keep, send, *dx = attend(
        where, pair_src, pair_slot, pair_valid, x, received, c, w_query, w_key, w_value, pieces=n_pair
    )
    other_core = [(i, i ^ 1) for i in range(n_lang)]
    other = lax.ppermute(send, "lang", other_core)
    back = [dx[0]]
    for s in range(1, n_lang):
        back.append(lax.ppermute(dx[s], "lang", [(i, (i + s) % n_lang) for i in range(n_lang)]))
    chip = (keep.astype(F32) + other.astype(F32)).astype(BF)
    pieces = lax.all_to_all(chip, "pair", split_axis=0, concat_axis=0, tiled=True)
    pieces, *back[1:6] = lax.optimization_barrier((pieces, *back[1:6]))
    n_y = n_lang // 2
    along_y = [[2 * y + core for y in range(n_y)] for core in range(2)]
    columns = lax.all_to_all(
        spread(pieces, n_y, 1.0), "lang", split_axis=0, concat_axis=0, axis_index_groups=along_y, tiled=True
    )
    factor = 1.0 / (sent_dev * n_lang * n_pair * length) ** 0.5
    near = lax.all_to_all(spread(columns, n_pair, factor), "pair", split_axis=0, concat_axis=0, tiled=True)
    near, *back[6:] = lax.optimization_barrier((near, *back[6:]))
    far = lax.ppermute(near, "lang", other_core)
    grad_sentences = combine(where, listed, dq, w_query, back)
    core = lax.rem(where, 2)
    grads = place(1 - core, far, place(core, near))
    grads = tuple(g.reshape(width, width) for g in grads)
    return (attended.reshape(sentences.shape), grad_sentences) + grads


def solution(mesh):
    split3, split2 = P(("lang", "pair"), None, None), P(("lang", "pair"), None)
    in_specs = (split3, split3, P(), P(), P(), split3, split2, split2, split2)
    out_specs = (split3, split3, P(), P(), P())
    return jax.shard_map(body, mesh=mesh, in_specs=in_specs, out_specs=out_specs, check_vma=False)
```

time: 237 us -> 409 us (1.73)
  Pallas kernels: 32.5 us -> 233 us
  blocking collectives: 109 us -> 12.4 us
  starting transfers between devices: 0.08 us -> 47.9 us
  waiting for transfers between devices: 49.6 us -> 93 us
  between operations: 14.2 us -> 0.95 us
  matrix products: 9.51 us -> 0 us
  local copies, waits for them, and re-layouts: 11.4 us -> 16.2 us
  other arithmetic: 10.1 us -> 5.8 us
    pallas_call x0 -> x5, Pallas kernels: none -> 199 us  [the longest x2 193 us: place(): pl.pallas_call(place_kernel, in_specs=[pl.BlockSpec(memory_space=pltpu.SM...]
    all_to_all x4 -> x1, blocking collectives: 109 us -> 12.4 us  [body(): lax.all_to_all(spread(pieces, n_y, 1.0), 'lang', split_axis=0, concat_axi...]
    all_to_all x0 -> x3, waiting for transfers between devices: none -> 62.6 us  [the longest x1 26.3 us: body(): lax.all_to_all(outgoing, 'lang', split_axis=0, concat_axis=0, tiled=True)]
    all_gather x1 -> x0, waiting for transfers between devices: 31.6 us -> none  [body(): lax.all_gather(group, 'lang', axis=0, tiled=True)]
    ppermute x0 -> x9, waiting for transfers between devices: none -> 30.4 us  [the longest x7 24.5 us: body(): lax.ppermute(dx[s], 'lang', [(i, (i + s) % n_lang) for i in range(n_lang)])]
    all_to_all x0 -> x3, starting transfers between devices: none -> 29.6 us  [the longest x1 12.7 us: body(): lax.all_to_all(spread(columns, n_pair, factor), 'pair', split_axis=0, con...]
    ppermute x0 -> x9, starting transfers between devices: none -> 18.3 us  [the longest x7 10.8 us: body(): lax.ppermute(dx[s], 'lang', [(i, (i + s) % n_lang) for i in range(n_lang)])]
    reduce_scatter x1 -> x0, waiting for transfers between devices: 18 us -> none  [body(): lax.psum_scatter(grads.reshape(-1, width), 'lang', scatter_dimension=0, t...]
  transfers between devices with their start and end apart: 2 -> 12, of which waited for: 2 -> 9; matrix products, arithmetic and copies ran while one was open for 8% -> 0% of each run, Pallas kernels for 0% -> 24%
where the time goes in v3:
time: 409 us
  Pallas kernels  233 us (57%)
  waiting for transfers between devices  93 us (23%)
  starting transfers between devices  47.9 us (12%)
  local copies, waits for them, and re-layouts  16.2 us (4%)
  blocking collectives  12.4 us (3%)
  other arithmetic  5.8 us (1%)
    pallas_call x2, Pallas kernels, place(): pl.pallas_call(place_kernel, in_specs=[pl.BlockSpec(memory_space=pltpu.SM...  193 us
    pallas_call x1, Pallas kernels, attend(): pl.pallas_call(functools.partial(attend_kernel, n_src=n_src, n_slot=n_slo...  33.4 us
    all_to_all x1, waiting for transfers between devices, body(): lax.all_to_all(outgoing, 'lang', split_axis=0, concat_axis=0, tiled=True)  26.3 us
    ppermute x7, waiting for transfers between devices, body(): lax.ppermute(dx[s], 'lang', [(i, (i + s) % n_lang) for i in range(n_lang)])  24.5 us
    all_to_all x1, waiting for transfers between devices, body(): lax.all_to_all(spread(columns, n_pair, factor), 'pair', split_axis=0, con...  23 us
    all_to_all x1, waiting for transfers between devices, body(): lax.all_to_all(chip, 'pair', split_axis=0, concat_axis=0, tiled=True)  13.3 us
    unnamed x40, local copies, waits for them, and re-layouts  13 us
    all_to_all x1, starting transfers between devices, body(): lax.all_to_all(spread(columns, n_pair, factor), 'pair', split_axis=0, con...  12.7 us
  transfers between devices with their start and end apart: 12, of which 9 were waited for; matrix products, arithmetic and copies ran while one was open for 0% of the time, Pallas kernels for 24%

profile of v3, /device:TPU:1, one launch (start us, length us, event | category | flops | bytes accessed | tf_op | source)
XLA Modules:
  0.0 408.6 jit_solution(8260398593515114543)
XLA Ops:
  0.6 0.7 pad_clamp_fusion
  1.3 3.2 gather_fusion
  4.5 6.0 %all-to-all-start = ((bf16[8,128,1024]{2,1,0:T(8,128)(2,1)}), bf16[8,128,1024]{2,1,0:T(8,128)(2,1)S(1)}, u32[]{:S(2)}, u32[]{:S(2)}) async-start(bf16[8,128,1024]{2,1,0:T(8,128)(2,1)} %gather_fusion), calls=%async_computation | async-start | bytes 4194304 | tf_op jit(solution)/shard_map/all_to_all | solution.py:302
  10.5 26.3 %all-to-all-done.r_hbm = bf16[8,128,1024]{2,1,0:T(8,128)(2,1)S(1)} async-done(((bf16[8,128,1024]{2,1,0:T(8,128)(2,1)}), bf16[8,128,1024]{2,1,0:T(8,128)(2,1)S(1)}, u32[]{:S(2)}, u32[]{:S(2)}) %all-to-all-start) | async-done | bytes 2097184 | tf_op jit(solution)/shard_map/all_to_all | solution.py:302
  36.8 1.3 copy-done.18
  38.1 33.4 %attend.1 = (bf16[512,1024]{1,0:T(8,128)(2,1)}, bf16[512,1024]{1,0:T(8,128)(2,1)}, bf16[16,3,32,1024]{3,2,1,0:T(8,128)(2,1)}, bf16[16,3,32,1024]{3,2,1,0:T(8,128...) custom-call(s32[1]{0:T(128)} %bitcast.me_ref, ...), custom_call_target="tpu_custom_call" | custom-call | flops 34896609280 | bytes 20971520 | tf_op jit(solution)/shard_map/attend/pallas_call | solution.py:190
  71.5 0.1 collective-permute-start
  71.6 5.9 %collective-permute-done = bf16[16,3,32,1024]{3,2,1,0:T(8,128)(2,1)S(1)} collective-permute-done((bf16[16,3,32,1024]{3,2,1,0:T(8,128)(2,1)}, bf16[16,3,32,1024]{3,2,1,0:T(8,128)(2,1)S(1)}, u32[]{:S(2)}, u32[]{:S(2)}) %collective-permute-start) | collective-permute-done | bytes 3145760 | tf_op jit(solution)/shard_map/ppermute | solution.py:310
  77.5 5.1 %add_convert_fusion = bf16[16,3,32,1024]{3,2,1,0:T(8,128)(2,1)} fusion(bf16[16,3,32,1024]{3,2,1,0:T(8,128)(2,1)S(1)} %collective-permute-done, bf16[16,3,32,1024]{3,2,1,0:T(8,128)(2,1)} %get-tuple-element.35), kind=kLoop, calls=%fused_computation.1 | loop fusion | flops 6291456 | bytes 9437184 | tf_op jit(solution)/shard_map/convert_element_type | solution.py:314
  82.6 10.9 %all-to-all-start.1 = ((bf16[16,3,32,1024]{3,2,1,0:T(8,128)(2,1)}), bf16[16,3,32,1024]{3,2,1,0:T(8,128)(2,1)S(1)}, u32[]{:S(2)}, u32[]{:S(2)}) async-start(bf16[16,3,32,1024]{3,2,1,0:T(8,128)(2,1)} %add_convert_fusion), calls=%async_computation.1 | async-start | bytes 6291456 | tf_op jit(solution)/shard_map/all_to_all | solution.py:315
  93.5 0.2 collective-permute-start.1
  93.7 3.1 collective-permute-start.3
  96.9 0.9 collective-permute-start.4
  97.7 2.6 collective-permute-start.5
  100.4 0.7 copy-done.3
  101.1 7.6 %collective-permute-done.2.rest_2_ = bf16[128,1024]{1,0:T(8,128)(2,1)S(1)} collective-permute-done((bf16[128,1024]{1,0:T(8,128)(2,1)}, bf16[128,1024]{1,0:T(8,128)(2,1)S(1)}, u32[]{:S(2)}, u32[]{:S(2)}) %collective-permute-start.2) | collective-permute-done | bytes 262176 | tf_op jit(solution)/shard_map/ppermute | solution.py:313
  108.7 0.7 copy-done.5
  109.4 1.4 collective-permute-done.3.rest_3_
  110.8 0.8 copy-done.7
  111.6 8.2 %collective-permute-done.4.rest_4_ = bf16[128,1024]{1,0:T(8,128)(2,1)S(1)} collective-permute-done((bf16[128,1024]{1,0:T(8,128)(2,1)}, bf16[128,1024]{1,0:T(8,128)(2,1)S(1)}, u32[]{:S(2)}, u32[]{:S(2)}) %collective-permute-start.4) | collective-permute-done | bytes 262176 | tf_op jit(solution)/shard_map/ppermute | solution.py:313
  119.8 0.7 copy-done.9
  120.5 0.7 copy-done.11
  121.2 13.3 %all-to-all-done.1.parts_ref = bf16[16,3,32,1024]{3,2,1,0:T(8,128)(2,1)S(1)} async-done(((bf16[16,3,32,1024]{3,2,1,0:T(8,128)(2,1)}), bf16[16,3,32,1024]{3,2,1,0:T(8,128)(2,1)S(1)}, u32[]{:S(2)}, u32[]{:S(2)}) %all-to-all-start.1) | async-done | bytes 3145760 | tf_op jit(solution)/shard_map/all_to_all | solution.py:315
  134.5 0.7 spread.2
  135.2 12.4 %all_to_all.20.parts_ref = bf16[4,3,32,1024]{3,2,1,0:T(8,128)(2,1)S(1)} all-to-all(bf16[4,3,32,1024]{3,2,1,0:T(8,128)(2,1)S(1)} %spread.2), channel_id=1, replica_groups={{0,32,64,96},{16,48,80,112},{1,33,65,97},{17,49,81,113},{2,34,66,98},{1..., dimensions={0} | all-to-all | bytes 1572864 | tf_op jit(solution)/shard_map/all_to_all | solution.py:319
  147.6 2.3 spread.3
  149.9 12.7 %all-to-all-start.3 = ((bf16[16,3,32,1024]{3,2,1,0:T(8,128)(2,1)}), bf16[16,3,32,1024]{3,2,1,0:T(8,128)(2,1)}, u32[]{:S(2)}, u32[]{:S(2)}) async-start(bf16[16,3,32,1024]{3,2,1,0:T(8,128)(2,1)} %spread.3), calls=%async_computation.3 | async-start | bytes 6291456 | tf_op jit(solution)/shard_map/all_to_all | solution.py:323
  162.6 0.0 copy-start
  162.6 0.0 copy-start.1
  162.6 0.0 copy-start.17
  162.6 0.9 collective-permute-start.6
  163.6 3.0 collective-permute-start.7
  166.6 1.5 collective-permute-done.6.rest_6_
  168.1 0.7 copy-done.13
  168.8 5.7 %collective-permute-done.7.rest_7_ = bf16[128,1024]{1,0:T(8,128)(2,1)S(1)} collective-permute-done((bf16[128,1024]{1,0:T(8,128)(2,1)}, bf16[128,1024]{1,0:T(8,128)(2,1)S(1)}, u32[]{:S(2)}, u32[]{:S(2)}) %collective-permute-start.7) | collective-permute-done | bytes 262176 | tf_op jit(solution)/shard_map/ppermute | solution.py:313
  174.6 0.7 copy-done.15
  175.3 23.0 %all-to-all-done.3.rows_hbm = bf16[16,3,32,1024]{3,2,1,0:T(8,128)(2,1)} async-done(((bf16[16,3,32,1024]{3,2,1,0:T(8,128)(2,1)}), bf16[16,3,32,1024]{3,2,1,0:T(8,128)(2,1)}, u32[]{:S(2)}, u32[]{:S(2)}) %all-to-all-start.3) | async-done | bytes 3145760 | tf_op jit(solution)/shard_map/all_to_all | solution.py:323
  198.2 7.4 %collective-permute-start.8 = (bf16[16,3,32,1024]{3,2,1,0:T(8,128)(2,1)}, bf16[16,3,32,1024]{3,2,1,0:T(8,128)(2,1)}, u32[]{:S(2)}, u32[]{:S(2)}) collective-permute-start(bf16[16,3,32,1024]{3,2,1,0:T(8,128)(2,1)} %all-to-all-done.3.rows_hbm), channel_id=1, source_target_pairs={{0,16},{16,0},{32,48},{48,32},{64,80},{80,64},{96,112},{112,96},{1... | collective-permute-start | bytes 9437192 | tf_op jit(solution)/shard_map/ppermute | solution.py:325
  205.6 96.4 %place.2 = (bf16[2,16,32,1024]{3,2,1,0:T(8,128)(2,1)}, bf16[2,16,32,1024]{3,2,1,0:T(8,128)(2,1)}, bf16[2,16,32,1024]{3,2,1,0:T(8,128)(2,1)}) custom-call(s32[1]{0:T(128)S(6)} %rem.18.half_ref, bf16[16,3,32,1024]{3,2,1,0:T(8,128)(2,1)} %all-to-all-done.3.rows_hbm), custom_call_target="tpu_custom_call" | custom-call | bytes 6291456 | tf_op jit(solution)/shard_map/place/pallas_call | solution.py:283
  302.1 0.9 copy-done.4
  303.0 0.9 copy-done.6
  304.0 0.9 copy-done.8
  304.9 0.9 copy-done.10
  305.9 0.9 copy-done.12
  306.8 0.9 copy-done.14
  307.8 0.9 copy-done.16
  308.7 3.3 combine.1
  312.0 96.4 %place.3 = (bf16[2,16,32,1024]{3,2,1,0:T(8,128)(2,1)}, bf16[2,16,32,1024]{3,2,1,0:T(8,128)(2,1)}, bf16[2,16,32,1024]{3,2,1,0:T(8,128)(2,1)}) custom-call(s32[1]{0:T(128)S(6)} %sub.3.half_ref, bf16[16,3,32,1024]{3,2,1,0:T(8,128)(2,1)} %collective-permute-done.8.rows_hbm, ...), custom_call_target="tpu_custom_call", output_to_operand_aliasing={{0}: (2, {}), {1}: (3, {}), {2}: (4, {})} | custom-call | bytes 6291456 | tf_op jit(solution)/shard_map/place/pallas_call | solution.py:283
  (26 shorter events, 0.0 us)
Async XLA Ops:
  4.5 32.3 %all-to-all-start = ((bf16[8,128,1024]{2,1,0:T(8,128)(2,1)}), bf16[8,128,1024]{2,1,0:T(8,128)(2,1)S(1)}, u32[]{:S(2)}, u32[]{:S(2)}) async-start(bf16[8,128,1024]{2,1,0:T(8,128)(2,1)} %gather_fusion), calls=%async_computation | async-start | bytes 4194304 | tf_op jit(solution)/shard_map/all_to_all | solution.py:302
  36.8 1.3 copy-start.18
  71.5 6.0 %collective-permute-start = (bf16[16,3,32,1024]{3,2,1,0:T(8,128)(2,1)}, bf16[16,3,32,1024]{3,2,1,0:T(8,128)(2,1)S(1)}, u32[]{:S(2)}, u32[]{:S(2)}) collective-permute-start(bf16[16,3,32,1024]{3,2,1,0:T(8,128)(2,1)} %get-tuple-element.36), channel_id=1, source_target_pairs={{0,16},{16,0},{32,48},{48,32},{64,80},{80,64},{96,112},{112,96},{1... | collective-permute-start | bytes 9437192 | tf_op jit(solution)/shard_map/ppermute | solution.py:310
  82.6 15.1 %copy-start.19 = (bf16[128,1024]{1,0:T(8,128)(2,1)S(1)}, bf16[128,1024]{1,0:T(8,128)(2,1)}, u32[]{:S(2)}) copy-start(bf16[128,1024]{1,0:T(8,128)(2,1)} %get-tuple-element.41) | copy-start | bytes 786436
  82.6 51.9 %all-to-all-start.1 = ((bf16[16,3,32,1024]{3,2,1,0:T(8,128)(2,1)}), bf16[16,3,32,1024]{3,2,1,0:T(8,128)(2,1)S(1)}, u32[]{:S(2)}, u32[]{:S(2)}) async-start(bf16[16,3,32,1024]{3,2,1,0:T(8,128)(2,1)} %add_convert_fusion), calls=%async_computation.1 | async-start | bytes 6291456 | tf_op jit(solution)/shard_map/all_to_all | solution.py:315
  93.5 6.8 %collective-permute-start.1 = (bf16[128,1024]{1,0:T(8,128)(2,1)}, bf16[128,1024]{1,0:T(8,128)(2,1)S(1)}, u32[]{:S(2)}, u32[]{:S(2)}) collective-permute-start(bf16[128,1024]{1,0:T(8,128)(2,1)} %get-tuple-element.37), channel_id=1, source_target_pairs={{0,16},{16,32},{32,48},{48,64},{64,80},{80,96},{96,112},{112,0},{1... | collective-permute-start | bytes 786440 | tf_op jit(solution)/shard_map/ppermute | solution.py:313
  93.7 14.9 %collective-permute-start.2 = (bf16[128,1024]{1,0:T(8,128)(2,1)}, bf16[128,1024]{1,0:T(8,128)(2,1)S(1)}, u32[]{:S(2)}, u32[]{:S(2)}) collective-permute-start(bf16[128,1024]{1,0:T(8,128)(2,1)} %get-tuple-element.38), channel_id=1, source_target_pairs={{0,32},{16,48},{32,64},{48,80},{64,96},{80,112},{96,0},{112,16},{1... | collective-permute-start | bytes 786440 | tf_op jit(solution)/shard_map/ppermute | solution.py:313
  93.7 17.1 %collective-permute-start.3 = (bf16[128,1024]{1,0:T(8,128)(2,1)}, bf16[128,1024]{1,0:T(8,128)(2,1)S(1)}, u32[]{:S(2)}, u32[]{:S(2)}) collective-permute-start(bf16[128,1024]{1,0:T(8,128)(2,1)} %get-tuple-element.39), channel_id=1, source_target_pairs={{0,48},{16,64},{32,80},{48,96},{64,112},{80,0},{96,16},{112,32},{1... | collective-permute-start | bytes 786440 | tf_op jit(solution)/shard_map/ppermute | solution.py:313
  96.9 23.0 %collective-permute-start.4 = (bf16[128,1024]{1,0:T(8,128)(2,1)}, bf16[128,1024]{1,0:T(8,128)(2,1)S(1)}, u32[]{:S(2)}, u32[]{:S(2)}) collective-permute-start(bf16[128,1024]{1,0:T(8,128)(2,1)} %get-tuple-element.40), channel_id=1, source_target_pairs={{0,64},{16,80},{32,96},{48,112},{64,0},{80,16},{96,32},{112,48},{1... | collective-permute-start | bytes 786440 | tf_op jit(solution)/shard_map/ppermute | solution.py:313
  97.7 22.8 %collective-permute-start.5 = (bf16[128,1024]{1,0:T(8,128)(2,1)S(1)}, bf16[128,1024]{1,0:T(8,128)(2,1)S(1)}, u32[]{:S(2)}, u32[]{:S(2)}) collective-permute-start(bf16[128,1024]{1,0:T(8,128)(2,1)S(1)} %copy-done.19), channel_id=1, source_target_pairs={{0,80},{16,96},{32,112},{48,0},{64,16},{80,32},{96,48},{112,64},{1... | collective-permute-start | bytes 786440 | tf_op jit(solution)/shard_map/ppermute | solution.py:313
  100.4 0.7 copy-start.3
  108.7 0.7 copy-start.5
  110.8 0.8 copy-start.7
  119.8 0.7 copy-start.9
  120.5 0.7 copy-start.11
  149.9 152.1 %copy-start.2 = (bf16[128,1024]{1,0:T(8,128)(2,1)S(1)}, bf16[128,1024]{1,0:T(8,128)(2,1)}, u32[]{:S(2)}) copy-start(bf16[128,1024]{1,0:T(8,128)(2,1)} %get-tuple-element.34.rest_0_) | copy-start | bytes 786436
  149.9 48.3 %all-to-all-start.3 = ((bf16[16,3,32,1024]{3,2,1,0:T(8,128)(2,1)}), bf16[16,3,32,1024]{3,2,1,0:T(8,128)(2,1)}, u32[]{:S(2)}, u32[]{:S(2)}) async-start(bf16[16,3,32,1024]{3,2,1,0:T(8,128)(2,1)} %spread.3), calls=%async_computation.3 | async-start | bytes 6291456 | tf_op jit(solution)/shard_map/all_to_all | solution.py:323
  162.6 139.4 %copy-start = (bf16[1024,1024]{1,0:T(8,128)(2,1)S(1)}, bf16[1024,1024]{1,0:T(8,128)(2,1)}, u32[]{:S(2)}) copy-start(bf16[1024,1024]{1,0:T(8,128)(2,1)} %wq_ref.1) | copy-start | bytes 6291460
  162.6 139.4 %copy-start.1 = (bf16[512,1024]{1,0:T(8,128)(2,1)S(1)}, bf16[512,1024]{1,0:T(8,128)(2,1)}, u32[]{:S(2)}) copy-start(bf16[512,1024]{1,0:T(8,128)(2,1)} %get-tuple-element.33.dq_ref) | copy-start | bytes 3145732
  162.6 139.4 %copy-start.17 = (s32[1,8,1]{1,2,0:T(1,128)S(1)}, s32[1,8,1]{1,2,0:T(1,128)}, u32[]{:S(2)}) copy-start(s32[1,8,1]{1,2,0:T(1,128)} %param.14) | copy-start | bytes 100
  162.6 5.5 %collective-permute-start.6 = (bf16[128,1024]{1,0:T(8,128)(2,1)}, bf16[128,1024]{1,0:T(8,128)(2,1)S(1)}, u32[]{:S(2)}, u32[]{:S(2)}) collective-permute-start(bf16[128,1024]{1,0:T(8,128)(2,1)} %get-tuple-element.48), channel_id=1, source_target_pairs={{0,96},{16,112},{32,0},{48,16},{64,32},{80,48},{96,64},{112,80},{1... | collective-permute-start | bytes 786440 | tf_op jit(solution)/shard_map/ppermute | solution.py:313
  163.6 11.0 %collective-permute-start.7 = (bf16[128,1024]{1,0:T(8,128)(2,1)}, bf16[128,1024]{1,0:T(8,128)(2,1)S(1)}, u32[]{:S(2)}, u32[]{:S(2)}) collective-permute-start(bf16[128,1024]{1,0:T(8,128)(2,1)} %get-tuple-element.49), channel_id=1, source_target_pairs={{0,112},{16,0},{32,16},{48,32},{64,48},{80,64},{96,80},{112,96},{1... | collective-permute-start | bytes 786440 | tf_op jit(solution)/shard_map/ppermute | solution.py:313
  168.1 0.7 copy-start.13
  174.6 0.7 copy-start.15
  198.2 113.8 %collective-permute-start.8 = (bf16[16,3,32,1024]{3,2,1,0:T(8,128)(2,1)}, bf16[16,3,32,1024]{3,2,1,0:T(8,128)(2,1)}, u32[]{:S(2)}, u32[]{:S(2)}) collective-permute-start(bf16[16,3,32,1024]{3,2,1,0:T(8,128)(2,1)} %all-to-all-done.3.rows_hbm), channel_id=1, source_target_pairs={{0,16},{16,0},{32,48},{48,32},{64,80},{80,64},{96,112},{112,96},{1... | collective-permute-start | bytes 9437192 | tf_op jit(solution)/shard_map/ppermute | solution.py:325
  302.1 1.0 copy-start.4
  303.0 0.9 copy-start.6
  304.0 0.9 copy-start.8
  304.9 0.9 copy-start.10
  305.9 0.9 copy-start.12
  306.8 0.9 copy-start.14
  307.8 0.9 copy-start.16

commit v4 on v3

--- a/solution.py
+++ b/solution.py
@@ -267,26 +267,27 @@
     )(parts)
 
 
-def place_kernel(half_ref, rows_hbm, *rest):
-    sem = rest[-1]
-    outs = rest[-4:-1]
-    copies = [pltpu.make_async_copy(rows_hbm.at[:, i], out.at[half_ref[0]], sem.at[i]) for i, out in enumerate(outs)]
-    for c in copies:
-        c.start()
-    for c in copies:
-        c.wait()
+def place_kernel(half_ref, rows_ref, *rest):
+    n = rows_ref.shape[1]
+    for i, out in enumerate(rest[-n:]):
+        out[0] = rows_ref[:, i]
 
 
 def place(half, rows, into=()):
     pieces, n, each, width = rows.shape
+    step = pieces // 4
     hbm = pl.BlockSpec(memory_space=pl.ANY)
     return pl.pallas_call(
         place_kernel,
-        in_specs=[pl.BlockSpec(memory_space=pltpu.SMEM), hbm] + [hbm] * len(into),
-        out_specs=[hbm] * n,
+        grid_spec=pltpu.PrefetchScalarGridSpec(
+            num_scalar_prefetch=1,
+            grid=(pieces // step,),
+            in_specs=[pl.BlockSpec((step, n, each, width), lambda p, half: (p, 0, 0, 0))] + [hbm] * len(into),
+            out_specs=[pl.BlockSpec((1, step, each, width), lambda p, half: (half[0], p, 0, 0))] * n,
+        ),
         out_shape=[jax.ShapeDtypeStruct((2, pieces, each, width), BF)] * n,
         input_output_aliases={2 + i: i for i in range(len(into))},
-        scratch_shapes=[pltpu.SemaphoreType.DMA((n,))],
+        compiler_params=pltpu.CompilerParams(vmem_limit_bytes=16 * 2**20),
         cost_estimate=pl.CostEstimate(flops=0, bytes_accessed=4 * rows.size, transcendentals=0),
         name="place",
     )(half, rows, *into)

time: 409 us -> 219 us (0.54)
  Pallas kernels: 233 us -> 43.5 us
    pallas_call x2, Pallas kernels: 193 us -> 4.22 us  [place(): pl.pallas_call(place_kernel, grid_spec=pltpu.PrefetchScalarGridSpec(num_s...]
    all_to_all x1, starting transfers between devices: 10.9 us -> 6.02 us  [body(): lax.all_to_all(chip, 'pair', split_axis=0, concat_axis=0, tiled=True)]
    unnamed x40 -> x42, local copies, waits for them, and re-layouts: 13 us -> 14.6 us
  transfers between devices with their start and end apart: 12 -> 12, of which waited for: 9 -> 9; matrix products, arithmetic and copies ran while one was open for 0% -> 0% of each run, Pallas kernels for 24% -> 2%
where the time goes in v4:
time: 219 us; the launch traced here: 218 us
  waiting for transfers between devices  90.9 us (42%)
  starting transfers between devices  45.7 us (21%)
  Pallas kernels  43.5 us (20%)
  local copies, waits for them, and re-layouts  17.8 us (8%)
  blocking collectives  13.6 us (6%)
  other arithmetic  5.79 us (3%)
    pallas_call x1, Pallas kernels, attend(): pl.pallas_call(functools.partial(attend_kernel, n_src=n_src, n_slot=n_slo...  34.6 us
    all_to_all x1, waiting for transfers between devices, body(): lax.all_to_all(outgoing, 'lang', split_axis=0, concat_axis=0, tiled=True)  26.3 us
    ppermute x7, waiting for transfers between devices, body(): lax.ppermute(dx[s], 'lang', [(i, (i + s) % n_lang) for i in range(n_lang)])  25.6 us
    all_to_all x1, waiting for transfers between devices, body(): lax.all_to_all(spread(columns, n_pair, factor), 'pair', split_axis=0, con...  22.6 us
    unnamed x42, local copies, waits for them, and re-layouts  14.6 us
    all_to_all x1, blocking collectives, body(): lax.all_to_all(spread(pieces, n_y, 1.0), 'lang', split_axis=0, concat_axi...  13.6 us
    all_to_all x1, starting transfers between devices, body(): lax.all_to_all(spread(columns, n_pair, factor), 'pair', split_axis=0, con...  12.4 us
    ppermute x7, starting transfers between devices, body(): lax.ppermute(dx[s], 'lang', [(i, (i + s) % n_lang) for i in range(n_lang)])  11.9 us
  transfers between devices with their start and end apart: 12, of which 9 were waited for; matrix products, arithmetic and copies ran while one was open for 0% of the time, Pallas kernels for 2%

profile of v4, /device:TPU:1, one launch (start us, length us, event | category | flops | bytes accessed | tf_op | source)
XLA Modules:
  0.0 218.0 jit_solution(9362097277254087105)
XLA Ops:
  0.6 0.7 pad_clamp_fusion
  1.3 3.2 %gather_fusion = bf16[8,128,1024]{2,1,0:T(8,128)(2,1)} fusion(bf16[4,128,1024]{2,1,0:T(8,128)(2,1)} %param.9, s32[1024]{0:T(1024)S(1)} %pad_clamp_fusion), kind=kCustom, calls=%fused_computation | custom fusion | bytes 4194336 | tf_op jit(solution)/shard_map/jit(_take)/gather | solution.py:302
  4.5 6.0 %all-to-all-start = ((bf16[8,128,1024]{2,1,0:T(8,128)(2,1)}), bf16[8,128,1024]{2,1,0:T(8,128)(2,1)S(1)}, u32[]{:S(2)}, u32[]{:S(2)}) async-start(bf16[8,128,1024]{2,1,0:T(8,128)(2,1)} %gather_fusion), calls=%async_computation | async-start | bytes 4194304 | tf_op jit(solution)/shard_map/all_to_all | solution.py:303
  10.5 26.3 %all-to-all-done.r_hbm = bf16[8,128,1024]{2,1,0:T(8,128)(2,1)S(1)} async-done(((bf16[8,128,1024]{2,1,0:T(8,128)(2,1)}), bf16[8,128,1024]{2,1,0:T(8,128)(2,1)S(1)}, u32[]{:S(2)}, u32[]{:S(2)}) %all-to-all-start) | async-done | bytes 2097184 | tf_op jit(solution)/shard_map/all_to_all | solution.py:303
  36.8 1.3 copy-done.19
  38.1 34.6 %attend.1 = (bf16[512,1024]{1,0:T(8,128)(2,1)}, bf16[512,1024]{1,0:T(8,128)(2,1)}, bf16[16,3,32,1024]{3,2,1,0:T(8,128)(2,1)}, bf16[16,3,32,1024]{3,2,1,0:T(8,128...) custom-call(s32[1]{0:T(128)} %bitcast.me_ref, ...), custom_call_target="tpu_custom_call" | custom-call | flops 34896609280 | bytes 20971520 | tf_op jit(solution)/shard_map/attend/pallas_call | solution.py:190
  72.7 2.1 collective-permute-start
  74.8 5.5 %collective-permute-done = bf16[16,3,32,1024]{3,2,1,0:T(8,128)(2,1)S(1)} collective-permute-done((bf16[16,3,32,1024]{3,2,1,0:T(8,128)(2,1)}, bf16[16,3,32,1024]{3,2,1,0:T(8,128)(2,1)S(1)}, u32[]{:S(2)}, u32[]{:S(2)}) %collective-permute-start) | collective-permute-done | bytes 3145760 | tf_op jit(solution)/shard_map/ppermute | solution.py:311
  80.3 5.1 %add_convert_fusion = bf16[16,3,32,1024]{3,2,1,0:T(8,128)(2,1)} fusion(bf16[16,3,32,1024]{3,2,1,0:T(8,128)(2,1)S(1)} %collective-permute-done, bf16[16,3,32,1024]{3,2,1,0:T(8,128)(2,1)} %get-tuple-element.35), kind=kLoop, calls=%fused_computation.1 | loop fusion | flops 6291456 | bytes 9437184 | tf_op jit(solution)/shard_map/convert_element_type | solution.py:315
  85.5 6.0 %all-to-all-start.1 = ((bf16[16,3,32,1024]{3,2,1,0:T(8,128)(2,1)}), bf16[16,3,32,1024]{3,2,1,0:T(8,128)(2,1)S(1)}, u32[]{:S(2)}, u32[]{:S(2)}) async-start(bf16[16,3,32,1024]{3,2,1,0:T(8,128)(2,1)} %add_convert_fusion), calls=%async_computation.1 | async-start | bytes 6291456 | tf_op jit(solution)/shard_map/all_to_all | solution.py:316
  91.5 1.8 collective-permute-start.1
  93.3 0.2 collective-permute-start.2
  93.5 3.4 %collective-permute-start.3 = (bf16[128,1024]{1,0:T(8,128)(2,1)}, bf16[128,1024]{1,0:T(8,128)(2,1)S(1)}, u32[]{:S(2)}, u32[]{:S(2)}) collective-permute-start(bf16[128,1024]{1,0:T(8,128)(2,1)} %get-tuple-element.39), channel_id=1, source_target_pairs={{0,48},{16,64},{32,80},{48,96},{64,112},{80,0},{96,16},{112,32},{1... | collective-permute-start | bytes 786440 | tf_op jit(solution)/shard_map/ppermute | solution.py:314
  96.9 2.3 %collective-permute-start.5 = (bf16[128,1024]{1,0:T(8,128)(2,1)S(1)}, bf16[128,1024]{1,0:T(8,128)(2,1)S(1)}, u32[]{:S(2)}, u32[]{:S(2)}) collective-permute-start(bf16[128,1024]{1,0:T(8,128)(2,1)S(1)} %copy-done.20), channel_id=1, source_target_pairs={{0,80},{16,96},{32,112},{48,0},{64,16},{80,32},{96,48},{112,64},{1... | collective-permute-start | bytes 786440 | tf_op jit(solution)/shard_map/ppermute | solution.py:314
  99.2 0.7 copy-done.4
  99.9 6.7 %collective-permute-done.2.rest_2_ = bf16[128,1024]{1,0:T(8,128)(2,1)S(1)} collective-permute-done((bf16[128,1024]{1,0:T(8,128)(2,1)}, bf16[128,1024]{1,0:T(8,128)(2,1)S(1)}, u32[]{:S(2)}, u32[]{:S(2)}) %collective-permute-start.2) | collective-permute-done | bytes 262176 | tf_op jit(solution)/shard_map/ppermute | solution.py:314
  106.6 0.7 copy-done.6
  107.3 3.1 %collective-permute-done.3.rest_3_ = bf16[128,1024]{1,0:T(8,128)(2,1)S(1)} collective-permute-done((bf16[128,1024]{1,0:T(8,128)(2,1)}, bf16[128,1024]{1,0:T(8,128)(2,1)S(1)}, u32[]{:S(2)}, u32[]{:S(2)}) %collective-permute-start.3) | collective-permute-done | bytes 262176 | tf_op jit(solution)/shard_map/ppermute | solution.py:314
  110.4 0.7 copy-done.8
  111.1 8.7 %collective-permute-done.4.rest_4_ = bf16[128,1024]{1,0:T(8,128)(2,1)S(1)} collective-permute-done((bf16[128,1024]{1,0:T(8,128)(2,1)}, bf16[128,1024]{1,0:T(8,128)(2,1)S(1)}, u32[]{:S(2)}, u32[]{:S(2)}) %collective-permute-start.4) | collective-permute-done | bytes 262176 | tf_op jit(solution)/shard_map/ppermute | solution.py:314
  119.7 0.7 copy-done.10
  120.5 0.0 collective-permute-done.5.rest_5_
  120.5 0.7 copy-done.12
  121.2 10.9 %all-to-all-done.1.parts_ref = bf16[16,3,32,1024]{3,2,1,0:T(8,128)(2,1)S(1)} async-done(((bf16[16,3,32,1024]{3,2,1,0:T(8,128)(2,1)}), bf16[16,3,32,1024]{3,2,1,0:T(8,128)(2,1)S(1)}, u32[]{:S(2)}, u32[]{:S(2)}) %all-to-all-start.1) | async-done | bytes 3145760 | tf_op jit(solution)/shard_map/all_to_all | solution.py:316
  132.1 0.7 spread.2
  132.8 13.6 %all_to_all.20.parts_ref = bf16[4,3,32,1024]{3,2,1,0:T(8,128)(2,1)S(1)} all-to-all(bf16[4,3,32,1024]{3,2,1,0:T(8,128)(2,1)S(1)} %spread.2), channel_id=1, replica_groups={{0,32,64,96},{16,48,80,112},{1,33,65,97},{17,49,81,113},{2,34,66,98},{1..., dimensions={0} | all-to-all | bytes 1572864 | tf_op jit(solution)/shard_map/all_to_all | solution.py:320
  146.4 0.7 spread.3
  147.1 1.6 copy-done
  148.7 12.4 %all-to-all-start.3 = ((bf16[16,3,32,1024]{3,2,1,0:T(8,128)(2,1)}), bf16[16,3,32,1024]{3,2,1,0:T(8,128)(2,1)S(1)}, u32[]{:S(2)}, u32[]{:S(2)}) async-start(bf16[16,3,32,1024]{3,2,1,0:T(8,128)(2,1)} %copy-done), calls=%async_computation.3 | async-start | bytes 6291456 | tf_op jit(solution)/shard_map/all_to_all | solution.py:324
  161.2 0.0 copy-start.18
  161.2 1.0 collective-permute-start.6
  162.1 3.3 %collective-permute-start.7 = (bf16[128,1024]{1,0:T(8,128)(2,1)}, bf16[128,1024]{1,0:T(8,128)(2,1)S(1)}, u32[]{:S(2)}, u32[]{:S(2)}) collective-permute-start(bf16[128,1024]{1,0:T(8,128)(2,1)} %get-tuple-element.49), channel_id=1, source_target_pairs={{0,112},{16,0},{32,16},{48,32},{64,48},{80,64},{96,80},{112,96},{1... | collective-permute-start | bytes 786440 | tf_op jit(solution)/shard_map/ppermute | solution.py:314
  165.4 1.3 collective-permute-done.6.rest_6_
  166.7 0.7 copy-done.14
  167.4 5.9 %collective-permute-done.7.rest_7_ = bf16[128,1024]{1,0:T(8,128)(2,1)S(1)} collective-permute-done((bf16[128,1024]{1,0:T(8,128)(2,1)}, bf16[128,1024]{1,0:T(8,128)(2,1)S(1)}, u32[]{:S(2)}, u32[]{:S(2)}) %collective-permute-start.7) | collective-permute-done | bytes 262176 | tf_op jit(solution)/shard_map/ppermute | solution.py:314
  173.3 0.7 copy-done.16
  174.0 22.6 %all-to-all-done.3.rows_ref = bf16[16,3,32,1024]{3,2,1,0:T(8,128)(2,1)S(1)} async-done(((bf16[16,3,32,1024]{3,2,1,0:T(8,128)(2,1)}), bf16[16,3,32,1024]{3,2,1,0:T(8,128)(2,1)S(1)}, u32[]{:S(2)}, u32[]{:S(2)}) %all-to-all-start.3) | async-done | bytes 3145760 | tf_op jit(solution)/shard_map/all_to_all | solution.py:324
  196.6 7.3 %collective-permute-start.8 = (bf16[16,3,32,1024]{3,2,1,0:T(8,128)(2,1)S(1)}, bf16[16,3,32,1024]{3,2,1,0:T(8,128)(2,1)S(1)}, u32[]{:S(2)}, u32[]{:S(2)}) collective-permute-start(bf16[16,3,32,1024]{3,2,1,0:T(8,128)(2,1)S(1)} %all-to-all-done.3.rows_ref), channel_id=1, source_target_pairs={{0,16},{16,0},{32,48},{48,32},{64,80},{80,64},{96,112},{112,96},{1... | collective-permute-start | bytes 9437192 | tf_op jit(solution)/shard_map/ppermute | solution.py:326
  203.8 2.1 place.2
  206.0 0.9 copy-done.5
  206.9 0.9 copy-done.7
  207.9 0.9 copy-done.9
  208.8 0.9 copy-done.11
  209.8 0.9 copy-done.13
  210.7 0.9 copy-done.15
  211.7 0.9 copy-done.17
  212.6 3.3 %combine.1 = bf16[4,128,1024]{2,1,0:T(8,128)(2,1)} custom-call(s32[1]{0:T(128)} %bitcast.me_ref, s32[8]{0:T(128)S(1)} %bitcast.9, bf16[512,1024]{1,0:T(8,128)(2,1)S(1)} %copy-done.2, bf16[1024,1024]{1,0:T(8,128)(2,1)S(1)} %copy-done.1, bf16[128,1024]{1,0:T(8,128)(2,1)S(1)} %copy-done.3, bf16[128,1024]{1,0:T(8,128)(2,1)S(1)} %copy-done.5, ...), custom_call_target="tpu_custom_call" | custom-call | flops 1073741824 | bytes 6291456 | tf_op jit(solution)/shard_map/combine/pallas_call | solution.py:238
  215.9 2.1 place.3
  (28 shorter events, 0.1 us)
Async XLA Ops:
  4.5 32.3 %all-to-all-start = ((bf16[8,128,1024]{2,1,0:T(8,128)(2,1)}), bf16[8,128,1024]{2,1,0:T(8,128)(2,1)S(1)}, u32[]{:S(2)}, u32[]{:S(2)}) async-start(bf16[8,128,1024]{2,1,0:T(8,128)(2,1)} %gather_fusion), calls=%async_computation | async-start | bytes 4194304 | tf_op jit(solution)/shard_map/all_to_all | solution.py:303
  36.8 1.3 copy-start.19
  72.7 7.6 %collective-permute-start = (bf16[16,3,32,1024]{3,2,1,0:T(8,128)(2,1)}, bf16[16,3,32,1024]{3,2,1,0:T(8,128)(2,1)S(1)}, u32[]{:S(2)}, u32[]{:S(2)}) collective-permute-start(bf16[16,3,32,1024]{3,2,1,0:T(8,128)(2,1)} %get-tuple-element.36), channel_id=1, source_target_pairs={{0,16},{16,0},{32,48},{48,32},{64,80},{80,64},{96,112},{112,96},{1... | collective-permute-start | bytes 9437192 | tf_op jit(solution)/shard_map/ppermute | solution.py:311
  85.5 11.4 %copy-start.20 = (bf16[128,1024]{1,0:T(8,128)(2,1)S(1)}, bf16[128,1024]{1,0:T(8,128)(2,1)}, u32[]{:S(2)}) copy-start(bf16[128,1024]{1,0:T(8,128)(2,1)} %get-tuple-element.41) | copy-start | bytes 786436
  85.5 46.6 %all-to-all-start.1 = ((bf16[16,3,32,1024]{3,2,1,0:T(8,128)(2,1)}), bf16[16,3,32,1024]{3,2,1,0:T(8,128)(2,1)S(1)}, u32[]{:S(2)}, u32[]{:S(2)}) async-start(bf16[16,3,32,1024]{3,2,1,0:T(8,128)(2,1)} %add_convert_fusion), calls=%async_computation.1 | async-start | bytes 6291456 | tf_op jit(solution)/shard_map/all_to_all | solution.py:316
  91.5 7.7 %collective-permute-start.1 = (bf16[128,1024]{1,0:T(8,128)(2,1)}, bf16[128,1024]{1,0:T(8,128)(2,1)S(1)}, u32[]{:S(2)}, u32[]{:S(2)}) collective-permute-start(bf16[128,1024]{1,0:T(8,128)(2,1)} %get-tuple-element.37), channel_id=1, source_target_pairs={{0,16},{16,32},{32,48},{48,64},{64,80},{80,96},{96,112},{112,0},{1... | collective-permute-start | bytes 786440 | tf_op jit(solution)/shard_map/ppermute | solution.py:314
  93.3 13.3 %collective-permute-start.2 = (bf16[128,1024]{1,0:T(8,128)(2,1)}, bf16[128,1024]{1,0:T(8,128)(2,1)S(1)}, u32[]{:S(2)}, u32[]{:S(2)}) collective-permute-start(bf16[128,1024]{1,0:T(8,128)(2,1)} %get-tuple-element.38), channel_id=1, source_target_pairs={{0,32},{16,48},{32,64},{48,80},{64,96},{80,112},{96,0},{112,16},{1... | collective-permute-start | bytes 786440 | tf_op jit(solution)/shard_map/ppermute | solution.py:314
  93.5 16.9 %collective-permute-start.3 = (bf16[128,1024]{1,0:T(8,128)(2,1)}, bf16[128,1024]{1,0:T(8,128)(2,1)S(1)}, u32[]{:S(2)}, u32[]{:S(2)}) collective-permute-start(bf16[128,1024]{1,0:T(8,128)(2,1)} %get-tuple-element.39), channel_id=1, source_target_pairs={{0,48},{16,64},{32,80},{48,96},{64,112},{80,0},{96,16},{112,32},{1... | collective-permute-start | bytes 786440 | tf_op jit(solution)/shard_map/ppermute | solution.py:314
  96.9 22.9 %collective-permute-start.4 = (bf16[128,1024]{1,0:T(8,128)(2,1)}, bf16[128,1024]{1,0:T(8,128)(2,1)S(1)}, u32[]{:S(2)}, u32[]{:S(2)}) collective-permute-start(bf16[128,1024]{1,0:T(8,128)(2,1)} %get-tuple-element.40), channel_id=1, source_target_pairs={{0,64},{16,80},{32,96},{48,112},{64,0},{80,16},{96,32},{112,48},{1... | collective-permute-start | bytes 786440 | tf_op jit(solution)/shard_map/ppermute | solution.py:314
  96.9 23.6 %collective-permute-start.5 = (bf16[128,1024]{1,0:T(8,128)(2,1)S(1)}, bf16[128,1024]{1,0:T(8,128)(2,1)S(1)}, u32[]{:S(2)}, u32[]{:S(2)}) collective-permute-start(bf16[128,1024]{1,0:T(8,128)(2,1)S(1)} %copy-done.20), channel_id=1, source_target_pairs={{0,80},{16,96},{32,112},{48,0},{64,16},{80,32},{96,48},{112,64},{1... | collective-permute-start | bytes 786440 | tf_op jit(solution)/shard_map/ppermute | solution.py:314
  99.2 0.7 copy-start.4
  106.6 0.7 copy-start.6
  110.4 0.7 copy-start.8
  119.7 0.7 copy-start.10
  120.5 0.7 copy-start.12
  147.1 1.6 copy-start
  148.7 57.2 %copy-start.3 = (bf16[128,1024]{1,0:T(8,128)(2,1)S(1)}, bf16[128,1024]{1,0:T(8,128)(2,1)}, u32[]{:S(2)}) copy-start(bf16[128,1024]{1,0:T(8,128)(2,1)} %get-tuple-element.34.rest_0_) | copy-start | bytes 786436
  148.7 47.9 %all-to-all-start.3 = ((bf16[16,3,32,1024]{3,2,1,0:T(8,128)(2,1)}), bf16[16,3,32,1024]{3,2,1,0:T(8,128)(2,1)S(1)}, u32[]{:S(2)}, u32[]{:S(2)}) async-start(bf16[16,3,32,1024]{3,2,1,0:T(8,128)(2,1)} %copy-done), calls=%async_computation.3 | async-start | bytes 6291456 | tf_op jit(solution)/shard_map/all_to_all | solution.py:324
  161.2 44.8 %copy-start.18 = (s32[1,8,1]{1,2,0:T(1,128)S(1)}, s32[1,8,1]{1,2,0:T(1,128)}, u32[]{:S(2)}) copy-start(s32[1,8,1]{1,2,0:T(1,128)} %param.14) | copy-start | bytes 100
  161.2 5.5 %collective-permute-start.6 = (bf16[128,1024]{1,0:T(8,128)(2,1)}, bf16[128,1024]{1,0:T(8,128)(2,1)S(1)}, u32[]{:S(2)}, u32[]{:S(2)}) collective-permute-start(bf16[128,1024]{1,0:T(8,128)(2,1)} %get-tuple-element.48), channel_id=1, source_target_pairs={{0,96},{16,112},{32,0},{48,16},{64,32},{80,48},{96,64},{112,80},{1... | collective-permute-start | bytes 786440 | tf_op jit(solution)/shard_map/ppermute | solution.py:314
  162.1 11.1 %collective-permute-start.7 = (bf16[128,1024]{1,0:T(8,128)(2,1)}, bf16[128,1024]{1,0:T(8,128)(2,1)S(1)}, u32[]{:S(2)}, u32[]{:S(2)}) collective-permute-start(bf16[128,1024]{1,0:T(8,128)(2,1)} %get-tuple-element.49), channel_id=1, source_target_pairs={{0,112},{16,0},{32,16},{48,32},{64,48},{80,64},{96,80},{112,96},{1... | collective-permute-start | bytes 786440 | tf_op jit(solution)/shard_map/ppermute | solution.py:314
  166.7 0.7 copy-start.14
  173.3 0.7 copy-start.16
  196.6 9.4 %copy-start.1 = (bf16[1024,1024]{1,0:T(8,128)(2,1)S(1)}, bf16[1024,1024]{1,0:T(8,128)(2,1)}, u32[]{:S(2)}) copy-start(bf16[1024,1024]{1,0:T(8,128)(2,1)} %wq_ref.1) | copy-start | bytes 6291460
  196.6 9.4 %copy-start.2 = (bf16[512,1024]{1,0:T(8,128)(2,1)S(1)}, bf16[512,1024]{1,0:T(8,128)(2,1)}, u32[]{:S(2)}) copy-start(bf16[512,1024]{1,0:T(8,128)(2,1)} %get-tuple-element.33.dq_ref) | copy-start | bytes 3145732
  196.6 19.3 %collective-permute-start.8 = (bf16[16,3,32,1024]{3,2,1,0:T(8,128)(2,1)S(1)}, bf16[16,3,32,1024]{3,2,1,0:T(8,128)(2,1)S(1)}, u32[]{:S(2)}, u32[]{:S(2)}) collective-permute-start(bf16[16,3,32,1024]{3,2,1,0:T(8,128)(2,1)S(1)} %all-to-all-done.3.rows_ref), channel_id=1, source_target_pairs={{0,16},{16,0},{32,48},{48,32},{64,80},{80,64},{96,112},{112,96},{1... | collective-permute-start | bytes 9437192 | tf_op jit(solution)/shard_map/ppermute | solution.py:326
  206.0 1.0 copy-start.5
  206.9 0.9 copy-start.7
  207.9 0.9 copy-start.9
  208.8 0.9 copy-start.11
  209.8 0.9 copy-start.13
  210.7 0.9 copy-start.15
  211.7 0.9 copy-start.17

commit v5 on v4

--- a/solution.py
+++ b/solution.py
@@ -22,24 +22,39 @@
 
 
 def attend_kernel(me_ref, src_ref, slot_ref, valid_ref, x_hbm, r_hbm, c_hbm, wq_hbm, wk_hbm, wv_hbm,
-                  *rest, n_src, n_slot, length):
-    outs, scratch = rest[:4 + n_slot], rest[4 + n_slot:]
+                  *rest, n_src, n_slot, length, lo, earlier):
+    if earlier:
+        (dk0_hbm, dv0_hbm), att_in, rest = rest[:2], rest[2], rest[3:]
+        n_out = 4 + n_slot
+    else:
+        n_out = 6
+    outs, scratch = rest[:n_out], rest[n_out:]
     att_hbm, dq_hbm, keep_hbm, send_hbm = outs[:4]
-    dx_hbm = outs[4:]
-    (mult, x_ref, r_ref, c_ref, wq_ref, wk_ref, wv_ref, att_v, dq_v, gw_v, dx_v,
-     xt, rt, q2, g2, k_s, v_s, kt, vt, ot, dqt, dk_acc, dv_acc, sem_in, sem_r, sem_out) = scratch
-    width = x_ref.shape[1]
+    (mult, x_ref, r_ref, c_ref, wq_ref, wk_ref, wv_ref, att_v, dq_v, gw_v,
+     xt, rt, q2, g2, k_s, v_s, kt, vt, ot, dqt, dk_acc, dv_acc, sem_in, sem_r, sem_out) = scratch[:25]
+    depth = x_ref.shape[1]
+    width = c_ref.shape[1]
     heads = width // LANES
     n_pairs = src_ref.shape[-1]
     me = me_ref[0]
     block = 256
+    mine = pl.ds(lo, width)
 
     copies = [pltpu.make_async_copy(a, b, sem_in.at[i]) for i, (a, b) in enumerate(
-        ((x_hbm, x_ref), (wq_hbm, wq_ref), (c_hbm, c_ref), (wk_hbm, wk_ref), (wv_hbm, wv_ref)))]
+        ((x_hbm, x_ref), (wq_hbm.at[:, mine], wq_ref), (c_hbm.at[:, mine], c_ref),
+         (wk_hbm.at[:, mine], wk_ref), (wv_hbm.at[:, mine], wv_ref)))]
     slots = [pltpu.make_async_copy(r_hbm.at[lax.rem(me + p, n_slot)], r_ref.at[pl.ds(p * length, length), :],
                                    sem_r.at[p]) for p in range(n_slot)]
     for c in copies[:4] + slots + copies[4:]:
         c.start()
+    before = []
+    if earlier:
+        dk0, dv0, wk0, wv0, dx_v, sem_b = scratch[25:]
+        old = pl.ds(0, lo)
+        before = [pltpu.make_async_copy(a, b, sem_b.at[i]) for i, (a, b) in enumerate(
+            ((dk0_hbm, dk0), (dv0_hbm, dv0), (wk_hbm.at[:, old], wk0), (wv_hbm.at[:, old], wv0)))]
+        for c in before:
+            c.start()
 
     for i in range(n_src * n_slot):
         mult[i] = 0
@@ -162,68 +177,88 @@
         out(gw_v.at[k], dst)
         if k == 0:
             out(dq_v, dq_hbm)
+            if not earlier:
+                for t in range(n_slot):
+                    out(k_s.at[t], outs[4].at[pl.ds(t * length, length), :])
+                    out(v_s.at[t], outs[5].at[pl.ds(t * length, length), :])
     for s in range(n_src):
         att_v[s * length:(s + 1) * length, :] = ot[s].T.astype(BF)
-    out(att_v, att_hbm)
-    for lo in range(0, n_slot, half):
-        rows = slice(lo * length, (lo + half) * length)
-        for n in range(0, width, block):
-            cols = slice(n, n + block)
-            dx_v[rows, cols] = (mm_nt(dk[rows], wk_ref[cols, :]) + mm_nt(dv[rows], wv_ref[cols, :])).astype(BF)
-        for t in range(lo, lo + half):
-            out(dx_v.at[pl.ds(t * length, length), :], dx_hbm[t])
+    out(att_v, att_hbm.at[:, mine])
+    if earlier:
+        for c in before:
+            c.wait()
+        half = n_slot // 2
+        for top in range(0, n_slot, half):
+            rows = slice(top * length, (top + half) * length)
+            for n in range(0, depth, block):
+                cols = slice(n, n + block)
+                dx = mm_nt(dk[rows], wk_ref[cols, :]) + mm_nt(dv[rows], wv_ref[cols, :])
+                dx += mm_nt(dk0[rows, :], wk0[cols, :]) + mm_nt(dv0[rows, :], wv0[cols, :])
+                dx_v[rows, cols] = dx.astype(BF)
+            for t in range(top, top + half):
+                out(dx_v.at[pl.ds(t * length, length), :], outs[4 + t])
     for c in done:
         c.wait()
 
 
-def attend(me, src, slot, valid, x, r, c, wq, wk, wv, *, pieces):
-    n_slot, length, width = r.shape
+def attend(me, src, slot, valid, x, r, c, wq, wk, wv, earlier=(), *, lo, width, pieces):
+    n_slot, length, depth = r.shape
     rows = x.shape[0]
     n_src = rows // length
-    each = width // 2 // pieces
+    each = depth // 2 // pieces
     heads = width // LANES
     smem = pl.BlockSpec(memory_space=pltpu.SMEM)
-    hbm = pl.BlockSpec(memory_space=pl.ANY)
+    hbm = pl.BlockSpec(memory_space=pltpu.HBM)
     shape = jax.ShapeDtypeStruct
     vm = pltpu.VMEM
-    macs = 2 * (n_src + 3 * n_slot) * length * width * width + 12 * 6 * length * length * width
+    tall = (n_slot * length, width)
+    out_shape = [shape((rows, depth), BF), shape((rows, width), BF)]
+    out_shape += [shape((pieces, 3, each, width), BF)] * 2
+    scratch = [
+        pltpu.SMEM((n_src * n_slot,), jnp.int32),
+        vm((rows, depth), BF), vm((n_slot * length, depth), BF), vm((rows, width), BF),
+        vm((depth, width), BF), vm((depth, width), BF), vm((depth, width), BF),
+        vm((rows, width), BF), vm((rows, width), BF), vm((2, pieces, 3, each, width), BF),
+        vm((depth, rows), BF), vm((depth, n_slot * length), BF),
+        vm((n_src, heads, 2 * length, LANES), BF), vm((n_src, heads, 2 * length, LANES), BF),
+        vm((n_slot, length, width), BF), vm((n_slot, length, width), BF),
+        vm((n_slot, width, length), BF), vm((n_slot, width, length), BF),
+        vm((n_src, width, length), F32), vm((n_src, width, length), F32),
+        vm((n_slot, length, width), F32), vm((n_slot, length, width), F32),
+        pltpu.SemaphoreType.DMA((5,)), pltpu.SemaphoreType.DMA((n_slot,)),
+        pltpu.SemaphoreType.DMA((4 + 2 * n_slot,)),
+    ]
+    if earlier:
+        out_shape += [shape((length, depth), BF)] * n_slot
+        scratch += [vm((n_slot * length, lo), BF), vm((n_slot * length, lo), BF), vm((depth, lo), BF),
+                    vm((depth, lo), BF), vm((n_slot * length, depth), BF), pltpu.SemaphoreType.DMA((4,))]
+    else:
+        out_shape += [shape(tall, BF)] * 2
+    macs = 2 * (n_src + 2 * n_slot) * length * depth * width + 12 * 6 * length * length * width
     return pl.pallas_call(
-        functools.partial(attend_kernel, n_src=n_src, n_slot=n_slot, length=length),
-        in_specs=[smem] * 4 + [hbm] * 6,
-        out_specs=[hbm] * (4 + n_slot),
-        out_shape=[shape((rows, width), BF), shape((rows, width), BF),
-                   shape((pieces, 3, each, width), BF), shape((pieces, 3, each, width), BF)]
-        + [shape((length, width), BF)] * n_slot,
-        scratch_shapes=[
-            pltpu.SMEM((n_src * n_slot,), jnp.int32),
-            vm((rows, width), BF), vm((n_slot * length, width), BF), vm((rows, width), BF),
-            vm((width, width), BF), vm((width, width), BF), vm((width, width), BF),
-            vm((rows, width), BF), vm((rows, width), BF),
-            vm((2, pieces, 3, each, width), BF), vm((n_slot * length, width), BF),
-            vm((width, rows), BF), vm((width, n_slot * length), BF),
-            vm((n_src, heads, 2 * length, LANES), BF), vm((n_src, heads, 2 * length, LANES), BF),
-            vm((n_slot, length, width), BF), vm((n_slot, length, width), BF),
-            vm((n_slot, width, length), BF), vm((n_slot, width, length), BF),
-            vm((n_src, width, length), F32), vm((n_src, width, length), F32),
-            vm((n_slot, length, width), F32), vm((n_slot, length, width), F32),
-            pltpu.SemaphoreType.DMA((5,)), pltpu.SemaphoreType.DMA((n_slot,)),
-            pltpu.SemaphoreType.DMA((4 + n_slot,)),
-        ],
-        compiler_params=pltpu.CompilerParams(vmem_limit_bytes=60 * 2**20),
-        cost_estimate=pl.CostEstimate(flops=4 * macs, bytes_accessed=20 * 2**20, transcendentals=0),
+        functools.partial(attend_kernel, n_src=n_src, n_slot=n_slot, length=length, lo=lo, earlier=bool(earlier)),
+        in_specs=[smem] * 4 + [hbm] * (6 + len(earlier)),
+        out_specs=[hbm] * len(out_shape),
+        out_shape=out_shape,
+        scratch_shapes=scratch,
+        input_output_aliases={12: 0} if earlier else {},
+        compiler_params=pltpu.CompilerParams(vmem_limit_bytes=56 * 2**20),
+        cost_estimate=pl.CostEstimate(flops=8 * macs, bytes_accessed=16 * 2**20, transcendentals=0),
         name="attend",
-    )(me, src, slot, valid, x, r, c, wq, wk, wv)
-
-
-def combine_kernel(me_ref, listed_ref, dq_ref, wq_ref, *rest):
+    )(me, src, slot, valid, x, r, c, wq, wk, wv, *earlier)
+
+
+def combine_kernel(me_ref, listed_ref, dq0_ref, dq1_ref, wq_ref, *rest):
     parts, (out_ref, acc) = rest[:-2], rest[-2:]
     n_slot = len(parts)
     length = parts[0].shape[0]
     me = me_ref[0]
     block = 256
+    lo = dq0_ref.shape[1]
     for n in range(0, acc.shape[2], block):
         cols = slice(n, n + block)
-        acc[:, :, cols] = mm_nt(dq_ref[...], wq_ref[cols, :]).reshape(acc.shape[0], length, block)
+        dx = mm_nt(dq0_ref[...], wq_ref[cols, :lo]) + mm_nt(dq1_ref[...], wq_ref[cols, lo:])
+        acc[:, :, cols] = dx.reshape(acc.shape[0], length, block)
     for s, part in enumerate(parts):
         at = listed_ref[lax.rem(me + n_slot - s, n_slot)]
         acc[at] += part[...].astype(F32)
@@ -232,39 +267,46 @@
 
 def combine(me, listed, dq, wq, parts):
     length, width = parts[0].shape
-    n_src = dq.shape[0] // length
+    n_src = dq[0].shape[0] // length
     smem = pl.BlockSpec(memory_space=pltpu.SMEM)
     vmem = pl.BlockSpec(memory_space=pltpu.VMEM)
     return pl.pallas_call(
         combine_kernel,
-        in_specs=[smem, smem] + [vmem] * (2 + len(parts)),
+        in_specs=[smem, smem] + [vmem] * (3 + len(parts)),
         out_specs=vmem,
         out_shape=jax.ShapeDtypeStruct((n_src, length, width), BF),
         scratch_shapes=[pltpu.VMEM((n_src, length, width), F32)],
         compiler_params=pltpu.CompilerParams(vmem_limit_bytes=24 * 2**20),
-        cost_estimate=pl.CostEstimate(flops=2 * dq.size * width, bytes_accessed=6 * 2**20, transcendentals=0),
+        cost_estimate=pl.CostEstimate(flops=2 * wq.size * n_src * length, bytes_accessed=6 * 2**20, transcendentals=0),
         name="combine",
-    )(me, listed, dq, wq, *parts)
-
-
-def spread_kernel(parts_ref, out_ref, *, factor):
-    total = jnp.sum(parts_ref[...].astype(F32), axis=0)
-    out_ref[...] = jnp.broadcast_to((total * factor).astype(BF)[None], out_ref.shape)
+    )(me, listed, *dq, wq, *parts)
+
+
+def spread_kernel(*refs, factor):
+    out_ref = refs[-1]
+    at = 0
+    for ref in refs[:-1]:
+        cols = slice(at, at + ref.shape[-1])
+        total = jnp.sum(ref[...].astype(F32), axis=0)
+        out_ref[:, :, :, cols] = jnp.broadcast_to((total * factor).astype(BF)[None], out_ref.shape[:3] + total.shape[-1:])
+        at = cols.stop
 
 
 def spread(parts, copies, factor):
-    shape = parts.shape[1:]
-    grid = shape[0]
+    n, each = parts[0].shape[1:3]
+    width = sum(p.shape[-1] for p in parts)
+    spec = lambda count, w: pl.BlockSpec((count, 1, each, w), lambda i: (0, i, 0, 0))
+    size = sum(p.size for p in parts)
     return pl.pallas_call(
         functools.partial(spread_kernel, factor=factor),
-        grid=(grid,),
-        in_specs=[pl.BlockSpec((parts.shape[0], 1) + shape[1:], lambda i: (0, i, 0, 0))],
-        out_specs=pl.BlockSpec((copies, 1) + shape[1:], lambda i: (0, i, 0, 0)),
-        out_shape=jax.ShapeDtypeStruct((copies,) + shape, BF),
+        grid=(n,),
+        in_specs=[spec(p.shape[0], p.shape[-1]) for p in parts],
+        out_specs=spec(copies, width),
+        out_shape=jax.ShapeDtypeStruct((copies, n, each, width), BF),
         compiler_params=pltpu.CompilerParams(vmem_limit_bytes=16 * 2**20),
-        cost_estimate=pl.CostEstimate(flops=parts.size, bytes_accessed=4 * parts.size, transcendentals=0),
+        cost_estimate=pl.CostEstimate(flops=size, bytes_accessed=4 * size, transcendentals=0),
         name="spread",
-    )(parts)
+    )(*parts)
 
 
 def place_kernel(half_ref, rows_ref, *rest):
@@ -276,7 +318,7 @@
 def place(half, rows, into=()):
     pieces, n, each, width = rows.shape
     step = pieces // 4
-    hbm = pl.BlockSpec(memory_space=pl.ANY)
+    hbm = pl.BlockSpec(memory_space=pltpu.HBM)
     return pl.pallas_call(
         place_kernel,
         grid_spec=pltpu.PrefetchScalarGridSpec(
@@ -304,27 +346,41 @@
     x = sentences.reshape(-1, width)
     c = cotangent.reshape(-1, width)
     where = me.reshape(1).astype(jnp.int32)
-    attended, dq, keep, send, *dx = attend(
-        where, pair_src, pair_slot, pair_valid, x, received, c, w_query, w_key, w_value, pieces=n_pair
+    other_core = [(i, i ^ 1) for i in range(n_lang)]
+
+    def chip_sum(keep, send):
+        other = lax.ppermute(send, "lang", other_core)
+        return (keep.astype(F32) + other.astype(F32)).astype(BF)
+
+    def over_pair(a):
+        return lax.all_to_all(a, "pair", split_axis=0, concat_axis=0, tiled=True)
+
+    half = width // 2
+    pairs = (where, pair_src, pair_slot, pair_valid)
+    attended, dq0, keep, send, dk0, dv0 = attend(
+        *pairs, x, received, c, w_query, w_key, w_value, lo=0, width=half, pieces=n_pair
     )
-    other_core = [(i, i ^ 1) for i in range(n_lang)]
-    other = lax.ppermute(send, "lang", other_core)
+    chip, x = lax.optimization_barrier((chip_sum(keep, send), x))
+    pieces0 = over_pair(chip)
+    attended, dq1, keep, send, *dx = attend(
+        *pairs, x, received, c, w_query, w_key, w_value, (dk0, dv0, attended), lo=half, width=half, pieces=n_pair
+    )
+    pieces0, dq1, keep, send, *dx = lax.optimization_barrier((pieces0, dq1, keep, send, *dx))
     back = [dx[0]]
     for s in range(1, n_lang):
         back.append(lax.ppermute(dx[s], "lang", [(i, (i + s) % n_lang) for i in range(n_lang)]))
-    chip = (keep.astype(F32) + other.astype(F32)).astype(BF)
-    pieces = lax.all_to_all(chip, "pair", split_axis=0, concat_axis=0, tiled=True)
-    pieces, *back[1:6] = lax.optimization_barrier((pieces, *back[1:6]))
+    pieces1 = over_pair(chip_sum(keep, send))
+    pieces1, *back[1:6] = lax.optimization_barrier((pieces1, *back[1:6]))
     n_y = n_lang // 2
     along_y = [[2 * y + core for y in range(n_y)] for core in range(2)]
     columns = lax.all_to_all(
-        spread(pieces, n_y, 1.0), "lang", split_axis=0, concat_axis=0, axis_index_groups=along_y, tiled=True
+        spread((pieces0, pieces1), n_y, 1.0), "lang", split_axis=0, concat_axis=0, axis_index_groups=along_y, tiled=True
     )
     factor = 1.0 / (sent_dev * n_lang * n_pair * length) ** 0.5
-    near = lax.all_to_all(spread(columns, n_pair, factor), "pair", split_axis=0, concat_axis=0, tiled=True)
-    near, *back[6:] = lax.optimization_barrier((near, *back[6:]))
+    near = over_pair(spread((columns,), n_pair, factor))
+    grad_sentences = combine(where, listed, (dq0, dq1), w_query, back)
+    near, grad_sentences = lax.optimization_barrier((near, grad_sentences))
     far = lax.ppermute(near, "lang", other_core)
-    grad_sentences = combine(where, listed, dq, w_query, back)
     core = lax.rem(where, 2)
     grads = place(1 - core, far, place(core, near))
     grads = tuple(g.reshape(width, width) for g in grads)

time: 219 us -> 218 us (level); the launches traced: 218 us -> 214 us
  waiting for transfers between devices: 90.9 us -> 83.4 us
  Pallas kernels: 43.5 us -> 46.6 us
    all_to_all x2 -> x3, waiting for transfers between devices: 33.5 us -> 19.6 us  [over_pair(): return lax.all_to_all(a, 'pair', split_axis=0, concat_axis=0, tiled=True)]
    ppermute x1, starting transfers between devices: 7.26 us -> 1.93 us  [body(): far = lax.ppermute(near, 'lang', other_core)]
    ppermute x1 -> x2, starting transfers between devices: 2.1 us -> 7.29 us  [chip_sum(): other = lax.ppermute(send, 'lang', other_core)]
    ppermute x7, starting transfers between devices: 11.9 us -> 8.42 us  [body(): lax.ppermute(dx[s], 'lang', [(i, (i + s) % n_lang) for i in range(n_lang)])]
    ppermute x1, waiting for transfers between devices: 0.01 us -> 3.18 us  [body(): far = lax.ppermute(near, 'lang', other_core)]
    pallas_call x1 -> x2, Pallas kernels: 34.6 us -> 37.6 us  [attend(): pl.pallas_call(functools.partial(attend_kernel, n_src=n_src, n_slot=n_slo...]
    ppermute x7, waiting for transfers between devices: 25.6 us -> 27.8 us  [body(): lax.ppermute(dx[s], 'lang', [(i, (i + s) % n_lang) for i in range(n_lang)])]
    all_to_all x2 -> x3, starting transfers between devices: 18.5 us -> 20.2 us  [over_pair(): return lax.all_to_all(a, 'pair', split_axis=0, concat_axis=0, tiled=True)]
  transfers between devices with their start and end apart: 12 -> 14, of which waited for: 9 -> 11; matrix products, arithmetic and copies ran while one was open for 0% -> 0% of each run, Pallas kernels for 2% -> 12%
where the time goes in v5:
time: 218 us; the launch traced here: 214 us
  waiting for transfers between devices  83.4 us (38%)
  Pallas kernels  46.6 us (21%)
  starting transfers between devices  43.8 us (20%)
  local copies, waits for them, and re-layouts  18.1 us (8%)
  blocking collectives  14.2 us (7%)
  other arithmetic  7.02 us (3%)
    pallas_call x2, Pallas kernels, attend(): pl.pallas_call(functools.partial(attend_kernel, n_src=n_src, n_slot=n_slo...  37.6 us
    ppermute x7, waiting for transfers between devices, body(): lax.ppermute(dx[s], 'lang', [(i, (i + s) % n_lang) for i in range(n_lang)])  27.8 us
    all_to_all x1, waiting for transfers between devices, body(): lax.all_to_all(outgoing, 'lang', split_axis=0, concat_axis=0, tiled=True)  26.3 us
    all_to_all x3, starting transfers between devices, over_pair(): return lax.all_to_all(a, 'pair', split_axis=0, concat_axis=0, tiled=True)  20.2 us
    all_to_all x3, waiting for transfers between devices, over_pair(): return lax.all_to_all(a, 'pair', split_axis=0, concat_axis=0, tiled=True)  19.6 us
    unnamed x36, local copies, waits for them, and re-layouts  14.9 us
    all_to_all x1, blocking collectives, body(): lax.all_to_all(spread((pieces0, pieces1), n_y, 1.0), 'lang', split_axis=0...  14.2 us
    ppermute x7, starting transfers between devices, body(): lax.ppermute(dx[s], 'lang', [(i, (i + s) % n_lang) for i in range(n_lang)])  8.42 us
  transfers between devices with their start and end apart: 14, of which 11 were waited for; matrix products, arithmetic and copies ran while one was open for 0% of the time, Pallas kernels for 12%

profile of v5, /device:TPU:1, one launch (start us, length us, event | category | flops | bytes accessed | tf_op | source)
XLA Modules:
  0.0 213.8 jit_solution(18104961146885890572)
XLA Ops:
  1.3 3.2 %gather_fusion = bf16[8,128,1024]{2,1,0:T(8,128)(2,1)} fusion(bf16[4,128,1024]{2,1,0:T(8,128)(2,1)} %param.9, s32[1024]{0:T(1024)S(1)} %pad_clamp_fusion), kind=kCustom, calls=%fused_computation | custom fusion | bytes 4194336 | tf_op jit(solution)/shard_map/jit(_take)/gather | solution.py:344
  4.5 6.0 %all-to-all-start = ((bf16[8,128,1024]{2,1,0:T(8,128)(2,1)}), bf16[8,128,1024]{2,1,0:T(8,128)(2,1)S(1)}, u32[]{:S(2)}, u32[]{:S(2)}) async-start(bf16[8,128,1024]{2,1,0:T(8,128)(2,1)} %gather_fusion), calls=%async_computation | async-start | bytes 4194304 | tf_op jit(solution)/shard_map/all_to_all | solution.py:345
  10.5 26.3 %all-to-all-done.r_hbm = bf16[8,128,1024]{2,1,0:T(8,128)(2,1)S(1)} async-done(((bf16[8,128,1024]{2,1,0:T(8,128)(2,1)}), bf16[8,128,1024]{2,1,0:T(8,128)(2,1)S(1)}, u32[]{:S(2)}, u32[]{:S(2)}) %all-to-all-start) | async-done | bytes 2097184 | tf_op jit(solution)/shard_map/all_to_all | solution.py:345
  36.8 1.3 copy-done.16
  38.1 16.6 %attend.2 = (bf16[512,1024]{1,0:T(8,128)(2,1)}, bf16[512,512]{1,0:T(8,128)(2,1)}, bf16[16,3,32,512]{3,2,1,0:T(8,128)(2,1)}, bf16[16,3,32,512]{3,2,1,0:T(8,128)(2...) custom-call(s32[1]{0:T(128)} %bitcast.me_ref, s32[1,16]{1,0:T(1,128)} %src_ref.3, s32[1,16]{1,0:T(1,128)} %slot_ref.3, ...), custom_call_target="tpu_custom_call" | custom-call | flops 26306674688 | bytes 16777216 | tf_op jit(solution)/shard_map/attend/pallas_call | solution.py:238
  54.8 4.3 %collective-permute-start = (bf16[16,3,32,512]{3,2,1,0:T(8,128)(2,1)}, bf16[16,3,32,512]{3,2,1,0:T(8,128)(2,1)S(1)}, u32[]{:S(2)}, u32[]{:S(2)}) collective-permute-start(bf16[16,3,32,512]{3,2,1,0:T(8,128)(2,1)} %get-tuple-element.52), channel_id=1, source_target_pairs={{0,16},{16,0},{32,48},{48,32},{64,80},{80,64},{96,112},{112,96},{1... | collective-permute-start | bytes 4718600 | tf_op jit(solution)/shard_map/ppermute | solution.py:352
  59.1 3.2 %collective-permute-done = bf16[16,3,32,512]{3,2,1,0:T(8,128)(2,1)S(1)} collective-permute-done((bf16[16,3,32,512]{3,2,1,0:T(8,128)(2,1)}, bf16[16,3,32,512]{3,2,1,0:T(8,128)(2,1)S(1)}, u32[]{:S(2)}, u32[]{:S(2)}) %collective-permute-start) | collective-permute-done | bytes 1572896 | tf_op jit(solution)/shard_map/ppermute | solution.py:352
  62.4 3.2 %add_convert_fusion.1 = bf16[16,3,32,512]{3,2,1,0:T(8,128)(2,1)} fusion(bf16[16,3,32,512]{3,2,1,0:T(8,128)(2,1)S(1)} %collective-permute-done, bf16[16,3,32,512]{3,2,1,0:T(8,128)(2,1)} %get-tuple-element.51), kind=kLoop, calls=%fused_computation.2 | loop fusion | flops 3145728 | bytes 4718592 | tf_op jit(solution)/shard_map/convert_element_type | solution.py:353
  65.6 6.9 %all-to-all-start.1 = ((bf16[16,3,32,512]{3,2,1,0:T(8,128)(2,1)}), bf16[16,3,32,512]{3,2,1,0:T(8,128)(2,1)S(1)}, u32[]{:S(2)}, u32[]{:S(2)}) async-start(bf16[16,3,32,512]{3,2,1,0:T(8,128)(2,1)} %add_convert_fusion.1), calls=%async_computation.1 | async-start | bytes 3145728 | tf_op jit(solution)/shard_map/all_to_all | solution.py:356
  72.5 21.0 %attend.3 = (bf16[512,1024]{1,0:T(8,128)(2,1)}, bf16[512,512]{1,0:T(8,128)(2,1)}, bf16[16,3,32,512]{3,2,1,0:T(8,128)(2,1)}, bf16[16,3,32,512]{3,2,1,0:T(8,128)(2...) custom-call(s32[1]{0:T(128)} %bitcast.me_ref, ...), custom_call_target="tpu_custom_call", output_to_operand_aliasing={{0}: (12, {})} | custom-call | flops 26306674688 | bytes 16777216 | tf_op jit(solution)/shard_map/attend/pallas_call | solution.py:238
  93.5 1.2 all-to-all-done.1.refs_0_
  94.7 2.9 %collective-permute-start.1 = (bf16[16,3,32,512]{3,2,1,0:T(8,128)(2,1)}, bf16[16,3,32,512]{3,2,1,0:T(8,128)(2,1)S(1)}, u32[]{:S(2)}, u32[]{:S(2)}) collective-permute-start(bf16[16,3,32,512]{3,2,1,0:T(8,128)(2,1)} %get-tuple-element.72), channel_id=1, source_target_pairs={{0,16},{16,0},{32,48},{48,32},{64,80},{80,64},{96,112},{112,96},{1... | collective-permute-start | bytes 4718600 | tf_op jit(solution)/shard_map/ppermute | solution.py:352
  97.7 3.2 %collective-permute-done.1 = bf16[16,3,32,512]{3,2,1,0:T(8,128)(2,1)S(1)} collective-permute-done((bf16[16,3,32,512]{3,2,1,0:T(8,128)(2,1)}, bf16[16,3,32,512]{3,2,1,0:T(8,128)(2,1)S(1)}, u32[]{:S(2)}, u32[]{:S(2)}) %collective-permute-start.1) | collective-permute-done | bytes 1572896 | tf_op jit(solution)/shard_map/ppermute | solution.py:352
  100.9 3.2 %add_convert_fusion = bf16[16,3,32,512]{3,2,1,0:T(8,128)(2,1)} fusion(bf16[16,3,32,512]{3,2,1,0:T(8,128)(2,1)S(1)} %collective-permute-done.1, bf16[16,3,32,512]{3,2,1,0:T(8,128)(2,1)} %get-tuple-element.71), kind=kLoop, calls=%fused_computation.1 | loop fusion | flops 3145728 | bytes 4718592 | tf_op jit(solution)/shard_map/convert_element_type | solution.py:353
  104.1 6.2 %all-to-all-start.2 = ((bf16[16,3,32,512]{3,2,1,0:T(8,128)(2,1)}), bf16[16,3,32,512]{3,2,1,0:T(8,128)(2,1)S(1)}, u32[]{:S(2)}, u32[]{:S(2)}) async-start(bf16[16,3,32,512]{3,2,1,0:T(8,128)(2,1)} %add_convert_fusion), calls=%async_computation.2 | async-start | bytes 3145728 | tf_op jit(solution)/shard_map/all_to_all | solution.py:356
  110.3 0.8 collective-permute-start.2
  111.1 3.4 %collective-permute-start.4 = (bf16[128,1024]{1,0:T(8,128)(2,1)}, bf16[128,1024]{1,0:T(8,128)(2,1)S(1)}, u32[]{:S(2)}, u32[]{:S(2)}) collective-permute-start(bf16[128,1024]{1,0:T(8,128)(2,1)} %get-tuple-element.75), channel_id=1, source_target_pairs={{0,48},{16,64},{32,80},{48,96},{64,112},{80,0},{96,16},{112,32},{1... | collective-permute-start | bytes 786440 | tf_op jit(solution)/shard_map/ppermute | solution.py:371
  114.6 2.6 %collective-permute-start.6 = (bf16[128,1024]{1,0:T(8,128)(2,1)S(1)}, bf16[128,1024]{1,0:T(8,128)(2,1)S(1)}, u32[]{:S(2)}, u32[]{:S(2)}) collective-permute-start(bf16[128,1024]{1,0:T(8,128)(2,1)S(1)} %copy-done.17), channel_id=1, source_target_pairs={{0,80},{16,96},{32,112},{48,0},{64,16},{80,32},{96,48},{112,64},{1... | collective-permute-start | bytes 786440 | tf_op jit(solution)/shard_map/ppermute | solution.py:371
  117.2 0.7 copy-done.5
  117.9 7.6 %collective-permute-done.3.rest_2_ = bf16[128,1024]{1,0:T(8,128)(2,1)S(1)} collective-permute-done((bf16[128,1024]{1,0:T(8,128)(2,1)}, bf16[128,1024]{1,0:T(8,128)(2,1)S(1)}, u32[]{:S(2)}, u32[]{:S(2)}) %collective-permute-start.3) | collective-permute-done | bytes 262176 | tf_op jit(solution)/shard_map/ppermute | solution.py:371
  125.5 0.7 copy-done.7
  126.2 2.0 collective-permute-done.4.rest_3_
  128.2 0.7 copy-done.9
  128.9 8.3 %collective-permute-done.5.rest_4_ = bf16[128,1024]{1,0:T(8,128)(2,1)S(1)} collective-permute-done((bf16[128,1024]{1,0:T(8,128)(2,1)}, bf16[128,1024]{1,0:T(8,128)(2,1)S(1)}, u32[]{:S(2)}, u32[]{:S(2)}) %collective-permute-start.5) | collective-permute-done | bytes 262176 | tf_op jit(solution)/shard_map/ppermute | solution.py:371
  137.2 0.7 copy-done.11
  137.9 0.7 copy-done.13
  138.6 0.7 spread.2
  139.3 14.2 %all_to_all.25.refs_0_ = bf16[4,3,32,1024]{3,2,1,0:T(8,128)(2,1)S(1)} all-to-all(bf16[4,3,32,1024]{3,2,1,0:T(8,128)(2,1)S(1)} %spread.2), channel_id=1, replica_groups={{0,32,64,96},{16,48,80,112},{1,33,65,97},{17,49,81,113},{2,34,66,98},{1..., dimensions={0} | all-to-all | bytes 1572864 | tf_op jit(solution)/shard_map/all_to_all | solution.py:376
  153.5 0.7 spread.3
  154.2 1.6 copy-done
  155.8 7.1 %all-to-all-start.4 = ((bf16[16,3,32,1024]{3,2,1,0:T(8,128)(2,1)}), bf16[16,3,32,1024]{3,2,1,0:T(8,128)(2,1)S(1)}, u32[]{:S(2)}, u32[]{:S(2)}) async-start(bf16[16,3,32,1024]{3,2,1,0:T(8,128)(2,1)} %copy-done), calls=%async_computation.4 | async-start | bytes 6291456 | tf_op jit(solution)/shard_map/all_to_all | solution.py:356
  162.9 1.0 collective-permute-start.7
  164.4 6.4 %collective-permute-done.7.rest_6_ = bf16[128,1024]{1,0:T(8,128)(2,1)S(1)} collective-permute-done((bf16[128,1024]{1,0:T(8,128)(2,1)}, bf16[128,1024]{1,0:T(8,128)(2,1)S(1)}, u32[]{:S(2)}, u32[]{:S(2)}) %collective-permute-start.7) | collective-permute-done | bytes 262176 | tf_op jit(solution)/shard_map/ppermute | solution.py:371
  170.8 3.6 %collective-permute-done.8.rest_7_ = bf16[128,1024]{1,0:T(8,128)(2,1)S(1)} collective-permute-done((bf16[128,1024]{1,0:T(8,128)(2,1)}, bf16[128,1024]{1,0:T(8,128)(2,1)S(1)}, u32[]{:S(2)}, u32[]{:S(2)}) %collective-permute-start.8) | collective-permute-done | bytes 262176 | tf_op jit(solution)/shard_map/ppermute | solution.py:371
  174.3 1.6 copy-done.1
  175.9 1.0 copy-done.2
  177.0 1.0 copy-done.3
  178.0 0.9 copy-done.6
  179.0 0.9 copy-done.8
  179.9 0.9 copy-done.10
  180.9 0.9 copy-done.12
  181.8 0.9 copy-done.14
  182.8 3.3 %combine.1 = bf16[4,128,1024]{2,1,0:T(8,128)(2,1)} custom-call(s32[1]{0:T(128)} %bitcast.me_ref, s32[8]{0:T(128)S(1)} %bitcast.9, bf16[512,512]{1,0:T(8,128)(2,1)S(1)} %copy-done.2, bf16[512,512]{1,0:T(8,128)(2,1)S(1)} %copy-done.3, bf16[1024,1024]{1,0:T(8,128)(2,1)S(1)} %copy-done.1, bf16[128,1024]{1,0:T(8,128)(2,1)S(1)} %copy-done.4, ...), custom_call_target="tpu_custom_call" | custom-call | flops 1073741824 | bytes 6291456 | tf_op jit(solution)/shard_map/combine/pallas_call | solution.py:273
  186.1 18.4 %all-to-all-done.4.rows_ref = bf16[16,3,32,1024]{3,2,1,0:T(8,128)(2,1)S(1)} async-done(((bf16[16,3,32,1024]{3,2,1,0:T(8,128)(2,1)}), bf16[16,3,32,1024]{3,2,1,0:T(8,128)(2,1)S(1)}, u32[]{:S(2)}, u32[]{:S(2)}) %all-to-all-start.4) | async-done | bytes 3145760 | tf_op jit(solution)/shard_map/all_to_all | solution.py:356
  204.4 1.9 collective-permute-start.9
  206.4 2.1 place.2
  208.5 3.2 %collective-permute-done.9.rows_ref = bf16[16,3,32,1024]{3,2,1,0:T(8,128)(2,1)S(1)} collective-permute-done((bf16[16,3,32,1024]{3,2,1,0:T(8,128)(2,1)S(1)}, bf16[16,3,32,1024]{3,2,1,0:T(8,128)(2,1)S(1)}, u32[]{:S(2)}, u32[]{:S(2)}) %collective-permute-start.9) | collective-permute-done | bytes 3145760 | tf_op jit(solution)/shard_map/ppermute | solution.py:383
  211.7 2.1 place.3
  (28 shorter events, 1.3 us)
Async XLA Ops:
  4.5 32.3 %all-to-all-start = ((bf16[8,128,1024]{2,1,0:T(8,128)(2,1)}), bf16[8,128,1024]{2,1,0:T(8,128)(2,1)S(1)}, u32[]{:S(2)}, u32[]{:S(2)}) async-start(bf16[8,128,1024]{2,1,0:T(8,128)(2,1)} %gather_fusion), calls=%async_computation | async-start | bytes 4194304 | tf_op jit(solution)/shard_map/all_to_all | solution.py:345
  36.8 1.3 copy-start.16
  54.8 7.6 %collective-permute-start = (bf16[16,3,32,512]{3,2,1,0:T(8,128)(2,1)}, bf16[16,3,32,512]{3,2,1,0:T(8,128)(2,1)S(1)}, u32[]{:S(2)}, u32[]{:S(2)}) collective-permute-start(bf16[16,3,32,512]{3,2,1,0:T(8,128)(2,1)} %get-tuple-element.52), channel_id=1, source_target_pairs={{0,16},{16,0},{32,48},{48,32},{64,80},{80,64},{96,112},{112,96},{1... | collective-permute-start | bytes 4718600 | tf_op jit(solution)/shard_map/ppermute | solution.py:352
  65.6 29.1 %all-to-all-start.1 = ((bf16[16,3,32,512]{3,2,1,0:T(8,128)(2,1)}), bf16[16,3,32,512]{3,2,1,0:T(8,128)(2,1)S(1)}, u32[]{:S(2)}, u32[]{:S(2)}) async-start(bf16[16,3,32,512]{3,2,1,0:T(8,128)(2,1)} %add_convert_fusion.1), calls=%async_computation.1 | async-start | bytes 3145728 | tf_op jit(solution)/shard_map/all_to_all | solution.py:356
  94.7 6.2 %collective-permute-start.1 = (bf16[16,3,32,512]{3,2,1,0:T(8,128)(2,1)}, bf16[16,3,32,512]{3,2,1,0:T(8,128)(2,1)S(1)}, u32[]{:S(2)}, u32[]{:S(2)}) collective-permute-start(bf16[16,3,32,512]{3,2,1,0:T(8,128)(2,1)} %get-tuple-element.72), channel_id=1, source_target_pairs={{0,16},{16,0},{32,48},{48,32},{64,80},{80,64},{96,112},{112,96},{1... | collective-permute-start | bytes 4718600 | tf_op jit(solution)/shard_map/ppermute | solution.py:352
  104.1 10.5 %copy-start.17 = (bf16[128,1024]{1,0:T(8,128)(2,1)S(1)}, bf16[128,1024]{1,0:T(8,128)(2,1)}, u32[]{:S(2)}) copy-start(bf16[128,1024]{1,0:T(8,128)(2,1)} %get-tuple-element.77) | copy-start | bytes 786436
  104.1 34.5 %all-to-all-start.2 = ((bf16[16,3,32,512]{3,2,1,0:T(8,128)(2,1)}), bf16[16,3,32,512]{3,2,1,0:T(8,128)(2,1)S(1)}, u32[]{:S(2)}, u32[]{:S(2)}) async-start(bf16[16,3,32,512]{3,2,1,0:T(8,128)(2,1)} %add_convert_fusion), calls=%async_computation.2 | async-start | bytes 3145728 | tf_op jit(solution)/shard_map/all_to_all | solution.py:356
  110.3 6.9 %collective-permute-start.2 = (bf16[128,1024]{1,0:T(8,128)(2,1)}, bf16[128,1024]{1,0:T(8,128)(2,1)S(1)}, u32[]{:S(2)}, u32[]{:S(2)}) collective-permute-start(bf16[128,1024]{1,0:T(8,128)(2,1)} %get-tuple-element.73), channel_id=1, source_target_pairs={{0,16},{16,32},{32,48},{48,64},{64,80},{80,96},{96,112},{112,0},{1... | collective-permute-start | bytes 786440 | tf_op jit(solution)/shard_map/ppermute | solution.py:371
  111.1 14.4 %collective-permute-start.3 = (bf16[128,1024]{1,0:T(8,128)(2,1)}, bf16[128,1024]{1,0:T(8,128)(2,1)S(1)}, u32[]{:S(2)}, u32[]{:S(2)}) collective-permute-start(bf16[128,1024]{1,0:T(8,128)(2,1)} %get-tuple-element.74), channel_id=1, source_target_pairs={{0,32},{16,48},{32,64},{48,80},{64,96},{80,112},{96,0},{112,16},{1... | collective-permute-start | bytes 786440 | tf_op jit(solution)/shard_map/ppermute | solution.py:371
  111.1 17.1 %collective-permute-start.4 = (bf16[128,1024]{1,0:T(8,128)(2,1)}, bf16[128,1024]{1,0:T(8,128)(2,1)S(1)}, u32[]{:S(2)}, u32[]{:S(2)}) collective-permute-start(bf16[128,1024]{1,0:T(8,128)(2,1)} %get-tuple-element.75), channel_id=1, source_target_pairs={{0,48},{16,64},{32,80},{48,96},{64,112},{80,0},{96,16},{112,32},{1... | collective-permute-start | bytes 786440 | tf_op jit(solution)/shard_map/ppermute | solution.py:371
  114.5 22.7 %collective-permute-start.5 = (bf16[128,1024]{1,0:T(8,128)(2,1)}, bf16[128,1024]{1,0:T(8,128)(2,1)S(1)}, u32[]{:S(2)}, u32[]{:S(2)}) collective-permute-start(bf16[128,1024]{1,0:T(8,128)(2,1)} %get-tuple-element.76), channel_id=1, source_target_pairs={{0,64},{16,80},{32,96},{48,112},{64,0},{80,16},{96,32},{112,48},{1... | collective-permute-start | bytes 786440 | tf_op jit(solution)/shard_map/ppermute | solution.py:371
  114.6 23.3 %collective-permute-start.6 = (bf16[128,1024]{1,0:T(8,128)(2,1)S(1)}, bf16[128,1024]{1,0:T(8,128)(2,1)S(1)}, u32[]{:S(2)}, u32[]{:S(2)}) collective-permute-start(bf16[128,1024]{1,0:T(8,128)(2,1)S(1)} %copy-done.17), channel_id=1, source_target_pairs={{0,80},{16,96},{32,112},{48,0},{64,16},{80,32},{96,48},{112,64},{1... | collective-permute-start | bytes 786440 | tf_op jit(solution)/shard_map/ppermute | solution.py:371
  117.2 0.7 copy-start.5
  125.5 0.7 copy-start.7
  128.2 0.7 copy-start.9
  137.2 0.7 copy-start.11
  137.9 0.7 copy-start.13
  154.2 1.6 copy-start
  155.8 18.5 %copy-start.4 = (bf16[128,1024]{1,0:T(8,128)(2,1)S(1)}, bf16[128,1024]{1,0:T(8,128)(2,1)}, u32[]{:S(2)}) copy-start(bf16[128,1024]{1,0:T(8,128)(2,1)} %get-tuple-element.81.rest_0_) | copy-start | bytes 786436
  155.8 18.5 %copy-start.15 = (s32[1,8,1]{1,2,0:T(1,128)S(1)}, s32[1,8,1]{1,2,0:T(1,128)}, u32[]{:S(2)}) copy-start(s32[1,8,1]{1,2,0:T(1,128)} %param.14) | copy-start | bytes 100
  155.8 48.6 %all-to-all-start.4 = ((bf16[16,3,32,1024]{3,2,1,0:T(8,128)(2,1)}), bf16[16,3,32,1024]{3,2,1,0:T(8,128)(2,1)S(1)}, u32[]{:S(2)}, u32[]{:S(2)}) async-start(bf16[16,3,32,1024]{3,2,1,0:T(8,128)(2,1)} %copy-done), calls=%async_computation.4 | async-start | bytes 6291456 | tf_op jit(solution)/shard_map/all_to_all | solution.py:356
  162.9 7.9 %collective-permute-start.7 = (bf16[128,1024]{1,0:T(8,128)(2,1)}, bf16[128,1024]{1,0:T(8,128)(2,1)S(1)}, u32[]{:S(2)}, u32[]{:S(2)}) collective-permute-start(bf16[128,1024]{1,0:T(8,128)(2,1)} %get-tuple-element.87), channel_id=1, source_target_pairs={{0,96},{16,112},{32,0},{48,16},{64,32},{80,48},{96,64},{112,80},{1... | collective-permute-start | bytes 786440 | tf_op jit(solution)/shard_map/ppermute | solution.py:371
  163.9 10.5 %collective-permute-start.8 = (bf16[128,1024]{1,0:T(8,128)(2,1)}, bf16[128,1024]{1,0:T(8,128)(2,1)S(1)}, u32[]{:S(2)}, u32[]{:S(2)}) collective-permute-start(bf16[128,1024]{1,0:T(8,128)(2,1)} %get-tuple-element.88), channel_id=1, source_target_pairs={{0,112},{16,0},{32,16},{48,32},{64,48},{80,64},{96,80},{112,96},{1... | collective-permute-start | bytes 786440 | tf_op jit(solution)/shard_map/ppermute | solution.py:371
  174.3 1.6 copy-start.1
  175.9 1.0 copy-start.2
  177.0 1.0 copy-start.3
  178.0 0.9 copy-start.6
  179.0 0.9 copy-start.8
  179.9 0.9 copy-start.10
  180.9 0.9 copy-start.12
  181.8 0.9 copy-start.14
  204.4 7.2 %collective-permute-start.9 = (bf16[16,3,32,1024]{3,2,1,0:T(8,128)(2,1)S(1)}, bf16[16,3,32,1024]{3,2,1,0:T(8,128)(2,1)S(1)}, u32[]{:S(2)}, u32[]{:S(2)}) collective-permute-start(bf16[16,3,32,1024]{3,2,1,0:T(8,128)(2,1)S(1)} %all-to-all-done.4.rows_ref), channel_id=1, source_target_pairs={{0,16},{16,0},{32,48},{48,32},{64,80},{80,64},{96,112},{112,96},{1... | collective-permute-start | bytes 9437192 | tf_op jit(solution)/shard_map/ppermute | solution.py:383

commit v6 on v4

--- a/solution.py
+++ b/solution.py
@@ -183,7 +183,7 @@
     each = width // 2 // pieces
     heads = width // LANES
     smem = pl.BlockSpec(memory_space=pltpu.SMEM)
-    hbm = pl.BlockSpec(memory_space=pl.ANY)
+    hbm = pl.BlockSpec(memory_space=pltpu.HBM)
     shape = jax.ShapeDtypeStruct
     vm = pltpu.VMEM
     macs = 2 * (n_src + 3 * n_slot) * length * width * width + 12 * 6 * length * length * width
@@ -215,18 +215,24 @@
     )(me, src, slot, valid, x, r, c, wq, wk, wv)
 
 
-def combine_kernel(me_ref, listed_ref, dq_ref, wq_ref, *rest):
-    parts, (out_ref, acc) = rest[:-2], rest[-2:]
-    n_slot = len(parts)
-    length = parts[0].shape[0]
+def combine_kernel(me_ref, listed_ref, dq_hbm, wq_hbm, *rest):
+    n_slot = len(rest) - 6
+    parts, (out_ref, acc, dq_ref, wq_ref, back, sem) = rest[:n_slot], rest[n_slot:]
+    length = back.shape[1]
     me = me_ref[0]
     block = 256
+    copies = [pltpu.make_async_copy(a, b, sem.at[i]) for i, (a, b) in enumerate(
+        [(dq_hbm, dq_ref), (wq_hbm, wq_ref)] + [(p, back.at[s]) for s, p in enumerate(parts)])]
+    for c in copies:
+        c.start()
+    for c in copies:
+        c.wait()
     for n in range(0, acc.shape[2], block):
         cols = slice(n, n + block)
         acc[:, :, cols] = mm_nt(dq_ref[...], wq_ref[cols, :]).reshape(acc.shape[0], length, block)
-    for s, part in enumerate(parts):
+    for s in range(n_slot):
         at = listed_ref[lax.rem(me + n_slot - s, n_slot)]
-        acc[at] += part[...].astype(F32)
+        acc[at] += back[s].astype(F32)
     out_ref[...] = acc[...].astype(BF)
 
 
@@ -234,37 +240,84 @@
     length, width = parts[0].shape
     n_src = dq.shape[0] // length
     smem = pl.BlockSpec(memory_space=pltpu.SMEM)
-    vmem = pl.BlockSpec(memory_space=pltpu.VMEM)
+    hbm = pl.BlockSpec(memory_space=pltpu.HBM)
     return pl.pallas_call(
         combine_kernel,
-        in_specs=[smem, smem] + [vmem] * (2 + len(parts)),
-        out_specs=vmem,
+        in_specs=[smem, smem] + [hbm] * (2 + len(parts)),
+        out_specs=pl.BlockSpec(memory_space=pltpu.VMEM),
         out_shape=jax.ShapeDtypeStruct((n_src, length, width), BF),
-        scratch_shapes=[pltpu.VMEM((n_src, length, width), F32)],
-        compiler_params=pltpu.CompilerParams(vmem_limit_bytes=24 * 2**20),
+        scratch_shapes=[
+            pltpu.VMEM((n_src, length, width), F32), pltpu.VMEM(dq.shape, BF), pltpu.VMEM(wq.shape, BF),
+            pltpu.VMEM((len(parts), length, width), BF), pltpu.SemaphoreType.DMA((2 + len(parts),)),
+        ],
+        compiler_params=pltpu.CompilerParams(vmem_limit_bytes=60 * 2**20),
         cost_estimate=pl.CostEstimate(flops=2 * dq.size * width, bytes_accessed=6 * 2**20, transcendentals=0),
         name="combine",
     )(me, listed, dq, wq, *parts)
 
 
-def spread_kernel(parts_ref, out_ref, *, factor):
-    total = jnp.sum(parts_ref[...].astype(F32), axis=0)
+def pick_kernel(listed_ref, x_hbm, out_hbm, x_ref, sem):
+    load = pltpu.make_async_copy(x_hbm, x_ref, sem.at[0])
+    load.start()
+    load.wait()
+    n = out_hbm.shape[0]
+    stores = [pltpu.make_async_copy(x_ref.at[listed_ref[i]], out_hbm.at[i], sem.at[1 + i]) for i in range(n)]
+    for c in stores:
+        c.start()
+    for c in stores:
+        c.wait()
+
+
+def pick(listed, x):
+    n = listed.shape[0]
+    hbm = pl.BlockSpec(memory_space=pltpu.HBM)
+    return pl.pallas_call(
+        pick_kernel,
+        in_specs=[pl.BlockSpec(memory_space=pltpu.SMEM), hbm],
+        out_specs=hbm,
+        out_shape=jax.ShapeDtypeStruct((n,) + x.shape[1:], x.dtype),
+        scratch_shapes=[pltpu.VMEM(x.shape, x.dtype), pltpu.SemaphoreType.DMA((1 + n,))],
+        compiler_params=pltpu.CompilerParams(vmem_limit_bytes=60 * 2**20),
+        name="pick",
+    )(listed, x)
+
+
+def sum_kernel(parts_ref, out_ref):
+    out_ref[...] = jnp.sum(parts_ref[...].astype(F32), axis=0).astype(BF)
+
+
+def sum_parts(parts):
+    count, n, each, width = parts.shape
+    return pl.pallas_call(
+        sum_kernel,
+        grid=(n,),
+        in_specs=[pl.BlockSpec((count, 1, each, width), lambda i: (0, i, 0, 0))],
+        out_specs=pl.BlockSpec((1, each, width), lambda i: (i, 0, 0)),
+        out_shape=jax.ShapeDtypeStruct((n, each, width), BF),
+        compiler_params=pltpu.CompilerParams(vmem_limit_bytes=16 * 2**20),
+        cost_estimate=pl.CostEstimate(flops=parts.size, bytes_accessed=2 * parts.size, transcendentals=0),
+        name="sum_parts",
+    )(parts)
+
+
+def spread_kernel(a_ref, b_ref, c_ref, d_ref, out_ref, *, factor):
+    a, b, c, d = (ref[...].astype(F32) for ref in (a_ref, b_ref, c_ref, d_ref))
+    total = (a + c) + (b + d)
     out_ref[...] = jnp.broadcast_to((total * factor).astype(BF)[None], out_ref.shape)
 
 
 def spread(parts, copies, factor):
-    shape = parts.shape[1:]
-    grid = shape[0]
+    n, each, width = parts[0].shape
     return pl.pallas_call(
         functools.partial(spread_kernel, factor=factor),
-        grid=(grid,),
-        in_specs=[pl.BlockSpec((parts.shape[0], 1) + shape[1:], lambda i: (0, i, 0, 0))],
-        out_specs=pl.BlockSpec((copies, 1) + shape[1:], lambda i: (0, i, 0, 0)),
-        out_shape=jax.ShapeDtypeStruct((copies,) + shape, BF),
-        compiler_params=pltpu.CompilerParams(vmem_limit_bytes=16 * 2**20),
-        cost_estimate=pl.CostEstimate(flops=parts.size, bytes_accessed=4 * parts.size, transcendentals=0),
+        grid=(n,),
+        in_specs=[pl.BlockSpec((1, each, width), lambda i: (i, 0, 0))] * len(parts),
+        out_specs=pl.BlockSpec((copies, 1, each, width), lambda i: (0, i, 0, 0)),
+        out_shape=jax.ShapeDtypeStruct((copies, n, each, width), BF),
+        compiler_params=pltpu.CompilerParams(vmem_limit_bytes=60 * 2**20),
+        cost_estimate=pl.CostEstimate(flops=4 * parts[0].size, bytes_accessed=2 * copies * parts[0].size, transcendentals=0),
         name="spread",
-    )(parts)
+    )(*parts)
 
 
 def place_kernel(half_ref, rows_ref, *rest):
@@ -299,7 +352,7 @@
     n_pair = lax.axis_size("pair")
     me = lax.axis_index("lang")
     listed = send_rows[0].reshape(-1)
-    outgoing = jnp.take(sentences, listed, axis=0, mode="clip")
+    outgoing = pick(listed, sentences)
     received = lax.all_to_all(outgoing, "lang", split_axis=0, concat_axis=0, tiled=True)
     x = sentences.reshape(-1, width)
     c = cotangent.reshape(-1, width)
@@ -314,17 +367,16 @@
         back.append(lax.ppermute(dx[s], "lang", [(i, (i + s) % n_lang) for i in range(n_lang)]))
     chip = (keep.astype(F32) + other.astype(F32)).astype(BF)
     pieces = lax.all_to_all(chip, "pair", split_axis=0, concat_axis=0, tiled=True)
-    pieces, *back[1:6] = lax.optimization_barrier((pieces, *back[1:6]))
-    n_y = n_lang // 2
-    along_y = [[2 * y + core for y in range(n_y)] for core in range(2)]
-    columns = lax.all_to_all(
-        spread(pieces, n_y, 1.0), "lang", split_axis=0, concat_axis=0, axis_index_groups=along_y, tiled=True
-    )
+    pieces, *back[1:4] = lax.optimization_barrier((pieces, *back[1:4]))
+    plane = sum_parts(pieces)
+    rings = [plane]
+    for y in range(1, n_lang // 2):
+        rings.append(lax.ppermute(plane, "lang", [(i, (i + 2 * y) % n_lang) for i in range(n_lang)]))
     factor = 1.0 / (sent_dev * n_lang * n_pair * length) ** 0.5
-    near = lax.all_to_all(spread(columns, n_pair, factor), "pair", split_axis=0, concat_axis=0, tiled=True)
-    near, *back[6:] = lax.optimization_barrier((near, *back[6:]))
+    near = lax.all_to_all(spread(rings, n_pair, factor), "pair", split_axis=0, concat_axis=0, tiled=True)
+    grad_sentences = combine(where, listed, dq, w_query, back)
+    near, grad_sentences = lax.optimization_barrier((near, grad_sentences))
     far = lax.ppermute(near, "lang", other_core)
-    grad_sentences = combine(where, listed, dq, w_query, back)
     core = lax.rem(where, 2)
     grads = place(1 - core, far, place(core, near))
     grads = tuple(g.reshape(width, width) for g in grads)

time: 219 us -> 214 us (0.977)
  local copies, waits for them, and re-layouts: 17.8 us -> 2.86 us
  waiting for transfers between devices: 90.9 us -> 105 us
  blocking collectives: 13.6 us -> 0 us
  Pallas kernels: 43.5 us -> 53.4 us
    all_to_all x1, waiting for transfers between devices: 22.6 us -> 8.8 us  [body(): lax.all_to_all(spread(rings, n_pair, factor), 'pair', split_axis=0, conca...]
    all_to_all x1 -> x0, blocking collectives: 13.6 us -> none  [body(): lax.all_to_all(spread(pieces, n_y, 1.0), 'lang', split_axis=0, concat_axi...]
    all_to_all x1, waiting for transfers between devices: 10.9 us -> 23.5 us  [body(): lax.all_to_all(chip, 'pair', split_axis=0, concat_axis=0, tiled=True)]
    unnamed x42 -> x20, local copies, waits for them, and re-layouts: 14.6 us -> 2.86 us
    pallas_call x3 -> x4, Pallas kernels: 4.7 us -> 13.5 us  [the longest x1 6.08 us: combine(): pl.pallas_call(combine_kernel, in_specs=[smem, smem] + [hbm] * (2 + len(p...]
    ppermute x0 -> x3, waiting for transfers between devices: none -> 8.52 us  [body(): lax.ppermute(plane, 'lang', [(i, (i + 2 * y) % n_lang) for i in range(n_l...]
    ppermute x0 -> x3, starting transfers between devices: none -> 4.16 us  [body(): lax.ppermute(plane, 'lang', [(i, (i + 2 * y) % n_lang) for i in range(n_l...]
    ppermute x7, waiting for transfers between devices: 25.6 us -> 28.8 us  [body(): lax.ppermute(dx[s], 'lang', [(i, (i + s) % n_lang) for i in range(n_lang)])]
  transfers between devices with their start and end apart: 12 -> 15, of which waited for: 9 -> 15; matrix products, arithmetic and copies ran while one was open for 0% -> 0% of each run, Pallas kernels for 2% -> 4%
where the time goes in v6:
time: 214 us; the launch traced here: 212 us
  waiting for transfers between devices  105 us (49%)
  Pallas kernels  53.4 us (25%)
  starting transfers between devices  45.3 us (21%)
  other arithmetic  5.17 us (2%)
  local copies, waits for them, and re-layouts  2.86 us (1%)
    pallas_call x1, Pallas kernels, attend(): pl.pallas_call(functools.partial(attend_kernel, n_src=n_src, n_slot=n_slo...  35.7 us
    ppermute x7, waiting for transfers between devices, body(): lax.ppermute(dx[s], 'lang', [(i, (i + s) % n_lang) for i in range(n_lang)])  28.8 us
    all_to_all x1, waiting for transfers between devices, body(): lax.all_to_all(outgoing, 'lang', split_axis=0, concat_axis=0, tiled=True)  26.3 us
    all_to_all x1, waiting for transfers between devices, body(): lax.all_to_all(chip, 'pair', split_axis=0, concat_axis=0, tiled=True)  23.5 us
    all_to_all x1, starting transfers between devices, body(): lax.all_to_all(spread(rings, n_pair, factor), 'pair', split_axis=0, conca...  11.8 us
    ppermute x7, starting transfers between devices, body(): lax.ppermute(dx[s], 'lang', [(i, (i + s) % n_lang) for i in range(n_lang)])  10.1 us
    all_to_all x1, waiting for transfers between devices, body(): lax.all_to_all(spread(rings, n_pair, factor), 'pair', split_axis=0, conca...  8.8 us
    ppermute x3, waiting for transfers between devices, body(): lax.ppermute(plane, 'lang', [(i, (i + 2 * y) % n_lang) for i in range(n_l...  8.52 us
  transfers between devices with their start and end apart: 15, of which 15 were waited for; matrix products, arithmetic and copies ran while one was open for 0% of the time, Pallas kernels for 4%

profile of v6, /device:TPU:1, one launch (start us, length us, event | category | flops | bytes accessed | tf_op | source)
XLA Modules:
  0.0 212.4 jit_solution(14617077342280264659)
XLA Ops:
  0.6 3.3 %pick.1 = bf16[8,128,1024]{2,1,0:T(8,128)(2,1)} custom-call(s32[8]{0:T(128)} %bitcast.12, bf16[4,128,1024]{2,1,0:T(8,128)(2,1)} %x_hbm.1), custom_call_target="tpu_custom_call" | custom-call | tf_op jit(solution)/shard_map/pick/pallas_call | solution.py:274
  3.9 6.0 %all-to-all-start = ((bf16[8,128,1024]{2,1,0:T(8,128)(2,1)}), bf16[8,128,1024]{2,1,0:T(8,128)(2,1)S(1)}, u32[]{:S(2)}, u32[]{:S(2)}) async-start(bf16[8,128,1024]{2,1,0:T(8,128)(2,1)} %pick.1), calls=%async_computation | async-start | bytes 4194304 | tf_op jit(solution)/shard_map/all_to_all | solution.py:356
  9.9 26.3 %all-to-all-done.r_hbm = bf16[8,128,1024]{2,1,0:T(8,128)(2,1)S(1)} async-done(((bf16[8,128,1024]{2,1,0:T(8,128)(2,1)}), bf16[8,128,1024]{2,1,0:T(8,128)(2,1)S(1)}, u32[]{:S(2)}, u32[]{:S(2)}) %all-to-all-start) | async-done | bytes 2097184 | tf_op jit(solution)/shard_map/all_to_all | solution.py:356
  36.2 1.3 copy-done.1
  37.5 35.7 %attend.1 = (bf16[512,1024]{1,0:T(8,128)(2,1)}, bf16[512,1024]{1,0:T(8,128)(2,1)}, bf16[16,3,32,1024]{3,2,1,0:T(8,128)(2,1)}, bf16[16,3,32,1024]{3,2,1,0:T(8,128...) custom-call(s32[1]{0:T(128)} %bitcast.me_ref, ...), custom_call_target="tpu_custom_call" | custom-call | flops 34896609280 | bytes 20971520 | tf_op jit(solution)/shard_map/attend/pallas_call | solution.py:190
  73.3 0.1 collective-permute-start
  73.4 5.9 %collective-permute-done = bf16[16,3,32,1024]{3,2,1,0:T(8,128)(2,1)S(1)} collective-permute-done((bf16[16,3,32,1024]{3,2,1,0:T(8,128)(2,1)}, bf16[16,3,32,1024]{3,2,1,0:T(8,128)(2,1)S(1)}, u32[]{:S(2)}, u32[]{:S(2)}) %collective-permute-start) | collective-permute-done | bytes 3145760 | tf_op jit(solution)/shard_map/ppermute | solution.py:364
  79.2 5.2 %add_convert_fusion = bf16[16,3,32,1024]{3,2,1,0:T(8,128)(2,1)} fusion(bf16[16,3,32,1024]{3,2,1,0:T(8,128)(2,1)S(1)} %collective-permute-done, bf16[16,3,32,1024]{3,2,1,0:T(8,128)(2,1)} %get-tuple-element.30), kind=kLoop, calls=%fused_computation | loop fusion | flops 6291456 | bytes 9437184 | tf_op jit(solution)/shard_map/convert_element_type | solution.py:368
  84.4 6.9 %all-to-all-start.1 = ((bf16[16,3,32,1024]{3,2,1,0:T(8,128)(2,1)}), bf16[16,3,32,1024]{3,2,1,0:T(8,128)(2,1)S(1)}, u32[]{:S(2)}, u32[]{:S(2)}) async-start(bf16[16,3,32,1024]{3,2,1,0:T(8,128)(2,1)} %add_convert_fusion), calls=%async_computation.1 | async-start | bytes 6291456 | tf_op jit(solution)/shard_map/all_to_all | solution.py:369
  91.3 2.3 %collective-permute-start.1 = (bf16[128,1024]{1,0:T(8,128)(2,1)}, bf16[128,1024]{1,0:T(8,128)(2,1)S(1)}, u32[]{:S(2)}, u32[]{:S(2)}) collective-permute-start(bf16[128,1024]{1,0:T(8,128)(2,1)} %get-tuple-element.32), channel_id=1, source_target_pairs={{0,16},{16,32},{32,48},{48,64},{64,80},{80,96},{96,112},{112,0},{1... | collective-permute-start | bytes 786440 | tf_op jit(solution)/shard_map/ppermute | solution.py:367
  93.6 1.1 collective-permute-start.2
  94.7 0.5 collective-permute-start.3
  95.2 4.3 %collective-permute-done.1.rest_1_ = bf16[128,1024]{1,0:T(8,128)(2,1)S(1)} collective-permute-done((bf16[128,1024]{1,0:T(8,128)(2,1)}, bf16[128,1024]{1,0:T(8,128)(2,1)S(1)}, u32[]{:S(2)}, u32[]{:S(2)}) %collective-permute-start.1) | collective-permute-done | bytes 262176 | tf_op jit(solution)/shard_map/ppermute | solution.py:367
  99.4 7.7 %collective-permute-done.2.rest_2_ = bf16[128,1024]{1,0:T(8,128)(2,1)S(1)} collective-permute-done((bf16[128,1024]{1,0:T(8,128)(2,1)}, bf16[128,1024]{1,0:T(8,128)(2,1)S(1)}, u32[]{:S(2)}, u32[]{:S(2)}) %collective-permute-start.2) | collective-permute-done | bytes 262176 | tf_op jit(solution)/shard_map/ppermute | solution.py:367
  107.1 0.7 copy-done.3
  107.9 0.6 collective-permute-done.3.rest_3_
  108.5 23.5 %all-to-all-done.1.parts_ref = bf16[16,3,32,1024]{3,2,1,0:T(8,128)(2,1)S(1)} async-done(((bf16[16,3,32,1024]{3,2,1,0:T(8,128)(2,1)}), bf16[16,3,32,1024]{3,2,1,0:T(8,128)(2,1)S(1)}, u32[]{:S(2)}, u32[]{:S(2)}) %all-to-all-start.1) | async-done | bytes 3145760 | tf_op jit(solution)/shard_map/all_to_all | solution.py:369
  132.0 0.7 sum_parts.1.a_ref
  132.6 0.0 copy-start
  132.7 1.0 collective-permute-start.6
  133.6 3.2 %collective-permute-start.5 = (bf16[3,32,1024]{2,1,0:T(8,128)(2,1)S(1)}, bf16[3,32,1024]{2,1,0:T(8,128)(2,1)S(1)}, u32[]{:S(2)}, u32[]{:S(2)}) collective-permute-start(bf16[3,32,1024]{2,1,0:T(8,128)(2,1)S(1)} %sum_parts.1.a_ref), channel_id=1, source_target_pairs={{0,64},{16,80},{32,96},{48,112},{64,0},{80,16},{96,32},{112,48},{1... | collective-permute-start | bytes 589832 | tf_op jit(solution)/shard_map/ppermute | solution.py:374
  136.8 0.0 collective-permute-start.4
  136.8 1.3 collective-permute-done.6.d_ref
  138.1 1.8 collective-permute-done.5.c_ref
  139.9 5.5 %collective-permute-done.4.b_ref = bf16[3,32,1024]{2,1,0:T(8,128)(2,1)S(1)} collective-permute-done((bf16[3,32,1024]{2,1,0:T(8,128)(2,1)S(1)}, bf16[3,32,1024]{2,1,0:T(8,128)(2,1)S(1)}, u32[]{:S(2)}, u32[]{:S(2)}) %collective-permute-start.4) | collective-permute-done | bytes 196640 | tf_op jit(solution)/shard_map/ppermute | solution.py:374
  145.3 0.0 copy-done
  145.4 0.0 copy-done.7
  145.4 0.0 copy-done.8
  145.4 0.0 copy-start.9
  145.4 0.7 copy-done.9
  146.0 3.4 %spread.1 = bf16[16,3,32,1024]{3,2,1,0:T(8,128)(2,1)} custom-call(bf16[3,32,1024]{2,1,0:T(8,128)(2,1)} %copy-done, bf16[3,32,1024]{2,1,0:T(8,128)(2,1)} %copy-done.9, bf16[3,32,1024]{2,1,0:T(8,128)(2,1)} %copy-done.8, bf16[3,32,1024]{2,1,0:T(8,128)(2,1)} %copy-done.7), custom_call_target="tpu_custom_call" | custom-call | flops 393216 | bytes 3145728 | tf_op jit(solution)/shard_map/spread/pallas_call | solution.py:311
  149.5 0.0 copy-done.2
  149.5 11.8 %all-to-all-start.2 = ((bf16[16,3,32,1024]{3,2,1,0:T(8,128)(2,1)}), bf16[16,3,32,1024]{3,2,1,0:T(8,128)(2,1)S(1)}, u32[]{:S(2)}, u32[]{:S(2)}) async-start(bf16[16,3,32,1024]{3,2,1,0:T(8,128)(2,1)} %spread.1), calls=%async_computation.2 | async-start | bytes 6291456 | tf_op jit(solution)/shard_map/all_to_all | solution.py:376
  161.3 0.1 collective-permute-start.7
  161.4 5.8 %collective-permute-start.8 = (bf16[128,1024]{1,0:T(8,128)(2,1)}, bf16[128,1024]{1,0:T(8,128)(2,1)S(1)}, u32[]{:S(2)}, u32[]{:S(2)}) collective-permute-start(bf16[128,1024]{1,0:T(8,128)(2,1)} %get-tuple-element.42), channel_id=1, source_target_pairs={{0,80},{16,96},{32,112},{48,0},{64,16},{80,32},{96,48},{112,64},{1... | collective-permute-start | bytes 786440 | tf_op jit(solution)/shard_map/ppermute | solution.py:367
  167.2 0.0 collective-permute-start.9
  167.2 0.4 collective-permute-start.10
  167.6 1.4 collective-permute-done.7.rest_4_
  169.0 8.5 %collective-permute-done.8.rest_5_ = bf16[128,1024]{1,0:T(8,128)(2,1)S(1)} collective-permute-done((bf16[128,1024]{1,0:T(8,128)(2,1)}, bf16[128,1024]{1,0:T(8,128)(2,1)S(1)}, u32[]{:S(2)}, u32[]{:S(2)}) %collective-permute-start.8) | collective-permute-done | bytes 262176 | tf_op jit(solution)/shard_map/ppermute | solution.py:367
  177.5 5.8 %collective-permute-done.9.rest_6_ = bf16[128,1024]{1,0:T(8,128)(2,1)S(1)} collective-permute-done((bf16[128,1024]{1,0:T(8,128)(2,1)}, bf16[128,1024]{1,0:T(8,128)(2,1)S(1)}, u32[]{:S(2)}, u32[]{:S(2)}) %collective-permute-start.9) | collective-permute-done | bytes 262176 | tf_op jit(solution)/shard_map/ppermute | solution.py:367
  183.3 0.6 collective-permute-done.10.rest_7_
  183.9 0.1 copy-done.6
  184.0 6.1 %combine.1 = bf16[4,128,1024]{2,1,0:T(8,128)(2,1)} custom-call(s32[1]{0:T(128)} %bitcast.me_ref, s32[8]{0:T(128)} %bitcast.13, bf16[512,1024]{1,0:T(8,128)(2,1)} %get-tuple-element.36.dq_hbm, bf16[1024,1024]{1,0:T(8,128)(2,1)} %wq_hbm.3, bf16[128,1024]{1,0:T(8,128)(2,1)} %get-tuple-element.37.rest_0_, bf16[128,1024]{1,0:T(8,128)(2,1)} %copy-done.2, ...), custom_call_target="tpu_custom_call" | custom-call | flops 1073741824 | bytes 6291456 | tf_op jit(solution)/shard_map/combine/pallas_call | solution.py:244
  190.1 8.8 %all-to-all-done.2.rows_ref = bf16[16,3,32,1024]{3,2,1,0:T(8,128)(2,1)S(1)} async-done(((bf16[16,3,32,1024]{3,2,1,0:T(8,128)(2,1)}), bf16[16,3,32,1024]{3,2,1,0:T(8,128)(2,1)S(1)}, u32[]{:S(2)}, u32[]{:S(2)}) %all-to-all-start.2) | async-done | bytes 3145760 | tf_op jit(solution)/shard_map/all_to_all | solution.py:376
  198.9 6.1 %collective-permute-start.11 = (bf16[16,3,32,1024]{3,2,1,0:T(8,128)(2,1)S(1)}, bf16[16,3,32,1024]{3,2,1,0:T(8,128)(2,1)S(1)}, u32[]{:S(2)}, u32[]{:S(2)}) collective-permute-start(bf16[16,3,32,1024]{3,2,1,0:T(8,128)(2,1)S(1)} %all-to-all-done.2.rows_ref), channel_id=1, source_target_pairs={{0,16},{16,0},{32,48},{48,32},{64,80},{80,64},{96,112},{112,96},{1... | collective-permute-start | bytes 9437192 | tf_op jit(solution)/shard_map/ppermute | solution.py:379
  205.1 2.1 place.2
  207.2 3.2 %collective-permute-done.11.rows_ref = bf16[16,3,32,1024]{3,2,1,0:T(8,128)(2,1)S(1)} collective-permute-done((bf16[16,3,32,1024]{3,2,1,0:T(8,128)(2,1)S(1)}, bf16[16,3,32,1024]{3,2,1,0:T(8,128)(2,1)S(1)}, u32[]{:S(2)}, u32[]{:S(2)}) %collective-permute-start.11) | collective-permute-done | bytes 3145760 | tf_op jit(solution)/shard_map/ppermute | solution.py:379
  210.3 2.1 place.3
  (10 shorter events, 0.0 us)
Async XLA Ops:
  3.9 32.3 %all-to-all-start = ((bf16[8,128,1024]{2,1,0:T(8,128)(2,1)}), bf16[8,128,1024]{2,1,0:T(8,128)(2,1)S(1)}, u32[]{:S(2)}, u32[]{:S(2)}) async-start(bf16[8,128,1024]{2,1,0:T(8,128)(2,1)} %pick.1), calls=%async_computation | async-start | bytes 4194304 | tf_op jit(solution)/shard_map/all_to_all | solution.py:356
  36.2 1.3 copy-start.1
  73.3 6.0 %collective-permute-start = (bf16[16,3,32,1024]{3,2,1,0:T(8,128)(2,1)}, bf16[16,3,32,1024]{3,2,1,0:T(8,128)(2,1)S(1)}, u32[]{:S(2)}, u32[]{:S(2)}) collective-permute-start(bf16[16,3,32,1024]{3,2,1,0:T(8,128)(2,1)} %get-tuple-element.31), channel_id=1, source_target_pairs={{0,16},{16,0},{32,48},{48,32},{64,80},{80,64},{96,112},{112,96},{1... | collective-permute-start | bytes 9437192 | tf_op jit(solution)/shard_map/ppermute | solution.py:364
  84.4 47.6 %all-to-all-start.1 = ((bf16[16,3,32,1024]{3,2,1,0:T(8,128)(2,1)}), bf16[16,3,32,1024]{3,2,1,0:T(8,128)(2,1)S(1)}, u32[]{:S(2)}, u32[]{:S(2)}) async-start(bf16[16,3,32,1024]{3,2,1,0:T(8,128)(2,1)} %add_convert_fusion), calls=%async_computation.1 | async-start | bytes 6291456 | tf_op jit(solution)/shard_map/all_to_all | solution.py:369
  91.3 8.1 %collective-permute-start.1 = (bf16[128,1024]{1,0:T(8,128)(2,1)}, bf16[128,1024]{1,0:T(8,128)(2,1)S(1)}, u32[]{:S(2)}, u32[]{:S(2)}) collective-permute-start(bf16[128,1024]{1,0:T(8,128)(2,1)} %get-tuple-element.32), channel_id=1, source_target_pairs={{0,16},{16,32},{32,48},{48,64},{64,80},{80,96},{96,112},{112,0},{1... | collective-permute-start | bytes 786440 | tf_op jit(solution)/shard_map/ppermute | solution.py:367
  93.6 13.5 %collective-permute-start.2 = (bf16[128,1024]{1,0:T(8,128)(2,1)}, bf16[128,1024]{1,0:T(8,128)(2,1)S(1)}, u32[]{:S(2)}, u32[]{:S(2)}) collective-permute-start(bf16[128,1024]{1,0:T(8,128)(2,1)} %get-tuple-element.33), channel_id=1, source_target_pairs={{0,32},{16,48},{32,64},{48,80},{64,96},{80,112},{96,0},{112,16},{1... | collective-permute-start | bytes 786440 | tf_op jit(solution)/shard_map/ppermute | solution.py:367
  94.7 13.8 %collective-permute-start.3 = (bf16[128,1024]{1,0:T(8,128)(2,1)}, bf16[128,1024]{1,0:T(8,128)(2,1)}, u32[]{:S(2)}, u32[]{:S(2)}) collective-permute-start(bf16[128,1024]{1,0:T(8,128)(2,1)} %get-tuple-element.34), channel_id=1, source_target_pairs={{0,48},{16,64},{32,80},{48,96},{64,112},{80,0},{96,16},{112,32},{1... | collective-permute-start | bytes 786440 | tf_op jit(solution)/shard_map/ppermute | solution.py:367
  99.4 50.0 %copy-start.2 = (bf16[128,1024]{1,0:T(8,128)(2,1)}, bf16[128,1024]{1,0:T(8,128)(2,1)S(1)}, u32[]{:S(2)}) copy-start(bf16[128,1024]{1,0:T(8,128)(2,1)S(1)} %collective-permute-done.1.rest_1_) | copy-start | bytes 786436
  107.1 0.7 copy-start.3
  132.6 12.7 %copy-start = (bf16[3,32,1024]{2,1,0:T(8,128)(2,1)}, bf16[3,32,1024]{2,1,0:T(8,128)(2,1)S(1)}, u32[]{:S(2)}) copy-start(bf16[3,32,1024]{2,1,0:T(8,128)(2,1)S(1)} %sum_parts.1.a_ref) | copy-start | bytes 589828
  132.7 5.4 %collective-permute-start.6 = (bf16[3,32,1024]{2,1,0:T(8,128)(2,1)S(1)}, bf16[3,32,1024]{2,1,0:T(8,128)(2,1)S(1)}, u32[]{:S(2)}, u32[]{:S(2)}) collective-permute-start(bf16[3,32,1024]{2,1,0:T(8,128)(2,1)S(1)} %sum_parts.1.a_ref), channel_id=1, source_target_pairs={{0,96},{16,112},{32,0},{48,16},{64,32},{80,48},{96,64},{112,80},{1... | collective-permute-start | bytes 589832 | tf_op jit(solution)/shard_map/ppermute | solution.py:374
  133.6 6.3 %collective-permute-start.5 = (bf16[3,32,1024]{2,1,0:T(8,128)(2,1)S(1)}, bf16[3,32,1024]{2,1,0:T(8,128)(2,1)S(1)}, u32[]{:S(2)}, u32[]{:S(2)}) collective-permute-start(bf16[3,32,1024]{2,1,0:T(8,128)(2,1)S(1)} %sum_parts.1.a_ref), channel_id=1, source_target_pairs={{0,64},{16,80},{32,96},{48,112},{64,0},{80,16},{96,32},{112,48},{1... | collective-permute-start | bytes 589832 | tf_op jit(solution)/shard_map/ppermute | solution.py:374
  136.8 8.5 %collective-permute-start.4 = (bf16[3,32,1024]{2,1,0:T(8,128)(2,1)S(1)}, bf16[3,32,1024]{2,1,0:T(8,128)(2,1)S(1)}, u32[]{:S(2)}, u32[]{:S(2)}) collective-permute-start(bf16[3,32,1024]{2,1,0:T(8,128)(2,1)S(1)} %sum_parts.1.a_ref), channel_id=1, source_target_pairs={{0,32},{16,48},{32,64},{48,80},{64,96},{80,112},{96,0},{112,16},{1... | collective-permute-start | bytes 589832 | tf_op jit(solution)/shard_map/ppermute | solution.py:374
  138.1 7.3 %copy-start.7 = (bf16[3,32,1024]{2,1,0:T(8,128)(2,1)}, bf16[3,32,1024]{2,1,0:T(8,128)(2,1)S(1)}, u32[]{:S(2)}) copy-start(bf16[3,32,1024]{2,1,0:T(8,128)(2,1)S(1)} %collective-permute-done.6.d_ref) | copy-start | bytes 589828
  139.9 5.5 %copy-start.8 = (bf16[3,32,1024]{2,1,0:T(8,128)(2,1)}, bf16[3,32,1024]{2,1,0:T(8,128)(2,1)S(1)}, u32[]{:S(2)}) copy-start(bf16[3,32,1024]{2,1,0:T(8,128)(2,1)S(1)} %collective-permute-done.5.c_ref) | copy-start | bytes 589828
  145.4 0.7 copy-start.9
  149.5 49.4 %all-to-all-start.2 = ((bf16[16,3,32,1024]{3,2,1,0:T(8,128)(2,1)}), bf16[16,3,32,1024]{3,2,1,0:T(8,128)(2,1)S(1)}, u32[]{:S(2)}, u32[]{:S(2)}) async-start(bf16[16,3,32,1024]{3,2,1,0:T(8,128)(2,1)} %spread.1), calls=%async_computation.2 | async-start | bytes 6291456 | tf_op jit(solution)/shard_map/all_to_all | solution.py:376
  161.3 7.7 %collective-permute-start.7 = (bf16[128,1024]{1,0:T(8,128)(2,1)}, bf16[128,1024]{1,0:T(8,128)(2,1)S(1)}, u32[]{:S(2)}, u32[]{:S(2)}) collective-permute-start(bf16[128,1024]{1,0:T(8,128)(2,1)} %get-tuple-element.41), channel_id=1, source_target_pairs={{0,64},{16,80},{32,96},{48,112},{64,0},{80,16},{96,32},{112,48},{1... | collective-permute-start | bytes 786440 | tf_op jit(solution)/shard_map/ppermute | solution.py:367
  161.4 16.2 %collective-permute-start.8 = (bf16[128,1024]{1,0:T(8,128)(2,1)}, bf16[128,1024]{1,0:T(8,128)(2,1)S(1)}, u32[]{:S(2)}, u32[]{:S(2)}) collective-permute-start(bf16[128,1024]{1,0:T(8,128)(2,1)} %get-tuple-element.42), channel_id=1, source_target_pairs={{0,80},{16,96},{32,112},{48,0},{64,16},{80,32},{96,48},{112,64},{1... | collective-permute-start | bytes 786440 | tf_op jit(solution)/shard_map/ppermute | solution.py:367
  167.2 16.1 %collective-permute-start.9 = (bf16[128,1024]{1,0:T(8,128)(2,1)}, bf16[128,1024]{1,0:T(8,128)(2,1)S(1)}, u32[]{:S(2)}, u32[]{:S(2)}) collective-permute-start(bf16[128,1024]{1,0:T(8,128)(2,1)} %get-tuple-element.43), channel_id=1, source_target_pairs={{0,96},{16,112},{32,0},{48,16},{64,32},{80,48},{96,64},{112,80},{1... | collective-permute-start | bytes 786440 | tf_op jit(solution)/shard_map/ppermute | solution.py:367
  167.2 16.7 %collective-permute-start.10 = (bf16[128,1024]{1,0:T(8,128)(2,1)}, bf16[128,1024]{1,0:T(8,128)(2,1)}, u32[]{:S(2)}, u32[]{:S(2)}) collective-permute-start(bf16[128,1024]{1,0:T(8,128)(2,1)} %get-tuple-element.44), channel_id=1, source_target_pairs={{0,112},{16,0},{32,16},{48,32},{64,48},{80,64},{96,80},{112,96},{1... | collective-permute-start | bytes 786440 | tf_op jit(solution)/shard_map/ppermute | solution.py:367
  169.0 14.9 %copy-start.4 = (bf16[128,1024]{1,0:T(8,128)(2,1)}, bf16[128,1024]{1,0:T(8,128)(2,1)S(1)}, u32[]{:S(2)}) copy-start(bf16[128,1024]{1,0:T(8,128)(2,1)S(1)} %collective-permute-done.7.rest_4_) | copy-start | bytes 786436
  177.5 6.4 %copy-start.5 = (bf16[128,1024]{1,0:T(8,128)(2,1)}, bf16[128,1024]{1,0:T(8,128)(2,1)S(1)}, u32[]{:S(2)}) copy-start(bf16[128,1024]{1,0:T(8,128)(2,1)S(1)} %collective-permute-done.8.rest_5_) | copy-start | bytes 786436
  183.3 0.7 copy-start.6
  198.9 11.4 %collective-permute-start.11 = (bf16[16,3,32,1024]{3,2,1,0:T(8,128)(2,1)S(1)}, bf16[16,3,32,1024]{3,2,1,0:T(8,128)(2,1)S(1)}, u32[]{:S(2)}, u32[]{:S(2)}) collective-permute-start(bf16[16,3,32,1024]{3,2,1,0:T(8,128)(2,1)S(1)} %all-to-all-done.2.rows_ref), channel_id=1, source_target_pairs={{0,16},{16,0},{32,48},{48,32},{64,80},{80,64},{96,112},{112,96},{1... | collective-permute-start | bytes 9437192 | tf_op jit(solution)/shard_map/ppermute | solution.py:379

commit v7 on v6

--- a/solution.py
+++ b/solution.py
@@ -150,15 +150,17 @@
         c.start()
         done.append(c)
 
-    _, pieces, _, each, _ = gw_v.shape
+    _, _, _, pieces, _, each, part = gw_v.shape
     core = lax.rem(me, 2)
     for k, dst in enumerate((send_hbm, keep_hbm)):
-        base = pl.multiple_of((core if k else 1 - core) * (pieces * each), LANES)
-        rows = pl.ds(base, pieces * each)
+        base = pl.multiple_of((core if k else 1 - core) * (2 * pieces * each), LANES)
+        rows = pl.ds(base, 2 * pieces * each)
         for n in range(0, width, block):
             cols = slice(n, n + block)
             for i, (lhs, rhs) in enumerate(((xt, dq_v[:, cols]), (rt, dk[:, cols]), (rt, dv[:, cols]))):
-                gw_v[k, :, i, :, cols] = mm(lhs[rows, :], rhs).astype(BF).reshape(pieces, each, block)
+                g = mm(lhs[rows, :], rhs).astype(BF).reshape(pieces, 2, each, block)
+                for up in range(2):
+                    gw_v[k, up, n // part, :, i, :, n % part:n % part + block] = g[:, up]
         out(gw_v.at[k], dst)
         if k == 0:
             out(dq_v, dq_hbm)
@@ -180,7 +182,8 @@
     n_slot, length, width = r.shape
     rows = x.shape[0]
     n_src = rows // length
-    each = width // 2 // pieces
+    each = width // 4 // pieces
+    share = (2, 2, pieces, 3, each, width // 2)
     heads = width // LANES
     smem = pl.BlockSpec(memory_space=pltpu.SMEM)
     hbm = pl.BlockSpec(memory_space=pltpu.HBM)
@@ -192,14 +195,14 @@
         in_specs=[smem] * 4 + [hbm] * 6,
         out_specs=[hbm] * (4 + n_slot),
         out_shape=[shape((rows, width), BF), shape((rows, width), BF),
-                   shape((pieces, 3, each, width), BF), shape((pieces, 3, each, width), BF)]
+                   shape(share, BF), shape(share, BF)]
         + [shape((length, width), BF)] * n_slot,
         scratch_shapes=[
             pltpu.SMEM((n_src * n_slot,), jnp.int32),
             vm((rows, width), BF), vm((n_slot * length, width), BF), vm((rows, width), BF),
             vm((width, width), BF), vm((width, width), BF), vm((width, width), BF),
             vm((rows, width), BF), vm((rows, width), BF),
-            vm((2, pieces, 3, each, width), BF), vm((n_slot * length, width), BF),
+            vm((2,) + share, BF), vm((n_slot * length, width), BF),
             vm((width, rows), BF), vm((width, n_slot * length), BF),
             vm((n_src, heads, 2 * length, LANES), BF), vm((n_src, heads, 2 * length, LANES), BF),
             vm((n_slot, length, width), BF), vm((n_slot, length, width), BF),
@@ -282,52 +285,56 @@
     )(listed, x)
 
 
-def sum_kernel(parts_ref, out_ref):
-    out_ref[...] = jnp.sum(parts_ref[...].astype(F32), axis=0).astype(BF)
-
-
-def sum_parts(parts):
+def add_kernel(a_ref, b_ref, out_ref):
+    out_ref[...] = (a_ref[...].astype(F32) + b_ref[...].astype(F32)).astype(BF)
+
+
+def add(a, b):
+    count, n, each, width = a.shape
+    spec = pl.BlockSpec((count // 4, n, each, width), lambda i: (i, 0, 0, 0))
+    return pl.pallas_call(
+        add_kernel,
+        grid=(4,),
+        in_specs=[spec, spec],
+        out_specs=spec,
+        out_shape=jax.ShapeDtypeStruct(a.shape, BF),
+        compiler_params=pltpu.CompilerParams(vmem_limit_bytes=16 * 2**20),
+        cost_estimate=pl.CostEstimate(flops=a.size, bytes_accessed=6 * a.size, transcendentals=0),
+        name="add",
+    )(a, b)
+
+
+def spread_kernel(parts_ref, out_ref, *, factor):
+    total = jnp.sum(parts_ref[...].astype(F32), axis=0) * factor
+    out_ref[...] = jnp.broadcast_to(total.astype(BF)[None], out_ref.shape)
+
+
+def spread(parts, factor):
     count, n, each, width = parts.shape
-    return pl.pallas_call(
-        sum_kernel,
-        grid=(n,),
-        in_specs=[pl.BlockSpec((count, 1, each, width), lambda i: (0, i, 0, 0))],
-        out_specs=pl.BlockSpec((1, each, width), lambda i: (i, 0, 0)),
-        out_shape=jax.ShapeDtypeStruct((n, each, width), BF),
-        compiler_params=pltpu.CompilerParams(vmem_limit_bytes=16 * 2**20),
-        cost_estimate=pl.CostEstimate(flops=parts.size, bytes_accessed=2 * parts.size, transcendentals=0),
-        name="sum_parts",
-    )(parts)
-
-
-def spread_kernel(a_ref, b_ref, c_ref, d_ref, out_ref, *, factor):
-    a, b, c, d = (ref[...].astype(F32) for ref in (a_ref, b_ref, c_ref, d_ref))
-    total = (a + c) + (b + d)
-    out_ref[...] = jnp.broadcast_to((total * factor).astype(BF)[None], out_ref.shape)
-
-
-def spread(parts, copies, factor):
-    n, each, width = parts[0].shape
+    spec = pl.BlockSpec((count, 1, each, width), lambda i: (0, i, 0, 0))
     return pl.pallas_call(
         functools.partial(spread_kernel, factor=factor),
         grid=(n,),
-        in_specs=[pl.BlockSpec((1, each, width), lambda i: (i, 0, 0))] * len(parts),
-        out_specs=pl.BlockSpec((copies, 1, each, width), lambda i: (0, i, 0, 0)),
-        out_shape=jax.ShapeDtypeStruct((copies, n, each, width), BF),
-        compiler_params=pltpu.CompilerParams(vmem_limit_bytes=60 * 2**20),
-        cost_estimate=pl.CostEstimate(flops=4 * parts[0].size, bytes_accessed=2 * copies * parts[0].size, transcendentals=0),
+        in_specs=[spec],
+        out_specs=spec,
+        out_shape=jax.ShapeDtypeStruct(parts.shape, BF),
+        compiler_params=pltpu.CompilerParams(vmem_limit_bytes=16 * 2**20),
+        cost_estimate=pl.CostEstimate(flops=parts.size, bytes_accessed=4 * parts.size, transcendentals=0),
         name="spread",
-    )(*parts)
+    )(parts)
 
 
 def place_kernel(half_ref, rows_ref, *rest):
-    n = rows_ref.shape[1]
+    n = rows_ref.shape[3]
+    width = rows_ref.shape[5]
     for i, out in enumerate(rest[-n:]):
-        out[0] = rows_ref[:, i]
+        for up in range(2):
+            for right in range(2):
+                out[0, :, up, :, right * width:(right + 1) * width] = rows_ref[up, right, :, i]
 
 
 def place(half, rows, into=()):
-    pieces, n, each, width = rows.shape
+    _, _, pieces, n, each, width = rows.shape
     step = pieces // 4
     hbm = pl.BlockSpec(memory_space=pl.ANY)
     return pl.pallas_call(
@@ -335,10 +342,10 @@
         grid_spec=pltpu.PrefetchScalarGridSpec(
             num_scalar_prefetch=1,
             grid=(pieces // step,),
-            in_specs=[pl.BlockSpec((step, n, each, width), lambda p, half: (p, 0, 0, 0))] + [hbm] * len(into),
-            out_specs=[pl.BlockSpec((1, step, each, width), lambda p, half: (half[0], p, 0, 0))] * n,
+            in_specs=[pl.BlockSpec((2, 2, step, n, each, width), lambda p, half: (0, 0, p, 0, 0, 0))] + [hbm] * len(into),
+            out_specs=[pl.BlockSpec((1, step, 2, each, 2 * width), lambda p, half: (half[0], p, 0, 0, 0))] * n,
         ),
-        out_shape=[jax.ShapeDtypeStruct((2, pieces, each, width), BF)] * n,
+        out_shape=[jax.ShapeDtypeStruct((2, pieces, 2, each, 2 * width), BF)] * n,
         input_output_aliases={2 + i: i for i in range(len(into))},
         compiler_params=pltpu.CompilerParams(vmem_limit_bytes=16 * 2**20),
         cost_estimate=pl.CostEstimate(flops=0, bytes_accessed=4 * rows.size, transcendentals=0),
@@ -365,15 +372,18 @@
     back = [dx[0]]
     for s in range(1, n_lang):
         back.append(lax.ppermute(dx[s], "lang", [(i, (i + s) % n_lang) for i in range(n_lang)]))
-    chip = (keep.astype(F32) + other.astype(F32)).astype(BF)
-    pieces = lax.all_to_all(chip, "pair", split_axis=0, concat_axis=0, tiled=True)
+    same_core = [[lang * n_pair + p for lang in range(core, n_lang, 2) for p in range(n_pair)] for core in range(2)]
+
+    def over_chips(a):
+        return lax.all_to_all(
+            a, ("lang", "pair"), split_axis=0, concat_axis=0, axis_index_groups=same_core, tiled=True
+        )
+
+    flat = (-1,) + keep.shape[3:]
+    pieces = over_chips(add(keep.reshape(flat), other.reshape(flat)))
     pieces, *back[1:4] = lax.optimization_barrier((pieces, *back[1:4]))
-    plane = sum_parts(pieces)
-    rings = [plane]
-    for y in range(1, n_lang // 2):
-        rings.append(lax.ppermute(plane, "lang", [(i, (i + 2 * y) % n_lang) for i in range(n_lang)]))
     factor = 1.0 / (sent_dev * n_lang * n_pair * length) ** 0.5
-    near = lax.all_to_all(spread(rings, n_pair, factor), "pair", split_axis=0, concat_axis=0, tiled=True)
+    near = over_chips(spread(pieces, factor)).reshape(keep.shape)
     grad_sentences = combine(where, listed, dq, w_query, back)
     near, grad_sentences = lax.optimization_barrier((near, grad_sentences))
     far = lax.ppermute(near, "lang", other_core)

time: 214 us -> 229 us (1.070)
  waiting for transfers between devices: 105 us -> 132 us
  Pallas kernels: 53.4 us -> 47.1 us
  other arithmetic: 5.17 us -> 0 us
  starting transfers between devices: 45.3 us -> 40.9 us
  local copies, waits for them, and re-layouts: 2.86 us -> 7.17 us
    ppermute x7, waiting for transfers between devices: 28.8 us -> 96.7 us  [body(): lax.ppermute(dx[s], 'lang', [(i, (i + s) % n_lang) for i in range(n_lang)])]
    all_to_all x2, waiting for transfers between devices: 32.3 us -> 0.01 us  [over_chips(): lax.all_to_all(a, ('lang', 'pair'), split_axis=0, concat_axis=0, axis_ind...]
    ppermute x3 -> x0, waiting for transfers between devices: 8.52 us -> none  [body(): lax.ppermute(plane, 'lang', [(i, (i + 2 * y) % n_lang) for i in range(n_l...]
    ppermute x1, starting transfers between devices: 6.15 us -> 0.09 us  [body(): far = lax.ppermute(near, 'lang', other_core)]
    convert_element_type x1 -> x0, other arithmetic: 5.17 us -> none  [body(): chip = (keep.astype(F32) + other.astype(F32)).astype(BF)]
    pallas_call x1, Pallas kernels: 35.7 us -> 31.1 us  [attend(): pl.pallas_call(functools.partial(attend_kernel, n_src=n_src, n_slot=n_slo...]
    unnamed x20 -> x18, local copies, waits for them, and re-layouts: 2.86 us -> 7.17 us
    ppermute x3 -> x0, starting transfers between devices: 4.16 us -> none  [body(): lax.ppermute(plane, 'lang', [(i, (i + 2 * y) % n_lang) for i in range(n_l...]
  transfers between devices with their start and end apart: 15 -> 12, of which waited for: 15 -> 9; matrix products, arithmetic and copies ran while one was open for 0% -> 0% of each run, Pallas kernels for 4% -> 4%
where the time goes in v7:
time: 229 us; the launch traced here: 228 us
  waiting for transfers between devices  132 us (58%)
  Pallas kernels  47.1 us (21%)
  starting transfers between devices  40.9 us (18%)
  local copies, waits for them, and re-layouts  7.17 us (3%)
    ppermute x7, waiting for transfers between devices, body(): lax.ppermute(dx[s], 'lang', [(i, (i + s) % n_lang) for i in range(n_lang)])  96.7 us
    pallas_call x1, Pallas kernels, attend(): pl.pallas_call(functools.partial(attend_kernel, n_src=n_src, n_slot=n_slo...  31.1 us
    all_to_all x1, waiting for transfers between devices, body(): lax.all_to_all(outgoing, 'lang', split_axis=0, concat_axis=0, tiled=True)  26.3 us
    all_to_all x2, starting transfers between devices, over_chips(): lax.all_to_all(a, ('lang', 'pair'), split_axis=0, concat_axis=0, axis_ind...  22.7 us
    ppermute x7, starting transfers between devices, body(): lax.ppermute(dx[s], 'lang', [(i, (i + s) % n_lang) for i in range(n_lang)])  11.2 us
    unnamed x18, local copies, waits for them, and re-layouts  7.17 us
    pallas_call x1, Pallas kernels, combine(): pl.pallas_call(combine_kernel, in_specs=[smem, smem] + [hbm] * (2 + len(p...  6.09 us
    all_to_all x1, starting transfers between devices, body(): lax.all_to_all(outgoing, 'lang', split_axis=0, concat_axis=0, tiled=True)  5.98 us
  transfers between devices with their start and end apart: 12, of which 9 were waited for; matrix products, arithmetic and copies ran while one was open for 0% of the time, Pallas kernels for 4%

profile of v7, /device:TPU:1, one launch (start us, length us, event | category | flops | bytes accessed | tf_op | source)
XLA Modules:
  0.0 227.7 jit_solution(5317072242667716385)
XLA Ops:
  0.6 3.3 %pick.1 = bf16[8,128,1024]{2,1,0:T(8,128)(2,1)} custom-call(s32[8]{0:T(128)} %bitcast.19, bf16[4,128,1024]{2,1,0:T(8,128)(2,1)} %x_hbm.1), custom_call_target="tpu_custom_call" | custom-call | tf_op jit(solution)/shard_map/pick/pallas_call | solution.py:277
  3.9 6.0 %all-to-all-start = ((bf16[8,128,1024]{2,1,0:T(8,128)(2,1)}), bf16[8,128,1024]{2,1,0:T(8,128)(2,1)S(1)}, u32[]{:S(2)}, u32[]{:S(2)}) async-start(bf16[8,128,1024]{2,1,0:T(8,128)(2,1)} %pick.1), calls=%async_computation | async-start | bytes 4194304 | tf_op jit(solution)/shard_map/all_to_all | solution.py:363
  9.9 26.3 %all-to-all-done.r_hbm = bf16[8,128,1024]{2,1,0:T(8,128)(2,1)S(1)} async-done(((bf16[8,128,1024]{2,1,0:T(8,128)(2,1)}), bf16[8,128,1024]{2,1,0:T(8,128)(2,1)S(1)}, u32[]{:S(2)}, u32[]{:S(2)}) %all-to-all-start) | async-done | bytes 2097184 | tf_op jit(solution)/shard_map/all_to_all | solution.py:363
  36.2 0.0 copy-start.3
  36.2 1.3 copy-done.3
  37.5 31.1 %attend.1 = (bf16[512,1024]{1,0:T(8,128)(2,1)}, bf16[512,1024]{1,0:T(8,128)(2,1)}, bf16[2,2,16,3,16,512]{5,4,3,2,1,0:T(8,128)(2,1)}, bf16[2,2,16,3,16,512]{5,4,3...) custom-call(s32[1]{0:T(128)} %bitcast.me_ref, ...), custom_call_target="tpu_custom_call" | custom-call | flops 34896609280 | bytes 20971520 | tf_op jit(solution)/shard_map/attend/pallas_call | solution.py:193
  68.7 0.9 collective-permute-start
  69.6 5.5 %collective-permute-done = bf16[2,2,16,3,16,512]{5,4,3,2,1,0:T(8,128)(2,1)S(1)} collective-permute-done((bf16[2,2,16,3,16,512]{5,4,3,2,1,0:T(8,128)(2,1)}, bf16[2,2,16,3,16,512]{5,4,3,2,1,0:T(8,128)(2,1)S(1)}, u32[]{:S(2)}, u32[]{:S(2)}) %collective-permute-start) | collective-permute-done | bytes 3145760 | tf_op jit(solution)/shard_map/ppermute | solution.py:371
  75.1 0.0 copy-start.2
  75.1 1.9 copy-done.2
  77.0 0.8 add.1
  77.8 0.0 copy-start.1
  77.8 1.6 copy-done.1
  79.4 14.6 %all-to-all-start.1 = ((bf16[64,3,16,512]{3,2,1,0:T(8,128)(2,1)}), bf16[64,3,16,512]{3,2,1,0:T(8,128)(2,1)S(1)}, u32[]{:S(2)}, u32[]{:S(2)}) async-start(bf16[64,3,16,512]{3,2,1,0:T(8,128)(2,1)} %copy-done.1), calls=%async_computation.1 | async-start | bytes 6291456 | tf_op jit(solution)/shard_map/all_to_all | solution.py:378
  94.0 1.8 collective-permute-start.1
  95.8 1.3 collective-permute-start.2
  97.1 1.7 collective-permute-start.3
  98.8 34.1 %collective-permute-done.1.rest_1_ = bf16[128,1024]{1,0:T(8,128)(2,1)S(1)} collective-permute-done((bf16[128,1024]{1,0:T(8,128)(2,1)}, bf16[128,1024]{1,0:T(8,128)(2,1)S(1)}, u32[]{:S(2)}, u32[]{:S(2)}) %collective-permute-start.1) | collective-permute-done | bytes 262176 | tf_op jit(solution)/shard_map/ppermute | solution.py:374
  132.9 0.0 copy-start.4
  132.9 13.1 %collective-permute-done.2.rest_2_ = bf16[128,1024]{1,0:T(8,128)(2,1)S(1)} collective-permute-done((bf16[128,1024]{1,0:T(8,128)(2,1)}, bf16[128,1024]{1,0:T(8,128)(2,1)S(1)}, u32[]{:S(2)}, u32[]{:S(2)}) %collective-permute-start.2) | collective-permute-done | bytes 262176 | tf_op jit(solution)/shard_map/ppermute | solution.py:374
  146.0 0.0 copy-start.5
  146.0 0.7 copy-done.5
  146.7 0.0 collective-permute-done.3.rest_3_
  146.7 0.0 all-to-all-done.1.parts_ref
  146.7 1.2 spread.1
  148.0 0.0 copy-done.4
  148.0 0.0 copy-start
  148.0 1.6 copy-done
  149.6 8.1 %all-to-all-start.2 = ((bf16[64,3,16,512]{3,2,1,0:T(8,128)(2,1)}), bf16[64,3,16,512]{3,2,1,0:T(8,128)(2,1)S(1)}, u32[]{:S(2)}, u32[]{:S(2)}) async-start(bf16[64,3,16,512]{3,2,1,0:T(8,128)(2,1)} %copy-done), calls=%async_computation.2 | async-start | bytes 6291456 | tf_op jit(solution)/shard_map/all_to_all | solution.py:378
  157.7 2.9 %collective-permute-start.4 = (bf16[128,1024]{1,0:T(8,128)(2,1)}, bf16[128,1024]{1,0:T(8,128)(2,1)S(1)}, u32[]{:S(2)}, u32[]{:S(2)}) collective-permute-start(bf16[128,1024]{1,0:T(8,128)(2,1)} %get-tuple-element.41), channel_id=1, source_target_pairs={{0,64},{16,80},{32,96},{48,112},{64,0},{80,16},{96,32},{112,48},{1... | collective-permute-start | bytes 786440 | tf_op jit(solution)/shard_map/ppermute | solution.py:374
  160.7 1.5 collective-permute-start.5
  162.2 0.0 collective-permute-start.6
  162.2 1.9 collective-permute-start.7
  164.1 36.6 %collective-permute-done.4.rest_4_ = bf16[128,1024]{1,0:T(8,128)(2,1)S(1)} collective-permute-done((bf16[128,1024]{1,0:T(8,128)(2,1)}, bf16[128,1024]{1,0:T(8,128)(2,1)S(1)}, u32[]{:S(2)}, u32[]{:S(2)}) %collective-permute-start.4) | collective-permute-done | bytes 262176 | tf_op jit(solution)/shard_map/ppermute | solution.py:374
  200.7 0.0 copy-start.6
  200.7 4.7 %collective-permute-done.5.rest_5_ = bf16[128,1024]{1,0:T(8,128)(2,1)S(1)} collective-permute-done((bf16[128,1024]{1,0:T(8,128)(2,1)}, bf16[128,1024]{1,0:T(8,128)(2,1)S(1)}, u32[]{:S(2)}, u32[]{:S(2)}) %collective-permute-start.5) | collective-permute-done | bytes 262176 | tf_op jit(solution)/shard_map/ppermute | solution.py:374
  205.4 0.0 copy-start.7
  205.4 5.8 %collective-permute-done.6.rest_6_ = bf16[128,1024]{1,0:T(8,128)(2,1)S(1)} collective-permute-done((bf16[128,1024]{1,0:T(8,128)(2,1)}, bf16[128,1024]{1,0:T(8,128)(2,1)S(1)}, u32[]{:S(2)}, u32[]{:S(2)}) %collective-permute-start.6) | collective-permute-done | bytes 262176 | tf_op jit(solution)/shard_map/ppermute | solution.py:374
  211.2 2.4 %collective-permute-done.7.rest_7_ = bf16[128,1024]{1,0:T(8,128)(2,1)} collective-permute-done((bf16[128,1024]{1,0:T(8,128)(2,1)}, bf16[128,1024]{1,0:T(8,128)(2,1)}, u32[]{:S(2)}, u32[]{:S(2)}) %collective-permute-start.7) | collective-permute-done | bytes 262176 | tf_op jit(solution)/shard_map/ppermute | solution.py:374
  213.6 0.0 copy-done.6
  213.6 0.0 copy-done.7
  213.6 0.0 copy-done.8
  213.6 6.1 %combine.1 = bf16[4,128,1024]{2,1,0:T(8,128)(2,1)} custom-call(s32[1]{0:T(128)} %bitcast.me_ref, s32[8]{0:T(128)} %bitcast.20, bf16[512,1024]{1,0:T(8,128)(2,1)} %get-tuple-element.36.dq_hbm, bf16[1024,1024]{1,0:T(8,128)(2,1)} %wq_hbm.3, bf16[128,1024]{1,0:T(8,128)(2,1)} %get-tuple-element.37.rest_0_, bf16[128,1024]{1,0:T(8,128)(2,1)} %copy-done.4, ...), custom_call_target="tpu_custom_call" | custom-call | flops 1073741824 | bytes 6291456 | tf_op jit(solution)/shard_map/combine/pallas_call | solution.py:247
  219.7 0.0 all-to-all-done.2
  219.7 0.1 collective-permute-start.8
  219.8 2.3 %place.2 = (bf16[2,16,2,16,1024]{4,3,2,1,0:T(8,128)(2,1)}, bf16[2,16,2,16,1024]{4,3,2,1,0:T(8,128)(2,1)}, bf16[2,16,2,16,1024]{4,3,2,1,0:T(8,128)(2,1)}) custom-call(s32[1]{0:T(128)S(6)} %rem.18.half_ref, bf16[2,2,16,3,16,512]{5,4,3,2,1,0:T(8,128)(2,1)S(1)} %bitcast.12), custom_call_target="tpu_custom_call" | custom-call | bytes 6291456 | tf_op jit(solution)/shard_map/place/pallas_call | solution.py:340
  222.1 3.3 %collective-permute-done.8.rows_ref = bf16[2,2,16,3,16,512]{5,4,3,2,1,0:T(8,128)(2,1)S(1)} collective-permute-done((bf16[2,2,16,3,16,512]{5,4,3,2,1,0:T(8,128)(2,1)S(1)}, bf16[2,2,16,3,16,512]{5,4,3,2,1,0:T(8,128)(2,1)S(1)}, u32[]{:S(2)}, u32[]{:S(2)}) %collective-permute-start.8) | collective-permute-done | bytes 3145760 | tf_op jit(solution)/shard_map/ppermute | solution.py:389
  225.4 2.3 %place.3 = (bf16[2,16,2,16,1024]{4,3,2,1,0:T(8,128)(2,1)}, bf16[2,16,2,16,1024]{4,3,2,1,0:T(8,128)(2,1)}, bf16[2,16,2,16,1024]{4,3,2,1,0:T(8,128)(2,1)}) custom-call(s32[1]{0:T(128)S(6)} %sub.3.half_ref, bf16[2,2,16,3,16,512]{5,4,3,2,1,0:T(8,128)(2,1)S(1)} %collective-permute-done.8.rows_ref, ...), custom_call_target="tpu_custom_call", output_to_operand_aliasing={{0}: (2, {}), {1}: (3, {}), {2}: (4, {})} | custom-call | bytes 6291456 | tf_op jit(solution)/shard_map/place/pallas_call | solution.py:340
  (1 shorter events, 0.0 us)
Async XLA Ops:
  3.9 32.3 %all-to-all-start = ((bf16[8,128,1024]{2,1,0:T(8,128)(2,1)}), bf16[8,128,1024]{2,1,0:T(8,128)(2,1)S(1)}, u32[]{:S(2)}, u32[]{:S(2)}) async-start(bf16[8,128,1024]{2,1,0:T(8,128)(2,1)} %pick.1), calls=%async_computation | async-start | bytes 4194304 | tf_op jit(solution)/shard_map/all_to_all | solution.py:363
  36.2 1.3 copy-start.3
  68.7 6.4 %collective-permute-start = (bf16[2,2,16,3,16,512]{5,4,3,2,1,0:T(8,128)(2,1)}, bf16[2,2,16,3,16,512]{5,4,3,2,1,0:T(8,128)(2,1)S(1)}, u32[]{:S(2)}, u32[]{:S(2)}) collective-permute-start(bf16[2,2,16,3,16,512]{5,4,3,2,1,0:T(8,128)(2,1)} %get-tuple-element.31), channel_id=1, source_target_pairs={{0,16},{16,0},{32,48},{48,32},{64,80},{80,64},{96,112},{112,96},{1... | collective-permute-start | bytes 9437192 | tf_op jit(solution)/shard_map/ppermute | solution.py:371
  75.1 1.9 copy-start.2
  77.8 1.6 copy-start.1
  79.4 67.3 %all-to-all-start.1 = ((bf16[64,3,16,512]{3,2,1,0:T(8,128)(2,1)}), bf16[64,3,16,512]{3,2,1,0:T(8,128)(2,1)S(1)}, u32[]{:S(2)}, u32[]{:S(2)}) async-start(bf16[64,3,16,512]{3,2,1,0:T(8,128)(2,1)} %copy-done.1), calls=%async_computation.1 | async-start | bytes 6291456 | tf_op jit(solution)/shard_map/all_to_all | solution.py:378
  94.0 38.9 %collective-permute-start.1 = (bf16[128,1024]{1,0:T(8,128)(2,1)}, bf16[128,1024]{1,0:T(8,128)(2,1)S(1)}, u32[]{:S(2)}, u32[]{:S(2)}) collective-permute-start(bf16[128,1024]{1,0:T(8,128)(2,1)} %get-tuple-element.32), channel_id=1, source_target_pairs={{0,16},{16,32},{32,48},{48,64},{64,80},{80,96},{96,112},{112,0},{1... | collective-permute-start | bytes 786440 | tf_op jit(solution)/shard_map/ppermute | solution.py:374
  95.8 50.2 %collective-permute-start.2 = (bf16[128,1024]{1,0:T(8,128)(2,1)}, bf16[128,1024]{1,0:T(8,128)(2,1)S(1)}, u32[]{:S(2)}, u32[]{:S(2)}) collective-permute-start(bf16[128,1024]{1,0:T(8,128)(2,1)} %get-tuple-element.33), channel_id=1, source_target_pairs={{0,32},{16,48},{32,64},{48,80},{64,96},{80,112},{96,0},{112,16},{1... | collective-permute-start | bytes 786440 | tf_op jit(solution)/shard_map/ppermute | solution.py:374
  97.1 49.6 %collective-permute-start.3 = (bf16[128,1024]{1,0:T(8,128)(2,1)}, bf16[128,1024]{1,0:T(8,128)(2,1)}, u32[]{:S(2)}, u32[]{:S(2)}) collective-permute-start(bf16[128,1024]{1,0:T(8,128)(2,1)} %get-tuple-element.34), channel_id=1, source_target_pairs={{0,48},{16,64},{32,80},{48,96},{64,112},{80,0},{96,16},{112,32},{1... | collective-permute-start | bytes 786440 | tf_op jit(solution)/shard_map/ppermute | solution.py:374
  132.9 15.1 %copy-start.4 = (bf16[128,1024]{1,0:T(8,128)(2,1)}, bf16[128,1024]{1,0:T(8,128)(2,1)S(1)}, u32[]{:S(2)}) copy-start(bf16[128,1024]{1,0:T(8,128)(2,1)S(1)} %collective-permute-done.1.rest_1_) | copy-start | bytes 786436
  146.0 0.7 copy-start.5
  148.0 1.6 copy-start
  149.6 70.1 %all-to-all-start.2 = ((bf16[64,3,16,512]{3,2,1,0:T(8,128)(2,1)}), bf16[64,3,16,512]{3,2,1,0:T(8,128)(2,1)S(1)}, u32[]{:S(2)}, u32[]{:S(2)}) async-start(bf16[64,3,16,512]{3,2,1,0:T(8,128)(2,1)} %copy-done), calls=%async_computation.2 | async-start | bytes 6291456 | tf_op jit(solution)/shard_map/all_to_all | solution.py:378
  157.7 43.0 %collective-permute-start.4 = (bf16[128,1024]{1,0:T(8,128)(2,1)}, bf16[128,1024]{1,0:T(8,128)(2,1)S(1)}, u32[]{:S(2)}, u32[]{:S(2)}) collective-permute-start(bf16[128,1024]{1,0:T(8,128)(2,1)} %get-tuple-element.41), channel_id=1, source_target_pairs={{0,64},{16,80},{32,96},{48,112},{64,0},{80,16},{96,32},{112,48},{1... | collective-permute-start | bytes 786440 | tf_op jit(solution)/shard_map/ppermute | solution.py:374
  160.7 44.8 %collective-permute-start.5 = (bf16[128,1024]{1,0:T(8,128)(2,1)}, bf16[128,1024]{1,0:T(8,128)(2,1)S(1)}, u32[]{:S(2)}, u32[]{:S(2)}) collective-permute-start(bf16[128,1024]{1,0:T(8,128)(2,1)} %get-tuple-element.42), channel_id=1, source_target_pairs={{0,80},{16,96},{32,112},{48,0},{64,16},{80,32},{96,48},{112,64},{1... | collective-permute-start | bytes 786440 | tf_op jit(solution)/shard_map/ppermute | solution.py:374
  162.2 49.0 %collective-permute-start.6 = (bf16[128,1024]{1,0:T(8,128)(2,1)}, bf16[128,1024]{1,0:T(8,128)(2,1)S(1)}, u32[]{:S(2)}, u32[]{:S(2)}) collective-permute-start(bf16[128,1024]{1,0:T(8,128)(2,1)} %get-tuple-element.43), channel_id=1, source_target_pairs={{0,96},{16,112},{32,0},{48,16},{64,32},{80,48},{96,64},{112,80},{1... | collective-permute-start | bytes 786440 | tf_op jit(solution)/shard_map/ppermute | solution.py:374
  162.2 51.4 %collective-permute-start.7 = (bf16[128,1024]{1,0:T(8,128)(2,1)}, bf16[128,1024]{1,0:T(8,128)(2,1)}, u32[]{:S(2)}, u32[]{:S(2)}) collective-permute-start(bf16[128,1024]{1,0:T(8,128)(2,1)} %get-tuple-element.44), channel_id=1, source_target_pairs={{0,112},{16,0},{32,16},{48,32},{64,48},{80,64},{96,80},{112,96},{1... | collective-permute-start | bytes 786440 | tf_op jit(solution)/shard_map/ppermute | solution.py:374
  200.7 12.9 %copy-start.6 = (bf16[128,1024]{1,0:T(8,128)(2,1)}, bf16[128,1024]{1,0:T(8,128)(2,1)S(1)}, u32[]{:S(2)}) copy-start(bf16[128,1024]{1,0:T(8,128)(2,1)S(1)} %collective-permute-done.4.rest_4_) | copy-start | bytes 786436
  205.4 8.2 %copy-start.7 = (bf16[128,1024]{1,0:T(8,128)(2,1)}, bf16[128,1024]{1,0:T(8,128)(2,1)S(1)}, u32[]{:S(2)}) copy-start(bf16[128,1024]{1,0:T(8,128)(2,1)S(1)} %collective-permute-done.5.rest_5_) | copy-start | bytes 786436
  211.2 2.4 %copy-start.8 = (bf16[128,1024]{1,0:T(8,128)(2,1)}, bf16[128,1024]{1,0:T(8,128)(2,1)S(1)}, u32[]{:S(2)}) copy-start(bf16[128,1024]{1,0:T(8,128)(2,1)S(1)} %collective-permute-done.6.rest_6_) | copy-start | bytes 786436
  219.7 5.7 %collective-permute-start.8 = (bf16[2,2,16,3,16,512]{5,4,3,2,1,0:T(8,128)(2,1)S(1)}, bf16[2,2,16,3,16,512]{5,4,3,2,1,0:T(8,128)(2,1)S(1)}, u32[]{:S(2)}, u32[]{:S(2)}) collective-permute-start(bf16[2,2,16,3,16,512]{5,4,3,2,1,0:T(8,128)(2,1)S(1)} %bitcast.11), channel_id=1, source_target_pairs={{0,16},{16,0},{32,48},{48,32},{64,80},{80,64},{96,112},{112,96},{1... | collective-permute-start | bytes 9437192 | tf_op jit(solution)/shard_map/ppermute | solution.py:389

commit v8 on v6

--- a/solution.py
+++ b/solution.py
@@ -23,9 +23,10 @@
 
 def attend_kernel(me_ref, src_ref, slot_ref, valid_ref, x_hbm, r_hbm, c_hbm, wq_hbm, wk_hbm, wv_hbm,
                   *rest, n_src, n_slot, length):
-    outs, scratch = rest[:4 + n_slot], rest[4 + n_slot:]
-    att_hbm, dq_hbm, keep_hbm, send_hbm = outs[:4]
-    dx_hbm = outs[4:]
+    outs, scratch = rest[:6 + n_slot], rest[6 + n_slot:]
+    att_hbm, dq_hbm = outs[:2]
+    gw_hbm = (outs[4:6], outs[2:4])
+    dx_hbm = outs[6:]
     (mult, x_ref, r_ref, c_ref, wq_ref, wk_ref, wv_ref, att_v, dq_v, gw_v, dx_v,
      xt, rt, q2, g2, k_s, v_s, kt, vt, ot, dqt, dk_acc, dv_acc, sem_in, sem_r, sem_out) = scratch
     width = x_ref.shape[1]
@@ -150,16 +151,19 @@
         c.start()
         done.append(c)
 
-    _, pieces, _, each, _ = gw_v.shape
+    _, _, pieces, _, each, _ = gw_v.shape
     core = lax.rem(me, 2)
-    for k, dst in enumerate((send_hbm, keep_hbm)):
-        base = pl.multiple_of((core if k else 1 - core) * (pieces * each), LANES)
-        rows = pl.ds(base, pieces * each)
+    for k, halves in enumerate(gw_hbm):
+        base = pl.multiple_of((core if k else 1 - core) * (2 * pieces * each), LANES)
+        rows = pl.ds(base, 2 * pieces * each)
         for n in range(0, width, block):
             cols = slice(n, n + block)
             for i, (lhs, rhs) in enumerate(((xt, dq_v[:, cols]), (rt, dk[:, cols]), (rt, dv[:, cols]))):
-                gw_v[k, :, i, :, cols] = mm(lhs[rows, :], rhs).astype(BF).reshape(pieces, each, block)
-        out(gw_v.at[k], dst)
+                g = mm(lhs[rows, :], rhs).astype(BF).reshape(2, pieces, each, block)
+                for part in range(2):
+                    gw_v[k, part, :, i, :, cols] = g[part]
+        for part, dst in enumerate(halves):
+            out(gw_v.at[k, part], dst)
         if k == 0:
             out(dq_v, dq_hbm)
     for s in range(n_src):
@@ -180,7 +184,8 @@
     n_slot, length, width = r.shape
     rows = x.shape[0]
     n_src = rows // length
-    each = width // 2 // pieces
+    each = width // 4 // pieces
+    share = (pieces, 3, each, width)
     heads = width // LANES
     smem = pl.BlockSpec(memory_space=pltpu.SMEM)
     hbm = pl.BlockSpec(memory_space=pltpu.HBM)
@@ -190,16 +195,15 @@
     return pl.pallas_call(
         functools.partial(attend_kernel, n_src=n_src, n_slot=n_slot, length=length),
         in_specs=[smem] * 4 + [hbm] * 6,
-        out_specs=[hbm] * (4 + n_slot),
-        out_shape=[shape((rows, width), BF), shape((rows, width), BF),
-                   shape((pieces, 3, each, width), BF), shape((pieces, 3, each, width), BF)]
+        out_specs=[hbm] * (6 + n_slot),
+        out_shape=[shape((rows, width), BF), shape((rows, width), BF)] + [shape(share, BF)] * 4
         + [shape((length, width), BF)] * n_slot,
         scratch_shapes=[
             pltpu.SMEM((n_src * n_slot,), jnp.int32),
             vm((rows, width), BF), vm((n_slot * length, width), BF), vm((rows, width), BF),
             vm((width, width), BF), vm((width, width), BF), vm((width, width), BF),
             vm((rows, width), BF), vm((rows, width), BF),
-            vm((2, pieces, 3, each, width), BF), vm((n_slot * length, width), BF),
+            vm((2, 2) + share, BF), vm((n_slot * length, width), BF),
             vm((width, rows), BF), vm((width, n_slot * length), BF),
             vm((n_src, heads, 2 * length, LANES), BF), vm((n_src, heads, 2 * length, LANES), BF),
             vm((n_slot, length, width), BF), vm((n_slot, length, width), BF),
@@ -207,7 +211,7 @@
             vm((n_src, width, length), F32), vm((n_src, width, length), F32),
             vm((n_slot, length, width), F32), vm((n_slot, length, width), F32),
             pltpu.SemaphoreType.DMA((5,)), pltpu.SemaphoreType.DMA((n_slot,)),
-            pltpu.SemaphoreType.DMA((4 + n_slot,)),
+            pltpu.SemaphoreType.DMA((6 + n_slot,)),
         ],
         compiler_params=pltpu.CompilerParams(vmem_limit_bytes=60 * 2**20),
         cost_estimate=pl.CostEstimate(flops=4 * macs, bytes_accessed=20 * 2**20, transcendentals=0),
@@ -282,68 +286,89 @@
     )(listed, x)
 
 
-def sum_kernel(parts_ref, out_ref):
-    out_ref[...] = jnp.sum(parts_ref[...].astype(F32), axis=0).astype(BF)
-
-
-def sum_parts(parts):
-    count, n, each, width = parts.shape
+def add_kernel(a_ref, b_ref, out_ref):
+    out_ref[...] = (a_ref[...].astype(F32) + b_ref[...].astype(F32)).astype(BF)
+
+
+def add(a, b):
+    count, n, each, width = a.shape
+    spec = pl.BlockSpec((count // 2, n, each, width), lambda i: (i, 0, 0, 0))
+    return pl.pallas_call(
+        add_kernel,
+        grid=(2,),
+        in_specs=[spec, spec],
+        out_specs=spec,
+        out_shape=jax.ShapeDtypeStruct(a.shape, BF),
+        compiler_params=pltpu.CompilerParams(vmem_limit_bytes=60 * 2**20),
+        cost_estimate=pl.CostEstimate(flops=a.size, bytes_accessed=6 * a.size, transcendentals=0),
+        name="add",
+    )(a, b)
+
+
+def sum_kernel(*refs):
+    for half, ref in enumerate(refs[:-1]):
+        refs[-1][half] = jnp.sum(ref[...].astype(F32), axis=0).astype(BF)
+
+
+def sum_parts(*halves):
+    count, n, each, width = halves[0].shape
+    size = len(halves) * halves[0].size
     return pl.pallas_call(
         sum_kernel,
         grid=(n,),
-        in_specs=[pl.BlockSpec((count, 1, each, width), lambda i: (0, i, 0, 0))],
-        out_specs=pl.BlockSpec((1, each, width), lambda i: (i, 0, 0)),
-        out_shape=jax.ShapeDtypeStruct((n, each, width), BF),
+        in_specs=[pl.BlockSpec((count, 1, each, width), lambda i: (0, i, 0, 0))] * len(halves),
+        out_specs=pl.BlockSpec((len(halves), 1, each, width), lambda i: (0, i, 0, 0)),
+        out_shape=jax.ShapeDtypeStruct((len(halves), n, each, width), BF),
         compiler_params=pltpu.CompilerParams(vmem_limit_bytes=16 * 2**20),
-        cost_estimate=pl.CostEstimate(flops=parts.size, bytes_accessed=2 * parts.size, transcendentals=0),
+        cost_estimate=pl.CostEstimate(flops=size, bytes_accessed=2 * size, transcendentals=0),
         name="sum_parts",
-    )(parts)
+    )(*halves)
 
 
 def spread_kernel(a_ref, b_ref, c_ref, d_ref, out_ref, *, factor):
-    a, b, c, d = (ref[...].astype(F32) for ref in (a_ref, b_ref, c_ref, d_ref))
+    a, b, c, d = (ref[0].astype(F32) for ref in (a_ref, b_ref, c_ref, d_ref))
     total = (a + c) + (b + d)
     out_ref[...] = jnp.broadcast_to((total * factor).astype(BF)[None], out_ref.shape)
 
 
-def spread(parts, copies, factor):
-    n, each, width = parts[0].shape
+def spread(parts, half, copies, factor):
+    _, n, each, width = parts[0].shape
     return pl.pallas_call(
         functools.partial(spread_kernel, factor=factor),
         grid=(n,),
-        in_specs=[pl.BlockSpec((1, each, width), lambda i: (i, 0, 0))] * len(parts),
+        in_specs=[pl.BlockSpec((1, 1, each, width), lambda i: (half, i, 0, 0))] * len(parts),
         out_specs=pl.BlockSpec((copies, 1, each, width), lambda i: (0, i, 0, 0)),
         out_shape=jax.ShapeDtypeStruct((copies, n, each, width), BF),
         compiler_params=pltpu.CompilerParams(vmem_limit_bytes=60 * 2**20),
-        cost_estimate=pl.CostEstimate(flops=4 * parts[0].size, bytes_accessed=2 * copies * parts[0].size, transcendentals=0),
+        cost_estimate=pl.CostEstimate(flops=4 * parts[0].size, bytes_accessed=copies * parts[0].size, transcendentals=0),
         name="spread",
     )(*parts)
 
 
-def place_kernel(half_ref, rows_ref, *rest):
+def place_kernel(quarter_ref, rows_ref, *rest):
     n = rows_ref.shape[1]
     for i, out in enumerate(rest[-n:]):
         out[0] = rows_ref[:, i]
 
 
-def place(half, rows, into=()):
+def place(quarter, rows, into=()):
     pieces, n, each, width = rows.shape
-    step = pieces // 4
+    step = pieces // 2
     hbm = pl.BlockSpec(memory_space=pl.ANY)
     return pl.pallas_call(
         place_kernel,
         grid_spec=pltpu.PrefetchScalarGridSpec(
             num_scalar_prefetch=1,
             grid=(pieces // step,),
-            in_specs=[pl.BlockSpec((step, n, each, width), lambda p, half: (p, 0, 0, 0))] + [hbm] * len(into),
-            out_specs=[pl.BlockSpec((1, step, each, width), lambda p, half: (half[0], p, 0, 0))] * n,
+            in_specs=[pl.BlockSpec((step, n, each, width), lambda p, at: (p, 0, 0, 0))] + [hbm] * len(into),
+            out_specs=[pl.BlockSpec((1, step, each, width), lambda p, at: (at[0], p, 0, 0))] * n,
         ),
-        out_shape=[jax.ShapeDtypeStruct((2, pieces, each, width), BF)] * n,
+        out_shape=[jax.ShapeDtypeStruct((4, pieces, each, width), BF)] * n,
         input_output_aliases={2 + i: i for i in range(len(into))},
         compiler_params=pltpu.CompilerParams(vmem_limit_bytes=16 * 2**20),
         cost_estimate=pl.CostEstimate(flops=0, bytes_accessed=4 * rows.size, transcendentals=0),
         name="place",
-    )(half, rows, *into)
+    )(quarter, rows, *into)
 
 
 def body(sentences, cotangent, w_query, w_key, w_value, send_rows, pair_src, pair_slot, pair_valid):
@@ -357,28 +382,41 @@
     x = sentences.reshape(-1, width)
     c = cotangent.reshape(-1, width)
     where = me.reshape(1).astype(jnp.int32)
-    attended, dq, keep, send, *dx = attend(
+    attended, dq, keep0, keep1, send0, send1, *dx = attend(
         where, pair_src, pair_slot, pair_valid, x, received, c, w_query, w_key, w_value, pieces=n_pair
     )
     other_core = [(i, i ^ 1) for i in range(n_lang)]
-    other = lax.ppermute(send, "lang", other_core)
+
+    def swap(a):
+        return lax.ppermute(a, "lang", other_core)
+
+    def over_pair(a):
+        return lax.all_to_all(a, "pair", split_axis=0, concat_axis=0, tiled=True)
+
     back = [dx[0]]
     for s in range(1, n_lang):
         back.append(lax.ppermute(dx[s], "lang", [(i, (i + s) % n_lang) for i in range(n_lang)]))
-    chip = (keep.astype(F32) + other.astype(F32)).astype(BF)
-    pieces = lax.all_to_all(chip, "pair", split_axis=0, concat_axis=0, tiled=True)
-    pieces, *back[1:4] = lax.optimization_barrier((pieces, *back[1:4]))
-    plane = sum_parts(pieces)
+    other0, other1 = swap(send0), swap(send1)
+    chip0 = add(keep0, other0)
+    chip0, other1 = lax.optimization_barrier((chip0, other1))
+    pieces0 = over_pair(chip0)
+    pieces1 = over_pair(add(keep1, other1))
+    pieces0, pieces1, *back[1:4] = lax.optimization_barrier((pieces0, pieces1, *back[1:4]))
+    plane = sum_parts(pieces0, pieces1)
     rings = [plane]
     for y in range(1, n_lang // 2):
         rings.append(lax.ppermute(plane, "lang", [(i, (i + 2 * y) % n_lang) for i in range(n_lang)]))
     factor = 1.0 / (sent_dev * n_lang * n_pair * length) ** 0.5
-    near = lax.all_to_all(spread(rings, n_pair, factor), "pair", split_axis=0, concat_axis=0, tiled=True)
+    near0 = over_pair(spread(rings, 0, n_pair, factor))
+    copies1, near0 = lax.optimization_barrier((spread(rings, 1, n_pair, factor), near0))
+    near1 = over_pair(copies1)
     grad_sentences = combine(where, listed, dq, w_query, back)
-    near, grad_sentences = lax.optimization_barrier((near, grad_sentences))
-    far = lax.ppermute(near, "lang", other_core)
+    far0 = swap(near0)
     core = lax.rem(where, 2)
-    grads = place(1 - core, far, place(core, near))
+    grads = place(2 - 2 * core, far0, place(2 * core, near0))
+    near1, grad_sentences, *grads = lax.optimization_barrier((near1, grad_sentences, *grads))
+    far1 = swap(near1)
+    grads = place(3 - 2 * core, far1, place(2 * core + 1, near1, grads))
     grads = tuple(g.reshape(width, width) for g in grads)
     return (attended.reshape(sentences.shape), grad_sentences) + grads
 

time: 214 us -> 224 us (1.047)
  Pallas kernels: 53.4 us -> 63.1 us
  starting transfers between devices: 45.3 us -> 51.5 us
  other arithmetic: 5.17 us -> 0 us
  waiting for transfers between devices: 105 us -> 102 us
    pallas_call x0 -> x2, Pallas kernels: none -> 5.84 us  [add(): pl.pallas_call(add_kernel, grid=(2,), in_specs=[spec, spec], out_specs=sp...]
    ppermute x3, waiting for transfers between devices: 8.52 us -> 3.09 us  [body(): lax.ppermute(plane, 'lang', [(i, (i + 2 * y) % n_lang) for i in range(n_l...]
    all_to_all x2 -> x4, waiting for transfers between devices: 32.3 us -> 37.6 us  [over_pair(): return lax.all_to_all(a, 'pair', split_axis=0, concat_axis=0, tiled=True)]
    convert_element_type x1 -> x0, other arithmetic: 5.17 us -> none  [body(): chip = (keep.astype(F32) + other.astype(F32)).astype(BF)]
    ppermute x2 -> x4, waiting for transfers between devices: 9.03 us -> 5.27 us  [swap(): return lax.ppermute(a, 'lang', other_core)]
    all_to_all x2 -> x4, starting transfers between devices: 18.7 us -> 21.6 us  [over_pair(): return lax.all_to_all(a, 'pair', split_axis=0, concat_axis=0, tiled=True)]
    ppermute x7, starting transfers between devices: 10.1 us -> 12.7 us  [body(): lax.ppermute(dx[s], 'lang', [(i, (i + s) % n_lang) for i in range(n_lang)])]
    pallas_call x1 -> x2, Pallas kernels: 3.44 us -> 5.46 us  [spread(): pl.pallas_call(functools.partial(spread_kernel, factor=factor), grid=(n,)...]
  transfers between devices with their start and end apart: 15 -> 19, of which waited for: 15 -> 15; matrix products, arithmetic and copies ran while one was open for 0% -> 0% of each run, Pallas kernels for 4% -> 9%
where the time goes in v8:
time: 224 us; the launch traced here: 222 us
  waiting for transfers between devices  102 us (46%)
  Pallas kernels  63.1 us (28%)
  starting transfers between devices  51.5 us (23%)
  local copies, waits for them, and re-layouts  4.52 us (2%)
    all_to_all x4, waiting for transfers between devices, over_pair(): return lax.all_to_all(a, 'pair', split_axis=0, concat_axis=0, tiled=True)  37.6 us
    pallas_call x1, Pallas kernels, attend(): pl.pallas_call(functools.partial(attend_kernel, n_src=n_src, n_slot=n_slo...  35.7 us
    ppermute x7, waiting for transfers between devices, body(): lax.ppermute(dx[s], 'lang', [(i, (i + s) % n_lang) for i in range(n_lang)])  29.5 us
    all_to_all x1, waiting for transfers between devices, body(): lax.all_to_all(outgoing, 'lang', split_axis=0, concat_axis=0, tiled=True)  26.3 us
    all_to_all x4, starting transfers between devices, over_pair(): return lax.all_to_all(a, 'pair', split_axis=0, concat_axis=0, tiled=True)  21.6 us
    ppermute x7, starting transfers between devices, body(): lax.ppermute(dx[s], 'lang', [(i, (i + s) % n_lang) for i in range(n_lang)])  12.7 us
    pallas_call x1, Pallas kernels, combine(): pl.pallas_call(combine_kernel, in_specs=[smem, smem] + [hbm] * (2 + len(p...  6.1 us
    pallas_call x4, Pallas kernels, place(): pl.pallas_call(place_kernel, grid_spec=pltpu.PrefetchScalarGridSpec(num_s...  6 us
  transfers between devices with their start and end apart: 19, of which 15 were waited for; matrix products, arithmetic and copies ran while one was open for 0% of the time, Pallas kernels for 9%

profile of v8, /device:TPU:1, one launch (start us, length us, event | category | flops | bytes accessed | tf_op | source)
XLA Modules:
  0.0 221.7 jit_solution(14271433470271257511)
XLA Ops:
  0.6 3.3 %pick.1 = bf16[8,128,1024]{2,1,0:T(8,128)(2,1)} custom-call(s32[8]{0:T(128)} %bitcast.12, bf16[4,128,1024]{2,1,0:T(8,128)(2,1)} %x_hbm.1), custom_call_target="tpu_custom_call" | custom-call | tf_op jit(solution)/shard_map/pick/pallas_call | solution.py:278
  3.9 6.0 %all-to-all-start = ((bf16[8,128,1024]{2,1,0:T(8,128)(2,1)}), bf16[8,128,1024]{2,1,0:T(8,128)(2,1)S(1)}, u32[]{:S(2)}, u32[]{:S(2)}) async-start(bf16[8,128,1024]{2,1,0:T(8,128)(2,1)} %pick.1), calls=%async_computation | async-start | bytes 4194304 | tf_op jit(solution)/shard_map/all_to_all | solution.py:381
  9.9 26.3 %all-to-all-done.r_hbm = bf16[8,128,1024]{2,1,0:T(8,128)(2,1)S(1)} async-done(((bf16[8,128,1024]{2,1,0:T(8,128)(2,1)}), bf16[8,128,1024]{2,1,0:T(8,128)(2,1)S(1)}, u32[]{:S(2)}, u32[]{:S(2)}) %all-to-all-start) | async-done | bytes 2097184 | tf_op jit(solution)/shard_map/all_to_all | solution.py:381
  36.2 1.3 copy-done.1
  37.5 35.7 %attend.1 = (bf16[512,1024]{1,0:T(8,128)(2,1)}, bf16[512,1024]{1,0:T(8,128)(2,1)}, bf16[16,3,16,1024]{3,2,1,0:T(8,128)(2,1)}, bf16[16,3,16,1024]{3,2,1,0:T(8,128...) custom-call(s32[1]{0:T(128)} %bitcast.me_ref, ...), custom_call_target="tpu_custom_call" | custom-call | flops 34896609280 | bytes 20971520 | tf_op jit(solution)/shard_map/attend/pallas_call | solution.py:195
  73.4 0.5 collective-permute-start.1
  73.9 3.1 %collective-permute-done.b_ref = bf16[16,3,16,1024]{3,2,1,0:T(8,128)(2,1)S(1)} collective-permute-done((bf16[16,3,16,1024]{3,2,1,0:T(8,128)(2,1)}, bf16[16,3,16,1024]{3,2,1,0:T(8,128)(2,1)S(1)}, u32[]{:S(2)}, u32[]{:S(2)}) %collective-permute-start) | collective-permute-done | bytes 1572896 | tf_op jit(solution)/shard_map/ppermute | solution.py:391
  77.0 1.1 copy-done.3
  78.1 2.9 %add.6 = bf16[16,3,16,1024]{3,2,1,0:T(8,128)(2,1)} custom-call(bf16[16,3,16,1024]{3,2,1,0:T(8,128)(2,1)} %get-tuple-element.46.a_ref, bf16[16,3,16,1024]{3,2,1,0:T(8,128)(2,1)} %copy-done.3), custom_call_target="tpu_custom_call" | custom-call | flops 786432 | bytes 4718592 | tf_op jit(solution)/shard_map/add/pallas_call | solution.py:296
  81.0 7.1 %all-to-all-start.1 = ((bf16[16,3,16,1024]{3,2,1,0:T(8,128)(2,1)}), bf16[16,3,16,1024]{3,2,1,0:T(8,128)(2,1)S(1)}, u32[]{:S(2)}, u32[]{:S(2)}) async-start(bf16[16,3,16,1024]{3,2,1,0:T(8,128)(2,1)} %add.6), calls=%async_computation.1 | async-start | bytes 3145728 | tf_op jit(solution)/shard_map/all_to_all | solution.py:394
  88.2 2.9 %add.7 = bf16[16,3,16,1024]{3,2,1,0:T(8,128)(2,1)} custom-call(bf16[16,3,16,1024]{3,2,1,0:T(8,128)(2,1)} %get-tuple-element.50.a_ref, bf16[16,3,16,1024]{3,2,1,0:T(8,128)(2,1)} %copy-done.2), custom_call_target="tpu_custom_call" | custom-call | flops 786432 | bytes 4718592 | tf_op jit(solution)/shard_map/add/pallas_call | solution.py:296
  91.1 19.3 %all-to-all-done.1.refs_0_ = bf16[16,3,16,1024]{3,2,1,0:T(8,128)(2,1)S(1)} async-done(((bf16[16,3,16,1024]{3,2,1,0:T(8,128)(2,1)}), bf16[16,3,16,1024]{3,2,1,0:T(8,128)(2,1)S(1)}, u32[]{:S(2)}, u32[]{:S(2)}) %all-to-all-start.1) | async-done | bytes 1572896 | tf_op jit(solution)/shard_map/all_to_all | solution.py:394
  110.4 4.1 %all-to-all-start.2 = ((bf16[16,3,16,1024]{3,2,1,0:T(8,128)(2,1)}), bf16[16,3,16,1024]{3,2,1,0:T(8,128)(2,1)S(1)}, u32[]{:S(2)}, u32[]{:S(2)}) async-start(bf16[16,3,16,1024]{3,2,1,0:T(8,128)(2,1)} %add.7), calls=%async_computation.2 | async-start | bytes 3145728 | tf_op jit(solution)/shard_map/all_to_all | solution.py:394
  114.5 2.4 %collective-permute-start.2 = (bf16[128,1024]{1,0:T(8,128)(2,1)}, bf16[128,1024]{1,0:T(8,128)(2,1)S(1)}, u32[]{:S(2)}, u32[]{:S(2)}) collective-permute-start(bf16[128,1024]{1,0:T(8,128)(2,1)} %get-tuple-element.52), channel_id=1, source_target_pairs={{0,16},{16,32},{32,48},{48,64},{64,80},{80,96},{96,112},{112,0},{1... | collective-permute-start | bytes 786440 | tf_op jit(solution)/shard_map/ppermute | solution.py:398
  116.9 1.8 collective-permute-start.3
  118.7 1.5 collective-permute-start.4
  120.2 2.5 %collective-permute-done.2.rest_1_ = bf16[128,1024]{1,0:T(8,128)(2,1)S(1)} collective-permute-done((bf16[128,1024]{1,0:T(8,128)(2,1)}, bf16[128,1024]{1,0:T(8,128)(2,1)S(1)}, u32[]{:S(2)}, u32[]{:S(2)}) %collective-permute-start.2) | collective-permute-done | bytes 262176 | tf_op jit(solution)/shard_map/ppermute | solution.py:398
  122.7 8.8 %collective-permute-done.3.rest_2_ = bf16[128,1024]{1,0:T(8,128)(2,1)S(1)} collective-permute-done((bf16[128,1024]{1,0:T(8,128)(2,1)}, bf16[128,1024]{1,0:T(8,128)(2,1)S(1)}, u32[]{:S(2)}, u32[]{:S(2)}) %collective-permute-start.3) | collective-permute-done | bytes 262176 | tf_op jit(solution)/shard_map/ppermute | solution.py:398
  131.6 0.7 copy-done.8
  132.3 0.3 collective-permute-done.4.rest_3_
  132.5 2.1 all-to-all-done.2.refs_1_
  134.7 0.7 sum_parts.1.a_ref
  135.4 0.2 collective-permute-start.5
  135.5 3.3 %collective-permute-start.6 = (bf16[2,3,16,1024]{3,2,1,0:T(8,128)(2,1)S(1)}, bf16[2,3,16,1024]{3,2,1,0:T(8,128)(2,1)S(1)}, u32[]{:S(2)}, u32[]{:S(2)}) collective-permute-start(bf16[2,3,16,1024]{3,2,1,0:T(8,128)(2,1)S(1)} %sum_parts.1.a_ref), channel_id=1, source_target_pairs={{0,64},{16,80},{32,96},{48,112},{64,0},{80,16},{96,32},{112,48},{1... | collective-permute-start | bytes 589832 | tf_op jit(solution)/shard_map/ppermute | solution.py:408
  138.8 2.0 collective-permute-start.7
  140.8 0.4 collective-permute-done.5.b_ref
  141.2 2.7 %collective-permute-done.6.c_ref = bf16[2,3,16,1024]{3,2,1,0:T(8,128)(2,1)S(1)} collective-permute-done((bf16[2,3,16,1024]{3,2,1,0:T(8,128)(2,1)S(1)}, bf16[2,3,16,1024]{3,2,1,0:T(8,128)(2,1)S(1)}, u32[]{:S(2)}, u32[]{:S(2)}) %collective-permute-start.6) | collective-permute-done | bytes 196640 | tf_op jit(solution)/shard_map/ppermute | solution.py:408
  143.9 0.7 copy-done.5
  144.6 0.7 copy-done.6
  145.2 2.7 %spread.3 = bf16[16,3,16,1024]{3,2,1,0:T(8,128)(2,1)} custom-call(bf16[2,3,16,1024]{3,2,1,0:T(8,128)(2,1)} %copy-done, bf16[2,3,16,1024]{3,2,1,0:T(8,128)(2,1)} %copy-done.4, bf16[2,3,16,1024]{3,2,1,0:T(8,128)(2,1)} %copy-done.5, bf16[2,3,16,1024]{3,2,1,0:T(8,128)(2,1)} %copy-done.6), custom_call_target="tpu_custom_call" | custom-call | flops 393216 | bytes 1572864 | tf_op jit(solution)/shard_map/spread/pallas_call | solution.py:336
  147.9 6.6 %all-to-all-start.3 = ((bf16[16,3,16,1024]{3,2,1,0:T(8,128)(2,1)}), bf16[16,3,16,1024]{3,2,1,0:T(8,128)(2,1)S(1)}, u32[]{:S(2)}, u32[]{:S(2)}) async-start(bf16[16,3,16,1024]{3,2,1,0:T(8,128)(2,1)} %spread.3), calls=%async_computation.3 | async-start | bytes 3145728 | tf_op jit(solution)/shard_map/all_to_all | solution.py:394
  154.6 2.8 %spread.2 = bf16[16,3,16,1024]{3,2,1,0:T(8,128)(2,1)} custom-call(bf16[2,3,16,1024]{3,2,1,0:T(8,128)(2,1)} %copy-done, bf16[2,3,16,1024]{3,2,1,0:T(8,128)(2,1)} %copy-done.4, bf16[2,3,16,1024]{3,2,1,0:T(8,128)(2,1)} %copy-done.5, bf16[2,3,16,1024]{3,2,1,0:T(8,128)(2,1)} %copy-done.6), custom_call_target="tpu_custom_call" | custom-call | flops 393216 | bytes 1572864 | tf_op jit(solution)/shard_map/spread/pallas_call | solution.py:336
  157.3 16.2 %all-to-all-done.3.rows_ref = bf16[16,3,16,1024]{3,2,1,0:T(8,128)(2,1)S(1)} async-done(((bf16[16,3,16,1024]{3,2,1,0:T(8,128)(2,1)}), bf16[16,3,16,1024]{3,2,1,0:T(8,128)(2,1)S(1)}, u32[]{:S(2)}, u32[]{:S(2)}) %all-to-all-start.3) | async-done | bytes 1572896 | tf_op jit(solution)/shard_map/all_to_all | solution.py:394
  173.5 5.3 %collective-permute-start.12 = (bf16[16,3,16,1024]{3,2,1,0:T(8,128)(2,1)S(1)}, bf16[16,3,16,1024]{3,2,1,0:T(8,128)(2,1)}, u32[]{:S(2)}, u32[]{:S(2)}) collective-permute-start(bf16[16,3,16,1024]{3,2,1,0:T(8,128)(2,1)S(1)} %all-to-all-done.3.rows_ref), channel_id=1, source_target_pairs={{0,16},{16,0},{32,48},{48,32},{64,80},{80,64},{96,112},{112,96},{1... | collective-permute-start | bytes 4718600 | tf_op jit(solution)/shard_map/ppermute | solution.py:391
  178.8 3.7 %all-to-all-start.4 = ((bf16[16,3,16,1024]{3,2,1,0:T(8,128)(2,1)}), bf16[16,3,16,1024]{3,2,1,0:T(8,128)(2,1)S(1)}, u32[]{:S(2)}, u32[]{:S(2)}) async-start(bf16[16,3,16,1024]{3,2,1,0:T(8,128)(2,1)} %spread.2), calls=%async_computation.4 | async-start | bytes 3145728 | tf_op jit(solution)/shard_map/all_to_all | solution.py:394
  182.5 2.8 %collective-permute-start.8 = (bf16[128,1024]{1,0:T(8,128)(2,1)}, bf16[128,1024]{1,0:T(8,128)(2,1)S(1)}, u32[]{:S(2)}, u32[]{:S(2)}) collective-permute-start(bf16[128,1024]{1,0:T(8,128)(2,1)} %get-tuple-element.63), channel_id=1, source_target_pairs={{0,64},{16,80},{32,96},{48,112},{64,0},{80,16},{96,32},{112,48},{1... | collective-permute-start | bytes 786440 | tf_op jit(solution)/shard_map/ppermute | solution.py:398
  185.2 3.2 %collective-permute-start.9 = (bf16[128,1024]{1,0:T(8,128)(2,1)}, bf16[128,1024]{1,0:T(8,128)(2,1)S(1)}, u32[]{:S(2)}, u32[]{:S(2)}) collective-permute-start(bf16[128,1024]{1,0:T(8,128)(2,1)} %get-tuple-element.64), channel_id=1, source_target_pairs={{0,80},{16,96},{32,112},{48,0},{64,16},{80,32},{96,48},{112,64},{1... | collective-permute-start | bytes 786440 | tf_op jit(solution)/shard_map/ppermute | solution.py:398
  188.4 1.1 collective-permute-start.11
  189.5 2.6 %collective-permute-done.8.rest_4_ = bf16[128,1024]{1,0:T(8,128)(2,1)S(1)} collective-permute-done((bf16[128,1024]{1,0:T(8,128)(2,1)}, bf16[128,1024]{1,0:T(8,128)(2,1)S(1)}, u32[]{:S(2)}, u32[]{:S(2)}) %collective-permute-start.8) | collective-permute-done | bytes 262176 | tf_op jit(solution)/shard_map/ppermute | solution.py:398
  192.2 8.8 %collective-permute-done.9.rest_5_ = bf16[128,1024]{1,0:T(8,128)(2,1)S(1)} collective-permute-done((bf16[128,1024]{1,0:T(8,128)(2,1)}, bf16[128,1024]{1,0:T(8,128)(2,1)S(1)}, u32[]{:S(2)}, u32[]{:S(2)}) %collective-permute-start.9) | collective-permute-done | bytes 262176 | tf_op jit(solution)/shard_map/ppermute | solution.py:398
  200.9 5.6 %collective-permute-done.10.rest_6_ = bf16[128,1024]{1,0:T(8,128)(2,1)S(1)} collective-permute-done((bf16[128,1024]{1,0:T(8,128)(2,1)}, bf16[128,1024]{1,0:T(8,128)(2,1)S(1)}, u32[]{:S(2)}, u32[]{:S(2)}) %collective-permute-start.10) | collective-permute-done | bytes 262176 | tf_op jit(solution)/shard_map/ppermute | solution.py:398
  206.6 0.9 collective-permute-done.11.rest_7_
  207.4 6.1 %combine.1 = bf16[4,128,1024]{2,1,0:T(8,128)(2,1)} custom-call(s32[1]{0:T(128)} %bitcast.me_ref, s32[8]{0:T(128)} %bitcast.13, bf16[512,1024]{1,0:T(8,128)(2,1)} %get-tuple-element.58.dq_hbm, bf16[1024,1024]{1,0:T(8,128)(2,1)} %wq_hbm.3, bf16[128,1024]{1,0:T(8,128)(2,1)} %get-tuple-element.59.rest_0_, bf16[128,1024]{1,0:T(8,128)(2,1)} %copy-done.7, ...), custom_call_target="tpu_custom_call" | custom-call | flops 1073741824 | bytes 6291456 | tf_op jit(solution)/shard_map/combine/pallas_call | solution.py:248
  213.5 1.2 place.4
  214.8 2.3 %place.5 = (bf16[4,16,16,1024]{3,2,1,0:T(8,128)(2,1)}, bf16[4,16,16,1024]{3,2,1,0:T(8,128)(2,1)}, bf16[4,16,16,1024]{3,2,1,0:T(8,128)(2,1)}) custom-call(s32[1]{0:T(128)S(6)} %sub.6.quarter_ref, bf16[16,3,16,1024]{3,2,1,0:T(8,128)(2,1)} %collective-permute-done.12.rows_ref, ...), custom_call_target="tpu_custom_call", output_to_operand_aliasing={{0}: (2, {}), {1}: (3, {}), {2}: (4, {})} | custom-call | bytes 3145728 | tf_op jit(solution)/shard_map/place/pallas_call | solution.py:358
  217.1 1.2 place.6
  218.4 2.2 collective-permute-done.13.rows_ref
  220.5 1.2 place.7
  (26 shorter events, 0.1 us)
Async XLA Ops:
  3.9 32.3 %all-to-all-start = ((bf16[8,128,1024]{2,1,0:T(8,128)(2,1)}), bf16[8,128,1024]{2,1,0:T(8,128)(2,1)S(1)}, u32[]{:S(2)}, u32[]{:S(2)}) async-start(bf16[8,128,1024]{2,1,0:T(8,128)(2,1)} %pick.1), calls=%async_computation | async-start | bytes 4194304 | tf_op jit(solution)/shard_map/all_to_all | solution.py:381
  36.2 1.3 copy-start.1
  73.3 3.7 %collective-permute-start = (bf16[16,3,16,1024]{3,2,1,0:T(8,128)(2,1)}, bf16[16,3,16,1024]{3,2,1,0:T(8,128)(2,1)S(1)}, u32[]{:S(2)}, u32[]{:S(2)}) collective-permute-start(bf16[16,3,16,1024]{3,2,1,0:T(8,128)(2,1)} %get-tuple-element.47), channel_id=1, source_target_pairs={{0,16},{16,0},{32,48},{48,32},{64,80},{80,64},{96,112},{112,96},{1... | collective-permute-start | bytes 4718600 | tf_op jit(solution)/shard_map/ppermute | solution.py:391
  73.4 7.7 %collective-permute-start.1 = (bf16[16,3,16,1024]{3,2,1,0:T(8,128)(2,1)}, bf16[16,3,16,1024]{3,2,1,0:T(8,128)(2,1)S(1)}, u32[]{:S(2)}, u32[]{:S(2)}) collective-permute-start(bf16[16,3,16,1024]{3,2,1,0:T(8,128)(2,1)} %get-tuple-element.48), channel_id=1, source_target_pairs={{0,16},{16,0},{32,48},{48,32},{64,80},{80,64},{96,112},{112,96},{1... | collective-permute-start | bytes 4718600 | tf_op jit(solution)/shard_map/ppermute | solution.py:391
  77.0 1.1 copy-start.3
  81.0 7.1 %copy-start.2 = (bf16[16,3,16,1024]{3,2,1,0:T(8,128)(2,1)}, bf16[16,3,16,1024]{3,2,1,0:T(8,128)(2,1)S(1)}, u32[]{:S(2)}) copy-start(bf16[16,3,16,1024]{3,2,1,0:T(8,128)(2,1)S(1)} %collective-permute-done.1.b_ref) | copy-start | bytes 4718596
  81.0 29.3 %all-to-all-start.1 = ((bf16[16,3,16,1024]{3,2,1,0:T(8,128)(2,1)}), bf16[16,3,16,1024]{3,2,1,0:T(8,128)(2,1)S(1)}, u32[]{:S(2)}, u32[]{:S(2)}) async-start(bf16[16,3,16,1024]{3,2,1,0:T(8,128)(2,1)} %add.6), calls=%async_computation.1 | async-start | bytes 3145728 | tf_op jit(solution)/shard_map/all_to_all | solution.py:394
  110.4 24.3 %all-to-all-start.2 = ((bf16[16,3,16,1024]{3,2,1,0:T(8,128)(2,1)}), bf16[16,3,16,1024]{3,2,1,0:T(8,128)(2,1)S(1)}, u32[]{:S(2)}, u32[]{:S(2)}) async-start(bf16[16,3,16,1024]{3,2,1,0:T(8,128)(2,1)} %add.7), calls=%async_computation.2 | async-start | bytes 3145728 | tf_op jit(solution)/shard_map/all_to_all | solution.py:394
  114.5 8.2 %collective-permute-start.2 = (bf16[128,1024]{1,0:T(8,128)(2,1)}, bf16[128,1024]{1,0:T(8,128)(2,1)S(1)}, u32[]{:S(2)}, u32[]{:S(2)}) collective-permute-start(bf16[128,1024]{1,0:T(8,128)(2,1)} %get-tuple-element.52), channel_id=1, source_target_pairs={{0,16},{16,32},{32,48},{48,64},{64,80},{80,96},{96,112},{112,0},{1... | collective-permute-start | bytes 786440 | tf_op jit(solution)/shard_map/ppermute | solution.py:398
  116.9 14.7 %collective-permute-start.3 = (bf16[128,1024]{1,0:T(8,128)(2,1)}, bf16[128,1024]{1,0:T(8,128)(2,1)S(1)}, u32[]{:S(2)}, u32[]{:S(2)}) collective-permute-start(bf16[128,1024]{1,0:T(8,128)(2,1)} %get-tuple-element.53), channel_id=1, source_target_pairs={{0,32},{16,48},{32,64},{48,80},{64,96},{80,112},{96,0},{112,16},{1... | collective-permute-start | bytes 786440 | tf_op jit(solution)/shard_map/ppermute | solution.py:398
  118.7 13.8 %collective-permute-start.4 = (bf16[128,1024]{1,0:T(8,128)(2,1)}, bf16[128,1024]{1,0:T(8,128)(2,1)}, u32[]{:S(2)}, u32[]{:S(2)}) collective-permute-start(bf16[128,1024]{1,0:T(8,128)(2,1)} %get-tuple-element.54), channel_id=1, source_target_pairs={{0,48},{16,64},{32,80},{48,96},{64,112},{80,0},{96,16},{112,32},{1... | collective-permute-start | bytes 786440 | tf_op jit(solution)/shard_map/ppermute | solution.py:398
  122.7 25.2 %copy-start.7 = (bf16[128,1024]{1,0:T(8,128)(2,1)}, bf16[128,1024]{1,0:T(8,128)(2,1)S(1)}, u32[]{:S(2)}) copy-start(bf16[128,1024]{1,0:T(8,128)(2,1)S(1)} %collective-permute-done.2.rest_1_) | copy-start | bytes 786436
  131.6 0.7 copy-start.8
  135.4 8.5 %copy-start = (bf16[2,3,16,1024]{3,2,1,0:T(8,128)(2,1)}, bf16[2,3,16,1024]{3,2,1,0:T(8,128)(2,1)S(1)}, u32[]{:S(2)}) copy-start(bf16[2,3,16,1024]{3,2,1,0:T(8,128)(2,1)S(1)} %sum_parts.1.a_ref) | copy-start | bytes 589828
  135.4 5.8 %collective-permute-start.5 = (bf16[2,3,16,1024]{3,2,1,0:T(8,128)(2,1)S(1)}, bf16[2,3,16,1024]{3,2,1,0:T(8,128)(2,1)S(1)}, u32[]{:S(2)}, u32[]{:S(2)}) collective-permute-start(bf16[2,3,16,1024]{3,2,1,0:T(8,128)(2,1)S(1)} %sum_parts.1.a_ref), channel_id=1, source_target_pairs={{0,32},{16,48},{32,64},{48,80},{64,96},{80,112},{96,0},{112,16},{1... | collective-permute-start | bytes 589832 | tf_op jit(solution)/shard_map/ppermute | solution.py:408
  135.5 8.3 %collective-permute-start.6 = (bf16[2,3,16,1024]{3,2,1,0:T(8,128)(2,1)S(1)}, bf16[2,3,16,1024]{3,2,1,0:T(8,128)(2,1)S(1)}, u32[]{:S(2)}, u32[]{:S(2)}) collective-permute-start(bf16[2,3,16,1024]{3,2,1,0:T(8,128)(2,1)S(1)} %sum_parts.1.a_ref), channel_id=1, source_target_pairs={{0,64},{16,80},{32,96},{48,112},{64,0},{80,16},{96,32},{112,48},{1... | collective-permute-start | bytes 589832 | tf_op jit(solution)/shard_map/ppermute | solution.py:408
  138.8 5.1 %collective-permute-start.7 = (bf16[2,3,16,1024]{3,2,1,0:T(8,128)(2,1)S(1)}, bf16[2,3,16,1024]{3,2,1,0:T(8,128)(2,1)S(1)}, u32[]{:S(2)}, u32[]{:S(2)}) collective-permute-start(bf16[2,3,16,1024]{3,2,1,0:T(8,128)(2,1)S(1)} %sum_parts.1.a_ref), channel_id=1, source_target_pairs={{0,96},{16,112},{32,0},{48,16},{64,32},{80,48},{96,64},{112,80},{1... | collective-permute-start | bytes 589832 | tf_op jit(solution)/shard_map/ppermute | solution.py:408
  141.2 2.7 %copy-start.4 = (bf16[2,3,16,1024]{3,2,1,0:T(8,128)(2,1)}, bf16[2,3,16,1024]{3,2,1,0:T(8,128)(2,1)S(1)}, u32[]{:S(2)}) copy-start(bf16[2,3,16,1024]{3,2,1,0:T(8,128)(2,1)S(1)} %collective-permute-done.5.b_ref) | copy-start | bytes 589828
  143.9 0.7 copy-start.5
  144.6 0.7 copy-start.6
  147.9 25.6 %all-to-all-start.3 = ((bf16[16,3,16,1024]{3,2,1,0:T(8,128)(2,1)}), bf16[16,3,16,1024]{3,2,1,0:T(8,128)(2,1)S(1)}, u32[]{:S(2)}, u32[]{:S(2)}) async-start(bf16[16,3,16,1024]{3,2,1,0:T(8,128)(2,1)} %spread.3), calls=%async_computation.3 | async-start | bytes 3145728 | tf_op jit(solution)/shard_map/all_to_all | solution.py:394
  173.5 41.3 %collective-permute-start.12 = (bf16[16,3,16,1024]{3,2,1,0:T(8,128)(2,1)S(1)}, bf16[16,3,16,1024]{3,2,1,0:T(8,128)(2,1)}, u32[]{:S(2)}, u32[]{:S(2)}) collective-permute-start(bf16[16,3,16,1024]{3,2,1,0:T(8,128)(2,1)S(1)} %all-to-all-done.3.rows_ref), channel_id=1, source_target_pairs={{0,16},{16,0},{32,48},{48,32},{64,80},{80,64},{96,112},{112,96},{1... | collective-permute-start | bytes 4718600 | tf_op jit(solution)/shard_map/ppermute | solution.py:391
  178.8 38.3 %all-to-all-start.4 = ((bf16[16,3,16,1024]{3,2,1,0:T(8,128)(2,1)}), bf16[16,3,16,1024]{3,2,1,0:T(8,128)(2,1)S(1)}, u32[]{:S(2)}, u32[]{:S(2)}) async-start(bf16[16,3,16,1024]{3,2,1,0:T(8,128)(2,1)} %spread.2), calls=%async_computation.4 | async-start | bytes 3145728 | tf_op jit(solution)/shard_map/all_to_all | solution.py:394
  182.5 9.7 %collective-permute-start.8 = (bf16[128,1024]{1,0:T(8,128)(2,1)}, bf16[128,1024]{1,0:T(8,128)(2,1)S(1)}, u32[]{:S(2)}, u32[]{:S(2)}) collective-permute-start(bf16[128,1024]{1,0:T(8,128)(2,1)} %get-tuple-element.63), channel_id=1, source_target_pairs={{0,64},{16,80},{32,96},{48,112},{64,0},{80,16},{96,32},{112,48},{1... | collective-permute-start | bytes 786440 | tf_op jit(solution)/shard_map/ppermute | solution.py:398
  185.2 15.7 %collective-permute-start.9 = (bf16[128,1024]{1,0:T(8,128)(2,1)}, bf16[128,1024]{1,0:T(8,128)(2,1)S(1)}, u32[]{:S(2)}, u32[]{:S(2)}) collective-permute-start(bf16[128,1024]{1,0:T(8,128)(2,1)} %get-tuple-element.64), channel_id=1, source_target_pairs={{0,80},{16,96},{32,112},{48,0},{64,16},{80,32},{96,48},{112,64},{1... | collective-permute-start | bytes 786440 | tf_op jit(solution)/shard_map/ppermute | solution.py:398
  188.4 18.1 %collective-permute-start.10 = (bf16[128,1024]{1,0:T(8,128)(2,1)}, bf16[128,1024]{1,0:T(8,128)(2,1)S(1)}, u32[]{:S(2)}, u32[]{:S(2)}) collective-permute-start(bf16[128,1024]{1,0:T(8,128)(2,1)} %get-tuple-element.65), channel_id=1, source_target_pairs={{0,96},{16,112},{32,0},{48,16},{64,32},{80,48},{96,64},{112,80},{1... | collective-permute-start | bytes 786440 | tf_op jit(solution)/shard_map/ppermute | solution.py:398
  188.4 19.0 %collective-permute-start.11 = (bf16[128,1024]{1,0:T(8,128)(2,1)}, bf16[128,1024]{1,0:T(8,128)(2,1)}, u32[]{:S(2)}, u32[]{:S(2)}) collective-permute-start(bf16[128,1024]{1,0:T(8,128)(2,1)} %get-tuple-element.66), channel_id=1, source_target_pairs={{0,112},{16,0},{32,16},{48,32},{64,48},{80,64},{96,80},{112,96},{1... | collective-permute-start | bytes 786440 | tf_op jit(solution)/shard_map/ppermute | solution.py:398
  192.2 15.3 %copy-start.9 = (bf16[128,1024]{1,0:T(8,128)(2,1)}, bf16[128,1024]{1,0:T(8,128)(2,1)S(1)}, u32[]{:S(2)}) copy-start(bf16[128,1024]{1,0:T(8,128)(2,1)S(1)} %collective-permute-done.8.rest_4_) | copy-start | bytes 786436
  200.9 6.5 %copy-start.10 = (bf16[128,1024]{1,0:T(8,128)(2,1)}, bf16[128,1024]{1,0:T(8,128)(2,1)S(1)}, u32[]{:S(2)}) copy-start(bf16[128,1024]{1,0:T(8,128)(2,1)S(1)} %collective-permute-done.9.rest_5_) | copy-start | bytes 786436
  206.6 0.9 copy-start.11
  217.1 3.4 %collective-permute-start.13 = (bf16[16,3,16,1024]{3,2,1,0:T(8,128)(2,1)S(1)}, bf16[16,3,16,1024]{3,2,1,0:T(8,128)(2,1)S(1)}, u32[]{:S(2)}, u32[]{:S(2)}) collective-permute-start(bf16[16,3,16,1024]{3,2,1,0:T(8,128)(2,1)S(1)} %all-to-all-done.4.rows_ref), channel_id=1, source_target_pairs={{0,16},{16,0},{32,48},{48,32},{64,80},{80,64},{96,112},{112,96},{1... | collective-permute-start | bytes 4718600 | tf_op jit(solution)/shard_map/ppermute | solution.py:391

commit v9 on v7

--- a/solution.py
+++ b/solution.py
@@ -218,45 +218,74 @@
     )(me, src, slot, valid, x, r, c, wq, wk, wv)
 
 
-def combine_kernel(me_ref, listed_ref, dq_hbm, wq_hbm, *rest):
-    n_slot = len(rest) - 6
-    parts, (out_ref, acc, dq_ref, wq_ref, back, sem) = rest[:n_slot], rest[n_slot:]
-    length = back.shape[1]
-    me = me_ref[0]
-    block = 256
-    copies = [pltpu.make_async_copy(a, b, sem.at[i]) for i, (a, b) in enumerate(
-        [(dq_hbm, dq_ref), (wq_hbm, wq_ref)] + [(p, back.at[s]) for s, p in enumerate(parts)])]
+def load(pairs, sem):
+    copies = [pltpu.make_async_copy(a, b, sem.at[i]) for i, (a, b) in enumerate(pairs)]
     for c in copies:
         c.start()
-    for c in copies:
-        c.wait()
-    for n in range(0, acc.shape[2], block):
+    return copies
+
+
+def add_parts(me_ref, listed_ref, acc, back, shifts, n_slot):
+    for i, s in enumerate(shifts):
+        at = listed_ref[lax.rem(me_ref[0] + n_slot - s, n_slot)]
+        acc[at] += back[i][...].astype(F32)
+
+
+def combine_kernel(me_ref, listed_ref, dq_hbm, wq_hbm, *rest, shifts, n_slot):
+    parts, (out_ref, dq_ref, wq_ref, back, sem) = rest[:len(shifts)], rest[len(shifts):]
+    length = back.shape[1]
+    block = 256
+    copies = load([(dq_hbm, dq_ref), (wq_hbm, wq_ref)] + [(p, back.at[i]) for i, p in enumerate(parts)], sem)
+    for c in copies[:2]:
+        c.wait()
+    for n in range(0, out_ref.shape[2], block):
         cols = slice(n, n + block)
-        acc[:, :, cols] = mm_nt(dq_ref[...], wq_ref[cols, :]).reshape(acc.shape[0], length, block)
-    for s in range(n_slot):
-        at = listed_ref[lax.rem(me + n_slot - s, n_slot)]
-        acc[at] += back[s].astype(F32)
+        out_ref[:, :, cols] = mm_nt(dq_ref[...], wq_ref[cols, :]).reshape(out_ref.shape[0], length, block)
+    for c in copies[2:]:
+        c.wait()
+    add_parts(me_ref, listed_ref, out_ref, back, shifts, n_slot)
+
+
+def finish_kernel(me_ref, listed_ref, acc_ref, *rest, shifts, n_slot):
+    parts, (out_ref, acc) = rest[:len(shifts)], rest[len(shifts):]
+    acc[...] = acc_ref[...]
+    add_parts(me_ref, listed_ref, acc, parts, shifts, n_slot)
     out_ref[...] = acc[...].astype(BF)
 
 
-def combine(me, listed, dq, wq, parts):
+def combine(me, listed, dq, wq, parts, shifts):
     length, width = parts[0].shape
     n_src = dq.shape[0] // length
     smem = pl.BlockSpec(memory_space=pltpu.SMEM)
-    hbm = pl.BlockSpec(memory_space=pltpu.HBM)
-    return pl.pallas_call(
-        combine_kernel,
+    hbm = pl.BlockSpec(memory_space=pl.ANY)
+    return pl.pallas_call(
+        functools.partial(combine_kernel, shifts=shifts, n_slot=listed.shape[0]),
         in_specs=[smem, smem] + [hbm] * (2 + len(parts)),
         out_specs=pl.BlockSpec(memory_space=pltpu.VMEM),
-        out_shape=jax.ShapeDtypeStruct((n_src, length, width), BF),
+        out_shape=jax.ShapeDtypeStruct((n_src, length, width), F32),
         scratch_shapes=[
-            pltpu.VMEM((n_src, length, width), F32), pltpu.VMEM(dq.shape, BF), pltpu.VMEM(wq.shape, BF),
+            pltpu.VMEM(dq.shape, BF), pltpu.VMEM(wq.shape, BF),
             pltpu.VMEM((len(parts), length, width), BF), pltpu.SemaphoreType.DMA((2 + len(parts),)),
         ],
-        compiler_params=pltpu.CompilerParams(vmem_limit_bytes=60 * 2**20),
+        compiler_params=pltpu.CompilerParams(vmem_limit_bytes=24 * 2**20),
         cost_estimate=pl.CostEstimate(flops=2 * dq.size * width, bytes_accessed=6 * 2**20, transcendentals=0),
         name="combine",
     )(me, listed, dq, wq, *parts)
+
+
+def finish(me, listed, acc, parts, shifts):
+    smem = pl.BlockSpec(memory_space=pltpu.SMEM)
+    vmem = pl.BlockSpec(memory_space=pltpu.VMEM)
+    return pl.pallas_call(
+        functools.partial(finish_kernel, shifts=shifts, n_slot=listed.shape[0]),
+        in_specs=[smem, smem] + [vmem] * (1 + len(parts)),
+        out_specs=vmem,
+        out_shape=jax.ShapeDtypeStruct(acc.shape, BF),
+        scratch_shapes=[pltpu.VMEM(acc.shape, F32)],
+        compiler_params=pltpu.CompilerParams(vmem_limit_bytes=16 * 2**20),
+        cost_estimate=pl.CostEstimate(flops=acc.size, bytes_accessed=8 * acc.size, transcendentals=0),
+        name="finish",
+    )(me, listed, acc, *parts)
 
 
 def pick_kernel(listed_ref, x_hbm, out_hbm, x_ref, sem):
@@ -380,13 +409,17 @@
         )
 
     flat = (-1,) + keep.shape[3:]
-    pieces = over_chips(add(keep.reshape(flat), other.reshape(flat)))
-    pieces, *back[1:4] = lax.optimization_barrier((pieces, *back[1:4]))
+    chip = add(keep.reshape(flat), other.reshape(flat))
+    chip, *back[1:4] = lax.optimization_barrier((chip, *back[1:4]))
     factor = 1.0 / (sent_dev * n_lang * n_pair * length) ** 0.5
-    near = over_chips(spread(pieces, factor)).reshape(keep.shape)
-    grad_sentences = combine(where, listed, dq, w_query, back)
-    near, grad_sentences = lax.optimization_barrier((near, grad_sentences))
+    copies = spread(over_chips(chip), factor)
+    copies, *back[4:6] = lax.optimization_barrier((copies, *back[4:6]))
+    near = over_chips(copies).reshape(keep.shape)
+    acc = combine(where, listed, dq, w_query, back[:6], tuple(range(6)))
+    near, acc = lax.optimization_barrier((near, acc))
     far = lax.ppermute(near, "lang", other_core)
+    far, *back[6:] = lax.optimization_barrier((far, *back[6:]))
+    grad_sentences = finish(where, listed, acc, back[6:], tuple(range(6, n_lang)))
     core = lax.rem(where, 2)
     grads = place(1 - core, far, place(core, near))
     grads = tuple(g.reshape(width, width) for g in grads)

time: 229 us -> 218 us (0.952)
  waiting for transfers between devices: 132 us -> 113 us
  local copies, waits for them, and re-layouts: 7.17 us -> 15.6 us
    ppermute x7, waiting for transfers between devices: 96.7 us -> 17.4 us  [body(): lax.ppermute(dx[s], 'lang', [(i, (i + s) % n_lang) for i in range(n_lang)])]
    all_to_all x2, waiting for transfers between devices: 0.01 us -> 64.5 us  [over_chips(): lax.all_to_all(a, ('lang', 'pair'), split_axis=0, concat_axis=0, axis_ind...]
    unnamed x18 -> x32, local copies, waits for them, and re-layouts: 7.17 us -> 15.6 us
    ppermute x7, starting transfers between devices: 11.2 us -> 6.8 us  [body(): lax.ppermute(dx[s], 'lang', [(i, (i + s) % n_lang) for i in range(n_lang)])]
    ppermute x1, waiting for transfers between devices: 3.31 us -> 0.01 us  [body(): far = lax.ppermute(near, 'lang', other_core)]
    ppermute x1, starting transfers between devices: 0.95 us -> 3.25 us  [body(): other = lax.ppermute(send, 'lang', other_core)]
    pallas_call x1 -> x2, Pallas kernels: 6.09 us -> 4.46 us  [the longest x1 2.61 us: combine(): pl.pallas_call(functools.partial(combine_kernel, shifts=shifts, n_slot=li...]
  transfers between devices with their start and end apart: 12 -> 12, of which waited for: 9 -> 9; matrix products, arithmetic and copies ran while one was open for 0% -> 0% of each run, Pallas kernels for 4% -> 3%
where the time goes in v9:
time: 218 us; the launch traced here: 219 us
  waiting for transfers between devices  113 us (52%)
  Pallas kernels  47.7 us (22%)
  starting transfers between devices  41.3 us (19%)
  local copies, waits for them, and re-layouts  15.6 us (7%)
    all_to_all x2, waiting for transfers between devices, over_chips(): lax.all_to_all(a, ('lang', 'pair'), split_axis=0, concat_axis=0, axis_ind...  64.5 us
    pallas_call x1, Pallas kernels, attend(): pl.pallas_call(functools.partial(attend_kernel, n_src=n_src, n_slot=n_slo...  33.4 us
    all_to_all x1, waiting for transfers between devices, body(): lax.all_to_all(outgoing, 'lang', split_axis=0, concat_axis=0, tiled=True)  26.3 us
    all_to_all x2, starting transfers between devices, over_chips(): lax.all_to_all(a, ('lang', 'pair'), split_axis=0, concat_axis=0, axis_ind...  23.7 us
    ppermute x7, waiting for transfers between devices, body(): lax.ppermute(dx[s], 'lang', [(i, (i + s) % n_lang) for i in range(n_lang)])  17.4 us
    unnamed x32, local copies, waits for them, and re-layouts  15.6 us
    ppermute x7, starting transfers between devices, body(): lax.ppermute(dx[s], 'lang', [(i, (i + s) % n_lang) for i in range(n_lang)])  6.8 us
    all_to_all x1, starting transfers between devices, body(): lax.all_to_all(outgoing, 'lang', split_axis=0, concat_axis=0, tiled=True)  5.98 us
  transfers between devices with their start and end apart: 12, of which 9 were waited for; matrix products, arithmetic and copies ran while one was open for 0% of the time, Pallas kernels for 3%

profile of v9, /device:TPU:1, one launch (start us, length us, event | category | flops | bytes accessed | tf_op | source)
XLA Modules:
  0.0 218.6 jit_solution(6687652127498723686)
XLA Ops:
  0.6 3.3 %pick.1 = bf16[8,128,1024]{2,1,0:T(8,128)(2,1)} custom-call(s32[8]{0:T(128)} %bitcast.15, bf16[4,128,1024]{2,1,0:T(8,128)(2,1)} %x_hbm.1), custom_call_target="tpu_custom_call" | custom-call | tf_op jit(solution)/shard_map/pick/pallas_call | solution.py:306
  3.9 6.0 %all-to-all-start = ((bf16[8,128,1024]{2,1,0:T(8,128)(2,1)}), bf16[8,128,1024]{2,1,0:T(8,128)(2,1)S(1)}, u32[]{:S(2)}, u32[]{:S(2)}) async-start(bf16[8,128,1024]{2,1,0:T(8,128)(2,1)} %pick.1), calls=%async_computation | async-start | bytes 4194304 | tf_op jit(solution)/shard_map/all_to_all | solution.py:392
  9.9 26.3 %all-to-all-done.r_hbm = bf16[8,128,1024]{2,1,0:T(8,128)(2,1)S(1)} async-done(((bf16[8,128,1024]{2,1,0:T(8,128)(2,1)}), bf16[8,128,1024]{2,1,0:T(8,128)(2,1)S(1)}, u32[]{:S(2)}, u32[]{:S(2)}) %all-to-all-start) | async-done | bytes 2097184 | tf_op jit(solution)/shard_map/all_to_all | solution.py:392
  36.2 1.3 copy-done.15
  37.5 33.4 %attend.1 = (bf16[512,1024]{1,0:T(8,128)(2,1)}, bf16[512,1024]{1,0:T(8,128)(2,1)}, bf16[2,2,16,3,16,512]{5,4,3,2,1,0:T(8,128)(2,1)}, bf16[2,2,16,3,16,512]{5,4,3...) custom-call(s32[1]{0:T(128)} %bitcast.me_ref, ...), custom_call_target="tpu_custom_call" | custom-call | flops 34896609280 | bytes 20971520 | tf_op jit(solution)/shard_map/attend/pallas_call | solution.py:193
  71.0 3.2 %collective-permute-start = (bf16[2,2,16,3,16,512]{5,4,3,2,1,0:T(8,128)(2,1)}, bf16[2,2,16,3,16,512]{5,4,3,2,1,0:T(8,128)(2,1)S(1)}, u32[]{:S(2)}, u32[]{:S(2)}) collective-permute-start(bf16[2,2,16,3,16,512]{5,4,3,2,1,0:T(8,128)(2,1)} %get-tuple-element.37), channel_id=1, source_target_pairs={{0,16},{16,0},{32,48},{48,32},{64,80},{80,64},{96,112},{112,96},{1... | collective-permute-start | bytes 9437192 | tf_op jit(solution)/shard_map/ppermute | solution.py:400
  74.2 0.0 collective-permute-start.1
  74.2 0.0 collective-permute-start.2
  74.2 0.5 collective-permute-start.3
  74.7 5.0 %collective-permute-done = bf16[2,2,16,3,16,512]{5,4,3,2,1,0:T(8,128)(2,1)S(1)} collective-permute-done((bf16[2,2,16,3,16,512]{5,4,3,2,1,0:T(8,128)(2,1)}, bf16[2,2,16,3,16,512]{5,4,3,2,1,0:T(8,128)(2,1)S(1)}, u32[]{:S(2)}, u32[]{:S(2)}) %collective-permute-start) | collective-permute-done | bytes 3145760 | tf_op jit(solution)/shard_map/ppermute | solution.py:400
  79.7 1.9 copy-done.4
  81.6 0.8 add.1
  82.4 1.6 copy-done.1
  84.0 0.0 collective-permute-done.1.rest_1_
  84.0 0.7 copy-done.8
  84.7 6.2 %collective-permute-done.2.rest_2_ = bf16[128,1024]{1,0:T(8,128)(2,1)S(1)} collective-permute-done((bf16[128,1024]{1,0:T(8,128)(2,1)}, bf16[128,1024]{1,0:T(8,128)(2,1)S(1)}, u32[]{:S(2)}, u32[]{:S(2)}) %collective-permute-start.2) | collective-permute-done | bytes 262176 | tf_op jit(solution)/shard_map/ppermute | solution.py:403
  90.9 0.7 copy-done.10
  91.6 0.4 collective-permute-done.3.rest_3_
  92.0 0.7 copy-done.12
  92.7 10.4 %all-to-all-start.1 = ((bf16[64,3,16,512]{3,2,1,0:T(8,128)(2,1)}), bf16[64,3,16,512]{3,2,1,0:T(8,128)(2,1)S(1)}, u32[]{:S(2)}, u32[]{:S(2)}) async-start(bf16[64,3,16,512]{3,2,1,0:T(8,128)(2,1)} %copy-done.1), calls=%async_computation.1 | async-start | bytes 6291456 | tf_op jit(solution)/shard_map/all_to_all | solution.py:407
  103.1 2.7 %collective-permute-start.4 = (bf16[128,1024]{1,0:T(8,128)(2,1)}, bf16[128,1024]{1,0:T(8,128)(2,1)}, u32[]{:S(2)}, u32[]{:S(2)}) collective-permute-start(bf16[128,1024]{1,0:T(8,128)(2,1)} %get-tuple-element.42), channel_id=1, source_target_pairs={{0,64},{16,80},{32,96},{48,112},{64,0},{80,16},{96,32},{112,48},{1... | collective-permute-start | bytes 786440 | tf_op jit(solution)/shard_map/ppermute | solution.py:403
  105.8 2.3 %collective-permute-start.5 = (bf16[128,1024]{1,0:T(8,128)(2,1)}, bf16[128,1024]{1,0:T(8,128)(2,1)}, u32[]{:S(2)}, u32[]{:S(2)}) collective-permute-start(bf16[128,1024]{1,0:T(8,128)(2,1)} %get-tuple-element.43), channel_id=1, source_target_pairs={{0,80},{16,96},{32,112},{48,0},{64,16},{80,32},{96,48},{112,64},{1... | collective-permute-start | bytes 786440 | tf_op jit(solution)/shard_map/ppermute | solution.py:403
  108.1 34.4 %all-to-all-done.1.parts_ref = bf16[64,3,16,512]{3,2,1,0:T(8,128)(2,1)S(1)} async-done(((bf16[64,3,16,512]{3,2,1,0:T(8,128)(2,1)}), bf16[64,3,16,512]{3,2,1,0:T(8,128)(2,1)S(1)}, u32[]{:S(2)}, u32[]{:S(2)}) %all-to-all-start.1) | async-done | bytes 3145760 | tf_op jit(solution)/shard_map/all_to_all | solution.py:407
  142.5 1.2 spread.1
  143.7 0.0 copy-start
  143.7 1.6 copy-done
  145.4 0.0 collective-permute-done.4.rest_4_
  145.4 3.4 %collective-permute-done.5.rest_5_ = bf16[128,1024]{1,0:T(8,128)(2,1)} collective-permute-done((bf16[128,1024]{1,0:T(8,128)(2,1)}, bf16[128,1024]{1,0:T(8,128)(2,1)}, u32[]{:S(2)}, u32[]{:S(2)}) %collective-permute-start.5) | collective-permute-done | bytes 262176 | tf_op jit(solution)/shard_map/ppermute | solution.py:403
  148.7 13.3 %all-to-all-start.2 = ((bf16[64,3,16,512]{3,2,1,0:T(8,128)(2,1)}), bf16[64,3,16,512]{3,2,1,0:T(8,128)(2,1)S(1)}, u32[]{:S(2)}, u32[]{:S(2)}) async-start(bf16[64,3,16,512]{3,2,1,0:T(8,128)(2,1)} %copy-done), calls=%async_computation.2 | async-start | bytes 6291456 | tf_op jit(solution)/shard_map/all_to_all | solution.py:407
  162.1 0.0 copy-start.5
  162.1 1.6 copy-done.5
  163.7 1.2 copy-done.6
  164.9 0.9 copy-done.9
  165.8 0.9 copy-done.11
  166.8 0.9 copy-done.13
  167.7 2.6 %combine.1.acc_ref = f32[4,128,1024]{2,1,0:T(8,128)S(1)} custom-call(s32[1]{0:T(128)} %bitcast.me_ref, s32[8]{0:T(128)S(1)} %bitcast.16, bf16[512,1024]{1,0:T(8,128)(2,1)S(1)} %copy-done.6, bf16[1024,1024]{1,0:T(8,128)(2,1)S(1)} %copy-done.5, bf16[128,1024]{1,0:T(8,128)(2,1)S(1)} %copy-done.7, bf16[128,1024]{1,0:T(8,128)(2,1)S(1)} %copy-done.9, ...), custom_call_target="tpu_custom_call" | custom-call | flops 1073741824 | bytes 6291456 | tf_op jit(solution)/shard_map/combine/pallas_call | solution.py:261
  170.4 1.3 copy-done.2
  171.7 30.1 %all-to-all-done.2 = bf16[64,3,16,512]{3,2,1,0:T(8,128)(2,1)S(1)} async-done(((bf16[64,3,16,512]{3,2,1,0:T(8,128)(2,1)}), bf16[64,3,16,512]{3,2,1,0:T(8,128)(2,1)S(1)}, u32[]{:S(2)}, u32[]{:S(2)}) %all-to-all-start.2) | async-done | bytes 3145760 | tf_op jit(solution)/shard_map/all_to_all | solution.py:407
  201.8 1.6 collective-permute-start.6
  203.4 1.0 collective-permute-start.7
  204.4 0.3 collective-permute-start.8
  204.7 2.3 %place.2 = (bf16[2,16,2,16,1024]{4,3,2,1,0:T(8,128)(2,1)}, bf16[2,16,2,16,1024]{4,3,2,1,0:T(8,128)(2,1)}, bf16[2,16,2,16,1024]{4,3,2,1,0:T(8,128)(2,1)}) custom-call(s32[1]{0:T(128)S(6)} %rem.18.half_ref, bf16[2,2,16,3,16,512]{5,4,3,2,1,0:T(8,128)(2,1)S(1)} %bitcast.12), custom_call_target="tpu_custom_call" | custom-call | bytes 6291456 | tf_op jit(solution)/shard_map/place/pallas_call | solution.py:369
  207.0 4.5 %collective-permute-done.7.rest_0_ = bf16[128,1024]{1,0:T(8,128)(2,1)S(1)} collective-permute-done((bf16[128,1024]{1,0:T(8,128)(2,1)}, bf16[128,1024]{1,0:T(8,128)(2,1)S(1)}, u32[]{:S(2)}, u32[]{:S(2)}) %collective-permute-start.7) | collective-permute-done | bytes 262176 | tf_op jit(solution)/shard_map/ppermute | solution.py:403
  211.6 2.9 %collective-permute-done.8.rest_1_ = bf16[128,1024]{1,0:T(8,128)(2,1)S(1)} collective-permute-done((bf16[128,1024]{1,0:T(8,128)(2,1)}, bf16[128,1024]{1,0:T(8,128)(2,1)S(1)}, u32[]{:S(2)}, u32[]{:S(2)}) %collective-permute-start.8) | collective-permute-done | bytes 262176 | tf_op jit(solution)/shard_map/ppermute | solution.py:403
  214.5 0.0 collective-permute-done.6.rows_ref
  214.5 0.0 copy-done.3
  214.5 1.9 finish.1
  216.3 2.3 %place.3 = (bf16[2,16,2,16,1024]{4,3,2,1,0:T(8,128)(2,1)}, bf16[2,16,2,16,1024]{4,3,2,1,0:T(8,128)(2,1)}, bf16[2,16,2,16,1024]{4,3,2,1,0:T(8,128)(2,1)}) custom-call(s32[1]{0:T(128)S(6)} %sub.3.half_ref, bf16[2,2,16,3,16,512]{5,4,3,2,1,0:T(8,128)(2,1)S(1)} %collective-permute-done.6.rows_ref, ...), custom_call_target="tpu_custom_call", output_to_operand_aliasing={{0}: (2, {}), {1}: (3, {}), {2}: (4, {})} | custom-call | bytes 6291456 | tf_op jit(solution)/shard_map/place/pallas_call | solution.py:369
  (16 shorter events, 0.0 us)
Async XLA Ops:
  3.9 32.3 %all-to-all-start = ((bf16[8,128,1024]{2,1,0:T(8,128)(2,1)}), bf16[8,128,1024]{2,1,0:T(8,128)(2,1)S(1)}, u32[]{:S(2)}, u32[]{:S(2)}) async-start(bf16[8,128,1024]{2,1,0:T(8,128)(2,1)} %pick.1), calls=%async_computation | async-start | bytes 4194304 | tf_op jit(solution)/shard_map/all_to_all | solution.py:392
  36.2 1.3 copy-start.15
  71.0 8.7 %collective-permute-start = (bf16[2,2,16,3,16,512]{5,4,3,2,1,0:T(8,128)(2,1)}, bf16[2,2,16,3,16,512]{5,4,3,2,1,0:T(8,128)(2,1)S(1)}, u32[]{:S(2)}, u32[]{:S(2)}) collective-permute-start(bf16[2,2,16,3,16,512]{5,4,3,2,1,0:T(8,128)(2,1)} %get-tuple-element.37), channel_id=1, source_target_pairs={{0,16},{16,0},{32,48},{48,32},{64,80},{80,64},{96,112},{112,96},{1... | collective-permute-start | bytes 9437192 | tf_op jit(solution)/shard_map/ppermute | solution.py:400
  74.2 9.8 %collective-permute-start.1 = (bf16[128,1024]{1,0:T(8,128)(2,1)}, bf16[128,1024]{1,0:T(8,128)(2,1)S(1)}, u32[]{:S(2)}, u32[]{:S(2)}) collective-permute-start(bf16[128,1024]{1,0:T(8,128)(2,1)} %get-tuple-element.38), channel_id=1, source_target_pairs={{0,16},{16,32},{32,48},{48,64},{64,80},{80,96},{96,112},{112,0},{1... | collective-permute-start | bytes 786440 | tf_op jit(solution)/shard_map/ppermute | solution.py:403
  74.2 16.7 %collective-permute-start.2 = (bf16[128,1024]{1,0:T(8,128)(2,1)}, bf16[128,1024]{1,0:T(8,128)(2,1)S(1)}, u32[]{:S(2)}, u32[]{:S(2)}) collective-permute-start(bf16[128,1024]{1,0:T(8,128)(2,1)} %get-tuple-element.39), channel_id=1, source_target_pairs={{0,32},{16,48},{32,64},{48,80},{64,96},{80,112},{96,0},{112,16},{1... | collective-permute-start | bytes 786440 | tf_op jit(solution)/shard_map/ppermute | solution.py:403
  74.2 17.8 %collective-permute-start.3 = (bf16[128,1024]{1,0:T(8,128)(2,1)}, bf16[128,1024]{1,0:T(8,128)(2,1)S(1)}, u32[]{:S(2)}, u32[]{:S(2)}) collective-permute-start(bf16[128,1024]{1,0:T(8,128)(2,1)} %get-tuple-element.40), channel_id=1, source_target_pairs={{0,48},{16,64},{32,80},{48,96},{64,112},{80,0},{96,16},{112,32},{1... | collective-permute-start | bytes 786440 | tf_op jit(solution)/shard_map/ppermute | solution.py:403
  79.7 1.9 copy-start.4
  82.4 1.6 copy-start.1
  84.0 0.7 copy-start.8
  90.9 0.7 copy-start.10
  92.0 0.7 copy-start.12
  92.7 49.8 %all-to-all-start.1 = ((bf16[64,3,16,512]{3,2,1,0:T(8,128)(2,1)}), bf16[64,3,16,512]{3,2,1,0:T(8,128)(2,1)S(1)}, u32[]{:S(2)}, u32[]{:S(2)}) async-start(bf16[64,3,16,512]{3,2,1,0:T(8,128)(2,1)} %copy-done.1), calls=%async_computation.1 | async-start | bytes 6291456 | tf_op jit(solution)/shard_map/all_to_all | solution.py:407
  103.1 42.3 %collective-permute-start.4 = (bf16[128,1024]{1,0:T(8,128)(2,1)}, bf16[128,1024]{1,0:T(8,128)(2,1)}, u32[]{:S(2)}, u32[]{:S(2)}) collective-permute-start(bf16[128,1024]{1,0:T(8,128)(2,1)} %get-tuple-element.42), channel_id=1, source_target_pairs={{0,64},{16,80},{32,96},{48,112},{64,0},{80,16},{96,32},{112,48},{1... | collective-permute-start | bytes 786440 | tf_op jit(solution)/shard_map/ppermute | solution.py:403
  105.8 43.0 %collective-permute-start.5 = (bf16[128,1024]{1,0:T(8,128)(2,1)}, bf16[128,1024]{1,0:T(8,128)(2,1)}, u32[]{:S(2)}, u32[]{:S(2)}) collective-permute-start(bf16[128,1024]{1,0:T(8,128)(2,1)} %get-tuple-element.43), channel_id=1, source_target_pairs={{0,80},{16,96},{32,112},{48,0},{64,16},{80,32},{96,48},{112,64},{1... | collective-permute-start | bytes 786440 | tf_op jit(solution)/shard_map/ppermute | solution.py:403
  143.7 1.6 copy-start
  145.3 16.7 %copy-start.7 = (bf16[128,1024]{1,0:T(8,128)(2,1)S(1)}, bf16[128,1024]{1,0:T(8,128)(2,1)}, u32[]{:S(2)}) copy-start(bf16[128,1024]{1,0:T(8,128)(2,1)} %get-tuple-element.46.rest_0_) | copy-start | bytes 786436
  145.3 16.7 %copy-start.14 = (s32[1,8,1]{1,2,0:T(1,128)S(1)}, s32[1,8,1]{1,2,0:T(1,128)}, u32[]{:S(2)}) copy-start(s32[1,8,1]{1,2,0:T(1,128)} %param.14) | copy-start | bytes 100
  148.7 53.1 %all-to-all-start.2 = ((bf16[64,3,16,512]{3,2,1,0:T(8,128)(2,1)}), bf16[64,3,16,512]{3,2,1,0:T(8,128)(2,1)S(1)}, u32[]{:S(2)}, u32[]{:S(2)}) async-start(bf16[64,3,16,512]{3,2,1,0:T(8,128)(2,1)} %copy-done), calls=%async_computation.2 | async-start | bytes 6291456 | tf_op jit(solution)/shard_map/all_to_all | solution.py:407
  162.1 1.6 copy-start.5
  163.7 1.2 copy-start.6
  164.9 0.9 copy-start.9
  165.8 0.9 copy-start.11
  166.8 0.9 copy-start.13
  170.4 1.3 copy-start.2
  201.8 12.6 %copy-start.3 = (f32[4,128,1024]{2,1,0:T(8,128)S(1)}, f32[4,128,1024]{2,1,0:T(8,128)}, u32[]{:S(2)}) copy-start(f32[4,128,1024]{2,1,0:T(8,128)} %copy-done.2) | copy-start | bytes 6291460
  201.8 12.6 %collective-permute-start.6 = (bf16[2,2,16,3,16,512]{5,4,3,2,1,0:T(8,128)(2,1)S(1)}, bf16[2,2,16,3,16,512]{5,4,3,2,1,0:T(8,128)(2,1)S(1)}, u32[]{:S(2)}, u32[]{:S(2)}) collective-permute-start(bf16[2,2,16,3,16,512]{5,4,3,2,1,0:T(8,128)(2,1)S(1)} %bitcast.11), channel_id=1, source_target_pairs={{0,16},{16,0},{32,48},{48,32},{64,80},{80,64},{96,112},{112,96},{1... | collective-permute-start | bytes 9437192 | tf_op jit(solution)/shard_map/ppermute | solution.py:420
  203.4 8.1 %collective-permute-start.7 = (bf16[128,1024]{1,0:T(8,128)(2,1)}, bf16[128,1024]{1,0:T(8,128)(2,1)S(1)}, u32[]{:S(2)}, u32[]{:S(2)}) collective-permute-start(bf16[128,1024]{1,0:T(8,128)(2,1)} %get-tuple-element.54), channel_id=1, source_target_pairs={{0,96},{16,112},{32,0},{48,16},{64,32},{80,48},{96,64},{112,80},{1... | collective-permute-start | bytes 786440 | tf_op jit(solution)/shard_map/ppermute | solution.py:403
  204.4 10.0 %collective-permute-start.8 = (bf16[128,1024]{1,0:T(8,128)(2,1)}, bf16[128,1024]{1,0:T(8,128)(2,1)S(1)}, u32[]{:S(2)}, u32[]{:S(2)}) collective-permute-start(bf16[128,1024]{1,0:T(8,128)(2,1)} %get-tuple-element.55), channel_id=1, source_target_pairs={{0,112},{16,0},{32,16},{48,32},{64,48},{80,64},{96,80},{112,96},{1... | collective-permute-start | bytes 786440 | tf_op jit(solution)/shard_map/ppermute | solution.py:403

commit v10 on v6

--- a/solution.py
+++ b/solution.py
@@ -23,10 +23,9 @@
 
 def attend_kernel(me_ref, src_ref, slot_ref, valid_ref, x_hbm, r_hbm, c_hbm, wq_hbm, wk_hbm, wv_hbm,
                   *rest, n_src, n_slot, length):
-    outs, scratch = rest[:4 + n_slot], rest[4 + n_slot:]
-    att_hbm, dq_hbm, keep_hbm, send_hbm = outs[:4]
-    dx_hbm = outs[4:]
-    (mult, x_ref, r_ref, c_ref, wq_ref, wk_ref, wv_ref, att_v, dq_v, gw_v, dx_v,
+    outs, scratch = rest[:6], rest[6:]
+    att_hbm, dq_hbm, keep_hbm, send_hbm, dk_hbm, dv_hbm = outs
+    (mult, x_ref, r_ref, c_ref, wq_ref, wk_ref, wv_ref, att_v, dq_v, gw_v,
      xt, rt, q2, g2, k_s, v_s, kt, vt, ot, dqt, dk_acc, dv_acc, sem_in, sem_r, sem_out) = scratch
     width = x_ref.shape[1]
     heads = width // LANES
@@ -162,16 +161,11 @@
         out(gw_v.at[k], dst)
         if k == 0:
             out(dq_v, dq_hbm)
+            out(k_s, dk_hbm)
+            out(v_s, dv_hbm)
     for s in range(n_src):
         att_v[s * length:(s + 1) * length, :] = ot[s].T.astype(BF)
     out(att_v, att_hbm)
-    for lo in range(0, n_slot, half):
-        rows = slice(lo * length, (lo + half) * length)
-        for n in range(0, width, block):
-            cols = slice(n, n + block)
-            dx_v[rows, cols] = (mm_nt(dk[rows], wk_ref[cols, :]) + mm_nt(dv[rows], wv_ref[cols, :])).astype(BF)
-        for t in range(lo, lo + half):
-            out(dx_v.at[pl.ds(t * length, length), :], dx_hbm[t])
     for c in done:
         c.wait()
 
@@ -186,20 +180,20 @@
     hbm = pl.BlockSpec(memory_space=pltpu.HBM)
     shape = jax.ShapeDtypeStruct
     vm = pltpu.VMEM
-    macs = 2 * (n_src + 3 * n_slot) * length * width * width + 12 * 6 * length * length * width
+    macs = 2 * (n_src + 2 * n_slot) * length * width * width + 12 * 6 * length * length * width
     return pl.pallas_call(
         functools.partial(attend_kernel, n_src=n_src, n_slot=n_slot, length=length),
         in_specs=[smem] * 4 + [hbm] * 6,
-        out_specs=[hbm] * (4 + n_slot),
+        out_specs=[hbm] * 6,
         out_shape=[shape((rows, width), BF), shape((rows, width), BF),
                    shape((pieces, 3, each, width), BF), shape((pieces, 3, each, width), BF)]
-        + [shape((length, width), BF)] * n_slot,
+        + [shape((n_slot, length, width), BF)] * 2,
         scratch_shapes=[
             pltpu.SMEM((n_src * n_slot,), jnp.int32),
             vm((rows, width), BF), vm((n_slot * length, width), BF), vm((rows, width), BF),
             vm((width, width), BF), vm((width, width), BF), vm((width, width), BF),
             vm((rows, width), BF), vm((rows, width), BF),
-            vm((2, pieces, 3, each, width), BF), vm((n_slot * length, width), BF),
+            vm((2, pieces, 3, each, width), BF),
             vm((width, rows), BF), vm((width, n_slot * length), BF),
             vm((n_src, heads, 2 * length, LANES), BF), vm((n_src, heads, 2 * length, LANES), BF),
             vm((n_slot, length, width), BF), vm((n_slot, length, width), BF),
@@ -207,12 +201,79 @@
             vm((n_src, width, length), F32), vm((n_src, width, length), F32),
             vm((n_slot, length, width), F32), vm((n_slot, length, width), F32),
             pltpu.SemaphoreType.DMA((5,)), pltpu.SemaphoreType.DMA((n_slot,)),
-            pltpu.SemaphoreType.DMA((4 + n_slot,)),
+            pltpu.SemaphoreType.DMA((6,)),
         ],
         compiler_params=pltpu.CompilerParams(vmem_limit_bytes=60 * 2**20),
         cost_estimate=pl.CostEstimate(flops=4 * macs, bytes_accessed=20 * 2**20, transcendentals=0),
         name="attend",
     )(me, src, slot, valid, x, r, c, wq, wk, wv)
+
+
+def input_kernel(dk_hbm, dv_hbm, wk_hbm, wv_hbm, *rest):
+    n_slot = dk_hbm.shape[0]
+    outs, (dk, dv, wk, wv, acc, dx, sem_in, sem_out) = rest[:n_slot], rest[n_slot:]
+    length, width = dk.shape[1:]
+    block, half = 256, n_slot // 2
+    loads = [pltpu.make_async_copy(a, b, sem_in.at[i]) for i, (a, b) in enumerate(
+        ((dk_hbm, dk), (wk_hbm, wk), (dv_hbm, dv), (wv_hbm, wv)))]
+    for c in loads:
+        c.start()
+    stores = [pltpu.make_async_copy(dx.at[t], outs[t], sem_out.at[t]) for t in range(n_slot)]
+    for d, w, final in ((dk, wk, False), (dv, wv, True)):
+        for c in loads[2 * final:2 * final + 2]:
+            c.wait()
+        for lo in range(0, n_slot, half):
+            rows = d[lo:lo + half].reshape(half * length, width)
+            for n in range(0, width, block):
+                cols = slice(n, n + block)
+                part = mm_nt(rows, w[cols, :]).reshape(half, length, block)
+                if final:
+                    dx[lo:lo + half, :, cols] = (acc[lo:lo + half, :, cols] + part).astype(BF)
+                else:
+                    acc[lo:lo + half, :, cols] = part
+            if final:
+                for c in stores[lo:lo + half]:
+                    c.start()
+    for c in stores:
+        c.wait()
+
+
+def input_grads(dk, dv, wk, wv):
+    n_slot, length, width = dk.shape
+    hbm = pl.BlockSpec(memory_space=pltpu.HBM)
+    vm = pltpu.VMEM
+    return pl.pallas_call(
+        input_kernel,
+        in_specs=[hbm] * 4,
+        out_specs=[hbm] * n_slot,
+        out_shape=[jax.ShapeDtypeStruct((length, width), BF)] * n_slot,
+        scratch_shapes=[
+            vm(dk.shape, BF), vm(dv.shape, BF), vm(wk.shape, BF), vm(wv.shape, BF), vm(dk.shape, F32), vm(dk.shape, BF),
+            pltpu.SemaphoreType.DMA((4,)), pltpu.SemaphoreType.DMA((n_slot,)),
+        ],
+        compiler_params=pltpu.CompilerParams(vmem_limit_bytes=60 * 2**20),
+        cost_estimate=pl.CostEstimate(flops=4 * dk.size * width, bytes_accessed=10 * 2**20, transcendentals=0),
+        name="input_grads",
+    )(dk, dv, wk, wv)
+
+
+def add_kernel(a_ref, b_ref, out_ref):
+    out_ref[...] = (a_ref[...].astype(F32) + b_ref[...].astype(F32)).astype(BF)
+
+
+def add(a, b):
+    count, n, each, width = a.shape
+    spec = pl.BlockSpec((count // 4, n, each, width), lambda i: (i, 0, 0, 0))
+    return pl.pallas_call(
+        add_kernel,
+        grid=(4,),
+        in_specs=[spec, spec],
+        out_specs=spec,
+        out_shape=jax.ShapeDtypeStruct(a.shape, BF),
+        compiler_params=pltpu.CompilerParams(vmem_limit_bytes=16 * 2**20),
+        cost_estimate=pl.CostEstimate(flops=a.size, bytes_accessed=6 * a.size, transcendentals=0),
+        name="add",
+    )(a, b)
 
 
 def combine_kernel(me_ref, listed_ref, dq_hbm, wq_hbm, *rest):
@@ -314,7 +375,7 @@
         in_specs=[pl.BlockSpec((1, each, width), lambda i: (i, 0, 0))] * len(parts),
         out_specs=pl.BlockSpec((copies, 1, each, width), lambda i: (0, i, 0, 0)),
         out_shape=jax.ShapeDtypeStruct((copies, n, each, width), BF),
-        compiler_params=pltpu.CompilerParams(vmem_limit_bytes=60 * 2**20),
+        compiler_params=pltpu.CompilerParams(vmem_limit_bytes=16 * 2**20),
         cost_estimate=pl.CostEstimate(flops=4 * parts[0].size, bytes_accessed=2 * copies * parts[0].size, transcendentals=0),
         name="spread",
     )(*parts)
@@ -357,15 +418,17 @@
     x = sentences.reshape(-1, width)
     c = cotangent.reshape(-1, width)
     where = me.reshape(1).astype(jnp.int32)
-    attended, dq, keep, send, *dx = attend(
+    attended, dq, keep, send, dk, dv = attend(
         where, pair_src, pair_slot, pair_valid, x, received, c, w_query, w_key, w_value, pieces=n_pair
     )
     other_core = [(i, i ^ 1) for i in range(n_lang)]
     other = lax.ppermute(send, "lang", other_core)
+    dx = input_grads(dk, dv, w_key, w_value)
+    other, *dx = lax.optimization_barrier((other, *dx))
+    chip = add(keep, other)
     back = [dx[0]]
     for s in range(1, n_lang):
         back.append(lax.ppermute(dx[s], "lang", [(i, (i + s) % n_lang) for i in range(n_lang)]))
-    chip = (keep.astype(F32) + other.astype(F32)).astype(BF)
     pieces = lax.all_to_all(chip, "pair", split_axis=0, concat_axis=0, tiled=True)
     pieces, *back[1:4] = lax.optimization_barrier((pieces, *back[1:4]))
     plane = sum_parts(pieces)

time: 214 us -> 211 us (0.986)
  other arithmetic: 5.17 us -> 0 us
  Pallas kernels: 53.4 us -> 57 us
  waiting for transfers between devices: 105 us -> 102 us
  local copies, waits for them, and re-layouts: 2.86 us -> 5.37 us
    pallas_call x0 -> x2, Pallas kernels: none -> 11 us  [the longest x1 8.07 us: input_grads(): pl.pallas_call(input_kernel, in_specs=[hbm] * 4, out_specs=[hbm] * n_slot...]
    ppermute x1, waiting for transfers between devices: 5.86 us -> 0.01 us  [body(): other = lax.ppermute(send, 'lang', other_core)]
    convert_element_type x1 -> x0, other arithmetic: 5.17 us -> none  [body(): chip = (keep.astype(F32) + other.astype(F32)).astype(BF)]
    pallas_call x1, Pallas kernels: 35.7 us -> 31.1 us  [attend(): pl.pallas_call(functools.partial(attend_kernel, n_src=n_src, n_slot=n_slo...]
    ppermute x7, waiting for transfers between devices: 28.8 us -> 31.8 us  [body(): lax.ppermute(dx[s], 'lang', [(i, (i + s) % n_lang) for i in range(n_lang)])]
    pallas_call x1, Pallas kernels: 3.44 us -> 0.62 us  [spread(): pl.pallas_call(functools.partial(spread_kernel, factor=factor), grid=(n,)...]
    all_to_all x1, starting transfers between devices: 6.94 us -> 9.63 us  [body(): lax.all_to_all(chip, 'pair', split_axis=0, concat_axis=0, tiled=True)]
    unnamed x20 -> x18, local copies, waits for them, and re-layouts: 2.86 us -> 5.37 us
  transfers between devices with their start and end apart: 15 -> 15, of which waited for: 15 -> 13; matrix products, arithmetic and copies ran while one was open for 0% -> 0% of each run, Pallas kernels for 4% -> 8%
where the time goes in v10:
time: 211 us; the launch traced here: 210 us
  waiting for transfers between devices  102 us (48%)
  Pallas kernels  57 us (27%)
  starting transfers between devices  44.9 us (21%)
  local copies, waits for them, and re-layouts  5.37 us (3%)
    ppermute x7, waiting for transfers between devices, body(): lax.ppermute(dx[s], 'lang', [(i, (i + s) % n_lang) for i in range(n_lang)])  31.8 us
    pallas_call x1, Pallas kernels, attend(): pl.pallas_call(functools.partial(attend_kernel, n_src=n_src, n_slot=n_slo...  31.1 us
    all_to_all x1, waiting for transfers between devices, body(): lax.all_to_all(outgoing, 'lang', split_axis=0, concat_axis=0, tiled=True)  26.3 us
    all_to_all x1, waiting for transfers between devices, body(): lax.all_to_all(chip, 'pair', split_axis=0, concat_axis=0, tiled=True)  21.6 us
    all_to_all x1, starting transfers between devices, body(): lax.all_to_all(spread(rings, n_pair, factor), 'pair', split_axis=0, conca...  11.7 us
    all_to_all x1, waiting for transfers between devices, body(): lax.all_to_all(spread(rings, n_pair, factor), 'pair', split_axis=0, conca...  10.4 us
    all_to_all x1, starting transfers between devices, body(): lax.all_to_all(chip, 'pair', split_axis=0, concat_axis=0, tiled=True)  9.63 us
    ppermute x3, waiting for transfers between devices, body(): lax.ppermute(plane, 'lang', [(i, (i + 2 * y) % n_lang) for i in range(n_l...  8.61 us
  transfers between devices with their start and end apart: 15, of which 13 were waited for; matrix products, arithmetic and copies ran while one was open for 0% of the time, Pallas kernels for 8%

profile of v10, /device:TPU:1, one launch (start us, length us, event | category | flops | bytes accessed | tf_op | source)
XLA Modules:
  0.0 210.0 jit_solution(10387109701915256168)
XLA Ops:
  0.6 3.3 %pick.1 = bf16[8,128,1024]{2,1,0:T(8,128)(2,1)} custom-call(s32[8]{0:T(128)} %bitcast.12, bf16[4,128,1024]{2,1,0:T(8,128)(2,1)} %x_hbm.1), custom_call_target="tpu_custom_call" | custom-call | tf_op jit(solution)/shard_map/pick/pallas_call | solution.py:335
  3.9 6.0 %all-to-all-start = ((bf16[8,128,1024]{2,1,0:T(8,128)(2,1)}), bf16[8,128,1024]{2,1,0:T(8,128)(2,1)S(1)}, u32[]{:S(2)}, u32[]{:S(2)}) async-start(bf16[8,128,1024]{2,1,0:T(8,128)(2,1)} %pick.1), calls=%async_computation | async-start | bytes 4194304 | tf_op jit(solution)/shard_map/all_to_all | solution.py:417
  9.9 26.3 %all-to-all-done.r_hbm = bf16[8,128,1024]{2,1,0:T(8,128)(2,1)S(1)} async-done(((bf16[8,128,1024]{2,1,0:T(8,128)(2,1)}), bf16[8,128,1024]{2,1,0:T(8,128)(2,1)S(1)}, u32[]{:S(2)}, u32[]{:S(2)}) %all-to-all-start) | async-done | bytes 2097184 | tf_op jit(solution)/shard_map/all_to_all | solution.py:417
  36.2 1.3 copy-done.3
  37.5 31.1 %attend.1 = (bf16[512,1024]{1,0:T(8,128)(2,1)}, bf16[512,1024]{1,0:T(8,128)(2,1)}, bf16[16,3,32,1024]{3,2,1,0:T(8,128)(2,1)}, bf16[16,3,32,1024]{3,2,1,0:T(8,128...) custom-call(s32[1]{0:T(128)} %bitcast.me_ref, s32[1,16]{1,0:T(1,128)} %src_ref.1, s32[1,16]{1,0:T(1,128)} %slot_ref.1, ...), custom_call_target="tpu_custom_call" | custom-call | flops 26306674688 | bytes 20971520 | tf_op jit(solution)/shard_map/attend/pallas_call | solution.py:184
  68.6 0.1 collective-permute-start
  68.7 0.0 copy-start.2
  68.7 8.1 %input_grads.1 = (bf16[128,1024]{1,0:T(8,128)(2,1)}, bf16[128,1024]{1,0:T(8,128)(2,1)}, bf16[128,1024]{1,0:T(8,128)(2,1)}, bf16[128,1024]{1,0:T(8,128)(2,1)}, bf...) custom-call(bf16[8,128,1024]{2,1,0:T(8,128)(2,1)} %get-tuple-element, ...), custom_call_target="tpu_custom_call" | custom-call | flops 4294967296 | bytes 10485760 | tf_op jit(solution)/shard_map/input_grads/pallas_call | solution.py:245
  76.8 0.0 collective-permute-done.b_ref
  76.8 0.0 copy-done.2
  76.8 3.0 %add.1 = bf16[16,3,32,1024]{3,2,1,0:T(8,128)(2,1)S(1)} custom-call(bf16[16,3,32,1024]{3,2,1,0:T(8,128)(2,1)S(1)} %copy-done.2, bf16[16,3,32,1024]{3,2,1,0:T(8,128)(2,1)} %collective-permute-done.b_ref), custom_call_target="tpu_custom_call" | custom-call | flops 1572864 | bytes 9437184 | tf_op jit(solution)/shard_map/add/pallas_call | solution.py:267
  79.8 0.0 copy-start.1
  79.8 1.6 copy-done.1
  81.4 9.6 %all-to-all-start.1 = ((bf16[16,3,32,1024]{3,2,1,0:T(8,128)(2,1)}), bf16[16,3,32,1024]{3,2,1,0:T(8,128)(2,1)S(1)}, u32[]{:S(2)}, u32[]{:S(2)}) async-start(bf16[16,3,32,1024]{3,2,1,0:T(8,128)(2,1)} %copy-done.1), calls=%async_computation.1 | async-start | bytes 6291456 | tf_op jit(solution)/shard_map/all_to_all | solution.py:432
  91.1 1.2 collective-permute-start.1
  92.2 0.5 collective-permute-start.2
  92.8 0.5 collective-permute-start.3
  93.2 4.7 %collective-permute-done.1.rest_1_ = bf16[128,1024]{1,0:T(8,128)(2,1)S(1)} collective-permute-done((bf16[128,1024]{1,0:T(8,128)(2,1)}, bf16[128,1024]{1,0:T(8,128)(2,1)S(1)}, u32[]{:S(2)}, u32[]{:S(2)}) %collective-permute-start.1) | collective-permute-done | bytes 262176 | tf_op jit(solution)/shard_map/ppermute | solution.py:431
  97.9 11.4 %collective-permute-done.2.rest_2_ = bf16[128,1024]{1,0:T(8,128)(2,1)S(1)} collective-permute-done((bf16[128,1024]{1,0:T(8,128)(2,1)}, bf16[128,1024]{1,0:T(8,128)(2,1)S(1)}, u32[]{:S(2)}, u32[]{:S(2)}) %collective-permute-start.2) | collective-permute-done | bytes 262176 | tf_op jit(solution)/shard_map/ppermute | solution.py:431
  109.3 0.7 copy-done.5
  110.0 0.0 collective-permute-done.3.rest_3_
  110.0 21.6 %all-to-all-done.1.parts_ref = bf16[16,3,32,1024]{3,2,1,0:T(8,128)(2,1)S(1)} async-done(((bf16[16,3,32,1024]{3,2,1,0:T(8,128)(2,1)}), bf16[16,3,32,1024]{3,2,1,0:T(8,128)(2,1)S(1)}, u32[]{:S(2)}, u32[]{:S(2)}) %all-to-all-start.1) | async-done | bytes 3145760 | tf_op jit(solution)/shard_map/all_to_all | solution.py:432
  131.6 0.7 sum_parts.1.a_ref
  132.3 0.1 collective-permute-start.6
  132.3 3.8 %collective-permute-start.5 = (bf16[3,32,1024]{2,1,0:T(8,128)(2,1)S(1)}, bf16[3,32,1024]{2,1,0:T(8,128)(2,1)S(1)}, u32[]{:S(2)}, u32[]{:S(2)}) collective-permute-start(bf16[3,32,1024]{2,1,0:T(8,128)(2,1)S(1)} %sum_parts.1.a_ref), channel_id=1, source_target_pairs={{0,64},{16,80},{32,96},{48,112},{64,0},{80,16},{96,32},{112,48},{1... | collective-permute-start | bytes 589832 | tf_op jit(solution)/shard_map/ppermute | solution.py:437
  136.2 0.0 collective-permute-start.4
  136.2 1.3 collective-permute-done.6.d_ref
  137.4 1.8 collective-permute-done.5.c_ref
  139.2 5.6 %collective-permute-done.4.b_ref = bf16[3,32,1024]{2,1,0:T(8,128)(2,1)S(1)} collective-permute-done((bf16[3,32,1024]{2,1,0:T(8,128)(2,1)S(1)}, bf16[3,32,1024]{2,1,0:T(8,128)(2,1)S(1)}, u32[]{:S(2)}, u32[]{:S(2)}) %collective-permute-start.4) | collective-permute-done | bytes 196640 | tf_op jit(solution)/shard_map/ppermute | solution.py:437
  144.8 0.6 spread.1
  145.4 0.0 copy-done.4
  145.4 1.6 copy-done
  147.1 11.7 %all-to-all-start.2 = ((bf16[16,3,32,1024]{3,2,1,0:T(8,128)(2,1)}), bf16[16,3,32,1024]{3,2,1,0:T(8,128)(2,1)S(1)}, u32[]{:S(2)}, u32[]{:S(2)}) async-start(bf16[16,3,32,1024]{3,2,1,0:T(8,128)(2,1)} %copy-done), calls=%async_computation.2 | async-start | bytes 6291456 | tf_op jit(solution)/shard_map/all_to_all | solution.py:439
  158.8 0.1 collective-permute-start.7
  158.9 5.8 %collective-permute-start.8 = (bf16[128,1024]{1,0:T(8,128)(2,1)}, bf16[128,1024]{1,0:T(8,128)(2,1)S(1)}, u32[]{:S(2)}, u32[]{:S(2)}) collective-permute-start(bf16[128,1024]{1,0:T(8,128)(2,1)} %get-tuple-element.64), channel_id=1, source_target_pairs={{0,80},{16,96},{32,112},{48,0},{64,16},{80,32},{96,48},{112,64},{1... | collective-permute-start | bytes 786440 | tf_op jit(solution)/shard_map/ppermute | solution.py:431
  164.7 0.0 collective-permute-start.9
  164.7 0.4 collective-permute-start.10
  165.1 1.4 collective-permute-done.7.rest_4_
  166.6 8.1 %collective-permute-done.8.rest_5_ = bf16[128,1024]{1,0:T(8,128)(2,1)S(1)} collective-permute-done((bf16[128,1024]{1,0:T(8,128)(2,1)}, bf16[128,1024]{1,0:T(8,128)(2,1)S(1)}, u32[]{:S(2)}, u32[]{:S(2)}) %collective-permute-start.8) | collective-permute-done | bytes 262176 | tf_op jit(solution)/shard_map/ppermute | solution.py:431
  174.7 5.6 %collective-permute-done.9.rest_6_ = bf16[128,1024]{1,0:T(8,128)(2,1)S(1)} collective-permute-done((bf16[128,1024]{1,0:T(8,128)(2,1)}, bf16[128,1024]{1,0:T(8,128)(2,1)S(1)}, u32[]{:S(2)}, u32[]{:S(2)}) %collective-permute-start.9) | collective-permute-done | bytes 262176 | tf_op jit(solution)/shard_map/ppermute | solution.py:431
  180.3 0.6 collective-permute-done.10.rest_7_
  180.9 0.1 copy-done.8
  181.0 6.1 %combine.1 = bf16[4,128,1024]{2,1,0:T(8,128)(2,1)} custom-call(s32[1]{0:T(128)} %bitcast.me_ref, s32[8]{0:T(128)} %bitcast.13, bf16[512,1024]{1,0:T(8,128)(2,1)} %get-tuple-element.58.dq_hbm, bf16[1024,1024]{1,0:T(8,128)(2,1)} %wq_hbm.3, bf16[128,1024]{1,0:T(8,128)(2,1)} %get-tuple-element.59.rest_0_, bf16[128,1024]{1,0:T(8,128)(2,1)} %copy-done.4, ...), custom_call_target="tpu_custom_call" | custom-call | flops 1073741824 | bytes 6291456 | tf_op jit(solution)/shard_map/combine/pallas_call | solution.py:305
  187.1 10.4 %all-to-all-done.2.rows_ref = bf16[16,3,32,1024]{3,2,1,0:T(8,128)(2,1)S(1)} async-done(((bf16[16,3,32,1024]{3,2,1,0:T(8,128)(2,1)}), bf16[16,3,32,1024]{3,2,1,0:T(8,128)(2,1)S(1)}, u32[]{:S(2)}, u32[]{:S(2)}) %all-to-all-start.2) | async-done | bytes 3145760 | tf_op jit(solution)/shard_map/all_to_all | solution.py:439
  197.5 5.1 %collective-permute-start.11 = (bf16[16,3,32,1024]{3,2,1,0:T(8,128)(2,1)S(1)}, bf16[16,3,32,1024]{3,2,1,0:T(8,128)(2,1)S(1)}, u32[]{:S(2)}, u32[]{:S(2)}) collective-permute-start(bf16[16,3,32,1024]{3,2,1,0:T(8,128)(2,1)S(1)} %all-to-all-done.2.rows_ref), channel_id=1, source_target_pairs={{0,16},{16,0},{32,48},{48,32},{64,80},{80,64},{96,112},{112,96},{1... | collective-permute-start | bytes 9437192 | tf_op jit(solution)/shard_map/ppermute | solution.py:442
  202.6 2.1 %place.2 = (bf16[2,16,32,1024]{3,2,1,0:T(8,128)(2,1)}, bf16[2,16,32,1024]{3,2,1,0:T(8,128)(2,1)}, bf16[2,16,32,1024]{3,2,1,0:T(8,128)(2,1)}) custom-call(s32[1]{0:T(128)S(6)} %rem.18.half_ref, bf16[16,3,32,1024]{3,2,1,0:T(8,128)(2,1)S(1)} %all-to-all-done.2.rows_ref), custom_call_target="tpu_custom_call" | custom-call | bytes 6291456 | tf_op jit(solution)/shard_map/place/pallas_call | solution.py:394
  204.7 3.2 %collective-permute-done.11.rows_ref = bf16[16,3,32,1024]{3,2,1,0:T(8,128)(2,1)S(1)} collective-permute-done((bf16[16,3,32,1024]{3,2,1,0:T(8,128)(2,1)S(1)}, bf16[16,3,32,1024]{3,2,1,0:T(8,128)(2,1)S(1)}, u32[]{:S(2)}, u32[]{:S(2)}) %collective-permute-start.11) | collective-permute-done | bytes 3145760 | tf_op jit(solution)/shard_map/ppermute | solution.py:442
  207.9 2.1 %place.3 = (bf16[2,16,32,1024]{3,2,1,0:T(8,128)(2,1)}, bf16[2,16,32,1024]{3,2,1,0:T(8,128)(2,1)}, bf16[2,16,32,1024]{3,2,1,0:T(8,128)(2,1)}) custom-call(s32[1]{0:T(128)S(6)} %sub.3.half_ref, bf16[16,3,32,1024]{3,2,1,0:T(8,128)(2,1)S(1)} %collective-permute-done.11.rows_ref, ...), custom_call_target="tpu_custom_call", output_to_operand_aliasing={{0}: (2, {}), {1}: (3, {}), {2}: (4, {})} | custom-call | bytes 6291456 | tf_op jit(solution)/shard_map/place/pallas_call | solution.py:394
  (9 shorter events, 0.0 us)
Async XLA Ops:
  3.9 32.3 %all-to-all-start = ((bf16[8,128,1024]{2,1,0:T(8,128)(2,1)}), bf16[8,128,1024]{2,1,0:T(8,128)(2,1)S(1)}, u32[]{:S(2)}, u32[]{:S(2)}) async-start(bf16[8,128,1024]{2,1,0:T(8,128)(2,1)} %pick.1), calls=%async_computation | async-start | bytes 4194304 | tf_op jit(solution)/shard_map/all_to_all | solution.py:417
  36.2 1.3 copy-start.3
  68.6 8.2 %collective-permute-start = (bf16[16,3,32,1024]{3,2,1,0:T(8,128)(2,1)}, bf16[16,3,32,1024]{3,2,1,0:T(8,128)(2,1)}, u32[]{:S(2)}, u32[]{:S(2)}) collective-permute-start(bf16[16,3,32,1024]{3,2,1,0:T(8,128)(2,1)} %get-tuple-element.42), channel_id=1, source_target_pairs={{0,16},{16,0},{32,48},{48,32},{64,80},{80,64},{96,112},{112,96},{1... | collective-permute-start | bytes 9437192 | tf_op jit(solution)/shard_map/ppermute | solution.py:425
  68.7 8.1 %copy-start.2 = (bf16[16,3,32,1024]{3,2,1,0:T(8,128)(2,1)S(1)}, bf16[16,3,32,1024]{3,2,1,0:T(8,128)(2,1)}, u32[]{:S(2)}) copy-start(bf16[16,3,32,1024]{3,2,1,0:T(8,128)(2,1)} %get-tuple-element.41.a_ref) | copy-start | bytes 9437188
  79.8 1.6 copy-start.1
  81.4 50.1 %all-to-all-start.1 = ((bf16[16,3,32,1024]{3,2,1,0:T(8,128)(2,1)}), bf16[16,3,32,1024]{3,2,1,0:T(8,128)(2,1)S(1)}, u32[]{:S(2)}, u32[]{:S(2)}) async-start(bf16[16,3,32,1024]{3,2,1,0:T(8,128)(2,1)} %copy-done.1), calls=%async_computation.1 | async-start | bytes 6291456 | tf_op jit(solution)/shard_map/all_to_all | solution.py:432
  91.1 6.9 %collective-permute-start.1 = (bf16[128,1024]{1,0:T(8,128)(2,1)}, bf16[128,1024]{1,0:T(8,128)(2,1)S(1)}, u32[]{:S(2)}, u32[]{:S(2)}) collective-permute-start(bf16[128,1024]{1,0:T(8,128)(2,1)} %get-tuple-element.54), channel_id=1, source_target_pairs={{0,16},{16,32},{32,48},{48,64},{64,80},{80,96},{96,112},{112,0},{1... | collective-permute-start | bytes 786440 | tf_op jit(solution)/shard_map/ppermute | solution.py:431
  92.2 17.0 %collective-permute-start.2 = (bf16[128,1024]{1,0:T(8,128)(2,1)}, bf16[128,1024]{1,0:T(8,128)(2,1)S(1)}, u32[]{:S(2)}, u32[]{:S(2)}) collective-permute-start(bf16[128,1024]{1,0:T(8,128)(2,1)} %get-tuple-element.55), channel_id=1, source_target_pairs={{0,32},{16,48},{32,64},{48,80},{64,96},{80,112},{96,0},{112,16},{1... | collective-permute-start | bytes 786440 | tf_op jit(solution)/shard_map/ppermute | solution.py:431
  92.8 17.2 %collective-permute-start.3 = (bf16[128,1024]{1,0:T(8,128)(2,1)}, bf16[128,1024]{1,0:T(8,128)(2,1)}, u32[]{:S(2)}, u32[]{:S(2)}) collective-permute-start(bf16[128,1024]{1,0:T(8,128)(2,1)} %get-tuple-element.56), channel_id=1, source_target_pairs={{0,48},{16,64},{32,80},{48,96},{64,112},{80,0},{96,16},{112,32},{1... | collective-permute-start | bytes 786440 | tf_op jit(solution)/shard_map/ppermute | solution.py:431
  97.9 47.5 %copy-start.4 = (bf16[128,1024]{1,0:T(8,128)(2,1)}, bf16[128,1024]{1,0:T(8,128)(2,1)S(1)}, u32[]{:S(2)}) copy-start(bf16[128,1024]{1,0:T(8,128)(2,1)S(1)} %collective-permute-done.1.rest_1_) | copy-start | bytes 786436
  109.3 0.7 copy-start.5
  132.3 5.2 %collective-permute-start.6 = (bf16[3,32,1024]{2,1,0:T(8,128)(2,1)S(1)}, bf16[3,32,1024]{2,1,0:T(8,128)(2,1)S(1)}, u32[]{:S(2)}, u32[]{:S(2)}) collective-permute-start(bf16[3,32,1024]{2,1,0:T(8,128)(2,1)S(1)} %sum_parts.1.a_ref), channel_id=1, source_target_pairs={{0,96},{16,112},{32,0},{48,16},{64,32},{80,48},{96,64},{112,80},{1... | collective-permute-start | bytes 589832 | tf_op jit(solution)/shard_map/ppermute | solution.py:437
  132.3 6.9 %collective-permute-start.5 = (bf16[3,32,1024]{2,1,0:T(8,128)(2,1)S(1)}, bf16[3,32,1024]{2,1,0:T(8,128)(2,1)S(1)}, u32[]{:S(2)}, u32[]{:S(2)}) collective-permute-start(bf16[3,32,1024]{2,1,0:T(8,128)(2,1)S(1)} %sum_parts.1.a_ref), channel_id=1, source_target_pairs={{0,64},{16,80},{32,96},{48,112},{64,0},{80,16},{96,32},{112,48},{1... | collective-permute-start | bytes 589832 | tf_op jit(solution)/shard_map/ppermute | solution.py:437
  136.2 8.6 %collective-permute-start.4 = (bf16[3,32,1024]{2,1,0:T(8,128)(2,1)S(1)}, bf16[3,32,1024]{2,1,0:T(8,128)(2,1)S(1)}, u32[]{:S(2)}, u32[]{:S(2)}) collective-permute-start(bf16[3,32,1024]{2,1,0:T(8,128)(2,1)S(1)} %sum_parts.1.a_ref), channel_id=1, source_target_pairs={{0,32},{16,48},{32,64},{48,80},{64,96},{80,112},{96,0},{112,16},{1... | collective-permute-start | bytes 589832 | tf_op jit(solution)/shard_map/ppermute | solution.py:437
  145.4 1.6 copy-start
  147.1 50.4 %all-to-all-start.2 = ((bf16[16,3,32,1024]{3,2,1,0:T(8,128)(2,1)}), bf16[16,3,32,1024]{3,2,1,0:T(8,128)(2,1)S(1)}, u32[]{:S(2)}, u32[]{:S(2)}) async-start(bf16[16,3,32,1024]{3,2,1,0:T(8,128)(2,1)} %copy-done), calls=%async_computation.2 | async-start | bytes 6291456 | tf_op jit(solution)/shard_map/all_to_all | solution.py:439
  158.8 7.8 %collective-permute-start.7 = (bf16[128,1024]{1,0:T(8,128)(2,1)}, bf16[128,1024]{1,0:T(8,128)(2,1)S(1)}, u32[]{:S(2)}, u32[]{:S(2)}) collective-permute-start(bf16[128,1024]{1,0:T(8,128)(2,1)} %get-tuple-element.63), channel_id=1, source_target_pairs={{0,64},{16,80},{32,96},{48,112},{64,0},{80,16},{96,32},{112,48},{1... | collective-permute-start | bytes 786440 | tf_op jit(solution)/shard_map/ppermute | solution.py:431
  158.9 15.8 %collective-permute-start.8 = (bf16[128,1024]{1,0:T(8,128)(2,1)}, bf16[128,1024]{1,0:T(8,128)(2,1)S(1)}, u32[]{:S(2)}, u32[]{:S(2)}) collective-permute-start(bf16[128,1024]{1,0:T(8,128)(2,1)} %get-tuple-element.64), channel_id=1, source_target_pairs={{0,80},{16,96},{32,112},{48,0},{64,16},{80,32},{96,48},{112,64},{1... | collective-permute-start | bytes 786440 | tf_op jit(solution)/shard_map/ppermute | solution.py:431
  164.7 15.6 %collective-permute-start.9 = (bf16[128,1024]{1,0:T(8,128)(2,1)}, bf16[128,1024]{1,0:T(8,128)(2,1)S(1)}, u32[]{:S(2)}, u32[]{:S(2)}) collective-permute-start(bf16[128,1024]{1,0:T(8,128)(2,1)} %get-tuple-element.65), channel_id=1, source_target_pairs={{0,96},{16,112},{32,0},{48,16},{64,32},{80,48},{96,64},{112,80},{1... | collective-permute-start | bytes 786440 | tf_op jit(solution)/shard_map/ppermute | solution.py:431
  164.7 16.2 %collective-permute-start.10 = (bf16[128,1024]{1,0:T(8,128)(2,1)}, bf16[128,1024]{1,0:T(8,128)(2,1)}, u32[]{:S(2)}, u32[]{:S(2)}) collective-permute-start(bf16[128,1024]{1,0:T(8,128)(2,1)} %get-tuple-element.66), channel_id=1, source_target_pairs={{0,112},{16,0},{32,16},{48,32},{64,48},{80,64},{96,80},{112,96},{1... | collective-permute-start | bytes 786440 | tf_op jit(solution)/shard_map/ppermute | solution.py:431
  166.5 14.3 %copy-start.6 = (bf16[128,1024]{1,0:T(8,128)(2,1)}, bf16[128,1024]{1,0:T(8,128)(2,1)S(1)}, u32[]{:S(2)}) copy-start(bf16[128,1024]{1,0:T(8,128)(2,1)S(1)} %collective-permute-done.7.rest_4_) | copy-start | bytes 786436
  174.7 6.2 %copy-start.7 = (bf16[128,1024]{1,0:T(8,128)(2,1)}, bf16[128,1024]{1,0:T(8,128)(2,1)S(1)}, u32[]{:S(2)}) copy-start(bf16[128,1024]{1,0:T(8,128)(2,1)S(1)} %collective-permute-done.8.rest_5_) | copy-start | bytes 786436
  180.3 0.7 copy-start.8
  197.5 10.4 %collective-permute-start.11 = (bf16[16,3,32,1024]{3,2,1,0:T(8,128)(2,1)S(1)}, bf16[16,3,32,1024]{3,2,1,0:T(8,128)(2,1)S(1)}, u32[]{:S(2)}, u32[]{:S(2)}) collective-permute-start(bf16[16,3,32,1024]{3,2,1,0:T(8,128)(2,1)S(1)} %all-to-all-done.2.rows_ref), channel_id=1, source_target_pairs={{0,16},{16,0},{32,48},{48,32},{64,80},{80,64},{96,112},{112,96},{1... | collective-permute-start | bytes 9437192 | tf_op jit(solution)/shard_map/ppermute | solution.py:442

commit v11 on v10

--- a/solution.py
+++ b/solution.py
@@ -23,8 +23,8 @@
 
 def attend_kernel(me_ref, src_ref, slot_ref, valid_ref, x_hbm, r_hbm, c_hbm, wq_hbm, wk_hbm, wv_hbm,
                   *rest, n_src, n_slot, length):
-    outs, scratch = rest[:6], rest[6:]
-    att_hbm, dq_hbm, keep_hbm, send_hbm, dk_hbm, dv_hbm = outs
+    outs, scratch = rest[:7], rest[7:]
+    att_hbm, dq_hbm, xk_hbm, rk_hbm, send_hbm, dk_hbm, dv_hbm = outs
     (mult, x_ref, r_ref, c_ref, wq_ref, wk_ref, wv_ref, att_v, dq_v, gw_v,
      xt, rt, q2, g2, k_s, v_s, kt, vt, ot, dqt, dk_acc, dv_acc, sem_in, sem_r, sem_out) = scratch
     width = x_ref.shape[1]
@@ -149,20 +149,21 @@
         c.start()
         done.append(c)
 
-    _, pieces, _, each, _ = gw_v.shape
+    pieces, _, each, _ = gw_v.shape
     core = lax.rem(me, 2)
-    for k, dst in enumerate((send_hbm, keep_hbm)):
-        base = pl.multiple_of((core if k else 1 - core) * (pieces * each), LANES)
-        rows = pl.ds(base, pieces * each)
-        for n in range(0, width, block):
-            cols = slice(n, n + block)
-            for i, (lhs, rhs) in enumerate(((xt, dq_v[:, cols]), (rt, dk[:, cols]), (rt, dv[:, cols]))):
-                gw_v[k, :, i, :, cols] = mm(lhs[rows, :], rhs).astype(BF).reshape(pieces, each, block)
-        out(gw_v.at[k], dst)
-        if k == 0:
-            out(dq_v, dq_hbm)
-            out(k_s, dk_hbm)
-            out(v_s, dv_hbm)
+    count = pieces * each
+    own = pl.ds(pl.multiple_of(core * count, LANES), count)
+    rows = pl.ds(pl.multiple_of((1 - core) * count, LANES), count)
+    out(dq_v, dq_hbm)
+    out(k_s, dk_hbm)
+    out(v_s, dv_hbm)
+    out(xt.at[own, :], xk_hbm)
+    out(rt.at[own, :], rk_hbm)
+    for n in range(0, width, block):
+        cols = slice(n, n + block)
+        for i, (lhs, rhs) in enumerate(((xt, dq_v[:, cols]), (rt, dk[:, cols]), (rt, dv[:, cols]))):
+            gw_v[:, i, :, cols] = mm(lhs[rows, :], rhs).astype(BF).reshape(pieces, each, block)
+    out(gw_v, send_hbm)
     for s in range(n_src):
         att_v[s * length:(s + 1) * length, :] = ot[s].T.astype(BF)
     out(att_v, att_hbm)
@@ -184,16 +185,17 @@
     return pl.pallas_call(
         functools.partial(attend_kernel, n_src=n_src, n_slot=n_slot, length=length),
         in_specs=[smem] * 4 + [hbm] * 6,
-        out_specs=[hbm] * 6,
+        out_specs=[hbm] * 7,
         out_shape=[shape((rows, width), BF), shape((rows, width), BF),
-                   shape((pieces, 3, each, width), BF), shape((pieces, 3, each, width), BF)]
+                   shape((width // 2, rows), BF), shape((width // 2, n_slot * length), BF),
+                   shape((pieces, 3, each, width), BF)]
         + [shape((n_slot, length, width), BF)] * 2,
         scratch_shapes=[
             pltpu.SMEM((n_src * n_slot,), jnp.int32),
             vm((rows, width), BF), vm((n_slot * length, width), BF), vm((rows, width), BF),
             vm((width, width), BF), vm((width, width), BF), vm((width, width), BF),
             vm((rows, width), BF), vm((rows, width), BF),
-            vm((2, pieces, 3, each, width), BF),
+            vm((pieces, 3, each, width), BF),
             vm((width, rows), BF), vm((width, n_slot * length), BF),
             vm((n_src, heads, 2 * length, LANES), BF), vm((n_src, heads, 2 * length, LANES), BF),
             vm((n_slot, length, width), BF), vm((n_slot, length, width), BF),
@@ -201,12 +203,51 @@
             vm((n_src, width, length), F32), vm((n_src, width, length), F32),
             vm((n_slot, length, width), F32), vm((n_slot, length, width), F32),
             pltpu.SemaphoreType.DMA((5,)), pltpu.SemaphoreType.DMA((n_slot,)),
-            pltpu.SemaphoreType.DMA((6,)),
+            pltpu.SemaphoreType.DMA((7,)),
         ],
         compiler_params=pltpu.CompilerParams(vmem_limit_bytes=60 * 2**20),
         cost_estimate=pl.CostEstimate(flops=4 * macs, bytes_accessed=20 * 2**20, transcendentals=0),
         name="attend",
     )(me, src, slot, valid, x, r, c, wq, wk, wv)
+
+
+def keep_kernel(x_hbm, r_hbm, dq_hbm, dk_hbm, dv_hbm, out_hbm, x, r, dq, dk, dv, gw, sem_in, sem_out):
+    n_slot, length, width = dk.shape
+    pieces, _, each, _ = gw.shape
+    block = 256
+    loads = [pltpu.make_async_copy(a, b, sem_in.at[i]) for i, (a, b) in enumerate(
+        ((x_hbm, x), (dq_hbm, dq), (r_hbm, r), (dk_hbm, dk), (dv_hbm, dv)))]
+    for c in loads:
+        c.start()
+    stores = [pltpu.make_async_copy(gw.at[:, i], out_hbm.at[:, i], sem_out.at[i]) for i in range(3)]
+    for i, (lhs, rhs, needs) in enumerate(((x, dq, loads[:2]), (r, dk, loads[2:4]), (r, dv, loads[4:]))):
+        for c in needs:
+            c.wait()
+        for n in range(0, width, block):
+            cols = slice(n, n + block)
+            d = rhs[:, cols] if i == 0 else rhs[:, :, cols].reshape(n_slot * length, block)
+            gw[:, i, :, cols] = mm(lhs[...], d).astype(BF).reshape(pieces, each, block)
+        stores[i].start()
+    for c in stores:
+        c.wait()
+
+
+def keep_grads(x, r, dq, dk, dv, pieces):
+    half, width = x.shape[0], dq.shape[1]
+    hbm = pl.BlockSpec(memory_space=pltpu.HBM)
+    vm = pltpu.VMEM
+    share = (pieces, 3, half // pieces, width)
+    return pl.pallas_call(
+        keep_kernel,
+        in_specs=[hbm] * 5,
+        out_specs=hbm,
+        out_shape=jax.ShapeDtypeStruct(share, BF),
+        scratch_shapes=[vm(a.shape, BF) for a in (x, r, dq, dk, dv)] + [
+            vm(share, BF), pltpu.SemaphoreType.DMA((5,)), pltpu.SemaphoreType.DMA((3,))],
+        compiler_params=pltpu.CompilerParams(vmem_limit_bytes=60 * 2**20),
+        cost_estimate=pl.CostEstimate(flops=2 * (x.size + 2 * r.size) * width, bytes_accessed=10 * 2**20, transcendentals=0),
+        name="keep_grads",
+    )(x, r, dq, dk, dv)
 
 
 def input_kernel(dk_hbm, dv_hbm, wk_hbm, wv_hbm, *rest):
@@ -418,14 +459,15 @@
     x = sentences.reshape(-1, width)
     c = cotangent.reshape(-1, width)
     where = me.reshape(1).astype(jnp.int32)
-    attended, dq, keep, send, dk, dv = attend(
+    attended, dq, xk, rk, send, dk, dv = attend(
         where, pair_src, pair_slot, pair_valid, x, received, c, w_query, w_key, w_value, pieces=n_pair
     )
     other_core = [(i, i ^ 1) for i in range(n_lang)]
     other = lax.ppermute(send, "lang", other_core)
+    keep = keep_grads(xk, rk, dq, dk, dv, n_pair)
+    other, keep = lax.optimization_barrier((other, keep))
+    chip, dk, dv = lax.optimization_barrier((add(keep, other), dk, dv))
     dx = input_grads(dk, dv, w_key, w_value)
-    other, *dx = lax.optimization_barrier((other, *dx))
-    chip = add(keep, other)
     back = [dx[0]]
     for s in range(1, n_lang):
         back.append(lax.ppermute(dx[s], "lang", [(i, (i + s) % n_lang) for i in range(n_lang)]))

time: 211 us -> 207 us (0.981)
  waiting for transfers between devices: 102 us -> 96.7 us
  starting transfers between devices: 44.9 us -> 40.6 us
  Pallas kernels: 57 us -> 60.4 us
    pallas_call x0 -> x1, Pallas kernels: none -> 6.05 us  [keep_grads(): pl.pallas_call(keep_kernel, in_specs=[hbm] * 5, out_specs=hbm, out_shape=...]
    ppermute x7, waiting for transfers between devices: 31.8 us -> 26.8 us  [body(): lax.ppermute(dx[s], 'lang', [(i, (i + s) % n_lang) for i in range(n_lang)])]
    all_to_all x1, waiting for transfers between devices: 21.6 us -> 18.1 us  [body(): lax.all_to_all(chip, 'pair', split_axis=0, concat_axis=0, tiled=True)]
    all_to_all x1, starting transfers between devices: 9.63 us -> 7.06 us  [body(): lax.all_to_all(chip, 'pair', split_axis=0, concat_axis=0, tiled=True)]
    pallas_call x1, Pallas kernels: 2.96 us -> 0.76 us  [add(): pl.pallas_call(add_kernel, grid=(4,), in_specs=[spec, spec], out_specs=sp...]
  transfers between devices with their start and end apart: 15 -> 15, of which waited for: 13 -> 13; matrix products, arithmetic and copies ran while one was open for 0% -> 0% of each run, Pallas kernels for 8% -> 11%
where the time goes in v11:
time: 207 us; the launch traced here: 206 us
  waiting for transfers between devices  96.7 us (47%)
  Pallas kernels  60.4 us (29%)
  starting transfers between devices  40.6 us (20%)
  local copies, waits for them, and re-layouts  7.16 us (3%)
    pallas_call x1, Pallas kernels, attend(): pl.pallas_call(functools.partial(attend_kernel, n_src=n_src, n_slot=n_slo...  30.8 us
    ppermute x7, waiting for transfers between devices, body(): lax.ppermute(dx[s], 'lang', [(i, (i + s) % n_lang) for i in range(n_lang)])  26.8 us
    all_to_all x1, waiting for transfers between devices, body(): lax.all_to_all(outgoing, 'lang', split_axis=0, concat_axis=0, tiled=True)  26.3 us
    all_to_all x1, waiting for transfers between devices, body(): lax.all_to_all(chip, 'pair', split_axis=0, concat_axis=0, tiled=True)  18.1 us
    all_to_all x1, waiting for transfers between devices, body(): lax.all_to_all(spread(rings, n_pair, factor), 'pair', split_axis=0, conca...  12.4 us
    all_to_all x1, starting transfers between devices, body(): lax.all_to_all(spread(rings, n_pair, factor), 'pair', split_axis=0, conca...  11.2 us
    ppermute x3, waiting for transfers between devices, body(): lax.ppermute(plane, 'lang', [(i, (i + 2 * y) % n_lang) for i in range(n_l...  9.93 us
    ppermute x7, starting transfers between devices, body(): lax.ppermute(dx[s], 'lang', [(i, (i + s) % n_lang) for i in range(n_lang)])  9.78 us
  transfers between devices with their start and end apart: 15, of which 13 were waited for; matrix products, arithmetic and copies ran while one was open for 0% of the time, Pallas kernels for 11%

profile of v11, /device:TPU:1, one launch (start us, length us, event | category | flops | bytes accessed | tf_op | source)
XLA Modules:
  0.0 205.7 jit_solution(11332232744096194219)
XLA Ops:
  0.6 3.3 %pick.1 = bf16[8,128,1024]{2,1,0:T(8,128)(2,1)} custom-call(s32[8]{0:T(128)} %bitcast.12, bf16[4,128,1024]{2,1,0:T(8,128)(2,1)} %x_hbm.1), custom_call_target="tpu_custom_call" | custom-call | tf_op jit(solution)/shard_map/pick/pallas_call | solution.py:376
  3.9 6.0 %all-to-all-start = ((bf16[8,128,1024]{2,1,0:T(8,128)(2,1)}), bf16[8,128,1024]{2,1,0:T(8,128)(2,1)S(1)}, u32[]{:S(2)}, u32[]{:S(2)}) async-start(bf16[8,128,1024]{2,1,0:T(8,128)(2,1)} %pick.1), calls=%async_computation | async-start | bytes 4194304 | tf_op jit(solution)/shard_map/all_to_all | solution.py:458
  9.9 26.3 %all-to-all-done.r_hbm = bf16[8,128,1024]{2,1,0:T(8,128)(2,1)S(1)} async-done(((bf16[8,128,1024]{2,1,0:T(8,128)(2,1)}), bf16[8,128,1024]{2,1,0:T(8,128)(2,1)S(1)}, u32[]{:S(2)}, u32[]{:S(2)}) %all-to-all-start) | async-done | bytes 2097184 | tf_op jit(solution)/shard_map/all_to_all | solution.py:458
  36.2 1.3 copy-done.3
  37.5 30.8 %attend.1 = (bf16[512,1024]{1,0:T(8,128)(2,1)}, bf16[512,1024]{1,0:T(8,128)(2,1)}, bf16[512,512]{1,0:T(8,128)(2,1)}, bf16[512,1024]{1,0:T(8,128)(2,1)}, bf16[16,...) custom-call(s32[1]{0:T(128)} %bitcast.me_ref, s32[1,16]{1,0:T(1,128)} %src_ref.1, ...), custom_call_target="tpu_custom_call" | custom-call | flops 26306674688 | bytes 20971520 | tf_op jit(solution)/shard_map/attend/pallas_call | solution.py:185
  68.4 0.3 collective-permute-start
  68.6 6.0 %keep_grads.1.a_ref = bf16[16,3,32,1024]{3,2,1,0:T(8,128)(2,1)} custom-call(bf16[512,512]{1,0:T(8,128)(2,1)} %get-tuple-element.39.x_hbm, bf16[512,1024]{1,0:T(8,128)(2,1)} %get-tuple-element.40.r_hbm, bf16[512,1024]{1,0:T(8,128)(2,1)} %get-tuple-element.41.dq_hbm, bf16[8,128,1024]{2,1,0:T(8,128)(2,1)} %get-tuple-element.47.dk_hbm, ...), custom_call_target="tpu_custom_call" | custom-call | flops 2684354560 | bytes 10485760 | tf_op jit(solution)/shard_map/keep_grads/pallas_call | solution.py:240
  74.7 0.0 collective-permute-done.b_ref
  74.7 0.0 copy-start
  74.7 1.9 copy-done
  76.6 0.8 add.1
  77.4 0.0 copy-start.2
  77.4 1.6 copy-done.2
  79.0 7.1 %all-to-all-start.1 = ((bf16[16,3,32,1024]{3,2,1,0:T(8,128)(2,1)}), bf16[16,3,32,1024]{3,2,1,0:T(8,128)(2,1)S(1)}, u32[]{:S(2)}, u32[]{:S(2)}) async-start(bf16[16,3,32,1024]{3,2,1,0:T(8,128)(2,1)} %copy-done.2), calls=%async_computation.1 | async-start | bytes 6291456 | tf_op jit(solution)/shard_map/all_to_all | solution.py:474
  86.1 7.9 %input_grads.1 = (bf16[128,1024]{1,0:T(8,128)(2,1)}, bf16[128,1024]{1,0:T(8,128)(2,1)}, bf16[128,1024]{1,0:T(8,128)(2,1)}, bf16[128,1024]{1,0:T(8,128)(2,1)}, bf...) custom-call(bf16[8,128,1024]{2,1,0:T(8,128)(2,1)} %get-tuple-element, ...), custom_call_target="tpu_custom_call" | custom-call | flops 4294967296 | bytes 10485760 | tf_op jit(solution)/shard_map/input_grads/pallas_call | solution.py:286
  94.0 0.7 collective-permute-start.1
  94.7 0.5 collective-permute-start.2
  95.1 3.4 %collective-permute-start.3 = (bf16[128,1024]{1,0:T(8,128)(2,1)}, bf16[128,1024]{1,0:T(8,128)(2,1)}, u32[]{:S(2)}, u32[]{:S(2)}) collective-permute-start(bf16[128,1024]{1,0:T(8,128)(2,1)} %get-tuple-element.51), channel_id=1, source_target_pairs={{0,48},{16,64},{32,80},{48,96},{64,112},{80,0},{96,16},{112,32},{1... | collective-permute-start | bytes 786440 | tf_op jit(solution)/shard_map/ppermute | solution.py:473
  98.5 1.8 collective-permute-done.1.rest_1_
  100.3 8.5 %collective-permute-done.2.rest_2_ = bf16[128,1024]{1,0:T(8,128)(2,1)S(1)} collective-permute-done((bf16[128,1024]{1,0:T(8,128)(2,1)}, bf16[128,1024]{1,0:T(8,128)(2,1)S(1)}, u32[]{:S(2)}, u32[]{:S(2)}) %collective-permute-start.2) | collective-permute-done | bytes 262176 | tf_op jit(solution)/shard_map/ppermute | solution.py:473
  108.8 0.7 copy-done.5
  109.5 0.0 collective-permute-done.3.rest_3_
  109.6 18.1 %all-to-all-done.1.parts_ref = bf16[16,3,32,1024]{3,2,1,0:T(8,128)(2,1)S(1)} async-done(((bf16[16,3,32,1024]{3,2,1,0:T(8,128)(2,1)}), bf16[16,3,32,1024]{3,2,1,0:T(8,128)(2,1)S(1)}, u32[]{:S(2)}, u32[]{:S(2)}) %all-to-all-start.1) | async-done | bytes 3145760 | tf_op jit(solution)/shard_map/all_to_all | solution.py:474
  127.7 0.7 sum_parts.1.a_ref
  128.4 1.2 collective-permute-start.6
  129.6 1.1 collective-permute-start.5
  130.7 0.0 collective-permute-start.4
  130.7 2.2 %collective-permute-done.6.d_ref = bf16[3,32,1024]{2,1,0:T(8,128)(2,1)S(1)} collective-permute-done((bf16[3,32,1024]{2,1,0:T(8,128)(2,1)S(1)}, bf16[3,32,1024]{2,1,0:T(8,128)(2,1)S(1)}, u32[]{:S(2)}, u32[]{:S(2)}) %collective-permute-start.6) | collective-permute-done | bytes 196640 | tf_op jit(solution)/shard_map/ppermute | solution.py:479
  133.0 2.8 %collective-permute-done.5.c_ref = bf16[3,32,1024]{2,1,0:T(8,128)(2,1)S(1)} collective-permute-done((bf16[3,32,1024]{2,1,0:T(8,128)(2,1)S(1)}, bf16[3,32,1024]{2,1,0:T(8,128)(2,1)S(1)}, u32[]{:S(2)}, u32[]{:S(2)}) %collective-permute-start.5) | collective-permute-done | bytes 196640 | tf_op jit(solution)/shard_map/ppermute | solution.py:479
  135.7 4.9 %collective-permute-done.4.b_ref = bf16[3,32,1024]{2,1,0:T(8,128)(2,1)S(1)} collective-permute-done((bf16[3,32,1024]{2,1,0:T(8,128)(2,1)S(1)}, bf16[3,32,1024]{2,1,0:T(8,128)(2,1)S(1)}, u32[]{:S(2)}, u32[]{:S(2)}) %collective-permute-start.4) | collective-permute-done | bytes 196640 | tf_op jit(solution)/shard_map/ppermute | solution.py:479
  140.6 0.6 spread.1
  141.3 1.6 copy-done.1
  142.9 11.2 %all-to-all-start.2 = ((bf16[16,3,32,1024]{3,2,1,0:T(8,128)(2,1)}), bf16[16,3,32,1024]{3,2,1,0:T(8,128)(2,1)S(1)}, u32[]{:S(2)}, u32[]{:S(2)}) async-start(bf16[16,3,32,1024]{3,2,1,0:T(8,128)(2,1)} %copy-done.1), calls=%async_computation.2 | async-start | bytes 6291456 | tf_op jit(solution)/shard_map/all_to_all | solution.py:481
  154.1 1.5 collective-permute-start.7
  155.6 3.3 %collective-permute-start.8 = (bf16[128,1024]{1,0:T(8,128)(2,1)}, bf16[128,1024]{1,0:T(8,128)(2,1)S(1)}, u32[]{:S(2)}, u32[]{:S(2)}) collective-permute-start(bf16[128,1024]{1,0:T(8,128)(2,1)} %get-tuple-element.58), channel_id=1, source_target_pairs={{0,80},{16,96},{32,112},{48,0},{64,16},{80,32},{96,48},{112,64},{1... | collective-permute-start | bytes 786440 | tf_op jit(solution)/shard_map/ppermute | solution.py:473
  158.9 0.2 collective-permute-start.9
  159.1 0.3 collective-permute-start.10
  159.4 2.9 %collective-permute-done.7.rest_4_ = bf16[128,1024]{1,0:T(8,128)(2,1)S(1)} collective-permute-done((bf16[128,1024]{1,0:T(8,128)(2,1)}, bf16[128,1024]{1,0:T(8,128)(2,1)S(1)}, u32[]{:S(2)}, u32[]{:S(2)}) %collective-permute-start.7) | collective-permute-done | bytes 262176 | tf_op jit(solution)/shard_map/ppermute | solution.py:473
  162.3 6.8 %collective-permute-done.8.rest_5_ = bf16[128,1024]{1,0:T(8,128)(2,1)S(1)} collective-permute-done((bf16[128,1024]{1,0:T(8,128)(2,1)}, bf16[128,1024]{1,0:T(8,128)(2,1)S(1)}, u32[]{:S(2)}, u32[]{:S(2)}) %collective-permute-start.8) | collective-permute-done | bytes 262176 | tf_op jit(solution)/shard_map/ppermute | solution.py:473
  169.1 5.8 %collective-permute-done.9.rest_6_ = bf16[128,1024]{1,0:T(8,128)(2,1)S(1)} collective-permute-done((bf16[128,1024]{1,0:T(8,128)(2,1)}, bf16[128,1024]{1,0:T(8,128)(2,1)S(1)}, u32[]{:S(2)}, u32[]{:S(2)}) %collective-permute-start.9) | collective-permute-done | bytes 262176 | tf_op jit(solution)/shard_map/ppermute | solution.py:473
  174.8 1.0 collective-permute-done.10.rest_7_
  175.9 0.0 copy-done.6
  175.9 6.1 %combine.1 = bf16[4,128,1024]{2,1,0:T(8,128)(2,1)} custom-call(s32[1]{0:T(128)} %bitcast.me_ref, s32[8]{0:T(128)} %bitcast.13, bf16[512,1024]{1,0:T(8,128)(2,1)} %get-tuple-element.41.dq_hbm, bf16[1024,1024]{1,0:T(8,128)(2,1)} %wq_hbm.3, bf16[128,1024]{1,0:T(8,128)(2,1)} %get-tuple-element.53.rest_0_, bf16[128,1024]{1,0:T(8,128)(2,1)} %copy-done.4, ...), custom_call_target="tpu_custom_call" | custom-call | flops 1073741824 | bytes 6291456 | tf_op jit(solution)/shard_map/combine/pallas_call | solution.py:346
  182.0 12.4 %all-to-all-done.2.rows_ref = bf16[16,3,32,1024]{3,2,1,0:T(8,128)(2,1)S(1)} async-done(((bf16[16,3,32,1024]{3,2,1,0:T(8,128)(2,1)}), bf16[16,3,32,1024]{3,2,1,0:T(8,128)(2,1)S(1)}, u32[]{:S(2)}, u32[]{:S(2)}) %all-to-all-start.2) | async-done | bytes 3145760 | tf_op jit(solution)/shard_map/all_to_all | solution.py:481
  194.4 3.9 %collective-permute-start.11 = (bf16[16,3,32,1024]{3,2,1,0:T(8,128)(2,1)S(1)}, bf16[16,3,32,1024]{3,2,1,0:T(8,128)(2,1)S(1)}, u32[]{:S(2)}, u32[]{:S(2)}) collective-permute-start(bf16[16,3,32,1024]{3,2,1,0:T(8,128)(2,1)S(1)} %all-to-all-done.2.rows_ref), channel_id=1, source_target_pairs={{0,16},{16,0},{32,48},{48,32},{64,80},{80,64},{96,112},{112,96},{1... | collective-permute-start | bytes 9437192 | tf_op jit(solution)/shard_map/ppermute | solution.py:484
  198.3 2.1 %place.2 = (bf16[2,16,32,1024]{3,2,1,0:T(8,128)(2,1)}, bf16[2,16,32,1024]{3,2,1,0:T(8,128)(2,1)}, bf16[2,16,32,1024]{3,2,1,0:T(8,128)(2,1)}) custom-call(s32[1]{0:T(128)S(6)} %rem.18.half_ref, bf16[16,3,32,1024]{3,2,1,0:T(8,128)(2,1)S(1)} %all-to-all-done.2.rows_ref), custom_call_target="tpu_custom_call" | custom-call | bytes 6291456 | tf_op jit(solution)/shard_map/place/pallas_call | solution.py:435
  200.4 3.2 %collective-permute-done.11.rows_ref = bf16[16,3,32,1024]{3,2,1,0:T(8,128)(2,1)S(1)} collective-permute-done((bf16[16,3,32,1024]{3,2,1,0:T(8,128)(2,1)S(1)}, bf16[16,3,32,1024]{3,2,1,0:T(8,128)(2,1)S(1)}, u32[]{:S(2)}, u32[]{:S(2)}) %collective-permute-start.11) | collective-permute-done | bytes 3145760 | tf_op jit(solution)/shard_map/ppermute | solution.py:484
  203.6 2.1 %place.3 = (bf16[2,16,32,1024]{3,2,1,0:T(8,128)(2,1)}, bf16[2,16,32,1024]{3,2,1,0:T(8,128)(2,1)}, bf16[2,16,32,1024]{3,2,1,0:T(8,128)(2,1)}) custom-call(s32[1]{0:T(128)S(6)} %sub.3.half_ref, bf16[16,3,32,1024]{3,2,1,0:T(8,128)(2,1)S(1)} %collective-permute-done.11.rows_ref, ...), custom_call_target="tpu_custom_call", output_to_operand_aliasing={{0}: (2, {}), {1}: (3, {}), {2}: (4, {})} | custom-call | bytes 6291456 | tf_op jit(solution)/shard_map/place/pallas_call | solution.py:435
  (10 shorter events, 0.0 us)
Async XLA Ops:
  3.9 32.3 %all-to-all-start = ((bf16[8,128,1024]{2,1,0:T(8,128)(2,1)}), bf16[8,128,1024]{2,1,0:T(8,128)(2,1)S(1)}, u32[]{:S(2)}, u32[]{:S(2)}) async-start(bf16[8,128,1024]{2,1,0:T(8,128)(2,1)} %pick.1), calls=%async_computation | async-start | bytes 4194304 | tf_op jit(solution)/shard_map/all_to_all | solution.py:458
  36.2 1.3 copy-start.3
  68.4 6.3 %collective-permute-start = (bf16[16,3,32,1024]{3,2,1,0:T(8,128)(2,1)}, bf16[16,3,32,1024]{3,2,1,0:T(8,128)(2,1)S(1)}, u32[]{:S(2)}, u32[]{:S(2)}) collective-permute-start(bf16[16,3,32,1024]{3,2,1,0:T(8,128)(2,1)} %get-tuple-element.38), channel_id=1, source_target_pairs={{0,16},{16,0},{32,48},{48,32},{64,80},{80,64},{96,112},{112,96},{1... | collective-permute-start | bytes 9437192 | tf_op jit(solution)/shard_map/ppermute | solution.py:466
  74.7 1.9 copy-start
  77.4 1.6 copy-start.2
  79.0 48.7 %all-to-all-start.1 = ((bf16[16,3,32,1024]{3,2,1,0:T(8,128)(2,1)}), bf16[16,3,32,1024]{3,2,1,0:T(8,128)(2,1)S(1)}, u32[]{:S(2)}, u32[]{:S(2)}) async-start(bf16[16,3,32,1024]{3,2,1,0:T(8,128)(2,1)} %copy-done.2), calls=%async_computation.1 | async-start | bytes 6291456 | tf_op jit(solution)/shard_map/all_to_all | solution.py:474
  94.0 6.3 %collective-permute-start.1 = (bf16[128,1024]{1,0:T(8,128)(2,1)}, bf16[128,1024]{1,0:T(8,128)(2,1)S(1)}, u32[]{:S(2)}, u32[]{:S(2)}) collective-permute-start(bf16[128,1024]{1,0:T(8,128)(2,1)} %get-tuple-element.49), channel_id=1, source_target_pairs={{0,16},{16,32},{32,48},{48,64},{64,80},{80,96},{96,112},{112,0},{1... | collective-permute-start | bytes 786440 | tf_op jit(solution)/shard_map/ppermute | solution.py:473
  94.7 14.2 %collective-permute-start.2 = (bf16[128,1024]{1,0:T(8,128)(2,1)}, bf16[128,1024]{1,0:T(8,128)(2,1)S(1)}, u32[]{:S(2)}, u32[]{:S(2)}) collective-permute-start(bf16[128,1024]{1,0:T(8,128)(2,1)} %get-tuple-element.50), channel_id=1, source_target_pairs={{0,32},{16,48},{32,64},{48,80},{64,96},{80,112},{96,0},{112,16},{1... | collective-permute-start | bytes 786440 | tf_op jit(solution)/shard_map/ppermute | solution.py:473
  95.1 14.4 %collective-permute-start.3 = (bf16[128,1024]{1,0:T(8,128)(2,1)}, bf16[128,1024]{1,0:T(8,128)(2,1)}, u32[]{:S(2)}, u32[]{:S(2)}) collective-permute-start(bf16[128,1024]{1,0:T(8,128)(2,1)} %get-tuple-element.51), channel_id=1, source_target_pairs={{0,48},{16,64},{32,80},{48,96},{64,112},{80,0},{96,16},{112,32},{1... | collective-permute-start | bytes 786440 | tf_op jit(solution)/shard_map/ppermute | solution.py:473
  100.3 40.9 %copy-start.4 = (bf16[128,1024]{1,0:T(8,128)(2,1)}, bf16[128,1024]{1,0:T(8,128)(2,1)S(1)}, u32[]{:S(2)}) copy-start(bf16[128,1024]{1,0:T(8,128)(2,1)S(1)} %collective-permute-done.1.rest_1_) | copy-start | bytes 786436
  108.8 0.7 copy-start.5
  128.4 4.6 %collective-permute-start.6 = (bf16[3,32,1024]{2,1,0:T(8,128)(2,1)S(1)}, bf16[3,32,1024]{2,1,0:T(8,128)(2,1)S(1)}, u32[]{:S(2)}, u32[]{:S(2)}) collective-permute-start(bf16[3,32,1024]{2,1,0:T(8,128)(2,1)S(1)} %sum_parts.1.a_ref), channel_id=1, source_target_pairs={{0,96},{16,112},{32,0},{48,16},{64,32},{80,48},{96,64},{112,80},{1... | collective-permute-start | bytes 589832 | tf_op jit(solution)/shard_map/ppermute | solution.py:479
  129.6 6.1 %collective-permute-start.5 = (bf16[3,32,1024]{2,1,0:T(8,128)(2,1)S(1)}, bf16[3,32,1024]{2,1,0:T(8,128)(2,1)S(1)}, u32[]{:S(2)}, u32[]{:S(2)}) collective-permute-start(bf16[3,32,1024]{2,1,0:T(8,128)(2,1)S(1)} %sum_parts.1.a_ref), channel_id=1, source_target_pairs={{0,64},{16,80},{32,96},{48,112},{64,0},{80,16},{96,32},{112,48},{1... | collective-permute-start | bytes 589832 | tf_op jit(solution)/shard_map/ppermute | solution.py:479
  130.7 9.9 %collective-permute-start.4 = (bf16[3,32,1024]{2,1,0:T(8,128)(2,1)S(1)}, bf16[3,32,1024]{2,1,0:T(8,128)(2,1)S(1)}, u32[]{:S(2)}, u32[]{:S(2)}) collective-permute-start(bf16[3,32,1024]{2,1,0:T(8,128)(2,1)S(1)} %sum_parts.1.a_ref), channel_id=1, source_target_pairs={{0,32},{16,48},{32,64},{48,80},{64,96},{80,112},{96,0},{112,16},{1... | collective-permute-start | bytes 589832 | tf_op jit(solution)/shard_map/ppermute | solution.py:479
  141.3 1.6 copy-start.1
  142.9 51.4 %all-to-all-start.2 = ((bf16[16,3,32,1024]{3,2,1,0:T(8,128)(2,1)}), bf16[16,3,32,1024]{3,2,1,0:T(8,128)(2,1)S(1)}, u32[]{:S(2)}, u32[]{:S(2)}) async-start(bf16[16,3,32,1024]{3,2,1,0:T(8,128)(2,1)} %copy-done.1), calls=%async_computation.2 | async-start | bytes 6291456 | tf_op jit(solution)/shard_map/all_to_all | solution.py:481
  154.1 8.1 %collective-permute-start.7 = (bf16[128,1024]{1,0:T(8,128)(2,1)}, bf16[128,1024]{1,0:T(8,128)(2,1)S(1)}, u32[]{:S(2)}, u32[]{:S(2)}) collective-permute-start(bf16[128,1024]{1,0:T(8,128)(2,1)} %get-tuple-element.57), channel_id=1, source_target_pairs={{0,64},{16,80},{32,96},{48,112},{64,0},{80,16},{96,32},{112,48},{1... | collective-permute-start | bytes 786440 | tf_op jit(solution)/shard_map/ppermute | solution.py:473
  155.6 13.5 %collective-permute-start.8 = (bf16[128,1024]{1,0:T(8,128)(2,1)}, bf16[128,1024]{1,0:T(8,128)(2,1)S(1)}, u32[]{:S(2)}, u32[]{:S(2)}) collective-permute-start(bf16[128,1024]{1,0:T(8,128)(2,1)} %get-tuple-element.58), channel_id=1, source_target_pairs={{0,80},{16,96},{32,112},{48,0},{64,16},{80,32},{96,48},{112,64},{1... | collective-permute-start | bytes 786440 | tf_op jit(solution)/shard_map/ppermute | solution.py:473
  158.9 15.9 %collective-permute-start.9 = (bf16[128,1024]{1,0:T(8,128)(2,1)}, bf16[128,1024]{1,0:T(8,128)(2,1)S(1)}, u32[]{:S(2)}, u32[]{:S(2)}) collective-permute-start(bf16[128,1024]{1,0:T(8,128)(2,1)} %get-tuple-element.59), channel_id=1, source_target_pairs={{0,96},{16,112},{32,0},{48,16},{64,32},{80,48},{96,64},{112,80},{1... | collective-permute-start | bytes 786440 | tf_op jit(solution)/shard_map/ppermute | solution.py:473
  159.1 16.8 %collective-permute-start.10 = (bf16[128,1024]{1,0:T(8,128)(2,1)}, bf16[128,1024]{1,0:T(8,128)(2,1)}, u32[]{:S(2)}, u32[]{:S(2)}) collective-permute-start(bf16[128,1024]{1,0:T(8,128)(2,1)} %get-tuple-element.60), channel_id=1, source_target_pairs={{0,112},{16,0},{32,16},{48,32},{64,48},{80,64},{96,80},{112,96},{1... | collective-permute-start | bytes 786440 | tf_op jit(solution)/shard_map/ppermute | solution.py:473
  162.3 13.6 %copy-start.6 = (bf16[128,1024]{1,0:T(8,128)(2,1)}, bf16[128,1024]{1,0:T(8,128)(2,1)S(1)}, u32[]{:S(2)}) copy-start(bf16[128,1024]{1,0:T(8,128)(2,1)S(1)} %collective-permute-done.7.rest_4_) | copy-start | bytes 786436
  169.1 6.8 %copy-start.7 = (bf16[128,1024]{1,0:T(8,128)(2,1)}, bf16[128,1024]{1,0:T(8,128)(2,1)S(1)}, u32[]{:S(2)}) copy-start(bf16[128,1024]{1,0:T(8,128)(2,1)S(1)} %collective-permute-done.8.rest_5_) | copy-start | bytes 786436
  174.8 1.0 copy-start.8
  194.4 9.2 %collective-permute-start.11 = (bf16[16,3,32,1024]{3,2,1,0:T(8,128)(2,1)S(1)}, bf16[16,3,32,1024]{3,2,1,0:T(8,128)(2,1)S(1)}, u32[]{:S(2)}, u32[]{:S(2)}) collective-permute-start(bf16[16,3,32,1024]{3,2,1,0:T(8,128)(2,1)S(1)} %all-to-all-done.2.rows_ref), channel_id=1, source_target_pairs={{0,16},{16,0},{32,48},{48,32},{64,80},{80,64},{96,112},{112,96},{1... | collective-permute-start | bytes 9437192 | tf_op jit(solution)/shard_map/ppermute | solution.py:484

commit v12 on v11

--- a/solution.py
+++ b/solution.py
@@ -159,11 +159,11 @@
     out(v_s, dv_hbm)
     out(xt.at[own, :], xk_hbm)
     out(rt.at[own, :], rk_hbm)
-    for n in range(0, width, block):
-        cols = slice(n, n + block)
-        for i, (lhs, rhs) in enumerate(((xt, dq_v[:, cols]), (rt, dk[:, cols]), (rt, dv[:, cols]))):
-            gw_v[:, i, :, cols] = mm(lhs[rows, :], rhs).astype(BF).reshape(pieces, each, block)
-    out(gw_v, send_hbm)
+    for i, (lhs, rhs) in enumerate(((xt, dq_v), (rt, dk), (rt, dv))):
+        for n in range(0, width, block):
+            cols = slice(n, n + block)
+            gw_v[:, i, :, cols] = mm(lhs[rows, :], rhs[:, cols]).astype(BF).reshape(pieces, each, block)
+        out(gw_v.at[:, i], send_hbm.at[:, i])
     for s in range(n_src):
         att_v[s * length:(s + 1) * length, :] = ot[s].T.astype(BF)
     out(att_v, att_hbm)
@@ -203,7 +203,7 @@
             vm((n_src, width, length), F32), vm((n_src, width, length), F32),
             vm((n_slot, length, width), F32), vm((n_slot, length, width), F32),
             pltpu.SemaphoreType.DMA((5,)), pltpu.SemaphoreType.DMA((n_slot,)),
-            pltpu.SemaphoreType.DMA((7,)),
+            pltpu.SemaphoreType.DMA((9,)),
         ],
         compiler_params=pltpu.CompilerParams(vmem_limit_bytes=60 * 2**20),
         cost_estimate=pl.CostEstimate(flops=4 * macs, bytes_accessed=20 * 2**20, transcendentals=0),

time: 207 us -> 207 us (level)
  Pallas kernels: 60.4 us -> 54.5 us
  starting transfers between devices: 40.6 us -> 46 us
  waiting for transfers between devices: 96.7 us -> 98.8 us
    pallas_call x1, Pallas kernels: 30.8 us -> 24.9 us  [attend(): pl.pallas_call(functools.partial(attend_kernel, n_src=n_src, n_slot=n_slo...]
    ppermute x1, starting transfers between devices: 0.27 us -> 4.61 us  [body(): other = lax.ppermute(send, 'lang', other_core)]
  transfers between devices with their start and end apart: 15 -> 15, of which waited for: 13 -> 14; matrix products, arithmetic and copies ran while one was open for 0% -> 0% of each run, Pallas kernels for 11% -> 11%
where the time goes in v12:
time: 207 us
  waiting for transfers between devices  98.8 us (48%)
  Pallas kernels  54.5 us (26%)
  starting transfers between devices  46 us (22%)
  local copies, waits for them, and re-layouts  7.16 us (3%)
    ppermute x7, waiting for transfers between devices, body(): lax.ppermute(dx[s], 'lang', [(i, (i + s) % n_lang) for i in range(n_lang)])  28.1 us
    all_to_all x1, waiting for transfers between devices, body(): lax.all_to_all(outgoing, 'lang', split_axis=0, concat_axis=0, tiled=True)  26.3 us
    pallas_call x1, Pallas kernels, attend(): pl.pallas_call(functools.partial(attend_kernel, n_src=n_src, n_slot=n_slo...  24.9 us
    all_to_all x1, waiting for transfers between devices, body(): lax.all_to_all(chip, 'pair', split_axis=0, concat_axis=0, tiled=True)  17.4 us
    all_to_all x1, waiting for transfers between devices, body(): lax.all_to_all(spread(rings, n_pair, factor), 'pair', split_axis=0, conca...  13.1 us
    all_to_all x1, starting transfers between devices, body(): lax.all_to_all(spread(rings, n_pair, factor), 'pair', split_axis=0, conca...  12 us
    ppermute x3, waiting for transfers between devices, body(): lax.ppermute(plane, 'lang', [(i, (i + 2 * y) % n_lang) for i in range(n_l...  10.7 us
    ppermute x7, starting transfers between devices, body(): lax.ppermute(dx[s], 'lang', [(i, (i + s) % n_lang) for i in range(n_lang)])  8.66 us
  transfers between devices with their start and end apart: 15, of which 14 were waited for; matrix products, arithmetic and copies ran while one was open for 0% of the time, Pallas kernels for 11%

profile of v12, /device:TPU:1, one launch (start us, length us, event | category | flops | bytes accessed | tf_op | source)
XLA Modules:
  0.0 207.3 jit_solution(12463974072843237815)
XLA Ops:
  0.6 3.3 %pick.1 = bf16[8,128,1024]{2,1,0:T(8,128)(2,1)} custom-call(s32[8]{0:T(128)} %bitcast.12, bf16[4,128,1024]{2,1,0:T(8,128)(2,1)} %x_hbm.1), custom_call_target="tpu_custom_call" | custom-call | tf_op jit(solution)/shard_map/pick/pallas_call | solution.py:376
  3.9 6.0 %all-to-all-start = ((bf16[8,128,1024]{2,1,0:T(8,128)(2,1)}), bf16[8,128,1024]{2,1,0:T(8,128)(2,1)S(1)}, u32[]{:S(2)}, u32[]{:S(2)}) async-start(bf16[8,128,1024]{2,1,0:T(8,128)(2,1)} %pick.1), calls=%async_computation | async-start | bytes 4194304 | tf_op jit(solution)/shard_map/all_to_all | solution.py:458
  9.9 26.3 %all-to-all-done.r_hbm = bf16[8,128,1024]{2,1,0:T(8,128)(2,1)S(1)} async-done(((bf16[8,128,1024]{2,1,0:T(8,128)(2,1)}), bf16[8,128,1024]{2,1,0:T(8,128)(2,1)S(1)}, u32[]{:S(2)}, u32[]{:S(2)}) %all-to-all-start) | async-done | bytes 2097184 | tf_op jit(solution)/shard_map/all_to_all | solution.py:458
  36.2 1.3 copy-done.3
  37.5 24.9 %attend.1 = (bf16[512,1024]{1,0:T(8,128)(2,1)}, bf16[512,1024]{1,0:T(8,128)(2,1)}, bf16[512,512]{1,0:T(8,128)(2,1)}, bf16[512,1024]{1,0:T(8,128)(2,1)}, bf16[16,...) custom-call(s32[1]{0:T(128)} %bitcast.me_ref, s32[1,16]{1,0:T(1,128)} %src_ref.1, ...), custom_call_target="tpu_custom_call" | custom-call | flops 26306674688 | bytes 20971520 | tf_op jit(solution)/shard_map/attend/pallas_call | solution.py:185
  62.5 4.6 %collective-permute-start = (bf16[16,3,32,1024]{3,2,1,0:T(8,128)(2,1)}, bf16[16,3,32,1024]{3,2,1,0:T(8,128)(2,1)S(1)}, u32[]{:S(2)}, u32[]{:S(2)}) collective-permute-start(bf16[16,3,32,1024]{3,2,1,0:T(8,128)(2,1)} %get-tuple-element.38), channel_id=1, source_target_pairs={{0,16},{16,0},{32,48},{48,32},{64,80},{80,64},{96,112},{112,96},{1... | collective-permute-start | bytes 9437192 | tf_op jit(solution)/shard_map/ppermute | solution.py:466
  67.1 6.0 %keep_grads.1.a_ref = bf16[16,3,32,1024]{3,2,1,0:T(8,128)(2,1)} custom-call(bf16[512,512]{1,0:T(8,128)(2,1)} %get-tuple-element.39.x_hbm, bf16[512,1024]{1,0:T(8,128)(2,1)} %get-tuple-element.40.r_hbm, bf16[512,1024]{1,0:T(8,128)(2,1)} %get-tuple-element.41.dq_hbm, bf16[8,128,1024]{2,1,0:T(8,128)(2,1)} %get-tuple-element.47.dk_hbm, ...), custom_call_target="tpu_custom_call" | custom-call | flops 2684354560 | bytes 10485760 | tf_op jit(solution)/shard_map/keep_grads/pallas_call | solution.py:240
  73.1 0.0 collective-permute-done.b_ref
  73.1 0.0 copy-start
  73.2 1.9 copy-done
  75.0 0.8 add.1
  75.8 0.0 copy-start.2
  75.8 1.6 copy-done.2
  77.4 8.4 %all-to-all-start.1 = ((bf16[16,3,32,1024]{3,2,1,0:T(8,128)(2,1)}), bf16[16,3,32,1024]{3,2,1,0:T(8,128)(2,1)S(1)}, u32[]{:S(2)}, u32[]{:S(2)}) async-start(bf16[16,3,32,1024]{3,2,1,0:T(8,128)(2,1)} %copy-done.2), calls=%async_computation.1 | async-start | bytes 6291456 | tf_op jit(solution)/shard_map/all_to_all | solution.py:474
  85.8 7.9 %input_grads.1 = (bf16[128,1024]{1,0:T(8,128)(2,1)}, bf16[128,1024]{1,0:T(8,128)(2,1)}, bf16[128,1024]{1,0:T(8,128)(2,1)}, bf16[128,1024]{1,0:T(8,128)(2,1)}, bf...) custom-call(bf16[8,128,1024]{2,1,0:T(8,128)(2,1)} %get-tuple-element, ...), custom_call_target="tpu_custom_call" | custom-call | flops 4294967296 | bytes 10485760 | tf_op jit(solution)/shard_map/input_grads/pallas_call | solution.py:286
  93.8 1.5 collective-permute-start.1
  95.2 0.0 collective-permute-start.2
  95.2 2.6 %collective-permute-start.3 = (bf16[128,1024]{1,0:T(8,128)(2,1)}, bf16[128,1024]{1,0:T(8,128)(2,1)}, u32[]{:S(2)}, u32[]{:S(2)}) collective-permute-start(bf16[128,1024]{1,0:T(8,128)(2,1)} %get-tuple-element.51), channel_id=1, source_target_pairs={{0,48},{16,64},{32,80},{48,96},{64,112},{80,0},{96,16},{112,32},{1... | collective-permute-start | bytes 786440 | tf_op jit(solution)/shard_map/ppermute | solution.py:473
  97.8 3.3 %collective-permute-done.1.rest_1_ = bf16[128,1024]{1,0:T(8,128)(2,1)S(1)} collective-permute-done((bf16[128,1024]{1,0:T(8,128)(2,1)}, bf16[128,1024]{1,0:T(8,128)(2,1)S(1)}, u32[]{:S(2)}, u32[]{:S(2)}) %collective-permute-start.1) | collective-permute-done | bytes 262176 | tf_op jit(solution)/shard_map/ppermute | solution.py:473
  101.1 7.5 %collective-permute-done.2.rest_2_ = bf16[128,1024]{1,0:T(8,128)(2,1)S(1)} collective-permute-done((bf16[128,1024]{1,0:T(8,128)(2,1)}, bf16[128,1024]{1,0:T(8,128)(2,1)S(1)}, u32[]{:S(2)}, u32[]{:S(2)}) %collective-permute-start.2) | collective-permute-done | bytes 262176 | tf_op jit(solution)/shard_map/ppermute | solution.py:473
  108.6 0.7 copy-done.5
  109.3 0.8 collective-permute-done.3.rest_3_
  110.1 17.4 %all-to-all-done.1.parts_ref = bf16[16,3,32,1024]{3,2,1,0:T(8,128)(2,1)S(1)} async-done(((bf16[16,3,32,1024]{3,2,1,0:T(8,128)(2,1)}), bf16[16,3,32,1024]{3,2,1,0:T(8,128)(2,1)S(1)}, u32[]{:S(2)}, u32[]{:S(2)}) %all-to-all-start.1) | async-done | bytes 3145760 | tf_op jit(solution)/shard_map/all_to_all | solution.py:474
  127.5 0.7 sum_parts.1.a_ref
  128.2 2.2 %collective-permute-start.6 = (bf16[3,32,1024]{2,1,0:T(8,128)(2,1)S(1)}, bf16[3,32,1024]{2,1,0:T(8,128)(2,1)S(1)}, u32[]{:S(2)}, u32[]{:S(2)}) collective-permute-start(bf16[3,32,1024]{2,1,0:T(8,128)(2,1)S(1)} %sum_parts.1.a_ref), channel_id=1, source_target_pairs={{0,96},{16,112},{32,0},{48,16},{64,32},{80,48},{96,64},{112,80},{1... | collective-permute-start | bytes 589832 | tf_op jit(solution)/shard_map/ppermute | solution.py:479
  130.4 0.0 collective-permute-start.5
  130.4 0.7 collective-permute-start.4
  131.1 3.6 %collective-permute-done.6.d_ref = bf16[3,32,1024]{2,1,0:T(8,128)(2,1)S(1)} collective-permute-done((bf16[3,32,1024]{2,1,0:T(8,128)(2,1)S(1)}, bf16[3,32,1024]{2,1,0:T(8,128)(2,1)S(1)}, u32[]{:S(2)}, u32[]{:S(2)}) %collective-permute-start.6) | collective-permute-done | bytes 196640 | tf_op jit(solution)/shard_map/ppermute | solution.py:479
  134.7 1.8 collective-permute-done.5.c_ref
  136.5 5.2 %collective-permute-done.4.b_ref = bf16[3,32,1024]{2,1,0:T(8,128)(2,1)S(1)} collective-permute-done((bf16[3,32,1024]{2,1,0:T(8,128)(2,1)S(1)}, bf16[3,32,1024]{2,1,0:T(8,128)(2,1)S(1)}, u32[]{:S(2)}, u32[]{:S(2)}) %collective-permute-start.4) | collective-permute-done | bytes 196640 | tf_op jit(solution)/shard_map/ppermute | solution.py:479
  141.8 0.6 spread.1
  142.4 1.6 copy-done.1
  144.0 12.0 %all-to-all-start.2 = ((bf16[16,3,32,1024]{3,2,1,0:T(8,128)(2,1)}), bf16[16,3,32,1024]{3,2,1,0:T(8,128)(2,1)S(1)}, u32[]{:S(2)}, u32[]{:S(2)}) async-start(bf16[16,3,32,1024]{3,2,1,0:T(8,128)(2,1)} %copy-done.1), calls=%async_computation.2 | async-start | bytes 6291456 | tf_op jit(solution)/shard_map/all_to_all | solution.py:481
  156.0 0.3 collective-permute-start.7
  156.3 2.3 %collective-permute-start.8 = (bf16[128,1024]{1,0:T(8,128)(2,1)}, bf16[128,1024]{1,0:T(8,128)(2,1)S(1)}, u32[]{:S(2)}, u32[]{:S(2)}) collective-permute-start(bf16[128,1024]{1,0:T(8,128)(2,1)} %get-tuple-element.58), channel_id=1, source_target_pairs={{0,80},{16,96},{32,112},{48,0},{64,16},{80,32},{96,48},{112,64},{1... | collective-permute-start | bytes 786440 | tf_op jit(solution)/shard_map/ppermute | solution.py:473
  158.6 2.1 collective-permute-start.9
  160.7 0.0 collective-permute-start.10
  160.7 3.8 %collective-permute-done.7.rest_4_ = bf16[128,1024]{1,0:T(8,128)(2,1)S(1)} collective-permute-done((bf16[128,1024]{1,0:T(8,128)(2,1)}, bf16[128,1024]{1,0:T(8,128)(2,1)S(1)}, u32[]{:S(2)}, u32[]{:S(2)}) %collective-permute-start.7) | collective-permute-done | bytes 262176 | tf_op jit(solution)/shard_map/ppermute | solution.py:473
  164.5 5.1 %collective-permute-done.8.rest_5_ = bf16[128,1024]{1,0:T(8,128)(2,1)S(1)} collective-permute-done((bf16[128,1024]{1,0:T(8,128)(2,1)}, bf16[128,1024]{1,0:T(8,128)(2,1)S(1)}, u32[]{:S(2)}, u32[]{:S(2)}) %collective-permute-start.8) | collective-permute-done | bytes 262176 | tf_op jit(solution)/shard_map/ppermute | solution.py:473
  169.5 6.3 %collective-permute-done.9.rest_6_ = bf16[128,1024]{1,0:T(8,128)(2,1)S(1)} collective-permute-done((bf16[128,1024]{1,0:T(8,128)(2,1)}, bf16[128,1024]{1,0:T(8,128)(2,1)S(1)}, u32[]{:S(2)}, u32[]{:S(2)}) %collective-permute-start.9) | collective-permute-done | bytes 262176 | tf_op jit(solution)/shard_map/ppermute | solution.py:473
  175.8 1.4 collective-permute-done.10.rest_7_
  177.2 0.0 copy-done.6
  177.2 6.1 %combine.1 = bf16[4,128,1024]{2,1,0:T(8,128)(2,1)} custom-call(s32[1]{0:T(128)} %bitcast.me_ref, s32[8]{0:T(128)} %bitcast.13, bf16[512,1024]{1,0:T(8,128)(2,1)} %get-tuple-element.41.dq_hbm, bf16[1024,1024]{1,0:T(8,128)(2,1)} %wq_hbm.3, bf16[128,1024]{1,0:T(8,128)(2,1)} %get-tuple-element.53.rest_0_, bf16[128,1024]{1,0:T(8,128)(2,1)} %copy-done.4, ...), custom_call_target="tpu_custom_call" | custom-call | flops 1073741824 | bytes 6291456 | tf_op jit(solution)/shard_map/combine/pallas_call | solution.py:346
  183.3 13.1 %all-to-all-done.2.rows_ref = bf16[16,3,32,1024]{3,2,1,0:T(8,128)(2,1)S(1)} async-done(((bf16[16,3,32,1024]{3,2,1,0:T(8,128)(2,1)}), bf16[16,3,32,1024]{3,2,1,0:T(8,128)(2,1)S(1)}, u32[]{:S(2)}, u32[]{:S(2)}) %all-to-all-start.2) | async-done | bytes 3145760 | tf_op jit(solution)/shard_map/all_to_all | solution.py:481
  196.4 3.5 %collective-permute-start.11 = (bf16[16,3,32,1024]{3,2,1,0:T(8,128)(2,1)S(1)}, bf16[16,3,32,1024]{3,2,1,0:T(8,128)(2,1)S(1)}, u32[]{:S(2)}, u32[]{:S(2)}) collective-permute-start(bf16[16,3,32,1024]{3,2,1,0:T(8,128)(2,1)S(1)} %all-to-all-done.2.rows_ref), channel_id=1, source_target_pairs={{0,16},{16,0},{32,48},{48,32},{64,80},{80,64},{96,112},{112,96},{1... | collective-permute-start | bytes 9437192 | tf_op jit(solution)/shard_map/ppermute | solution.py:484
  199.9 2.1 %place.2 = (bf16[2,16,32,1024]{3,2,1,0:T(8,128)(2,1)}, bf16[2,16,32,1024]{3,2,1,0:T(8,128)(2,1)}, bf16[2,16,32,1024]{3,2,1,0:T(8,128)(2,1)}) custom-call(s32[1]{0:T(128)S(6)} %rem.18.half_ref, bf16[16,3,32,1024]{3,2,1,0:T(8,128)(2,1)S(1)} %all-to-all-done.2.rows_ref), custom_call_target="tpu_custom_call" | custom-call | bytes 6291456 | tf_op jit(solution)/shard_map/place/pallas_call | solution.py:435
  202.0 3.2 %collective-permute-done.11.rows_ref = bf16[16,3,32,1024]{3,2,1,0:T(8,128)(2,1)S(1)} collective-permute-done((bf16[16,3,32,1024]{3,2,1,0:T(8,128)(2,1)S(1)}, bf16[16,3,32,1024]{3,2,1,0:T(8,128)(2,1)S(1)}, u32[]{:S(2)}, u32[]{:S(2)}) %collective-permute-start.11) | collective-permute-done | bytes 3145760 | tf_op jit(solution)/shard_map/ppermute | solution.py:484
  205.2 2.1 %place.3 = (bf16[2,16,32,1024]{3,2,1,0:T(8,128)(2,1)}, bf16[2,16,32,1024]{3,2,1,0:T(8,128)(2,1)}, bf16[2,16,32,1024]{3,2,1,0:T(8,128)(2,1)}) custom-call(s32[1]{0:T(128)S(6)} %sub.3.half_ref, bf16[16,3,32,1024]{3,2,1,0:T(8,128)(2,1)S(1)} %collective-permute-done.11.rows_ref, ...), custom_call_target="tpu_custom_call", output_to_operand_aliasing={{0}: (2, {}), {1}: (3, {}), {2}: (4, {})} | custom-call | bytes 6291456 | tf_op jit(solution)/shard_map/place/pallas_call | solution.py:435
  (10 shorter events, 0.0 us)
Async XLA Ops:
  3.9 32.3 %all-to-all-start = ((bf16[8,128,1024]{2,1,0:T(8,128)(2,1)}), bf16[8,128,1024]{2,1,0:T(8,128)(2,1)S(1)}, u32[]{:S(2)}, u32[]{:S(2)}) async-start(bf16[8,128,1024]{2,1,0:T(8,128)(2,1)} %pick.1), calls=%async_computation | async-start | bytes 4194304 | tf_op jit(solution)/shard_map/all_to_all | solution.py:458
  36.2 1.3 copy-start.3
  62.5 10.7 %collective-permute-start = (bf16[16,3,32,1024]{3,2,1,0:T(8,128)(2,1)}, bf16[16,3,32,1024]{3,2,1,0:T(8,128)(2,1)S(1)}, u32[]{:S(2)}, u32[]{:S(2)}) collective-permute-start(bf16[16,3,32,1024]{3,2,1,0:T(8,128)(2,1)} %get-tuple-element.38), channel_id=1, source_target_pairs={{0,16},{16,0},{32,48},{48,32},{64,80},{80,64},{96,112},{112,96},{1... | collective-permute-start | bytes 9437192 | tf_op jit(solution)/shard_map/ppermute | solution.py:466
  73.1 1.9 copy-start
  75.8 1.6 copy-start.2
  77.4 50.0 %all-to-all-start.1 = ((bf16[16,3,32,1024]{3,2,1,0:T(8,128)(2,1)}), bf16[16,3,32,1024]{3,2,1,0:T(8,128)(2,1)S(1)}, u32[]{:S(2)}, u32[]{:S(2)}) async-start(bf16[16,3,32,1024]{3,2,1,0:T(8,128)(2,1)} %copy-done.2), calls=%async_computation.1 | async-start | bytes 6291456 | tf_op jit(solution)/shard_map/all_to_all | solution.py:474
  93.8 7.3 %collective-permute-start.1 = (bf16[128,1024]{1,0:T(8,128)(2,1)}, bf16[128,1024]{1,0:T(8,128)(2,1)S(1)}, u32[]{:S(2)}, u32[]{:S(2)}) collective-permute-start(bf16[128,1024]{1,0:T(8,128)(2,1)} %get-tuple-element.49), channel_id=1, source_target_pairs={{0,16},{16,32},{32,48},{48,64},{64,80},{80,96},{96,112},{112,0},{1... | collective-permute-start | bytes 786440 | tf_op jit(solution)/shard_map/ppermute | solution.py:473
  95.2 13.3 %collective-permute-start.2 = (bf16[128,1024]{1,0:T(8,128)(2,1)}, bf16[128,1024]{1,0:T(8,128)(2,1)S(1)}, u32[]{:S(2)}, u32[]{:S(2)}) collective-permute-start(bf16[128,1024]{1,0:T(8,128)(2,1)} %get-tuple-element.50), channel_id=1, source_target_pairs={{0,32},{16,48},{32,64},{48,80},{64,96},{80,112},{96,0},{112,16},{1... | collective-permute-start | bytes 786440 | tf_op jit(solution)/shard_map/ppermute | solution.py:473
  95.2 14.9 %collective-permute-start.3 = (bf16[128,1024]{1,0:T(8,128)(2,1)}, bf16[128,1024]{1,0:T(8,128)(2,1)}, u32[]{:S(2)}, u32[]{:S(2)}) collective-permute-start(bf16[128,1024]{1,0:T(8,128)(2,1)} %get-tuple-element.51), channel_id=1, source_target_pairs={{0,48},{16,64},{32,80},{48,96},{64,112},{80,0},{96,16},{112,32},{1... | collective-permute-start | bytes 786440 | tf_op jit(solution)/shard_map/ppermute | solution.py:473
  101.1 41.3 %copy-start.4 = (bf16[128,1024]{1,0:T(8,128)(2,1)}, bf16[128,1024]{1,0:T(8,128)(2,1)S(1)}, u32[]{:S(2)}) copy-start(bf16[128,1024]{1,0:T(8,128)(2,1)S(1)} %collective-permute-done.1.rest_1_) | copy-start | bytes 786436
  108.6 0.7 copy-start.5
  128.2 6.5 %collective-permute-start.6 = (bf16[3,32,1024]{2,1,0:T(8,128)(2,1)S(1)}, bf16[3,32,1024]{2,1,0:T(8,128)(2,1)S(1)}, u32[]{:S(2)}, u32[]{:S(2)}) collective-permute-start(bf16[3,32,1024]{2,1,0:T(8,128)(2,1)S(1)} %sum_parts.1.a_ref), channel_id=1, source_target_pairs={{0,96},{16,112},{32,0},{48,16},{64,32},{80,48},{96,64},{112,80},{1... | collective-permute-start | bytes 589832 | tf_op jit(solution)/shard_map/ppermute | solution.py:479
  130.4 6.1 %collective-permute-start.5 = (bf16[3,32,1024]{2,1,0:T(8,128)(2,1)S(1)}, bf16[3,32,1024]{2,1,0:T(8,128)(2,1)S(1)}, u32[]{:S(2)}, u32[]{:S(2)}) collective-permute-start(bf16[3,32,1024]{2,1,0:T(8,128)(2,1)S(1)} %sum_parts.1.a_ref), channel_id=1, source_target_pairs={{0,64},{16,80},{32,96},{48,112},{64,0},{80,16},{96,32},{112,48},{1... | collective-permute-start | bytes 589832 | tf_op jit(solution)/shard_map/ppermute | solution.py:479
  130.4 11.4 %collective-permute-start.4 = (bf16[3,32,1024]{2,1,0:T(8,128)(2,1)S(1)}, bf16[3,32,1024]{2,1,0:T(8,128)(2,1)S(1)}, u32[]{:S(2)}, u32[]{:S(2)}) collective-permute-start(bf16[3,32,1024]{2,1,0:T(8,128)(2,1)S(1)} %sum_parts.1.a_ref), channel_id=1, source_target_pairs={{0,32},{16,48},{32,64},{48,80},{64,96},{80,112},{96,0},{112,16},{1... | collective-permute-start | bytes 589832 | tf_op jit(solution)/shard_map/ppermute | solution.py:479
  142.4 1.6 copy-start.1
  144.0 52.4 %all-to-all-start.2 = ((bf16[16,3,32,1024]{3,2,1,0:T(8,128)(2,1)}), bf16[16,3,32,1024]{3,2,1,0:T(8,128)(2,1)S(1)}, u32[]{:S(2)}, u32[]{:S(2)}) async-start(bf16[16,3,32,1024]{3,2,1,0:T(8,128)(2,1)} %copy-done.1), calls=%async_computation.2 | async-start | bytes 6291456 | tf_op jit(solution)/shard_map/all_to_all | solution.py:481
  156.0 8.5 %collective-permute-start.7 = (bf16[128,1024]{1,0:T(8,128)(2,1)}, bf16[128,1024]{1,0:T(8,128)(2,1)S(1)}, u32[]{:S(2)}, u32[]{:S(2)}) collective-permute-start(bf16[128,1024]{1,0:T(8,128)(2,1)} %get-tuple-element.57), channel_id=1, source_target_pairs={{0,64},{16,80},{32,96},{48,112},{64,0},{80,16},{96,32},{112,48},{1... | collective-permute-start | bytes 786440 | tf_op jit(solution)/shard_map/ppermute | solution.py:473
  156.3 13.3 %collective-permute-start.8 = (bf16[128,1024]{1,0:T(8,128)(2,1)}, bf16[128,1024]{1,0:T(8,128)(2,1)S(1)}, u32[]{:S(2)}, u32[]{:S(2)}) collective-permute-start(bf16[128,1024]{1,0:T(8,128)(2,1)} %get-tuple-element.58), channel_id=1, source_target_pairs={{0,80},{16,96},{32,112},{48,0},{64,16},{80,32},{96,48},{112,64},{1... | collective-permute-start | bytes 786440 | tf_op jit(solution)/shard_map/ppermute | solution.py:473
  158.6 17.3 %collective-permute-start.9 = (bf16[128,1024]{1,0:T(8,128)(2,1)}, bf16[128,1024]{1,0:T(8,128)(2,1)S(1)}, u32[]{:S(2)}, u32[]{:S(2)}) collective-permute-start(bf16[128,1024]{1,0:T(8,128)(2,1)} %get-tuple-element.59), channel_id=1, source_target_pairs={{0,96},{16,112},{32,0},{48,16},{64,32},{80,48},{96,64},{112,80},{1... | collective-permute-start | bytes 786440 | tf_op jit(solution)/shard_map/ppermute | solution.py:473
  160.7 16.5 %collective-permute-start.10 = (bf16[128,1024]{1,0:T(8,128)(2,1)}, bf16[128,1024]{1,0:T(8,128)(2,1)}, u32[]{:S(2)}, u32[]{:S(2)}) collective-permute-start(bf16[128,1024]{1,0:T(8,128)(2,1)} %get-tuple-element.60), channel_id=1, source_target_pairs={{0,112},{16,0},{32,16},{48,32},{64,48},{80,64},{96,80},{112,96},{1... | collective-permute-start | bytes 786440 | tf_op jit(solution)/shard_map/ppermute | solution.py:473
  164.5 12.7 %copy-start.6 = (bf16[128,1024]{1,0:T(8,128)(2,1)}, bf16[128,1024]{1,0:T(8,128)(2,1)S(1)}, u32[]{:S(2)}) copy-start(bf16[128,1024]{1,0:T(8,128)(2,1)S(1)} %collective-permute-done.7.rest_4_) | copy-start | bytes 786436
  169.5 7.7 %copy-start.7 = (bf16[128,1024]{1,0:T(8,128)(2,1)}, bf16[128,1024]{1,0:T(8,128)(2,1)S(1)}, u32[]{:S(2)}) copy-start(bf16[128,1024]{1,0:T(8,128)(2,1)S(1)} %collective-permute-done.8.rest_5_) | copy-start | bytes 786436
  175.8 1.4 copy-start.8
  196.4 8.8 %collective-permute-start.11 = (bf16[16,3,32,1024]{3,2,1,0:T(8,128)(2,1)S(1)}, bf16[16,3,32,1024]{3,2,1,0:T(8,128)(2,1)S(1)}, u32[]{:S(2)}, u32[]{:S(2)}) collective-permute-start(bf16[16,3,32,1024]{3,2,1,0:T(8,128)(2,1)S(1)} %all-to-all-done.2.rows_ref), channel_id=1, source_target_pairs={{0,16},{16,0},{32,48},{48,32},{64,80},{80,64},{96,112},{112,96},{1... | collective-permute-start | bytes 9437192 | tf_op jit(solution)/shard_map/ppermute | solution.py:484
